TPU v7x, 32 devices: a whole 2x2x4 slice. The times are simulated.
32 devices in a mesh: bead: 16 (over z, x, core), space: 2 (over y).
Axes of the slice: x: 2, y: 2, z: 4, core: 2. Of those that a mesh axis runs over, the one named last changes fastest.
Arguments:
- positions: float32 [16, 3, 1024], P('bead', None, 'space'), may hold values from -6 to 6
- momenta: float32 [16, 3, 1024], P('bead', None, 'space'), may hold values from -6 to 6
- species: int32 [1024], P('space'), may hold values from 0 to 1
- neighbours: int32 [8, 1024], P(None, 'space'), may hold values from 0 to 1023
- send_list: int32 [1024], P('space'), may hold values from 0 to 511
- embedding: float32 [2, 128], replicated, may hold values from -4 to 4
- radial_one: float32 [8, 128], replicated, may hold values from -4 to 4
- radial_two: float32 [8, 128], replicated, may hold values from -4 to 4
- mix_one: float32 [128, 384], replicated, may hold values from -0.3125 to 0.3125
- mix_two: float32 [128, 384], replicated, may hold values from -0.3125 to 0.3125
- read_one: float32 [128], replicated, may hold values from -0.5 to 0.5
- read_two: float32 [128], replicated, may hold values from -0.5 to 0.5
Outputs:
- new_positions: float32 [16, 3, 1024], P('bead', None, 'space')
- new_momenta: float32 [16, 3, 1024], P('bead', None, 'space')
Inputs may be any that keep to these rules, and one draw needn't show every extreme that they name: `neighbours`: positions in the extended set of the atom's own domain: below 256 the ghosts from the lower domain, then the 512 own atoms, then the ghosts from the upper domain. `send_list`: entries d * 512 to d * 512 + 255 are sent to domain d - 1, the next 256 to domain d + 1.
All inputs are finite; a program needn't handle non-finite values.
Results may differ from a plain program's by a relative error of at most 0.0003.
Values sent between devices are 32-bit elements; how exact they have to be, the bound alone decides.
No kernel may reach another device: no remote copies, remote signals or barrier semaphores. Data moves between devices by JAX's collectives and lax.ppermute only.
A program may use at most 128 MiB of HBM per device.

v0:
```python
import functools
import math

import jax
import jax.numpy as jnp
import numpy as np
from jax import lax
from jax.experimental import pallas as pl
from jax.experimental.pallas import tpu as pltpu
from jax.sharding import PartitionSpec as P

STEP = 2.0
HALF_STEP = 1.0
HEAVY = 16.0
SQRT3 = math.sqrt(3.0)
SQRT5 = math.sqrt(5.0)
SQRT15 = math.sqrt(15.0)
LANES = 128
ORDERS = 9
GROUP = (0, 1, 1, 1, 2, 2, 2, 2, 2)
HEAD = 8
MIB = 1024 * 1024
f32 = jnp.float32
bf16 = jnp.bfloat16
HIGH = lax.Precision.HIGH


def split(x):
    hi = x.astype(bf16)
    return hi, (x - hi.astype(f32)).astype(bf16)


def split_rows(x):
    hi = x.astype(bf16).astype(f32)
    return jnp.concatenate([hi, x - hi], axis=0)


def dot(a, b, precision=None):
    return jnp.dot(a, b, preferred_element_type=f32, precision=precision)


def dot_nt(a, b):
    return lax.dot_general(a, b, (((1,), (1,)), ((), ())), preferred_element_type=f32)


def row(x, rows=8):
    return jnp.broadcast_to(x, (rows, x.shape[1]))


def lookup(chunks, wanted, position):
    out = None
    for number, chunk in chunks:
        got = jnp.take_along_axis(row(chunk), position, axis=1, mode="promise_in_bounds")
        out = got if out is None else jnp.where(wanted == number, got, out)
    return out


def harmonics(ux, uy, uz):
    return [
        None,
        SQRT3 * ux,
        SQRT3 * uy,
        SQRT3 * uz,
        SQRT15 * ux * uy,
        SQRT15 * uy * uz,
        0.5 * SQRT5 * (2.0 * uz * uz - ux * ux - uy * uy),
        SQRT15 * ux * uz,
        0.5 * SQRT15 * (ux * ux - uy * uy),
    ]


def silu_parts(v):
    gate = 1.0 / (1.0 + jnp.exp(-v))
    return v * gate, gate * (1.0 + v * (1.0 - gate))


def force_kernel(plan, *refs):
    atoms, near, wide, before, after = plan
    n_wide = len(wide)
    blocks = refs[:n_wide]
    sources = refs[n_wide : n_wide + 8]
    push_ref, mass_ref = refs[n_wide + 8 : n_wide + 10]
    (
        geo_ref, y_ref, yb_ref, bk_ref, bt_ref, gidx_ref, as_ref, m1_ref, sp1_ref, hs_ref, oh_ref,
        hj_ref, w_ref, car_ref, m2_ref, inv_ref, dinv_ref, p_ref, dhe_ref, dw_ref, da_ref, q_ref,
        val_ref, ohlo_ref, moment_ref, emb_ref, rad1_ref, rad2_ref, mix1_ref, mix2_ref, read1_ref, read2_ref, sems,
    ) = refs[n_wide + 10 :]
    held = (moment_ref, emb_ref, rad1_ref, rad2_ref, mix1_ref, mix2_ref, read1_ref, read2_ref)
    fetches = [pltpu.make_async_copy(src, dst, sems.at[i]) for i, (src, dst) in enumerate(zip(sources, held))]
    for fetch in fetches:
        fetch.start()
    chan = emb_ref.shape[1]
    bases = rad1_ref.shape[0]
    slots = gidx_ref.shape[0]
    n_near = len(near) * atoms
    tiles = atoms // LANES
    half = atoms // 2
    half_tiles = half // LANES
    edges = slots * atoms
    top_rows = val_ref.shape[0] // 6

    order_col = lax.broadcasted_iota(jnp.int32, (bases, LANES), 0).astype(f32)
    tables = []
    for quantity in range(4):
        chunks = []
        for g in range(n_wide):
            for t in range(tiles):
                chunks.append((g * tiles + t, blocks[g][quantity : quantity + 1, t * LANES : (t + 1) * LANES]))
        tables.append(chunks)
    for q in range(len(near)):
        ghosts = []
        for t in range(half_tiles):
            ghosts.append(
                (t, blocks[before[q]][4:5, half + t * LANES : half + (t + 1) * LANES] + float(before[q] * atoms))
            )
        for t in range(half_tiles):
            ghosts.append(
                (
                    half_tiles + tiles + t,
                    blocks[after[q]][4:5, t * LANES : (t + 1) * LANES] + float(after[q] * atoms),
                )
            )
        for t in range(tiles):
            cols = slice(t * LANES, (t + 1) * LANES)
            here = slice(q * atoms + t * LANES, q * atoms + (t + 1) * LANES)
            slot = blocks[q][HEAD : HEAD + slots, cols].astype(jnp.int32)
            chunk_no = slot >> 7
            far = lookup(ghosts, chunk_no, slot & 127).astype(jnp.int32)
            own = (slot >= half) & (slot < half + atoms)
            gidx = jnp.where(own, slot + (q * atoms - half), far)
            gidx_ref[:, here] = gidx
            chunk_no = gidx >> 7
            place = gidx & 127
            xj, yj, zj, fj = [lookup(tables[i], chunk_no, place) for i in range(4)]
            rx = xj - row(blocks[q][0:1, cols])
            ry = yj - row(blocks[q][1:2, cols])
            rz = zj - row(blocks[q][2:3, cols])
            soft = jnp.sqrt(rx * rx + ry * ry + rz * rz + 1.0)
            back = 1.0 / soft
            ux, uy, uz = rx * back, ry * back, rz * back
            for i, value in enumerate((ux, uy, uz, back, soft, fj)):
                geo_ref[i, :, here] = value
            sphere = harmonics(ux, uy, uz)
            for l in range(1, ORDERS):
                y_ref[l, :, here] = sphere[l]
                if q == 0:
                    for k in range(slots):
                        yb_ref[l, k, :, cols] = row(sphere[l][k : k + 1, :])
            for n in range(bases):
                bk_ref[n, :, here] = jnp.exp(-0.5 * (soft - (1.0 + n)) ** 2)
            for k in range(slots):
                basis = jnp.exp(-0.5 * (row(soft[k : k + 1, :], bases) - (1.0 + order_col)) ** 2)
                bt_ref[k, 0:bases, here] = basis
                bt_ref[k, bases : 2 * bases, here] = basis * row(fj[k : k + 1, :], bases)

    for fetch in fetches:
        fetch.wait()
    emb0 = emb_ref[0:1, :]
    emb_d = emb_ref[1:2, :] - emb0
    rr = jnp.concatenate([rad1_ref[...] * emb0, rad1_ref[...] * emb_d], axis=0) * (1.0 / slots)
    rr_hi = rr.astype(bf16).astype(f32)
    rr_lo = rr - rr_hi
    r2 = rad2_ref[...] * (1.0 / slots)
    r2_hi = r2.astype(bf16).astype(f32)
    r2_lo = r2 - r2_hi
    zeros = jnp.zeros((8, chan), f32)
    turned1 = jnp.concatenate([rr_hi, rr_hi, rr_lo, rr_lo] + [zeros] * 8, axis=0).T
    sides = jnp.concatenate([emb0, emb_d, read1_ref[...], read2_ref[...], zeros[:4]], axis=0)
    turned2 = jnp.concatenate([r2_hi, r2_hi, r2_lo, r2_lo, sides] + [zeros] * 11, axis=0).T
    rr_cols = turned1[:, : 8 * bases].astype(bf16)
    r2_cols = turned2[:, : 4 * bases].astype(bf16)
    emb0_col = turned2[:, 4 * bases : 4 * bases + 1]
    embd_col = turned2[:, 4 * bases + 1 : 4 * bases + 2]
    read1_col = turned2[:, 4 * bases + 2 : 4 * bases + 3]
    read2_col = turned2[:, 4 * bases + 3 : 4 * bases + 4]
    rr_rows = jnp.concatenate(
        [jnp.concatenate([rr_hi, rr_hi], axis=1), jnp.concatenate([rr_lo, jnp.zeros_like(rr_lo)], axis=1)], axis=0
    ).astype(bf16)
    r2_rows = jnp.concatenate(
        [jnp.concatenate([r2_hi, r2_hi], axis=1), jnp.concatenate([r2_lo, jnp.zeros_like(r2_lo)], axis=1)], axis=0
    ).astype(bf16)

    def sums(t, carry):
        here = pl.ds(pl.multiple_of(t * LANES, LANES), LANES)
        low = [None] * ORDERS
        for k in range(slots):
            basis = bt_ref[k, :, here]
            for l in range(ORDERS):
                term = basis if l == 0 else basis * row(y_ref[l, k : k + 1, here], 2 * bases)
                low[l] = term if low[l] is None else low[l] + term
        for l in range(ORDERS):
            both = split_rows(low[l]).astype(bf16)
            as_ref[l, 0 : 4 * bases, here] = both
            as_ref[l, 4 * bases : 8 * bases, here] = both
        return carry

    lax.fori_loop(0, n_near // LANES, sums, 0)

    flags_row = jnp.concatenate([blocks[q][3:4, :] for q in range(len(near))], axis=1)
    wide_cols = 2 * LANES

    def first(j, carry):
        here = pl.ds(pl.multiple_of(j * wide_cols, wide_cols), wide_cols)
        inv = [None, None, None]
        for l in range(ORDERS):
            m = dot(rr_cols, as_ref[l, :, here])
            m1_ref[l, :, here] = m
            inv[GROUP[l]] = m * m if inv[GROUP[l]] is None else inv[GROUP[l]] + m * m
        value = dot(mix1_ref[...], jnp.concatenate(inv, axis=0), HIGH)
        act, slope = silu_parts(value)
        sp1_ref[:, here] = slope
        hidden = act + emb0_col + embd_col * q_ref[0:1, here]
        hi, lo = split(hidden)
        hs_ref[0:chan, here] = hi
        hs_ref[chan : 2 * chan, here] = lo
        return carry

    q_ref[0:1, :] = flags_row
    lax.fori_loop(0, n_near // wide_cols, first, 0)

    def gather(k, carry):
        here = pl.ds(pl.multiple_of(k * atoms, atoms), atoms)
        wanted = gidx_ref[pl.ds(k, 1), 0:atoms]
        for r in range(n_near // LANES):
            ids = lax.broadcasted_iota(jnp.int32, (LANES, atoms), 0) + r * LANES
            oh_ref[r * LANES : (r + 1) * LANES, here] = jnp.where(ids == wanted, 1.0, 0.0).astype(bf16)
        both = dot(hs_ref[...], oh_ref[:, here])
        feat = both[:chan] + both[chan:]
        basis = split_rows(bt_ref[k, 0:bases, 0:atoms])
        weight = dot(r2_cols, jnp.concatenate([basis, basis], axis=0).astype(bf16))
        hj_ref[:, here] = feat
        w_ref[:, here] = weight
        car_ref[:, here] = feat * weight
        return carry

    lax.fori_loop(0, slots, gather, 0)

    pairs = chan // 16

    def moments(step, carry):
        t = step // pairs
        c = step % pairs
        cols = pl.ds(pl.multiple_of(t * LANES, LANES), LANES)
        base = pl.multiple_of(c * 16, 16)
        acc = [[None] * ORDERS, [None] * ORDERS]
        for k in range(slots):
            at = pl.ds(pl.multiple_of(k * atoms + t * LANES, LANES), LANES)
            got = car_ref[pl.ds(base, 16), at]
            for l in range(ORDERS):
                yb = yb_ref[l, k, :, cols] if l else None
                for h in range(2):
                    part = got[8 * h : 8 * h + 8]
                    term = part * yb if l else part
                    acc[h][l] = term if acc[h][l] is None else acc[h][l] + term
        inv = [[None] * 3, [None] * 3]
        for l in range(ORDERS):
            m2_ref[l, pl.ds(base, 16), cols] = jnp.concatenate([acc[0][l], acc[1][l]], axis=0)
            for h in range(2):
                sq = acc[h][l] * acc[h][l]
                g = GROUP[l]
                inv[h][g] = sq if inv[h][g] is None else inv[h][g] + sq
        for g in range(3):
            inv_ref[pl.ds(pl.multiple_of(g * chan + c * 16, 16), 16), cols] = jnp.concatenate(
                [inv[0][g], inv[1][g]], axis=0
            )
        return carry

    lax.fori_loop(0, tiles * pairs, moments, 0)

    for t in range(atoms // wide_cols):
        cols = slice(t * wide_cols, (t + 1) * wide_cols)
        value = dot(mix2_ref[...], inv_ref[:, cols], HIGH)
        _, slope = silu_parts(value)
        slope = slope * (2.0 * read2_col)
        for g in range(3):
            mixed = mix2_ref[:, g * chan : (g + 1) * chan].T
            dinv_ref[g * chan : (g + 1) * chan, cols] = dot(mixed, slope, HIGH)

    k_step = slots // 2

    def back_moments(step, carry):
        t = step // 2
        k0 = (step % 2) * k_step
        cols = pl.ds(pl.multiple_of(t * LANES, LANES), LANES)

        def over(c, acc):
            acc = list(acc)
            base = pl.multiple_of(c * 16, 16)
            dm = []
            scale = [dinv_ref[pl.ds(pl.multiple_of(g * chan + c * 16, 16), 16), cols] for g in range(3)]
            for l in range(ORDERS):
                dm.append(m2_ref[l, pl.ds(base, 16), cols] * scale[GROUP[l]])
            for kk in range(k_step):
                k = k0 + kk
                at = pl.ds(pl.multiple_of(k * atoms + t * LANES, LANES), LANES)
                got = car_ref[pl.ds(base, 16), at]
                out = [dm[0][:8], dm[0][8:]]
                for l in range(1, ORDERS):
                    yb = yb_ref[l, k, :, cols]
                    i = kk * (ORDERS - 1) + l - 1
                    for h in range(2):
                        part = dm[l][8 * h : 8 * h + 8]
                        out[h] = out[h] + part * yb
                        acc[i] = acc[i] + part * got[8 * h : 8 * h + 8]
                dcar = jnp.concatenate(out, axis=0)
                for ref, other in ((dhe_ref, w_ref), (dw_ref, hj_ref)):
                    hi, lo = split(dcar * other[pl.ds(base, 16), at])
                    ref[pl.ds(base, 16), at] = hi
                    ref[pl.ds(pl.multiple_of(chan + c * 16, 16), 16), at] = lo
            return tuple(acc)

        start = tuple(jnp.zeros((8, LANES), f32) for _ in range(k_step * (ORDERS - 1)))
        acc = lax.fori_loop(0, pairs, over, start)
        for kk in range(k_step):
            for l in range(1, ORDERS):
                p_ref[l, pl.ds(pl.multiple_of((k0 + kk) * 8, 8), 8), cols] = acc[kk * (ORDERS - 1) + l - 1]
        return carry

    lax.fori_loop(0, tiles * 2, back_moments, 0)

    for k in range(slots):
        here = slice(k * atoms, (k + 1) * atoms)
        both = dot(r2_rows, dw_ref[:, here])
        dbasis = both[:bases] + both[bases:]
        basis = bt_ref[k, 0:bases, 0:atoms]
        reach = 1.0 + lax.broadcasted_iota(jnp.int32, (bases, atoms), 0).astype(f32)
        p_ref[0, k * 8 : k * 8 + 8, :] = dbasis * basis * (reach - row(geo_ref[4, k : k + 1, 0:atoms], bases))

    def back_first(j, carry):
        start = pl.multiple_of(j * wide_cols, wide_cols)
        here = pl.ds(start, wide_cols)
        both = dot_nt(dhe_ref[...], oh_ref[here, :])
        dh = both[:chan] + both[chan:]
        mine = jnp.where(start < atoms, 1.0, 0.0)
        dtop = (dh + read1_col * mine) * sp1_ref[:, here] * 2.0
        scale = []
        for g in range(3):
            scale.append(dot(mix1_ref[:, g * chan : (g + 1) * chan].T, dtop, HIGH))
        for l in range(ORDERS):
            hi, lo = split(m1_ref[l, :, here] * scale[GROUP[l]])
            out = dot(rr_rows, jnp.concatenate([hi, lo], axis=0))
            da_ref[l, :, here] = out[: 2 * bases] + out[2 * bases :]
        return carry

    lax.fori_loop(0, n_near // wide_cols, back_first, 0)

    lane = lax.broadcasted_iota(jnp.int32, (slots, 16 * slots), 1)
    sub = lax.broadcasted_iota(jnp.int32, (slots, 16 * slots), 0)
    adder = jnp.where(((lane >> 3) & (slots - 1)) == sub, 1.0, 0.0).astype(bf16)
    for l in range(ORDERS):
        q_ref[8 * l : 8 * l + 8, 0:atoms] = dot(adder, split_rows(p_ref[l, :, :]).astype(bf16))

    def back_geometry(t, mine):
        here = pl.ds(pl.multiple_of(t * LANES, LANES), LANES)
        ux, uy, uz, back, soft, fj = [geo_ref[i, :, here] for i in range(6)]
        dy = [None] * ORDERS
        ds = None
        for n in range(bases):
            basis = bk_ref[n, :, here]
            db = None
            for l in range(ORDERS):
                g = row(da_ref[l, n : n + 1, here]) + fj * row(da_ref[l, bases + n : bases + n + 1, here])
                if l:
                    dy[l] = g * basis if dy[l] is None else dy[l] + g * basis
                    db = db + g * y_ref[l, :, here]
                else:
                    db = g
            db = db * basis * ((1.0 + n) - soft)
            ds = db if ds is None else ds + db
        if mine:
            ds = ds + q_ref[0:8, here]
            for l in range(1, ORDERS):
                dy[l] = dy[l] + q_ref[8 * l : 8 * l + 8, here]
        dux = SQRT3 * dy[1] + SQRT15 * (uy * dy[4] + uz * dy[7] + ux * dy[8]) - SQRT5 * ux * dy[6]
        duy = SQRT3 * dy[2] + SQRT15 * (ux * dy[4] + uz * dy[5] - uy * dy[8]) - SQRT5 * uy * dy[6]
        duz = SQRT3 * dy[3] + SQRT15 * (uy * dy[5] + ux * dy[7]) + 2.0 * SQRT5 * uz * dy[6]
        along = ds - (ux * dux + uy * duy + uz * duz) * back
        dr = [dux * back + along * ux, duy * back + along * uy, duz * back + along * uz]
        for i in range(3):
            geo_ref[i, :, here] = dr[i]
        return dr

    def mine_tile(t, carry):
        back_geometry(t, True)
        return carry

    def other_tile(t, carry):
        back_geometry(t, False)
        return carry

    lax.fori_loop(0, tiles, mine_tile, 0)
    lax.fori_loop(tiles, n_near // LANES, other_tile, 0)

    def place_tile(t, carry):
        here = pl.ds(pl.multiple_of(t * LANES, LANES), LANES)
        gidx = gidx_ref[:, here]
        chunk_no = gidx >> 7
        place = gidx & 127
        parts = []
        for i in range(3):
            value = geo_ref[i, :, here]
            hi = value.astype(bf16).astype(f32)
            parts.append((hi, value - hi))
        chunk_ids = lax.broadcasted_iota(jnp.int32, (top_rows, LANES), 0)
        place_ids = lax.broadcasted_iota(jnp.int32, (LANES, LANES), 0)
        for k in range(slots):
            at = pl.ds(pl.multiple_of(k * n_near + t * LANES, LANES), LANES)
            hit = chunk_ids == row(chunk_no[k : k + 1, :], top_rows)
            for i in range(3):
                both = [jnp.where(hit, row(part[k : k + 1, :], top_rows), 0.0) for part in parts[i]]
                val_ref[2 * i * top_rows : 2 * (i + 1) * top_rows, at] = jnp.concatenate(both, axis=0).astype(bf16)
            ohlo_ref[:, at] = jnp.where(place_ids == row(place[k : k + 1, :], LANES), 1.0, 0.0).astype(bf16)
        return carry

    lax.fori_loop(0, n_near // LANES, place_tile, 0)
    landed = dot_nt(val_ref[...], ohlo_ref[...])
    lines = push_ref.shape[0] // (n_wide + 1)
    for i in range(3):
        total = (
            landed[2 * i * top_rows : (2 * i + 1) * top_rows] + landed[(2 * i + 1) * top_rows : (2 * i + 2) * top_rows]
        )
        for g in range(n_wide):
            for t in range(tiles):
                cols = slice(t * LANES, (t + 1) * LANES)
                line = total[g * tiles + t : g * tiles + t + 1, :]
                if g < len(near):
                    here = slice(g * atoms + t * LANES, g * atoms + (t + 1) * LANES)
                    line = line - jnp.sum(geo_ref[i, :, here], axis=0, keepdims=True)
                line = -HALF_STEP * line
                at = i * tiles + t
                if g == 0:
                    line = line + moment_ref[i, :, cols]
                    push_ref[at : at + 1, :] = blocks[0][i : i + 1, cols]
                push_ref[(1 + g) * lines + at : (1 + g) * lines + at + 1, :] = line
                mass = HEAVY - (HEAVY - 1.0) * blocks[g][3:4, cols]
                mass_ref[g * lines + at : g * lines + at + 1, :] = mass
    if lines > 3 * tiles:
        for g in range(n_wide + 1):
            blank = slice(g * lines + 3 * tiles, (g + 1) * lines)
            push_ref[blank, :] = jnp.zeros((lines - 3 * tiles, LANES), f32)
            if g < n_wide:
                mass_ref[blank, :] = jnp.ones((lines - 3 * tiles, LANES), f32)


def line_count(atoms):
    return -(-3 * (atoms // LANES) // 8) * 8


def ring_plan(domains, atoms):
    near = list(dict.fromkeys(o % domains for o in (0, 1, -1)))
    wide = list(dict.fromkeys(near + [o % domains for o in (2, -2)]))
    before = tuple(wide.index((o - 1) % domains) for o in near)
    after = tuple(wide.index((o + 1) % domains) for o in near)
    return atoms, tuple(near), tuple(wide), before, after


def pushes(plan, blocks, momenta, embedding, radial_one, radial_two, mix_one, mix_two, read_one, read_two):
    atoms, near, wide, _, _ = plan
    chan = embedding.shape[1]
    bases = radial_one.shape[0]
    slots = blocks[0].shape[0] - HEAD
    n_near = len(near) * atoms
    edges = slots * atoms
    top_rows = -(-len(wide) * atoms // LANES // 8) * 8
    lines = line_count(atoms)
    vmem = pl.BlockSpec(memory_space=pltpu.VMEM)
    far = pl.BlockSpec(memory_space=pltpu.HBM)
    sources = (momenta, embedding, radial_one, radial_two, mix_one, mix_two, read_one[None], read_two[None])
    return pl.pallas_call(
        functools.partial(force_kernel, plan),
        out_shape=(
            jax.ShapeDtypeStruct(((len(wide) + 1) * lines, LANES), f32),
            jax.ShapeDtypeStruct((len(wide) * lines, LANES), f32),
        ),
        in_specs=[vmem] * len(wide) + [far] * len(sources),
        out_specs=(vmem, vmem),
        scratch_shapes=[
            pltpu.VMEM((6, slots, n_near), f32),
            pltpu.VMEM((ORDERS, slots, n_near), f32),
            pltpu.VMEM((ORDERS, slots, 8, atoms), f32),
            pltpu.VMEM((bases, slots, n_near), f32),
            pltpu.VMEM((slots, 2 * bases, n_near), f32),
            pltpu.VMEM((slots, n_near), jnp.int32),
            pltpu.VMEM((ORDERS, 8 * bases, n_near), bf16),
            pltpu.VMEM((ORDERS, chan, n_near), f32),
            pltpu.VMEM((chan, n_near), f32),
            pltpu.VMEM((2 * chan, n_near), bf16),
            pltpu.VMEM((n_near, edges), bf16),
            pltpu.VMEM((chan, edges), f32),
            pltpu.VMEM((chan, edges), f32),
            pltpu.VMEM((chan, edges), f32),
            pltpu.VMEM((ORDERS, chan, atoms), f32),
            pltpu.VMEM((3 * chan, atoms), f32),
            pltpu.VMEM((3 * chan, atoms), f32),
            pltpu.VMEM((ORDERS, 8 * slots, atoms), f32),
            pltpu.VMEM((2 * chan, edges), bf16),
            pltpu.VMEM((2 * chan, edges), bf16),
            pltpu.VMEM((ORDERS, 2 * bases, n_near), f32),
            pltpu.VMEM((8 * ORDERS, n_near), f32),
            pltpu.VMEM((6 * top_rows, slots * n_near), bf16),
            pltpu.VMEM((LANES, slots * n_near), bf16),
        ]
        + [pltpu.VMEM(source.shape, f32) for source in sources]
        + [pltpu.SemaphoreType.DMA((len(sources),))],
        compiler_params=pltpu.CompilerParams(vmem_limit_bytes=(26 + 10 * len(near)) * MIB),
        name="forces",
    )(*blocks, *sources)


def mode_turns(bead_total):
    bead = np.arange(bead_total, dtype=np.float64)[:, None]
    mode = np.arange(bead_total, dtype=np.float64)[None, :]
    phase = 2.0 * np.pi * bead * mode / bead_total
    half_total = bead_total // 2
    table = math.sqrt(2.0 / bead_total) * np.where(mode < half_total, np.cos(phase), np.sin(phase))
    table = np.where(mode == half_total, np.cos(np.pi * bead) / math.sqrt(bead_total), table)
    table = np.where(mode == 0, 1.0 / math.sqrt(bead_total), table)
    angles = bead_total * np.sin(np.pi * mode[0] / bead_total)
    safe = np.where(mode[0] == 0, 1.0, angles)
    reach = np.where(mode[0] == 0, STEP, STEP * np.sin(angles) / safe)
    stiff = angles * np.sin(angles) / STEP
    return [[float(x) for x in (table * factor[None, :]) @ table[0]] for factor in (np.cos(angles), reach, stiff)]


def pack_kernel(coord_src, species_src, send_src, slot_src, block_ref, coord_ref, species_ref, send_ref, slot_ref, sems):
    pairs = ((coord_src, coord_ref), (species_src, species_ref), (send_src, send_ref), (slot_src, slot_ref))
    fetches = [pltpu.make_async_copy(src, dst, sems.at[i]) for i, (src, dst) in enumerate(pairs)]
    for fetch in fetches:
        fetch.start()
    for fetch in fetches:
        fetch.wait()
    atoms = block_ref.shape[1]
    for i in range(3):
        block_ref[i : i + 1, :] = coord_ref[i]
    block_ref[3:4, :] = species_ref[...].astype(f32)
    block_ref[4:5, :] = send_ref[...].astype(f32)
    block_ref[5:HEAD, :] = jnp.zeros((HEAD - 5, atoms), f32)
    block_ref[HEAD:, :] = slot_ref[...].astype(f32)


def turn_kernel(shape, bead_ref, mass_ref, *refs):
    outer, inner, n_wide = shape
    sources, messages = refs[:outer], refs[outer:]
    turns = mode_turns(outer * inner)
    lines = mass_ref.shape[0] // n_wide
    my_inner = jnp.full((lines, LANES), lax.rem(bead_ref[0], inner))
    for s in range(inner):
        wraps = my_inner + s >= inner
        weights = []
        for turn in turns:
            row_of = []
            for sh in range(outer):
                there = turn[(sh * inner + s) % (outer * inner)]
                round_it = turn[(sh * inner + s - inner) % (outer * inner)]
                row_of.append(jnp.where(wraps, jnp.full((lines, LANES), round_it), jnp.full((lines, LANES), there)))
            weights.append(row_of)
        for g in range(n_wide):
            mass = mass_ref[g * lines : (g + 1) * lines, :]
            turned = drift = spring = None
            for sh in range(outer):
                kick = sources[sh][(1 + g) * lines : (2 + g) * lines, :]
                turned = weights[0][sh] * kick if sh == 0 else turned + weights[0][sh] * kick
                drift = weights[1][sh] * kick if sh == 0 else drift + weights[1][sh] * kick
            new_q = drift / mass
            new_p = turned
            if g == 0:
                for sh in range(outer):
                    coord = sources[sh][0:lines, :]
                    new_q = new_q + weights[0][sh] * coord
                    spring = weights[2][sh] * coord if sh == 0 else spring + weights[2][sh] * coord
                new_p = new_p - mass * spring
            message = messages[g * inner + s]
            message[0:lines, :] = new_q
            message[lines:, :] = new_p


def sum_kernel(*refs):
    q_ref, p_ref = refs[-2:]
    total = refs[0][...]
    for ref in refs[1:-2]:
        total = total + ref[...]
    lines = total.shape[0] // 2
    tiles = q_ref.shape[2] // LANES
    for i in range(3):
        for t in range(tiles):
            at = i * tiles + t
            q_ref[i, :, t * LANES : (t + 1) * LANES] = total[at : at + 1]
            p_ref[i, :, t * LANES : (t + 1) * LANES] = total[lines + at : lines + at + 1]


def shards(
    positions, momenta, species, neighbours, send_list, embedding, radial_one, radial_two, mix_one, mix_two,
    read_one, read_two,
):
    slots, atoms = neighbours.shape
    domains = lax.axis_size("space")
    beads = lax.axis_size("bead")
    inner = next(d for d in range(1, beads + 1) if beads % d == 0 and d * d >= beads)
    outer = beads // inner
    plan = ring_plan(domains, atoms)
    wide = plan[2]
    vmem = pl.BlockSpec(memory_space=pltpu.VMEM)
    smem = pl.BlockSpec(memory_space=pltpu.SMEM)
    far = pl.BlockSpec(memory_space=pltpu.HBM)
    small = pltpu.CompilerParams(vmem_limit_bytes=4 * MIB)
    coord_rows = jnp.transpose(positions, (1, 0, 2))
    moment_rows = jnp.transpose(momenta, (1, 0, 2))
    block = pl.pallas_call(
        pack_kernel,
        out_shape=jax.ShapeDtypeStruct((HEAD + slots, atoms), f32),
        in_specs=[far] * 4,
        out_specs=vmem,
        scratch_shapes=[
            pltpu.VMEM(coord_rows.shape, f32),
            pltpu.VMEM((1, atoms), jnp.int32),
            pltpu.VMEM((1, atoms), jnp.int32),
            pltpu.VMEM((slots, atoms), jnp.int32),
            pltpu.SemaphoreType.DMA((4,)),
        ],
        compiler_params=small,
        name="pack",
    )(coord_rows, species[None], send_list[None], neighbours)
    blocks = [block]
    for offset in wide[1:]:
        blocks.append(lax.ppermute(block, "space", [(i, (i - offset) % domains) for i in range(domains)]))
    pushed, masses = pushes(
        plan, blocks, moment_rows, embedding, radial_one, radial_two, mix_one, mix_two, read_one, read_two
    )
    sources = [pushed]
    for sh in range(1, outer):
        sources.append(lax.ppermute(pushed, "bead", [(b, (b + sh * inner) % beads) for b in range(beads)]))
    bead = lax.axis_index("bead").astype(jnp.int32).reshape(1)
    lines = line_count(atoms)
    messages = pl.pallas_call(
        functools.partial(turn_kernel, (outer, inner, len(wide))),
        out_shape=(jax.ShapeDtypeStruct((2 * lines, LANES), f32),) * (inner * len(wide)),
        in_specs=[smem] + [vmem] * (1 + outer),
        out_specs=(vmem,) * (inner * len(wide)),
        compiler_params=small,
        name="turn",
    )(bead, masses, *sources)
    arrived = []
    for g, offset in enumerate(wide):
        for s in range(inner):
            message = messages[g * inner + s]
            if g or s:
                pairs = []
                for b in range(beads):
                    to_bead = b - b % inner + (b + s) % inner
                    for d in range(domains):
                        pairs.append((b * domains + d, to_bead * domains + (d + offset) % domains))
                message = lax.ppermute(message, ("bead", "space"), pairs)
            arrived.append(message)
    new_q, new_p = pl.pallas_call(
        sum_kernel,
        out_shape=(jax.ShapeDtypeStruct((3, 1, atoms), f32),) * 2,
        in_specs=[vmem] * len(arrived),
        out_specs=(vmem, vmem),
        compiler_params=small,
        name="sum",
    )(*arrived)
    return (jnp.transpose(new_q, (1, 0, 2)), jnp.transpose(new_p, (1, 0, 2)))


def solution(mesh):
    placed = (
        P("bead", None, "space"),
        P("bead", None, "space"),
        P("space"),
        P(None, "space"),
        P("space"),
        P(),
        P(),
        P(),
        P(),
        P(),
        P(),
        P(),
    )
    return jax.shard_map(
        shards,
        mesh=mesh,
        in_specs=placed,
        out_specs=(P("bead", None, "space"), P("bead", None, "space")),
        check_vma=False,
    )
```

profile of v0, /device:TPU:1, one launch (start us, length us, event | category | flops | bytes accessed | tf_op | source)
XLA Modules:
  0.0 58.8 jit_solution(2707331695218524423)
XLA Ops:
  0.7 0.7 %copy-done.8 = s32[512]{0:T(512)S(1)} copy-done((s32[512]{0:T(512)S(1)}, s32[512]{0:T(512)}, u32[]{:S(2)}) %copy-start.8) | copy-done | bytes 2072
  1.3 0.0 copy-done.7
  1.3 0.7 %copy-done.2 = s32[8,512]{1,0:T(8,128)S(1)} copy-done((s32[8,512]{1,0:T(8,128)S(1)}, s32[8,512]{1,0:T(8,128)}, u32[]{:S(2)}) %copy-start.2) | copy-done | bytes 16408
  2.1 0.7 %copy-done.3 = f32[1,3,512]{2,0,1:T(1,128)S(1)} copy-done((f32[1,3,512]{2,0,1:T(1,128)S(1)}, f32[1,3,512]{2,0,1:T(1,128)}, u32[]{:S(2)}) %copy-start.3) | copy-done | bytes 6168
  2.7 0.1 pack.1.refs_0_
  2.8 0.0 copy-start.5
  2.8 2.1 %collective-permute-start = (f32[16,512]{1,0:T(8,128)S(1)}, f32[16,512]{1,0:T(8,128)S(1)}, u32[]{:S(2)}, u32[]{:S(2)}) collective-permute-start(f32[16,512]{1,0:T(8,128)S(1)} %pack.1.refs_0_), channel_id=1, source_target_pairs={{0,1},{1,0},{2,3},{3,2},{4,5},{5,4},{6,7},{7,6},{8,9},{9,8},{10,11... | collective-permute-start | bytes 98312 | tf_op jit(solution)/shard_map/ppermute | solution.py:625
  5.0 1.3 %collective-permute-done.refs_1_ = f32[16,512]{1,0:T(8,128)S(1)} collective-permute-done((f32[16,512]{1,0:T(8,128)S(1)}, f32[16,512]{1,0:T(8,128)S(1)}, u32[]{:S(2)}, u32[]{:S(2)}) %collective-permute-start) | collective-permute-done | bytes 32800 | tf_op jit(solution)/shard_map/ppermute | solution.py:625
  6.3 0.6 %copy-done.9 = f32[2,128]{1,0:T(2,128)S(1)} copy-done((f32[2,128]{1,0:T(2,128)S(1)}, f32[2,128]{1,0:T(2,128)}, u32[]{:S(2)}) %copy-start.9) | copy-done | bytes 1048
  7.0 0.9 %copy-done = f32[128,384]{1,0:T(8,128)S(1)} copy-done((f32[128,384]{1,0:T(8,128)S(1)}, f32[128,384]{1,0:T(8,128)}, u32[]{:S(2)}) %copy-start) | copy-done | bytes 196632
  7.9 0.9 %copy-done.1 = f32[128,384]{1,0:T(8,128)S(1)} copy-done((f32[128,384]{1,0:T(8,128)S(1)}, f32[128,384]{1,0:T(8,128)}, u32[]{:S(2)}) %copy-start.1) | copy-done | bytes 196632
  8.8 27.1 %forces.1 = (f32[48,128]{1,0:T(8,128)S(1)}, f32[32,128]{1,0:T(8,128)S(1)}) custom-call(f32[16,512]{1,0:T(8,128)S(1)} %pack.1.refs_0_, f32[16,512]{1,0:T(8,128)S(1)} %collective-permute-done.refs_1_, f32[3,1,512]{2,1,0:T(1,128)S(1)} %bitcast.10, f32[2,128]{1,0:T(2,128)S(1)} %copy-done.9, f32[8,128]{1,0:T(8,128)S(1)} %copy-done.5, f32[8,128]{1,0:T(8,128)S(1)} %copy-done.6, ...), custom_call_target="tpu_custom_call" | custom-call | tf_op jit(solution)/shard_map/forces/pallas_call | solution.py:469
  35.9 3.6 %collective-permute-start.3 = (f32[48,128]{1,0:T(8,128)S(1)}, f32[48,128]{1,0:T(8,128)S(1)}, u32[]{:S(2)}, u32[]{:S(2)}) collective-permute-start(f32[48,128]{1,0:T(8,128)S(1)} %get-tuple-element.15.refs_0_), channel_id=1, source_target_pairs={{0,24},{2,26},{4,28},{6,30},{8,0},{10,2},{12,4},{14,6},{16,8},{18,... | collective-permute-start | bytes 73736 | tf_op jit(solution)/shard_map/ppermute | solution.py:631
  39.5 0.0 collective-permute-start.2
  39.5 0.4 collective-permute-start.1
  39.9 0.5 collective-permute-done.3.refs_3_
  40.4 2.6 %collective-permute-done.2.refs_2_ = f32[48,128]{1,0:T(8,128)S(1)} collective-permute-done((f32[48,128]{1,0:T(8,128)S(1)}, f32[48,128]{1,0:T(8,128)S(1)}, u32[]{:S(2)}, u32[]{:S(2)}) %collective-permute-start.2) | collective-permute-done | bytes 24608 | tf_op jit(solution)/shard_map/ppermute | solution.py:631
  43.1 0.9 %collective-permute-done.1.refs_1_ = f32[48,128]{1,0:T(8,128)S(1)} collective-permute-done((f32[48,128]{1,0:T(8,128)S(1)}, f32[48,128]{1,0:T(8,128)S(1)}, u32[]{:S(2)}, u32[]{:S(2)}) %collective-permute-start.1) | collective-permute-done | bytes 24608 | tf_op jit(solution)/shard_map/ppermute | solution.py:631
  44.0 0.1 turn.1
  44.0 4.4 %collective-permute-start.4 = (f32[32,128]{1,0:T(8,128)S(1)}, f32[32,128]{1,0:T(8,128)S(1)}, u32[]{:S(2)}, u32[]{:S(2)}) collective-permute-start(f32[32,128]{1,0:T(8,128)S(1)} %get-tuple-element.17), channel_id=1, source_target_pairs={{0,2},{1,3},{2,4},{3,5},{4,6},{5,7},{6,0},{7,1},{8,10},{9,11},{10,... | collective-permute-start | bytes 49160 | tf_op jit(solution)/shard_map/ppermute | solution.py:652
  48.4 0.3 collective-permute-start.5
  48.7 0.2 collective-permute-start.6
  48.9 1.2 %collective-permute-start.7 = (f32[32,128]{1,0:T(8,128)S(1)}, f32[32,128]{1,0:T(8,128)S(1)}, u32[]{:S(2)}, u32[]{:S(2)}) collective-permute-start(f32[32,128]{1,0:T(8,128)S(1)} %get-tuple-element.20), channel_id=1, source_target_pairs={{0,1},{1,0},{2,3},{3,2},{4,5},{5,4},{6,7},{7,6},{8,9},{9,8},{10,11... | collective-permute-start | bytes 49160 | tf_op jit(solution)/shard_map/ppermute | solution.py:652
  50.1 1.7 %collective-permute-start.8 = (f32[32,128]{1,0:T(8,128)S(1)}, f32[32,128]{1,0:T(8,128)S(1)}, u32[]{:S(2)}, u32[]{:S(2)}) collective-permute-start(f32[32,128]{1,0:T(8,128)S(1)} %get-tuple-element.21), channel_id=1, source_target_pairs={{0,3},{1,2},{2,5},{3,4},{4,7},{5,6},{6,1},{7,0},{8,11},{9,10},{10,... | collective-permute-start | bytes 49160 | tf_op jit(solution)/shard_map/ppermute | solution.py:652
  51.9 2.2 %collective-permute-start.9 = (f32[32,128]{1,0:T(8,128)S(1)}, f32[32,128]{1,0:T(8,128)S(1)}, u32[]{:S(2)}, u32[]{:S(2)}) collective-permute-start(f32[32,128]{1,0:T(8,128)S(1)} %get-tuple-element.22), channel_id=1, source_target_pairs={{0,5},{1,4},{2,7},{3,6},{4,1},{5,0},{6,3},{7,2},{8,13},{9,12},{10,... | collective-permute-start | bytes 49160 | tf_op jit(solution)/shard_map/ppermute | solution.py:652
  54.1 0.0 collective-permute-done.5.refs_2_
  54.1 0.0 collective-permute-start.10
  54.1 0.0 collective-permute-done.6.refs_3_
  54.1 0.0 collective-permute-done.8.refs_5_
  54.1 1.4 %collective-permute-done.9.refs_6_ = f32[32,128]{1,0:T(8,128)S(1)} collective-permute-done((f32[32,128]{1,0:T(8,128)S(1)}, f32[32,128]{1,0:T(8,128)S(1)}, u32[]{:S(2)}, u32[]{:S(2)}) %collective-permute-start.9) | collective-permute-done | bytes 16416 | tf_op jit(solution)/shard_map/ppermute | solution.py:652
  55.5 2.7 %collective-permute-done.10.refs_7_ = f32[32,128]{1,0:T(8,128)S(1)} collective-permute-done((f32[32,128]{1,0:T(8,128)S(1)}, f32[32,128]{1,0:T(8,128)S(1)}, u32[]{:S(2)}, u32[]{:S(2)}) %collective-permute-start.10) | collective-permute-done | bytes 16416 | tf_op jit(solution)/shard_map/ppermute | solution.py:652
  58.1 0.6 %sum.1 = (f32[3,1,512]{2,1,0:T(1,128)}, f32[3,1,512]{2,1,0:T(1,128)}) custom-call(f32[32,128]{1,0:T(8,128)S(1)} %get-tuple-element.16.refs_0_, f32[32,128]{1,0:T(8,128)S(1)} %collective-permute-done.4.refs_1_, f32[32,128]{1,0:T(8,128)S(1)} %collective-permute-done.5.refs_2_, f32[32,128]{1,0:T(8,128)S(1)} %collective-permute-done.6.refs_3_, ...), custom_call_target="tpu_custom_call" | custom-call | tf_op jit(solution)/shard_map/sum/pallas_call | solution.py:654
  (18 shorter events, 0.0 us)
Async XLA Ops:
  0.6 0.7 %copy-start.8 = (s32[512]{0:T(512)S(1)}, s32[512]{0:T(512)}, u32[]{:S(2)}) copy-start(s32[512]{0:T(512)} %param.16) | copy-start | bytes 6148
  0.6 0.7 %copy-start.7 = (s32[512]{0:T(512)S(1)}, s32[512]{0:T(512)}, u32[]{:S(2)}) copy-start(s32[512]{0:T(512)} %param.14) | copy-start | bytes 6148
  1.3 0.7 %copy-start.2 = (s32[8,512]{1,0:T(8,128)S(1)}, s32[8,512]{1,0:T(8,128)}, u32[]{:S(2)}) copy-start(s32[8,512]{1,0:T(8,128)} %slot_src.1) | copy-start | bytes 49156
  2.0 0.7 %copy-start.3 = (f32[1,3,512]{2,0,1:T(1,128)S(1)}, f32[1,3,512]{2,0,1:T(1,128)}, u32[]{:S(2)}) copy-start(f32[1,3,512]{2,0,1:T(1,128)} %param.12) | copy-start | bytes 18436
  2.7 3.5 %copy-start.4 = (f32[1,3,512]{2,0,1:T(1,128)S(1)}, f32[1,3,512]{2,0,1:T(1,128)}, u32[]{:S(2)}) copy-start(f32[1,3,512]{2,0,1:T(1,128)} %param.13) | copy-start | bytes 18436
  2.7 3.5 %copy-start.6 = (f32[8,128]{1,0:T(8,128)S(1)}, f32[8,128]{1,0:T(8,128)}, u32[]{:S(2)}) copy-start(f32[8,128]{1,0:T(8,128)} %refs_5_.1) | copy-start | bytes 12292
  2.7 3.5 %copy-start.11 = (f32[128]{0:T(128)S(1)}, f32[128]{0:T(128)}, u32[]{:S(2)}) copy-start(f32[128]{0:T(128)} %param.23) | copy-start | bytes 1540
  2.8 3.5 %copy-start.5 = (f32[8,128]{1,0:T(8,128)S(1)}, f32[8,128]{1,0:T(8,128)}, u32[]{:S(2)}) copy-start(f32[8,128]{1,0:T(8,128)} %refs_4_.1) | copy-start | bytes 12292
  2.8 3.4 %collective-permute-start = (f32[16,512]{1,0:T(8,128)S(1)}, f32[16,512]{1,0:T(8,128)S(1)}, u32[]{:S(2)}, u32[]{:S(2)}) collective-permute-start(f32[16,512]{1,0:T(8,128)S(1)} %pack.1.refs_0_), channel_id=1, source_target_pairs={{0,1},{1,0},{2,3},{3,2},{4,5},{5,4},{6,7},{7,6},{8,9},{9,8},{10,11... | collective-permute-start | bytes 98312 | tf_op jit(solution)/shard_map/ppermute | solution.py:625
  6.3 0.7 %copy-start.9 = (f32[2,128]{1,0:T(2,128)S(1)}, f32[2,128]{1,0:T(2,128)}, u32[]{:S(2)}) copy-start(f32[2,128]{1,0:T(2,128)} %refs_3_.1) | copy-start | bytes 3076
  6.3 0.7 %copy-start.10 = (f32[128]{0:T(128)S(1)}, f32[128]{0:T(128)}, u32[]{:S(2)}) copy-start(f32[128]{0:T(128)} %param.22) | copy-start | bytes 1540
  7.0 0.9 %copy-start = (f32[128,384]{1,0:T(8,128)S(1)}, f32[128,384]{1,0:T(8,128)}, u32[]{:S(2)}) copy-start(f32[128,384]{1,0:T(8,128)} %refs_6_.1) | copy-start | bytes 589828
  7.9 0.9 %copy-start.1 = (f32[128,384]{1,0:T(8,128)S(1)}, f32[128,384]{1,0:T(8,128)}, u32[]{:S(2)}) copy-start(f32[128,384]{1,0:T(8,128)} %refs_7_.1) | copy-start | bytes 589828
  35.9 4.5 %collective-permute-start.3 = (f32[48,128]{1,0:T(8,128)S(1)}, f32[48,128]{1,0:T(8,128)S(1)}, u32[]{:S(2)}, u32[]{:S(2)}) collective-permute-start(f32[48,128]{1,0:T(8,128)S(1)} %get-tuple-element.15.refs_0_), channel_id=1, source_target_pairs={{0,24},{2,26},{4,28},{6,30},{8,0},{10,2},{12,4},{14,6},{16,8},{18,... | collective-permute-start | bytes 73736 | tf_op jit(solution)/shard_map/ppermute | solution.py:631
  39.5 3.6 %collective-permute-start.2 = (f32[48,128]{1,0:T(8,128)S(1)}, f32[48,128]{1,0:T(8,128)S(1)}, u32[]{:S(2)}, u32[]{:S(2)}) collective-permute-start(f32[48,128]{1,0:T(8,128)S(1)} %get-tuple-element.15.refs_0_), channel_id=1, source_target_pairs={{0,16},{2,18},{4,20},{6,22},{8,24},{10,26},{12,28},{14,30},{16,0},... | collective-permute-start | bytes 73736 | tf_op jit(solution)/shard_map/ppermute | solution.py:631
  39.5 4.5 %collective-permute-start.1 = (f32[48,128]{1,0:T(8,128)S(1)}, f32[48,128]{1,0:T(8,128)S(1)}, u32[]{:S(2)}, u32[]{:S(2)}) collective-permute-start(f32[48,128]{1,0:T(8,128)S(1)} %get-tuple-element.15.refs_0_), channel_id=1, source_target_pairs={{0,8},{2,10},{4,12},{6,14},{8,16},{10,18},{12,20},{14,22},{16,24},... | collective-permute-start | bytes 73736 | tf_op jit(solution)/shard_map/ppermute | solution.py:631
  44.0 7.9 %collective-permute-start.4 = (f32[32,128]{1,0:T(8,128)S(1)}, f32[32,128]{1,0:T(8,128)S(1)}, u32[]{:S(2)}, u32[]{:S(2)}) collective-permute-start(f32[32,128]{1,0:T(8,128)S(1)} %get-tuple-element.17), channel_id=1, source_target_pairs={{0,2},{1,3},{2,4},{3,5},{4,6},{5,7},{6,0},{7,1},{8,10},{9,11},{10,... | collective-permute-start | bytes 49160 | tf_op jit(solution)/shard_map/ppermute | solution.py:652
  48.4 5.6 %collective-permute-start.5 = (f32[32,128]{1,0:T(8,128)S(1)}, f32[32,128]{1,0:T(8,128)S(1)}, u32[]{:S(2)}, u32[]{:S(2)}) collective-permute-start(f32[32,128]{1,0:T(8,128)S(1)} %get-tuple-element.18), channel_id=1, source_target_pairs={{0,4},{1,5},{2,6},{3,7},{4,0},{5,1},{6,2},{7,3},{8,12},{9,13},{10,... | collective-permute-start | bytes 49160 | tf_op jit(solution)/shard_map/ppermute | solution.py:652
  48.7 5.4 %collective-permute-start.6 = (f32[32,128]{1,0:T(8,128)S(1)}, f32[32,128]{1,0:T(8,128)S(1)}, u32[]{:S(2)}, u32[]{:S(2)}) collective-permute-start(f32[32,128]{1,0:T(8,128)S(1)} %get-tuple-element.19), channel_id=1, source_target_pairs={{0,6},{1,7},{2,0},{3,1},{4,2},{5,3},{6,4},{7,5},{8,14},{9,15},{10,... | collective-permute-start | bytes 49160 | tf_op jit(solution)/shard_map/ppermute | solution.py:652
  48.9 5.2 %collective-permute-start.7 = (f32[32,128]{1,0:T(8,128)S(1)}, f32[32,128]{1,0:T(8,128)S(1)}, u32[]{:S(2)}, u32[]{:S(2)}) collective-permute-start(f32[32,128]{1,0:T(8,128)S(1)} %get-tuple-element.20), channel_id=1, source_target_pairs={{0,1},{1,0},{2,3},{3,2},{4,5},{5,4},{6,7},{7,6},{8,9},{9,8},{10,11... | collective-permute-start | bytes 49160 | tf_op jit(solution)/shard_map/ppermute | solution.py:652
  50.1 3.9 %collective-permute-start.8 = (f32[32,128]{1,0:T(8,128)S(1)}, f32[32,128]{1,0:T(8,128)S(1)}, u32[]{:S(2)}, u32[]{:S(2)}) collective-permute-start(f32[32,128]{1,0:T(8,128)S(1)} %get-tuple-element.21), channel_id=1, source_target_pairs={{0,3},{1,2},{2,5},{3,4},{4,7},{5,6},{6,1},{7,0},{8,11},{9,10},{10,... | collective-permute-start | bytes 49160 | tf_op jit(solution)/shard_map/ppermute | solution.py:652
  51.9 3.6 %collective-permute-start.9 = (f32[32,128]{1,0:T(8,128)S(1)}, f32[32,128]{1,0:T(8,128)S(1)}, u32[]{:S(2)}, u32[]{:S(2)}) collective-permute-start(f32[32,128]{1,0:T(8,128)S(1)} %get-tuple-element.22), channel_id=1, source_target_pairs={{0,5},{1,4},{2,7},{3,6},{4,1},{5,0},{6,3},{7,2},{8,13},{9,12},{10,... | collective-permute-start | bytes 49160 | tf_op jit(solution)/shard_map/ppermute | solution.py:652
  54.1 4.1 %collective-permute-start.10 = (f32[32,128]{1,0:T(8,128)S(1)}, f32[32,128]{1,0:T(8,128)S(1)}, u32[]{:S(2)}, u32[]{:S(2)}) collective-permute-start(f32[32,128]{1,0:T(8,128)S(1)} %get-tuple-element.23), channel_id=1, source_target_pairs={{0,7},{1,6},{2,1},{3,0},{4,3},{5,2},{6,5},{7,4},{8,15},{9,14},{10,... | collective-permute-start | bytes 49160 | tf_op jit(solution)/shard_map/ppermute | solution.py:652
where the time goes:
time: 59.1 us; the launch traced here: 58.8 us
  Pallas kernels  27.8 us (47%)
  starting transfers between devices  16.2 us (27%)
  waiting for transfers between devices  9.38 us (16%)
  local copies, waits for them, and re-layouts  4.61 us (8%)
  between operations  0.73 us (1%)
    pallas_call x1, Pallas kernels, pushes(): pl.pallas_call(functools.partial(force_kernel, plan), out_shape=(jax.Shap...  27.1 us
    ppermute x7, starting transfers between devices, shards(): message = lax.ppermute(message, ('bead', 'space'), pairs)  10 us
    unnamed x24, local copies, waits for them, and re-layouts  4.61 us
    ppermute x3, starting transfers between devices, shards(): lax.ppermute(pushed, 'bead', [(b, (b + sh * inner) % beads) for b in rang...  4.05 us
    ppermute x7, waiting for transfers between devices, shards(): message = lax.ppermute(message, ('bead', 'space'), pairs)  4.05 us
    ppermute x3, waiting for transfers between devices, shards(): lax.ppermute(pushed, 'bead', [(b, (b + sh * inner) % beads) for b in rang...  4.02 us
    ppermute x1, starting transfers between devices, shards(): lax.ppermute(block, 'space', [(i, (i - offset) % domains) for i in range(...  2.13 us
    ppermute x1, waiting for transfers between devices, shards(): lax.ppermute(block, 'space', [(i, (i - offset) % domains) for i in range(...  1.3 us
  transfers between devices with their start and end apart: 11, of which 6 were waited for; matrix products, arithmetic and copies ran while one was open for 0% of the time, Pallas kernels for 0%

commit v1 on v0

--- a/solution.py
+++ b/solution.py
@@ -414,7 +414,8 @@
 
     lax.fori_loop(0, n_near // LANES, place_tile, 0)
     landed = dot_nt(val_ref[...], ohlo_ref[...])
-    lines = push_ref.shape[0] // (n_wide + 1)
+    lines = push_ref.shape[1] // (n_wide + 1)
+    one = push_ref.at[0]
     for i in range(3):
         total = (
             landed[2 * i * top_rows : (2 * i + 1) * top_rows] + landed[(2 * i + 1) * top_rows : (2 * i + 2) * top_rows]
@@ -430,16 +431,19 @@
                 at = i * tiles + t
                 if g == 0:
                     line = line + moment_ref[i, :, cols]
-                    push_ref[at : at + 1, :] = blocks[0][i : i + 1, cols]
-                push_ref[(1 + g) * lines + at : (1 + g) * lines + at + 1, :] = line
+                    one[at : at + 1, :] = blocks[0][i : i + 1, cols]
+                one[(1 + g) * lines + at : (1 + g) * lines + at + 1, :] = line
                 mass = HEAVY - (HEAVY - 1.0) * blocks[g][3:4, cols]
                 mass_ref[g * lines + at : g * lines + at + 1, :] = mass
     if lines > 3 * tiles:
         for g in range(n_wide + 1):
             blank = slice(g * lines + 3 * tiles, (g + 1) * lines)
-            push_ref[blank, :] = jnp.zeros((lines - 3 * tiles, LANES), f32)
+            one[blank, :] = jnp.zeros((lines - 3 * tiles, LANES), f32)
             if g < n_wide:
                 mass_ref[blank, :] = jnp.ones((lines - 3 * tiles, LANES), f32)
+    whole = push_ref[0]
+    for copy in range(1, push_ref.shape[0]):
+        push_ref[copy] = whole
 
 
 def line_count(atoms):
@@ -454,7 +458,11 @@
     return atoms, tuple(near), tuple(wide), before, after
 
 
-def pushes(plan, blocks, momenta, embedding, radial_one, radial_two, mix_one, mix_two, read_one, read_two):
+def in_hbm(x):
+    return pltpu.with_memory_space_constraint(x, pltpu.HBM)
+
+
+def pushes(plan, outer, blocks, momenta, embedding, radial_one, radial_two, mix_one, mix_two, read_one, read_two):
     atoms, near, wide, _, _ = plan
     chan = embedding.shape[1]
     bases = radial_one.shape[0]
@@ -465,11 +473,14 @@
     lines = line_count(atoms)
     vmem = pl.BlockSpec(memory_space=pltpu.VMEM)
     far = pl.BlockSpec(memory_space=pltpu.HBM)
-    sources = (momenta, embedding, radial_one, radial_two, mix_one, mix_two, read_one[None], read_two[None])
+    sources = [
+        in_hbm(x)
+        for x in (momenta, embedding, radial_one, radial_two, mix_one, mix_two, read_one[None], read_two[None])
+    ]
     return pl.pallas_call(
         functools.partial(force_kernel, plan),
         out_shape=(
-            jax.ShapeDtypeStruct(((len(wide) + 1) * lines, LANES), f32),
+            jax.ShapeDtypeStruct((outer, (len(wide) + 1) * lines, LANES), f32),
             jax.ShapeDtypeStruct((len(wide) * lines, LANES), f32),
         ),
         in_specs=[vmem] * len(wide) + [far] * len(sources),
@@ -538,47 +549,48 @@
     block_ref[HEAD:, :] = slot_ref[...].astype(f32)
 
 
-def turn_kernel(shape, bead_ref, mass_ref, *refs):
-    outer, inner, n_wide = shape
-    sources, messages = refs[:outer], refs[outer:]
+def turn_kernel(shape, bead_ref, mass_ref, source_ref, message_ref):
+    outer, inner, domains, wide = shape
     turns = mode_turns(outer * inner)
-    lines = mass_ref.shape[0] // n_wide
-    my_inner = jnp.full((lines, LANES), lax.rem(bead_ref[0], inner))
+    lines = mass_ref.shape[0] // len(wide)
+    my_domain = bead_ref[1]
+    my_outer = bead_ref[0] // inner
+    my_inner = bead_ref[0] - my_outer * inner
+    if domains > len(wide):
+        message_ref[...] = jnp.zeros_like(message_ref)
+    masses = [mass_ref[g * lines : (g + 1) * lines, :] for g in range(len(wide))]
+    sources = []
+    for z in range(outer):
+        at = lax.rem(my_outer + outer - z, outer)
+        sources.append([source_ref[at, pl.ds(g * lines, lines), :] for g in range(len(wide) + 1)])
     for s in range(inner):
-        wraps = my_inner + s >= inner
+        wraps = jnp.full((lines, LANES), my_inner + s) >= inner
         weights = []
         for turn in turns:
             row_of = []
-            for sh in range(outer):
-                there = turn[(sh * inner + s) % (outer * inner)]
-                round_it = turn[(sh * inner + s - inner) % (outer * inner)]
+            for z in range(outer):
+                there = turn[(z * inner + s) % (outer * inner)]
+                round_it = turn[(z * inner + s - inner) % (outer * inner)]
                 row_of.append(jnp.where(wraps, jnp.full((lines, LANES), round_it), jnp.full((lines, LANES), there)))
             weights.append(row_of)
-        for g in range(n_wide):
-            mass = mass_ref[g * lines : (g + 1) * lines, :]
-            turned = drift = spring = None
-            for sh in range(outer):
-                kick = sources[sh][(1 + g) * lines : (2 + g) * lines, :]
-                turned = weights[0][sh] * kick if sh == 0 else turned + weights[0][sh] * kick
-                drift = weights[1][sh] * kick if sh == 0 else drift + weights[1][sh] * kick
-            new_q = drift / mass
+        to_inner = lax.rem(my_inner + s, inner)
+        for g in range(len(wide)):
+            turned = sum(weights[0][z] * sources[z][1 + g] for z in range(outer))
+            drift = sum(weights[1][z] * sources[z][1 + g] for z in range(outer))
+            new_q = drift / masses[g]
             new_p = turned
             if g == 0:
-                for sh in range(outer):
-                    coord = sources[sh][0:lines, :]
-                    new_q = new_q + weights[0][sh] * coord
-                    spring = weights[2][sh] * coord if sh == 0 else spring + weights[2][sh] * coord
-                new_p = new_p - mass * spring
-            message = messages[g * inner + s]
-            message[0:lines, :] = new_q
-            message[lines:, :] = new_p
-
-
-def sum_kernel(*refs):
-    q_ref, p_ref = refs[-2:]
-    total = refs[0][...]
-    for ref in refs[1:-2]:
-        total = total + ref[...]
+                new_q = new_q + sum(weights[0][z] * sources[z][0] for z in range(outer))
+                new_p = new_p - masses[g] * sum(weights[2][z] * sources[z][0] for z in range(outer))
+            to = to_inner * domains + lax.rem(my_domain + wide[g], domains)
+            message_ref[to, 0:lines, :] = new_q
+            message_ref[to, lines:, :] = new_p
+
+
+def sum_kernel(arrived_ref, q_ref, p_ref):
+    total = arrived_ref[0]
+    for i in range(1, arrived_ref.shape[0]):
+        total = total + arrived_ref[i]
     lines = total.shape[0] // 2
     tiles = q_ref.shape[2] // LANES
     for i in range(3):
@@ -619,46 +631,35 @@
         ],
         compiler_params=small,
         name="pack",
-    )(coord_rows, species[None], send_list[None], neighbours)
+    )(in_hbm(coord_rows), in_hbm(species[None]), in_hbm(send_list[None]), in_hbm(neighbours))
     blocks = [block]
     for offset in wide[1:]:
         blocks.append(lax.ppermute(block, "space", [(i, (i - offset) % domains) for i in range(domains)]))
     pushed, masses = pushes(
-        plan, blocks, moment_rows, embedding, radial_one, radial_two, mix_one, mix_two, read_one, read_two
+        plan, outer, blocks, moment_rows, embedding, radial_one, radial_two, mix_one, mix_two, read_one, read_two
     )
-    sources = [pushed]
-    for sh in range(1, outer):
-        sources.append(lax.ppermute(pushed, "bead", [(b, (b + sh * inner) % beads) for b in range(beads)]))
-    bead = lax.axis_index("bead").astype(jnp.int32).reshape(1)
+    columns = [[z * inner + i for z in range(outer)] for i in range(inner)]
+    sources = lax.all_to_all(pushed, "bead", 0, 0, axis_index_groups=columns, tiled=True)
+    here = jnp.stack([lax.axis_index("bead"), lax.axis_index("space")]).astype(jnp.int32)
     lines = line_count(atoms)
     messages = pl.pallas_call(
-        functools.partial(turn_kernel, (outer, inner, len(wide))),
-        out_shape=(jax.ShapeDtypeStruct((2 * lines, LANES), f32),) * (inner * len(wide)),
-        in_specs=[smem] + [vmem] * (1 + outer),
-        out_specs=(vmem,) * (inner * len(wide)),
+        functools.partial(turn_kernel, (outer, inner, domains, wide)),
+        out_shape=jax.ShapeDtypeStruct((inner * domains, 2 * lines, LANES), f32),
+        in_specs=[smem, vmem, vmem],
+        out_specs=vmem,
         compiler_params=small,
         name="turn",
-    )(bead, masses, *sources)
-    arrived = []
-    for g, offset in enumerate(wide):
-        for s in range(inner):
-            message = messages[g * inner + s]
-            if g or s:
-                pairs = []
-                for b in range(beads):
-                    to_bead = b - b % inner + (b + s) % inner
-                    for d in range(domains):
-                        pairs.append((b * domains + d, to_bead * domains + (d + offset) % domains))
-                message = lax.ppermute(message, ("bead", "space"), pairs)
-            arrived.append(message)
+    )(here, masses, sources)
+    rows = [[z * inner * domains + i for i in range(inner * domains)] for z in range(outer)]
+    arrived = lax.all_to_all(messages, ("bead", "space"), 0, 0, axis_index_groups=rows, tiled=True)
     new_q, new_p = pl.pallas_call(
         sum_kernel,
         out_shape=(jax.ShapeDtypeStruct((3, 1, atoms), f32),) * 2,
-        in_specs=[vmem] * len(arrived),
+        in_specs=[vmem],
         out_specs=(vmem, vmem),
         compiler_params=small,
         name="sum",
-    )(*arrived)
+    )(arrived)
     return (jnp.transpose(new_q, (1, 0, 2)), jnp.transpose(new_p, (1, 0, 2)))
 
 

time: 59.1 us -> 54.9 us (0.929)
  the two profiles are of different devices: /device:TPU:1 before, /device:TPU:0 now
where the time goes in v1:
time: 54.9 us; the launch traced here: 54.6 us
  Pallas kernels  29.3 us (53%)
  blocking collectives  8.47 us (15%)
  starting transfers between devices  8.41 us (15%)
  waiting for transfers between devices  7.65 us (14%)
  between operations  0.66 us (1%)
    pallas_call x1, Pallas kernels, pushes(): pl.pallas_call(functools.partial(force_kernel, plan), out_shape=(jax.Shap...  27.3 us
    all_to_all x1, blocking collectives, shards(): lax.all_to_all(messages, ('bead', 'space'), 0, 0, axis_index_groups=rows,...  8.47 us
    all_to_all x1, waiting for transfers between devices, shards(): lax.all_to_all(pushed, 'bead', 0, 0, axis_index_groups=columns, tiled=True)  5.76 us
    all_to_all x1, starting transfers between devices, shards(): lax.all_to_all(pushed, 'bead', 0, 0, axis_index_groups=columns, tiled=True)  5.38 us
    ppermute x1, starting transfers between devices, shards(): lax.ppermute(block, 'space', [(i, (i - offset) % domains) for i in range(...  3.03 us
    ppermute x1, waiting for transfers between devices, shards(): lax.ppermute(block, 'space', [(i, (i - offset) % domains) for i in range(...  1.89 us
  transfers between devices with their start and end apart: 2, of which 2 were waited for; matrix products, arithmetic and copies ran while one was open for 0% of the time, Pallas kernels for 0%

profile of v1, /device:TPU:0, one launch (start us, length us, event | category | flops | bytes accessed | tf_op | source)
XLA Modules:
  0.0 54.6 jit_solution(4934557807142427276)
XLA Ops:
  0.6 0.8 %pack.1.refs_0_ = f32[16,512]{1,0:T(8,128)S(1)} custom-call(f32[3,1,512]{2,1,0:T(1,128)} %bitcast.10, s32[1,512]{1,0:T(1,128)} %bitcast.12, s32[1,512]{1,0:T(1,128)} %bitcast.13, s32[8,512]{1,0:T(8,128)} %slot_src.1), custom_call_target="tpu_custom_call" | custom-call | tf_op jit(solution)/shard_map/pack/pallas_call | solution.py:620
  1.4 3.0 %collective-permute-start = (f32[16,512]{1,0:T(8,128)S(1)}, f32[16,512]{1,0:T(8,128)S(1)}, u32[]{:S(2)}, u32[]{:S(2)}) collective-permute-start(f32[16,512]{1,0:T(8,128)S(1)} %pack.1.refs_0_), channel_id=1, source_target_pairs={{0,1},{1,0},{2,3},{3,2},{4,5},{5,4},{6,7},{7,6},{8,9},{9,8},{10,11... | collective-permute-start | bytes 98312 | tf_op jit(solution)/shard_map/ppermute | solution.py:637
  4.5 1.9 %collective-permute-done.refs_1_ = f32[16,512]{1,0:T(8,128)S(1)} collective-permute-done((f32[16,512]{1,0:T(8,128)S(1)}, f32[16,512]{1,0:T(8,128)S(1)}, u32[]{:S(2)}, u32[]{:S(2)}) %collective-permute-start) | collective-permute-done | bytes 32800 | tf_op jit(solution)/shard_map/ppermute | solution.py:637
  6.4 27.3 %forces.1 = (f32[4,48,128]{2,1,0:T(8,128)}, f32[32,128]{1,0:T(8,128)S(1)}) custom-call(f32[16,512]{1,0:T(8,128)S(1)} %pack.1.refs_0_, f32[16,512]{1,0:T(8,128)S(1)} %collective-permute-done.refs_1_, f32[3,1,512]{2,1,0:T(1,128)} %bitcast.11, f32[2,128]{1,0:T(2,128)} %refs_3_.1, f32[8,128]{1,0:T(8,128)} %refs_4_.1, f32[8,128]{1,0:T(8,128)} %refs_5_.1, ...), custom_call_target="tpu_custom_call" | custom-call | tf_op jit(solution)/shard_map/forces/pallas_call | solution.py:480
  33.6 5.4 %all-to-all-start = ((f32[4,48,128]{2,1,0:T(8,128)}), f32[4,48,128]{2,1,0:T(8,128)S(1)}, u32[]{:S(2)}, u32[]{:S(2)}) async-start(f32[4,48,128]{2,1,0:T(8,128)} %get-tuple-element.7), calls=%async_computation | async-start | bytes 196608 | tf_op jit(solution)/shard_map/all_to_all | solution.py:642
  39.0 0.1 pad_add_fusion.bead_ref
  39.1 5.8 %all-to-all-done.source_ref = f32[4,48,128]{2,1,0:T(8,128)S(1)} async-done(((f32[4,48,128]{2,1,0:T(8,128)}), f32[4,48,128]{2,1,0:T(8,128)S(1)}, u32[]{:S(2)}, u32[]{:S(2)}) %all-to-all-start) | async-done | bytes 98336 | tf_op jit(solution)/shard_map/all_to_all | solution.py:642
  44.8 0.6 %turn.1 = f32[8,32,128]{2,1,0:T(8,128)S(1)} custom-call(s32[2]{0:T(128)S(1)} %pad_add_fusion.bead_ref, f32[32,128]{1,0:T(8,128)S(1)} %get-tuple-element.6.mass_ref, f32[4,48,128]{2,1,0:T(8,128)S(1)} %all-to-all-done.source_ref), custom_call_target="tpu_custom_call" | custom-call | tf_op jit(solution)/shard_map/turn/pallas_call | solution.py:645
  45.5 8.5 %all_to_all.10.arrived_ref = f32[8,32,128]{2,1,0:T(8,128)S(1)} all-to-all(f32[8,32,128]{2,1,0:T(8,128)S(1)} %turn.1), channel_id=1, replica_groups={{0,1,2,3,4,5,6,7},{8,9,10,11,12,13,14,15},{16,17,18,19,20,21,22,23},{24..., dimensions={0} | all-to-all | bytes 262144 | tf_op jit(solution)/shard_map/all_to_all | solution.py:654
  54.0 0.6 %sum.1 = (f32[3,1,512]{2,1,0:T(1,128)}, f32[3,1,512]{2,1,0:T(1,128)}) custom-call(f32[8,32,128]{2,1,0:T(8,128)S(1)} %all_to_all.10.arrived_ref), custom_call_target="tpu_custom_call" | custom-call | tf_op jit(solution)/shard_map/sum/pallas_call | solution.py:655
Async XLA Ops:
  1.4 4.9 %collective-permute-start = (f32[16,512]{1,0:T(8,128)S(1)}, f32[16,512]{1,0:T(8,128)S(1)}, u32[]{:S(2)}, u32[]{:S(2)}) collective-permute-start(f32[16,512]{1,0:T(8,128)S(1)} %pack.1.refs_0_), channel_id=1, source_target_pairs={{0,1},{1,0},{2,3},{3,2},{4,5},{5,4},{6,7},{7,6},{8,9},{9,8},{10,11... | collective-permute-start | bytes 98312 | tf_op jit(solution)/shard_map/ppermute | solution.py:637
  33.6 11.2 %all-to-all-start = ((f32[4,48,128]{2,1,0:T(8,128)}), f32[4,48,128]{2,1,0:T(8,128)S(1)}, u32[]{:S(2)}, u32[]{:S(2)}) async-start(f32[4,48,128]{2,1,0:T(8,128)} %get-tuple-element.7), calls=%async_computation | async-start | bytes 196608 | tf_op jit(solution)/shard_map/all_to_all | solution.py:642

commit v2 on v1

--- a/solution.py
+++ b/solution.py
@@ -198,9 +198,28 @@
 
     flags_row = jnp.concatenate([blocks[q][3:4, :] for q in range(len(near))], axis=1)
     wide_cols = 2 * LANES
+    ids16 = lax.broadcasted_iota(jnp.int32, (LANES, atoms), 0).astype(jnp.int16)
+    one16 = jnp.ones((LANES, atoms), bf16)
+    zero16 = jnp.zeros((LANES, atoms), bf16)
+
+    def row16(x, rows):
+        return jnp.broadcast_to(x, (rows, x.shape[1])).astype(jnp.int16)
+
+    blocks_of_rows = n_near // LANES
+    builds = slots * blocks_of_rows // (n_near // wide_cols)
+
+    def build(i):
+        k = i // blocks_of_rows
+        r = i % blocks_of_rows
+        wanted = gidx_ref[pl.ds(k, 1), 0:atoms] - r * LANES
+        hit = row16(wanted, LANES) == ids16
+        at = pl.ds(pl.multiple_of(r * LANES, LANES), LANES)
+        oh_ref[at, pl.ds(pl.multiple_of(k * atoms, LANES), atoms)] = jnp.where(hit, one16, zero16)
 
     def first(j, carry):
         here = pl.ds(pl.multiple_of(j * wide_cols, wide_cols), wide_cols)
+        for i in range(builds):
+            build(j * builds + i)
         inv = [None, None, None]
         for l in range(ORDERS):
             m = dot(rr_cols, as_ref[l, :, here])
@@ -220,10 +239,6 @@
 
     def gather(k, carry):
         here = pl.ds(pl.multiple_of(k * atoms, atoms), atoms)
-        wanted = gidx_ref[pl.ds(k, 1), 0:atoms]
-        for r in range(n_near // LANES):
-            ids = lax.broadcasted_iota(jnp.int32, (LANES, atoms), 0) + r * LANES
-            oh_ref[r * LANES : (r + 1) * LANES, here] = jnp.where(ids == wanted, 1.0, 0.0).astype(bf16)
         both = dot(hs_ref[...], oh_ref[:, here])
         feat = both[:chan] + both[chan:]
         basis = split_rows(bt_ref[k, 0:bases, 0:atoms])
@@ -267,14 +282,14 @@
 
     lax.fori_loop(0, tiles * pairs, moments, 0)
 
+    mix2_turned = [mix2_ref[:, g * chan : (g + 1) * chan].T for g in range(3)]
     for t in range(atoms // wide_cols):
         cols = slice(t * wide_cols, (t + 1) * wide_cols)
         value = dot(mix2_ref[...], inv_ref[:, cols], HIGH)
         _, slope = silu_parts(value)
         slope = slope * (2.0 * read2_col)
         for g in range(3):
-            mixed = mix2_ref[:, g * chan : (g + 1) * chan].T
-            dinv_ref[g * chan : (g + 1) * chan, cols] = dot(mixed, slope, HIGH)
+            dinv_ref[g * chan : (g + 1) * chan, cols] = dot(mix2_turned[g], slope, HIGH)
 
     k_step = slots // 2
 
@@ -326,16 +341,18 @@
         reach = 1.0 + lax.broadcasted_iota(jnp.int32, (bases, atoms), 0).astype(f32)
         p_ref[0, k * 8 : k * 8 + 8, :] = dbasis * basis * (reach - row(geo_ref[4, k : k + 1, 0:atoms], bases))
 
+    mix1_turned = [mix1_ref[:, g * chan : (g + 1) * chan].T for g in range(3)]
+
     def back_first(j, carry):
         start = pl.multiple_of(j * wide_cols, wide_cols)
         here = pl.ds(start, wide_cols)
-        both = dot_nt(dhe_ref[...], oh_ref[here, :])
-        dh = both[:chan] + both[chan:]
+        both = dot_nt(oh_ref[here, :], dhe_ref[...])
+        dh = (both[:, :chan] + both[:, chan:]).T
         mine = jnp.where(start < atoms, 1.0, 0.0)
         dtop = (dh + read1_col * mine) * sp1_ref[:, here] * 2.0
         scale = []
         for g in range(3):
-            scale.append(dot(mix1_ref[:, g * chan : (g + 1) * chan].T, dtop, HIGH))
+            scale.append(dot(mix1_turned[g], dtop, HIGH))
         for l in range(ORDERS):
             hi, lo = split(m1_ref[l, :, here] * scale[GROUP[l]])
             out = dot(rr_rows, jnp.concatenate([hi, lo], axis=0))
@@ -413,7 +430,7 @@
         return carry
 
     lax.fori_loop(0, n_near // LANES, place_tile, 0)
-    landed = dot_nt(val_ref[...], ohlo_ref[...])
+    landed = dot_nt(ohlo_ref[...], val_ref[...]).T
     lines = push_ref.shape[1] // (n_wide + 1)
     one = push_ref.at[0]
     for i in range(3):

time: 54.9 us -> 55.8 us (1.016)
  Pallas kernels: 29.3 us -> 30.2 us
    pallas_call x1, Pallas kernels: 27.3 us -> 28.1 us  [pushes(): pl.pallas_call(functools.partial(force_kernel, plan), out_shape=(jax.Shap...]
where the time goes in v2:
time: 55.8 us; the launch traced here: 55.4 us
  Pallas kernels  30.2 us (54%)
  blocking collectives  8.47 us (15%)
  starting transfers between devices  8.41 us (15%)
  waiting for transfers between devices  7.65 us (14%)
  between operations  0.66 us (1%)
    pallas_call x1, Pallas kernels, pushes(): pl.pallas_call(functools.partial(force_kernel, plan), out_shape=(jax.Shap...  28.1 us
    all_to_all x1, blocking collectives, shards(): lax.all_to_all(messages, ('bead', 'space'), 0, 0, axis_index_groups=rows,...  8.47 us
    all_to_all x1, waiting for transfers between devices, shards(): lax.all_to_all(pushed, 'bead', 0, 0, axis_index_groups=columns, tiled=True)  5.76 us
    all_to_all x1, starting transfers between devices, shards(): lax.all_to_all(pushed, 'bead', 0, 0, axis_index_groups=columns, tiled=True)  5.37 us
    ppermute x1, starting transfers between devices, shards(): lax.ppermute(block, 'space', [(i, (i - offset) % domains) for i in range(...  3.03 us
    ppermute x1, waiting for transfers between devices, shards(): lax.ppermute(block, 'space', [(i, (i - offset) % domains) for i in range(...  1.89 us
  transfers between devices with their start and end apart: 2, of which 2 were waited for; matrix products, arithmetic and copies ran while one was open for 0% of the time, Pallas kernels for 0%

profile of v2, /device:TPU:0, one launch (start us, length us, event | category | flops | bytes accessed | tf_op | source)
XLA Modules:
  0.0 55.4 jit_solution(4770325324452589152)
XLA Ops:
  0.6 0.8 %pack.1.refs_0_ = f32[16,512]{1,0:T(8,128)S(1)} custom-call(f32[3,1,512]{2,1,0:T(1,128)} %bitcast.10, s32[1,512]{1,0:T(1,128)} %bitcast.12, s32[1,512]{1,0:T(1,128)} %bitcast.13, s32[8,512]{1,0:T(8,128)} %slot_src.1), custom_call_target="tpu_custom_call" | custom-call | tf_op jit(solution)/shard_map/pack/pallas_call | solution.py:637
  1.4 3.0 %collective-permute-start = (f32[16,512]{1,0:T(8,128)S(1)}, f32[16,512]{1,0:T(8,128)S(1)}, u32[]{:S(2)}, u32[]{:S(2)}) collective-permute-start(f32[16,512]{1,0:T(8,128)S(1)} %pack.1.refs_0_), channel_id=1, source_target_pairs={{0,1},{1,0},{2,3},{3,2},{4,5},{5,4},{6,7},{7,6},{8,9},{9,8},{10,11... | collective-permute-start | bytes 98312 | tf_op jit(solution)/shard_map/ppermute | solution.py:654
  4.5 1.9 %collective-permute-done.refs_1_ = f32[16,512]{1,0:T(8,128)S(1)} collective-permute-done((f32[16,512]{1,0:T(8,128)S(1)}, f32[16,512]{1,0:T(8,128)S(1)}, u32[]{:S(2)}, u32[]{:S(2)}) %collective-permute-start) | collective-permute-done | bytes 32800 | tf_op jit(solution)/shard_map/ppermute | solution.py:654
  6.4 28.1 %forces.1 = (f32[4,48,128]{2,1,0:T(8,128)}, f32[32,128]{1,0:T(8,128)S(1)}) custom-call(f32[16,512]{1,0:T(8,128)S(1)} %pack.1.refs_0_, f32[16,512]{1,0:T(8,128)S(1)} %collective-permute-done.refs_1_, f32[3,1,512]{2,1,0:T(1,128)} %bitcast.11, f32[2,128]{1,0:T(2,128)} %refs_3_.1, f32[8,128]{1,0:T(8,128)} %refs_4_.1, f32[8,128]{1,0:T(8,128)} %refs_5_.1, ...), custom_call_target="tpu_custom_call" | custom-call | tf_op jit(solution)/shard_map/forces/pallas_call | solution.py:497
  34.5 5.4 %all-to-all-start = ((f32[4,48,128]{2,1,0:T(8,128)}), f32[4,48,128]{2,1,0:T(8,128)S(1)}, u32[]{:S(2)}, u32[]{:S(2)}) async-start(f32[4,48,128]{2,1,0:T(8,128)} %get-tuple-element.7), calls=%async_computation | async-start | bytes 196608 | tf_op jit(solution)/shard_map/all_to_all | solution.py:659
  39.9 0.1 pad_add_fusion.bead_ref
  39.9 5.8 %all-to-all-done.source_ref = f32[4,48,128]{2,1,0:T(8,128)S(1)} async-done(((f32[4,48,128]{2,1,0:T(8,128)}), f32[4,48,128]{2,1,0:T(8,128)S(1)}, u32[]{:S(2)}, u32[]{:S(2)}) %all-to-all-start) | async-done | bytes 98336 | tf_op jit(solution)/shard_map/all_to_all | solution.py:659
  45.7 0.6 %turn.1 = f32[8,32,128]{2,1,0:T(8,128)S(1)} custom-call(s32[2]{0:T(128)S(1)} %pad_add_fusion.bead_ref, f32[32,128]{1,0:T(8,128)S(1)} %get-tuple-element.6.mass_ref, f32[4,48,128]{2,1,0:T(8,128)S(1)} %all-to-all-done.source_ref), custom_call_target="tpu_custom_call" | custom-call | tf_op jit(solution)/shard_map/turn/pallas_call | solution.py:662
  46.3 8.5 %all_to_all.10.arrived_ref = f32[8,32,128]{2,1,0:T(8,128)S(1)} all-to-all(f32[8,32,128]{2,1,0:T(8,128)S(1)} %turn.1), channel_id=1, replica_groups={{0,1,2,3,4,5,6,7},{8,9,10,11,12,13,14,15},{16,17,18,19,20,21,22,23},{24..., dimensions={0} | all-to-all | bytes 262144 | tf_op jit(solution)/shard_map/all_to_all | solution.py:671
  54.8 0.6 %sum.1 = (f32[3,1,512]{2,1,0:T(1,128)}, f32[3,1,512]{2,1,0:T(1,128)}) custom-call(f32[8,32,128]{2,1,0:T(8,128)S(1)} %all_to_all.10.arrived_ref), custom_call_target="tpu_custom_call" | custom-call | tf_op jit(solution)/shard_map/sum/pallas_call | solution.py:672
Async XLA Ops:
  1.4 4.9 %collective-permute-start = (f32[16,512]{1,0:T(8,128)S(1)}, f32[16,512]{1,0:T(8,128)S(1)}, u32[]{:S(2)}, u32[]{:S(2)}) collective-permute-start(f32[16,512]{1,0:T(8,128)S(1)} %pack.1.refs_0_), channel_id=1, source_target_pairs={{0,1},{1,0},{2,3},{3,2},{4,5},{5,4},{6,7},{7,6},{8,9},{9,8},{10,11... | collective-permute-start | bytes 98312 | tf_op jit(solution)/shard_map/ppermute | solution.py:654
  34.5 11.2 %all-to-all-start = ((f32[4,48,128]{2,1,0:T(8,128)}), f32[4,48,128]{2,1,0:T(8,128)S(1)}, u32[]{:S(2)}, u32[]{:S(2)}) async-start(f32[4,48,128]{2,1,0:T(8,128)} %get-tuple-element.7), calls=%async_computation | async-start | bytes 196608 | tf_op jit(solution)/shard_map/all_to_all | solution.py:659

commit v3 on v1

--- a/solution.py
+++ b/solution.py
@@ -22,7 +22,6 @@
 MIB = 1024 * 1024
 f32 = jnp.float32
 bf16 = jnp.bfloat16
-HIGH = lax.Precision.HIGH
 
 
 def split(x):
@@ -35,8 +34,8 @@
     return jnp.concatenate([hi, x - hi], axis=0)
 
 
-def dot(a, b, precision=None):
-    return jnp.dot(a, b, preferred_element_type=f32, precision=precision)
+def dot(a, b):
+    return jnp.dot(a, b, preferred_element_type=f32)
 
 
 def dot_nt(a, b):
@@ -74,31 +73,79 @@
     return v * gate, gate * (1.0 + v * (1.0 - gate))
 
 
-def force_kernel(plan, *refs):
-    atoms, near, wide, before, after = plan
-    n_wide = len(wide)
-    blocks = refs[:n_wide]
-    sources = refs[n_wide : n_wide + 8]
-    push_ref, mass_ref = refs[n_wide + 8 : n_wide + 10]
-    (
-        geo_ref, y_ref, yb_ref, bk_ref, bt_ref, gidx_ref, as_ref, m1_ref, sp1_ref, hs_ref, oh_ref,
-        hj_ref, w_ref, car_ref, m2_ref, inv_ref, dinv_ref, p_ref, dhe_ref, dw_ref, da_ref, q_ref,
-        val_ref, ohlo_ref, moment_ref, emb_ref, rad1_ref, rad2_ref, mix1_ref, mix2_ref, read1_ref, read2_ref, sems,
-    ) = refs[n_wide + 10 :]
-    held = (moment_ref, emb_ref, rad1_ref, rad2_ref, mix1_ref, mix2_ref, read1_ref, read2_ref)
+def choose_kernel(block_ref, *refs):
+    sources = refs[:7]
+    oh_ref, rrc_ref, r2c_ref, side_ref, rrr_ref, r2r_ref, mixa_ref, mixt_ref = refs[7:15]
+    held = refs[15:22]
+    sems = refs[22]
+    emb_ref, rad1_ref, rad2_ref, mix1_ref, mix2_ref, read1_ref, read2_ref = held
     fetches = [pltpu.make_async_copy(src, dst, sems.at[i]) for i, (src, dst) in enumerate(zip(sources, held))]
     for fetch in fetches:
         fetch.start()
     chan = emb_ref.shape[1]
     bases = rad1_ref.shape[0]
+    atoms = block_ref.shape[1]
+    slots = block_ref.shape[0] - HEAD
+
+    ids16 = lax.broadcasted_iota(jnp.int32, (LANES, atoms), 0).astype(jnp.int16)
+    one16 = jnp.ones((LANES, atoms), bf16)
+    zero16 = jnp.zeros((LANES, atoms), bf16)
+    for k in range(slots):
+        slot = block_ref[HEAD + k : HEAD + k + 1, :].astype(jnp.int32)
+        wanted = jnp.broadcast_to(slot, (LANES, atoms)).astype(jnp.int16)
+        for r in range(oh_ref.shape[0] // LANES):
+            hit = wanted - jnp.int16(r * LANES) == ids16
+            oh_ref[r * LANES : (r + 1) * LANES, k * atoms : (k + 1) * atoms] = jnp.where(hit, one16, zero16)
+
+    for fetch in fetches:
+        fetch.wait()
+    emb0 = emb_ref[0:1, :]
+    emb_d = emb_ref[1:2, :] - emb0
+    rr = jnp.concatenate([rad1_ref[...] * emb0, rad1_ref[...] * emb_d], axis=0) * (1.0 / slots)
+    rr_hi = rr.astype(bf16).astype(f32)
+    rr_lo = rr - rr_hi
+    r2 = rad2_ref[...] * (1.0 / slots)
+    r2_hi = r2.astype(bf16).astype(f32)
+    r2_lo = r2 - r2_hi
+    zeros = jnp.zeros((8, chan), f32)
+    turned1 = jnp.concatenate([rr_hi, rr_hi, rr_lo, rr_lo] + [zeros] * 8, axis=0).T
+    sides = jnp.concatenate([emb0, emb_d, read1_ref[...], read2_ref[...], zeros[:4]], axis=0)
+    turned2 = jnp.concatenate([r2_hi, r2_hi, r2_lo, r2_lo] + [zeros] * 12, axis=0).T
+    rrc_ref[...] = turned1[:, : 8 * bases].astype(bf16)
+    r2c_ref[...] = turned2[:, : 4 * bases].astype(bf16)
+    side_ref[...] = jnp.concatenate([sides] + [zeros] * 15, axis=0).T
+    rrr_ref[...] = jnp.concatenate(
+        [jnp.concatenate([rr_hi, rr_hi], axis=1), jnp.concatenate([rr_lo, jnp.zeros_like(rr_lo)], axis=1)], axis=0
+    ).astype(bf16)
+    r2r_ref[...] = jnp.concatenate(
+        [jnp.concatenate([r2_hi, r2_hi], axis=1), jnp.concatenate([r2_lo, jnp.zeros_like(r2_lo)], axis=1)], axis=0
+    ).astype(bf16)
+    for i, ref in enumerate((mix1_ref, mix2_ref)):
+        hi, lo = split(ref[...])
+        mixa_ref[i, 0:chan, :] = hi
+        mixa_ref[i, chan:, :] = lo
+        for g in range(3):
+            hi, lo = split(ref[:, g * chan : (g + 1) * chan].T)
+            mixt_ref[i, g, 0:chan, :] = hi
+            mixt_ref[i, g, chan:, :] = lo
+
+
+def dot_parts(both, hi, lo):
+    rows = both.shape[0] // 2
+    first = dot(both, hi)
+    return first[:rows] + first[rows:] + dot(both[:rows], lo)
+
+
+def edge_kernel(plan, *refs):
+    atoms, near, wide, before, after = plan
+    n_wide = len(wide)
+    blocks = refs[:n_wide]
+    geo_ref, y_ref, yb_ref, bk_ref, bt_ref, gidx_ref, pick_ref = refs[n_wide:]
+    bases = bk_ref.shape[0]
     slots = gidx_ref.shape[0]
-    n_near = len(near) * atoms
     tiles = atoms // LANES
     half = atoms // 2
     half_tiles = half // LANES
-    edges = slots * atoms
-    top_rows = val_ref.shape[0] // 6
-
     order_col = lax.broadcasted_iota(jnp.int32, (bases, LANES), 0).astype(f32)
     tables = []
     for quantity in range(4):
@@ -120,6 +167,13 @@
                     blocks[after[q]][4:5, t * LANES : (t + 1) * LANES] + float(after[q] * atoms),
                 )
             )
+        if q == 0:
+            ids16 = lax.broadcasted_iota(jnp.int32, (pick_ref.shape[0], LANES), 0).astype(jnp.int16)
+            one16 = jnp.ones(ids16.shape, bf16)
+            zero16 = jnp.zeros(ids16.shape, bf16)
+            for t, (_, chunk) in enumerate(ghosts):
+                wanted = jnp.broadcast_to(chunk.astype(jnp.int32), ids16.shape).astype(jnp.int16)
+                pick_ref[:, t * LANES : (t + 1) * LANES] = jnp.where(wanted == ids16, one16, zero16)
         for t in range(tiles):
             cols = slice(t * LANES, (t + 1) * LANES)
             here = slice(q * atoms + t * LANES, q * atoms + (t + 1) * LANES)
@@ -142,10 +196,10 @@
                 geo_ref[i, :, here] = value
             sphere = harmonics(ux, uy, uz)
             for l in range(1, ORDERS):
-                y_ref[l, :, here] = sphere[l]
+                y_ref[l - 1, :, here] = sphere[l]
                 if q == 0:
                     for k in range(slots):
-                        yb_ref[l, k, :, cols] = row(sphere[l][k : k + 1, :])
+                        yb_ref[l - 1, k, :, cols] = row(sphere[l][k : k + 1, :])
             for n in range(bases):
                 bk_ref[n, :, here] = jnp.exp(-0.5 * (soft - (1.0 + n)) ** 2)
             for k in range(slots):
@@ -153,32 +207,16 @@
                 bt_ref[k, 0:bases, here] = basis
                 bt_ref[k, bases : 2 * bases, here] = basis * row(fj[k : k + 1, :], bases)
 
-    for fetch in fetches:
-        fetch.wait()
-    emb0 = emb_ref[0:1, :]
-    emb_d = emb_ref[1:2, :] - emb0
-    rr = jnp.concatenate([rad1_ref[...] * emb0, rad1_ref[...] * emb_d], axis=0) * (1.0 / slots)
-    rr_hi = rr.astype(bf16).astype(f32)
-    rr_lo = rr - rr_hi
-    r2 = rad2_ref[...] * (1.0 / slots)
-    r2_hi = r2.astype(bf16).astype(f32)
-    r2_lo = r2 - r2_hi
-    zeros = jnp.zeros((8, chan), f32)
-    turned1 = jnp.concatenate([rr_hi, rr_hi, rr_lo, rr_lo] + [zeros] * 8, axis=0).T
-    sides = jnp.concatenate([emb0, emb_d, read1_ref[...], read2_ref[...], zeros[:4]], axis=0)
-    turned2 = jnp.concatenate([r2_hi, r2_hi, r2_lo, r2_lo, sides] + [zeros] * 11, axis=0).T
-    rr_cols = turned1[:, : 8 * bases].astype(bf16)
-    r2_cols = turned2[:, : 4 * bases].astype(bf16)
-    emb0_col = turned2[:, 4 * bases : 4 * bases + 1]
-    embd_col = turned2[:, 4 * bases + 1 : 4 * bases + 2]
-    read1_col = turned2[:, 4 * bases + 2 : 4 * bases + 3]
-    read2_col = turned2[:, 4 * bases + 3 : 4 * bases + 4]
-    rr_rows = jnp.concatenate(
-        [jnp.concatenate([rr_hi, rr_hi], axis=1), jnp.concatenate([rr_lo, jnp.zeros_like(rr_lo)], axis=1)], axis=0
-    ).astype(bf16)
-    r2_rows = jnp.concatenate(
-        [jnp.concatenate([r2_hi, r2_hi], axis=1), jnp.concatenate([r2_lo, jnp.zeros_like(r2_lo)], axis=1)], axis=0
-    ).astype(bf16)
+
+def first_kernel(plan, *refs):
+    atoms, near, wide, _, _ = plan
+    n_wide = len(wide)
+    blocks = refs[:n_wide]
+    y_ref, bt_ref, rrc_ref, side_ref, mixa_ref, m1_ref, sp1_ref, hs_ref, as_ref, flag_ref = refs[n_wide:]
+    slots = bt_ref.shape[0]
+    bases = bt_ref.shape[1] // 2
+    chan = m1_ref.shape[1]
+    n_near = m1_ref.shape[2]
 
     def sums(t, carry):
         here = pl.ds(pl.multiple_of(t * LANES, LANES), LANES)
@@ -186,7 +224,7 @@
         for k in range(slots):
             basis = bt_ref[k, :, here]
             for l in range(ORDERS):
-                term = basis if l == 0 else basis * row(y_ref[l, k : k + 1, here], 2 * bases)
+                term = basis if l == 0 else basis * row(y_ref[l - 1, k : k + 1, here], 2 * bases)
                 low[l] = term if low[l] is None else low[l] + term
         for l in range(ORDERS):
             both = split_rows(low[l]).astype(bf16)
@@ -195,39 +233,49 @@
         return carry
 
     lax.fori_loop(0, n_near // LANES, sums, 0)
-
-    flags_row = jnp.concatenate([blocks[q][3:4, :] for q in range(len(near))], axis=1)
+    for q in range(len(near)):
+        flag_ref[0:1, q * atoms : (q + 1) * atoms] = blocks[q][3:4, :]
     wide_cols = 2 * LANES
+    emb0_col = side_ref[:, 0:1]
+    embd_col = side_ref[:, 1:2]
 
     def first(j, carry):
         here = pl.ds(pl.multiple_of(j * wide_cols, wide_cols), wide_cols)
         inv = [None, None, None]
         for l in range(ORDERS):
-            m = dot(rr_cols, as_ref[l, :, here])
+            m = dot(rrc_ref[...], as_ref[l, :, here])
             m1_ref[l, :, here] = m
             inv[GROUP[l]] = m * m if inv[GROUP[l]] is None else inv[GROUP[l]] + m * m
-        value = dot(mix1_ref[...], jnp.concatenate(inv, axis=0), HIGH)
+        hi, lo = split(jnp.concatenate(inv, axis=0))
+        value = dot_parts(mixa_ref[0], hi, lo)
         act, slope = silu_parts(value)
         sp1_ref[:, here] = slope
-        hidden = act + emb0_col + embd_col * q_ref[0:1, here]
+        hidden = act + emb0_col + embd_col * flag_ref[0:1, here]
         hi, lo = split(hidden)
         hs_ref[0:chan, here] = hi
         hs_ref[chan : 2 * chan, here] = lo
         return carry
 
-    q_ref[0:1, :] = flags_row
     lax.fori_loop(0, n_near // wide_cols, first, 0)
 
+
+def gather_kernel(hs_ref, oh_ref, pick_ref, bt_ref, r2c_ref, hj_ref, w_ref, car_ref, ext_ref):
+    slots = bt_ref.shape[0]
+    bases = bt_ref.shape[1] // 2
+    chan = hj_ref.shape[0]
+    atoms = hj_ref.shape[1] // slots
+    half = atoms // 2
+    ghosts = dot(hs_ref[...], pick_ref[...]).astype(bf16)
+    ext_ref[:, 0:half] = ghosts[:, :half]
+    ext_ref[:, half : half + atoms] = hs_ref[:, 0:atoms]
+    ext_ref[:, half + atoms :] = ghosts[:, half:]
+
     def gather(k, carry):
-        here = pl.ds(pl.multiple_of(k * atoms, atoms), atoms)
-        wanted = gidx_ref[pl.ds(k, 1), 0:atoms]
-        for r in range(n_near // LANES):
-            ids = lax.broadcasted_iota(jnp.int32, (LANES, atoms), 0) + r * LANES
-            oh_ref[r * LANES : (r + 1) * LANES, here] = jnp.where(ids == wanted, 1.0, 0.0).astype(bf16)
-        both = dot(hs_ref[...], oh_ref[:, here])
+        here = pl.ds(pl.multiple_of(k * atoms, LANES), atoms)
+        both = dot(ext_ref[...], oh_ref[:, here])
         feat = both[:chan] + both[chan:]
         basis = split_rows(bt_ref[k, 0:bases, 0:atoms])
-        weight = dot(r2_cols, jnp.concatenate([basis, basis], axis=0).astype(bf16))
+        weight = dot(r2c_ref[...], jnp.concatenate([basis, basis], axis=0).astype(bf16))
         hj_ref[:, here] = feat
         w_ref[:, here] = weight
         car_ref[:, here] = feat * weight
@@ -235,7 +283,13 @@
 
     lax.fori_loop(0, slots, gather, 0)
 
+
+def moment_kernel(car_ref, yb_ref, mixa_ref, mixt_ref, side_ref, m2_ref, dinv_ref, inv_ref):
+    slots = yb_ref.shape[1]
+    chan, atoms = m2_ref.shape[1:]
+    tiles = atoms // LANES
     pairs = chan // 16
+    wide_cols = 2 * LANES
 
     def moments(step, carry):
         t = step // pairs
@@ -247,7 +301,7 @@
             at = pl.ds(pl.multiple_of(k * atoms + t * LANES, LANES), LANES)
             got = car_ref[pl.ds(base, 16), at]
             for l in range(ORDERS):
-                yb = yb_ref[l, k, :, cols] if l else None
+                yb = yb_ref[l - 1, k, :, cols] if l else None
                 for h in range(2):
                     part = got[8 * h : 8 * h + 8]
                     term = part * yb if l else part
@@ -266,16 +320,23 @@
         return carry
 
     lax.fori_loop(0, tiles * pairs, moments, 0)
-
+    read2_col = side_ref[:, 3:4]
     for t in range(atoms // wide_cols):
         cols = slice(t * wide_cols, (t + 1) * wide_cols)
-        value = dot(mix2_ref[...], inv_ref[:, cols], HIGH)
-        _, slope = silu_parts(value)
-        slope = slope * (2.0 * read2_col)
+        hi, lo = split(inv_ref[:, cols])
+        _, slope = silu_parts(dot_parts(mixa_ref[1], hi, lo))
+        hi, lo = split(slope * (2.0 * read2_col))
         for g in range(3):
-            mixed = mix2_ref[:, g * chan : (g + 1) * chan].T
-            dinv_ref[g * chan : (g + 1) * chan, cols] = dot(mixed, slope, HIGH)
-
+            dinv_ref[g * chan : (g + 1) * chan, cols] = dot_parts(mixt_ref[1, g], hi, lo)
+
+
+def back_second_kernel(m2_ref, dinv_ref, car_ref, hj_ref, w_ref, yb_ref, bt_ref, geo_ref, r2r_ref,
+                       dhe_ref, q_ref, dw_ref, p_ref):
+    slots = yb_ref.shape[1]
+    bases = bt_ref.shape[1] // 2
+    chan, atoms = m2_ref.shape[1:]
+    tiles = atoms // LANES
+    pairs = chan // 16
     k_step = slots // 2
 
     def back_moments(step, carry):
@@ -296,7 +357,7 @@
                 got = car_ref[pl.ds(base, 16), at]
                 out = [dm[0][:8], dm[0][8:]]
                 for l in range(1, ORDERS):
-                    yb = yb_ref[l, k, :, cols]
+                    yb = yb_ref[l - 1, k, :, cols]
                     i = kk * (ORDERS - 1) + l - 1
                     for h in range(2):
                         part = dm[l][8 * h : 8 * h + 8]
@@ -317,38 +378,59 @@
         return carry
 
     lax.fori_loop(0, tiles * 2, back_moments, 0)
-
     for k in range(slots):
         here = slice(k * atoms, (k + 1) * atoms)
-        both = dot(r2_rows, dw_ref[:, here])
+        both = dot(r2r_ref[...], dw_ref[:, here])
         dbasis = both[:bases] + both[bases:]
         basis = bt_ref[k, 0:bases, 0:atoms]
         reach = 1.0 + lax.broadcasted_iota(jnp.int32, (bases, atoms), 0).astype(f32)
         p_ref[0, k * 8 : k * 8 + 8, :] = dbasis * basis * (reach - row(geo_ref[4, k : k + 1, 0:atoms], bases))
-
-    def back_first(j, carry):
-        start = pl.multiple_of(j * wide_cols, wide_cols)
-        here = pl.ds(start, wide_cols)
-        both = dot_nt(dhe_ref[...], oh_ref[here, :])
-        dh = both[:chan] + both[chan:]
-        mine = jnp.where(start < atoms, 1.0, 0.0)
-        dtop = (dh + read1_col * mine) * sp1_ref[:, here] * 2.0
-        scale = []
-        for g in range(3):
-            scale.append(dot(mix1_ref[:, g * chan : (g + 1) * chan].T, dtop, HIGH))
-        for l in range(ORDERS):
-            hi, lo = split(m1_ref[l, :, here] * scale[GROUP[l]])
-            out = dot(rr_rows, jnp.concatenate([hi, lo], axis=0))
-            da_ref[l, :, here] = out[: 2 * bases] + out[2 * bases :]
-        return carry
-
-    lax.fori_loop(0, n_near // wide_cols, back_first, 0)
-
     lane = lax.broadcasted_iota(jnp.int32, (slots, 16 * slots), 1)
     sub = lax.broadcasted_iota(jnp.int32, (slots, 16 * slots), 0)
     adder = jnp.where(((lane >> 3) & (slots - 1)) == sub, 1.0, 0.0).astype(bf16)
     for l in range(ORDERS):
-        q_ref[8 * l : 8 * l + 8, 0:atoms] = dot(adder, split_rows(p_ref[l, :, :]).astype(bf16))
+        q_ref[8 * l : 8 * l + 8, :] = dot(adder, split_rows(p_ref[l, :, :]).astype(bf16))
+
+
+def back_first_kernel(oh_ref, pick_ref, dhe_ref, sp1_ref, m1_ref, mixt_ref, rrr_ref, side_ref, da_ref, dh_ref):
+    chan, n_near = sp1_ref.shape
+    atoms = pick_ref.shape[1]
+    half = atoms // 2
+    rows = rrr_ref.shape[0] // 2
+    both = dot_nt(oh_ref[...], dhe_ref[...])
+    ext = both[:, :chan] + both[:, chan:]
+    hi, lo = split(jnp.concatenate([ext[:half], ext[half + atoms :]], axis=0))
+    spread = dot(pick_ref[...], jnp.concatenate([hi, lo], axis=1))
+    spread = spread[:, :chan] + spread[:, chan:]
+    dh_ref[:, 0:atoms] = (spread[:atoms] + ext[half : half + atoms]).T + side_ref[:, 2:3]
+    if n_near > atoms:
+        dh_ref[:, atoms:] = spread[atoms:].T
+    wide_cols = 2 * LANES
+
+    def back_first(j, carry):
+        here = pl.ds(pl.multiple_of(j * wide_cols, wide_cols), wide_cols)
+        hi, lo = split(dh_ref[:, here] * sp1_ref[:, here] * 2.0)
+        scale = [dot_parts(mixt_ref[0, g], hi, lo) for g in range(3)]
+        for l in range(ORDERS):
+            hi, lo = split(m1_ref[l, :, here] * scale[GROUP[l]])
+            out = dot(rrr_ref[...], jnp.concatenate([hi, lo], axis=0))
+            da_ref[l, :, here] = out[:rows] + out[rows:]
+        return carry
+
+    lax.fori_loop(0, n_near // wide_cols, back_first, 0)
+
+
+def back_edge_kernel(plan, *refs):
+    atoms, near, wide, _, _ = plan
+    n_wide = len(wide)
+    blocks = refs[:n_wide]
+    moment_src, geo_ref, y_ref, bk_ref, gidx_ref, da_ref, q_ref = refs[n_wide : n_wide + 7]
+    push_ref, mass_ref, val_ref, ohlo_ref, dr_ref, moment_ref, sem = refs[n_wide + 7 :]
+    fetch = pltpu.make_async_copy(moment_src, moment_ref, sem)
+    fetch.start()
+    bases, slots, n_near = bk_ref.shape
+    tiles = atoms // LANES
+    top_rows = val_ref.shape[0] // 6
 
     def back_geometry(t, mine):
         here = pl.ds(pl.multiple_of(t * LANES, LANES), LANES)
@@ -362,7 +444,7 @@
                 g = row(da_ref[l, n : n + 1, here]) + fj * row(da_ref[l, bases + n : bases + n + 1, here])
                 if l:
                     dy[l] = g * basis if dy[l] is None else dy[l] + g * basis
-                    db = db + g * y_ref[l, :, here]
+                    db = db + g * y_ref[l - 1, :, here]
                 else:
                     db = g
             db = db * basis * ((1.0 + n) - soft)
@@ -375,10 +457,8 @@
         duy = SQRT3 * dy[2] + SQRT15 * (ux * dy[4] + uz * dy[5] - uy * dy[8]) - SQRT5 * uy * dy[6]
         duz = SQRT3 * dy[3] + SQRT15 * (uy * dy[5] + ux * dy[7]) + 2.0 * SQRT5 * uz * dy[6]
         along = ds - (ux * dux + uy * duy + uz * duz) * back
-        dr = [dux * back + along * ux, duy * back + along * uy, duz * back + along * uz]
-        for i in range(3):
-            geo_ref[i, :, here] = dr[i]
-        return dr
+        for i, value in enumerate((dux * back + along * ux, duy * back + along * uy, duz * back + along * uz)):
+            dr_ref[i, :, here] = value
 
     def mine_tile(t, carry):
         back_geometry(t, True)
@@ -398,7 +478,7 @@
         place = gidx & 127
         parts = []
         for i in range(3):
-            value = geo_ref[i, :, here]
+            value = dr_ref[i, :, here]
             hi = value.astype(bf16).astype(f32)
             parts.append((hi, value - hi))
         chunk_ids = lax.broadcasted_iota(jnp.int32, (top_rows, LANES), 0)
@@ -413,7 +493,8 @@
         return carry
 
     lax.fori_loop(0, n_near // LANES, place_tile, 0)
-    landed = dot_nt(val_ref[...], ohlo_ref[...])
+    landed = dot_nt(ohlo_ref[...], val_ref[...]).T
+    fetch.wait()
     lines = push_ref.shape[1] // (n_wide + 1)
     one = push_ref.at[0]
     for i in range(3):
@@ -426,7 +507,7 @@
                 line = total[g * tiles + t : g * tiles + t + 1, :]
                 if g < len(near):
                     here = slice(g * atoms + t * LANES, g * atoms + (t + 1) * LANES)
-                    line = line - jnp.sum(geo_ref[i, :, here], axis=0, keepdims=True)
+                    line = line - jnp.sum(dr_ref[i, :, here], axis=0, keepdims=True)
                 line = -HALF_STEP * line
                 at = i * tiles + t
                 if g == 0:
@@ -446,6 +527,132 @@
         push_ref[copy] = whole
 
 
+def in_hbm(x):
+    return pltpu.with_memory_space_constraint(x, pltpu.HBM)
+
+
+def run(name, body, operands, results, scratch=(), far=(), mib=20, cost=None):
+    specs = [pl.BlockSpec(memory_space=pltpu.HBM if i in far else pltpu.VMEM) for i in range(len(operands))]
+    return pl.pallas_call(
+        body,
+        out_shape=tuple(jax.ShapeDtypeStruct(shape, dtype) for shape, dtype in results),
+        in_specs=specs,
+        out_specs=tuple(pl.BlockSpec(memory_space=pltpu.VMEM) for _ in results),
+        scratch_shapes=list(scratch),
+        compiler_params=pltpu.CompilerParams(vmem_limit_bytes=mib * MIB),
+        cost_estimate=cost,
+        name=name,
+    )(*[in_hbm(x) if i in far else x for i, x in enumerate(operands)])
+
+
+def choose(block, embedding, radial_one, radial_two, mix_one, mix_two, read_one, read_two):
+    atoms = block.shape[1]
+    slots = block.shape[0] - HEAD
+    chan = embedding.shape[1]
+    bases = radial_one.shape[0]
+    weights = (embedding, radial_one, radial_two, mix_one, mix_two, read_one[None], read_two[None])
+    return run(
+        "choose",
+        choose_kernel,
+        (block, *weights),
+        (
+            ((2 * atoms, slots * atoms), bf16),
+            ((chan, 8 * bases), bf16),
+            ((chan, 4 * bases), bf16),
+            ((chan, LANES), f32),
+            ((4 * bases, 2 * chan), bf16),
+            ((2 * bases, 2 * chan), bf16),
+            ((2, 2 * chan, 3 * chan), bf16),
+            ((2, 3, 2 * chan, chan), bf16),
+        ),
+        [pltpu.VMEM(w.shape, f32) for w in weights] + [pltpu.SemaphoreType.DMA((len(weights),))],
+        range(1, 1 + len(weights)),
+        cost=pl.CostEstimate(flops=2 * 10**9, bytes_accessed=2 * 10**6, transcendentals=0),
+    )
+
+
+def pushes(plan, outer, blocks, momenta, chosen):
+    atoms, near, wide, _, _ = plan
+    oh, rrc, r2c, sides, rrr, r2r, mixa, mixt = chosen
+    chan = rrc.shape[0]
+    bases = r2r.shape[0] // 2
+    slots = blocks[0].shape[0] - HEAD
+    n_near = len(near) * atoms
+    edges = slots * atoms
+    top_rows = -(-len(wide) * atoms // LANES // 8) * 8
+    lines = line_count(atoms)
+    mib = 12 + 6 * len(near)
+    geo, y, yb, bk, bt, gidx, pick = run(
+        "edges",
+        functools.partial(edge_kernel, plan),
+        blocks,
+        (
+            ((6, slots, n_near), f32),
+            ((ORDERS - 1, slots, n_near), f32),
+            ((ORDERS - 1, slots, 8, atoms), f32),
+            ((bases, slots, n_near), f32),
+            ((slots, 2 * bases, n_near), f32),
+            ((slots, n_near), jnp.int32),
+            ((n_near, atoms), bf16),
+        ),
+    )
+    m1, sp1, hs = run(
+        "first",
+        functools.partial(first_kernel, plan),
+        (*blocks, y, bt, rrc, sides, mixa),
+        (((ORDERS, chan, n_near), f32), ((chan, n_near), f32), ((2 * chan, n_near), bf16)),
+        [pltpu.VMEM((ORDERS, 8 * bases, n_near), bf16), pltpu.VMEM((8, n_near), f32)],
+        mib=mib,
+    )
+    hj, w, car = run(
+        "gather",
+        gather_kernel,
+        (hs, oh, pick, bt, r2c),
+        (((chan, edges), f32),) * 3,
+        [pltpu.VMEM((2 * chan, 2 * atoms), bf16)],
+        mib=mib,
+    )
+    m2, dinv = run(
+        "moments",
+        moment_kernel,
+        (car, yb, mixa, mixt, sides),
+        (((ORDERS, chan, atoms), f32), ((3 * chan, atoms), f32)),
+        [pltpu.VMEM((3 * chan, atoms), f32)],
+        mib=mib,
+    )
+    dhe, q = run(
+        "back_second",
+        back_second_kernel,
+        (m2, dinv, car, hj, w, yb, bt, geo, r2r),
+        (((2 * chan, edges), bf16), ((8 * ORDERS, atoms), f32)),
+        [pltpu.VMEM((2 * chan, edges), bf16), pltpu.VMEM((ORDERS, 8 * slots, atoms), f32)],
+        mib=mib,
+    )
+    (da,) = run(
+        "back_first",
+        back_first_kernel,
+        (oh, pick, dhe, sp1, m1, mixt, rrr, sides),
+        (((ORDERS, 2 * bases, n_near), f32),),
+        [pltpu.VMEM((chan, n_near), f32)],
+        mib=mib,
+    )
+    return run(
+        "back_edges",
+        functools.partial(back_edge_kernel, plan),
+        (*blocks, momenta, geo, y, bk, gidx, da, q),
+        (((outer, (len(wide) + 1) * lines, LANES), f32), ((len(wide) * lines, LANES), f32)),
+        [
+            pltpu.VMEM((6 * top_rows, slots * n_near), bf16),
+            pltpu.VMEM((LANES, slots * n_near), bf16),
+            pltpu.VMEM((3, slots, n_near), f32),
+            pltpu.VMEM(momenta.shape, f32),
+            pltpu.SemaphoreType.DMA(()),
+        ],
+        (len(blocks),),
+        mib=mib,
+    )
+
+
 def line_count(atoms):
     return -(-3 * (atoms // LANES) // 8) * 8
 
@@ -456,66 +663,6 @@
     before = tuple(wide.index((o - 1) % domains) for o in near)
     after = tuple(wide.index((o + 1) % domains) for o in near)
     return atoms, tuple(near), tuple(wide), before, after
-
-
-def in_hbm(x):
-    return pltpu.with_memory_space_constraint(x, pltpu.HBM)
-
-
-def pushes(plan, outer, blocks, momenta, embedding, radial_one, radial_two, mix_one, mix_two, read_one, read_two):
-    atoms, near, wide, _, _ = plan
-    chan = embedding.shape[1]
-    bases = radial_one.shape[0]
-    slots = blocks[0].shape[0] - HEAD
-    n_near = len(near) * atoms
-    edges = slots * atoms
-    top_rows = -(-len(wide) * atoms // LANES // 8) * 8
-    lines = line_count(atoms)
-    vmem = pl.BlockSpec(memory_space=pltpu.VMEM)
-    far = pl.BlockSpec(memory_space=pltpu.HBM)
-    sources = [
-        in_hbm(x)
-        for x in (momenta, embedding, radial_one, radial_two, mix_one, mix_two, read_one[None], read_two[None])
-    ]
-    return pl.pallas_call(
-        functools.partial(force_kernel, plan),
-        out_shape=(
-            jax.ShapeDtypeStruct((outer, (len(wide) + 1) * lines, LANES), f32),
-            jax.ShapeDtypeStruct((len(wide) * lines, LANES), f32),
-        ),
-        in_specs=[vmem] * len(wide) + [far] * len(sources),
-        out_specs=(vmem, vmem),
-        scratch_shapes=[
-            pltpu.VMEM((6, slots, n_near), f32),
-            pltpu.VMEM((ORDERS, slots, n_near), f32),
-            pltpu.VMEM((ORDERS, slots, 8, atoms), f32),
-            pltpu.VMEM((bases, slots, n_near), f32),
-            pltpu.VMEM((slots, 2 * bases, n_near), f32),
-            pltpu.VMEM((slots, n_near), jnp.int32),
-            pltpu.VMEM((ORDERS, 8 * bases, n_near), bf16),
-            pltpu.VMEM((ORDERS, chan, n_near), f32),
-            pltpu.VMEM((chan, n_near), f32),
-            pltpu.VMEM((2 * chan, n_near), bf16),
-            pltpu.VMEM((n_near, edges), bf16),
-            pltpu.VMEM((chan, edges), f32),
-            pltpu.VMEM((chan, edges), f32),
-            pltpu.VMEM((chan, edges), f32),
-            pltpu.VMEM((ORDERS, chan, atoms), f32),
-            pltpu.VMEM((3 * chan, atoms), f32),
-            pltpu.VMEM((3 * chan, atoms), f32),
-            pltpu.VMEM((ORDERS, 8 * slots, atoms), f32),
-            pltpu.VMEM((2 * chan, edges), bf16),
-            pltpu.VMEM((2 * chan, edges), bf16),
-            pltpu.VMEM((ORDERS, 2 * bases, n_near), f32),
-            pltpu.VMEM((8 * ORDERS, n_near), f32),
-            pltpu.VMEM((6 * top_rows, slots * n_near), bf16),
-            pltpu.VMEM((LANES, slots * n_near), bf16),
-        ]
-        + [pltpu.VMEM(source.shape, f32) for source in sources]
-        + [pltpu.SemaphoreType.DMA((len(sources),))],
-        compiler_params=pltpu.CompilerParams(vmem_limit_bytes=(26 + 10 * len(near)) * MIB),
-        name="forces",
-    )(*blocks, *sources)
 
 
 def mode_turns(bead_total):
@@ -635,9 +782,8 @@
     blocks = [block]
     for offset in wide[1:]:
         blocks.append(lax.ppermute(block, "space", [(i, (i - offset) % domains) for i in range(domains)]))
-    pushed, masses = pushes(
-        plan, outer, blocks, moment_rows, embedding, radial_one, radial_two, mix_one, mix_two, read_one, read_two
-    )
+    chosen = choose(block, embedding, radial_one, radial_two, mix_one, mix_two, read_one, read_two)
+    pushed, masses = pushes(plan, outer, blocks, moment_rows, chosen)
     columns = [[z * inner + i for z in range(outer)] for i in range(inner)]
     sources = lax.all_to_all(pushed, "bead", 0, 0, axis_index_groups=columns, tiled=True)
     here = jnp.stack([lax.axis_index("bead"), lax.axis_index("space")]).astype(jnp.int32)

time: 54.9 us -> 53.6 us (0.976)
  waiting for transfers between devices: 7.65 us -> 6.19 us
    ppermute x1, waiting for transfers between devices: 1.89 us -> 0.43 us  [shards(): lax.ppermute(block, 'space', [(i, (i - offset) % domains) for i in range(...]
    pallas_call x1 -> x8, Pallas kernels: 27.3 us -> 27.4 us  [run(): pl.pallas_call(body, out_shape=tuple((jax.ShapeDtypeStruct(shape, dtype)...]
  transfers between devices with their start and end apart: 2 -> 2, of which waited for: 2 -> 2; matrix products, arithmetic and copies ran while one was open for 0% -> 0% of each run, Pallas kernels for 0% -> 3%
where the time goes in v3:
time: 53.6 us; the launch traced here: 53.2 us
  Pallas kernels  29.4 us (55%)
  blocking collectives  8.49 us (16%)
  starting transfers between devices  8.39 us (16%)
  waiting for transfers between devices  6.19 us (12%)
  between operations  0.7 us (1%)
    pallas_call x8, Pallas kernels, run(): pl.pallas_call(body, out_shape=tuple((jax.ShapeDtypeStruct(shape, dtype)...  27.4 us
    all_to_all x1, blocking collectives, shards(): lax.all_to_all(messages, ('bead', 'space'), 0, 0, axis_index_groups=rows,...  8.49 us
    all_to_all x1, waiting for transfers between devices, shards(): lax.all_to_all(pushed, 'bead', 0, 0, axis_index_groups=columns, tiled=True)  5.76 us
    all_to_all x1, starting transfers between devices, shards(): lax.all_to_all(pushed, 'bead', 0, 0, axis_index_groups=columns, tiled=True)  5.36 us
    ppermute x1, starting transfers between devices, shards(): lax.ppermute(block, 'space', [(i, (i - offset) % domains) for i in range(...  3.03 us
  transfers between devices with their start and end apart: 2, of which 2 were waited for; matrix products, arithmetic and copies ran while one was open for 0% of the time, Pallas kernels for 3%

profile of v3, /device:TPU:0, one launch (start us, length us, event | category | flops | bytes accessed | tf_op | source)
XLA Modules:
  0.0 53.2 jit_solution(17799979914878615363)
XLA Ops:
  0.6 0.8 %pack.1.refs_0_.block_ref = f32[16,512]{1,0:T(8,128)S(1)} custom-call(f32[3,1,512]{2,1,0:T(1,128)} %bitcast.11, s32[1,512]{1,0:T(1,128)} %bitcast.12, s32[1,512]{1,0:T(1,128)} %bitcast.13, s32[8,512]{1,0:T(8,128)} %slot_src.1), custom_call_target="tpu_custom_call" | custom-call | tf_op jit(solution)/shard_map/pack/pallas_call | solution.py:767
  1.4 3.0 %collective-permute-start = (f32[16,512]{1,0:T(8,128)S(1)}, f32[16,512]{1,0:T(8,128)S(1)}, u32[]{:S(2)}, u32[]{:S(2)}) collective-permute-start(f32[16,512]{1,0:T(8,128)S(1)} %pack.1.refs_0_.block_ref), channel_id=1, source_target_pairs={{0,1},{1,0},{2,3},{3,2},{4,5},{5,4},{6,7},{7,6},{8,9},{9,8},{10,11... | collective-permute-start | bytes 98312 | tf_op jit(solution)/shard_map/ppermute | solution.py:784
  4.5 1.5 %choose.1 = (bf16[1024,4096]{1,0:T(8,128)(2,1)S(1)}, bf16[128,64]{1,0:T(8,128)(2,1)S(1)}, bf16[128,32]{1,0:T(8,128)(2,1)S(1)}, f32[128,128]{1,0:T(8,128)S(1)}, b...) custom-call(f32[16,512]{1,0:T(8,128)S(1)} %pack.1.refs_0_.block_ref,, ...), custom_call_target="tpu_custom_call" | custom-call | flops 2000000000 | bytes 2000000 | tf_op jit(solution)/shard_map/choose/pallas_call | solution.py:536
  5.9 0.4 collective-permute-done.refs_1_
  6.4 1.2 %edges.1 = (f32[6,8,1024]{2,1,0:T(8,128)S(1)}, f32[8,8,1024]{2,1,0:T(8,128)S(1)}, f32[8,8,8,512]{3,2,1,0:T(8,128)S(1)}, f32[8,8,1024]{2,1,0:T(8,128)S(1)}, f32[8...) custom-call(f32[16,512]{1,0:T(8,128)S(1)} %pack.1.refs_0_.block_ref, ...), custom_call_target="tpu_custom_call" | custom-call | tf_op jit(solution)/shard_map/edges/pallas_call | solution.py:536
  7.5 3.1 %first.1 = (f32[9,128,1024]{2,1,0:T(8,128)S(1)}, f32[128,1024]{1,0:T(8,128)S(1)}, bf16[256,1024]{1,0:T(8,128)(2,1)S(1)}) custom-call(f32[16,512]{1,0:T(8,128)S(1)} %pack.1.refs_0_.block_ref, f32[16,512]{1,0:T(8,128)S(1)} %collective-permute-done.refs_1_, f32[8,8,1024]{2,1,0:T(8,128)S(1)} %get-tuple-element.32.refs_2_.refs_4_, ...), custom_call_target="tpu_custom_call" | custom-call | tf_op jit(solution)/shard_map/first/pallas_call | solution.py:536
  10.6 4.3 %gather.1 = (f32[128,4096]{1,0:T(8,128)S(1)}, f32[128,4096]{1,0:T(8,128)S(1)}, f32[128,4096]{1,0:T(8,128)S(1)}) custom-call(bf16[256,1024]{1,0:T(8,128)(2,1)S(1)} %get-tuple-element.41.hs_ref, bf16[1024,4096]{1,0:T(8,128)(2,1)S(1)} %get-tuple-element.35.oh_ref, bf16[1024,512]{1,0:T(8,128)(2,1)S(1)} %get-tuple-element.36.pick_ref, ...), custom_call_target="tpu_custom_call" | custom-call | tf_op jit(solution)/shard_map/gather/pallas_call | solution.py:536
  14.9 3.0 %moments.1 = (f32[9,128,512]{2,1,0:T(8,128)S(1)}, f32[384,512]{1,0:T(8,128)S(1)}) custom-call(f32[128,4096]{1,0:T(8,128)S(1)} %get-tuple-element.43.car_ref, f32[8,8,8,512]{3,2,1,0:T(8,128)S(1)} %get-tuple-element.44.yb_ref, bf16[2,256,384]{2,1,0:T(8,128)(2,1)S(1)} %get-tuple-element.40.refs_6_.mixa_ref, ...), custom_call_target="tpu_custom_call" | custom-call | tf_op jit(solution)/shard_map/moments/pallas_call | solution.py:536
  17.9 5.5 %back_second.1 = (bf16[256,4096]{1,0:T(8,128)(2,1)S(1)}, f32[72,512]{1,0:T(8,128)S(1)}) custom-call(f32[9,128,512]{2,1,0:T(8,128)S(1)} %get-tuple-element.46.m2_ref, f32[384,512]{1,0:T(8,128)S(1)} %get-tuple-element.47.dinv_ref, f32[128,4096]{1,0:T(8,128)S(1)} %get-tuple-element.43.car_ref, f32[128,4096]{1,0:T(8,128)S(1)} %get-tuple-element.48.hj_ref, ...), custom_call_target="tpu_custom_call" | custom-call | tf_op jit(solution)/shard_map/back_second/pallas_call | solution.py:536
  23.3 5.6 %back_first.1.refs_7_ = f32[9,16,1024]{2,1,0:T(8,128)S(1)} custom-call(bf16[1024,4096]{1,0:T(8,128)(2,1)S(1)} %get-tuple-element.35.oh_ref, bf16[1024,512]{1,0:T(8,128)(2,1)S(1)} %get-tuple-element.36.pick_ref, bf16[256,4096]{1,0:T(8,128)(2,1)S(1)} %get-tuple-element.51.dhe_ref, f32[128,1024]{1,0:T(8,128)S(1)} %get-tuple-element.52.sp1_ref, ...), custom_call_target="tpu_custom_call" | custom-call | tf_op jit(solution)/shard_map/back_first/pallas_call | solution.py:536
  28.9 3.4 %back_edges.1 = (f32[4,48,128]{2,1,0:T(8,128)}, f32[32,128]{1,0:T(8,128)S(1)}) custom-call(f32[16,512]{1,0:T(8,128)S(1)} %pack.1.refs_0_.block_ref, f32[16,512]{1,0:T(8,128)S(1)} %collective-permute-done.refs_1_, f32[3,1,512]{2,1,0:T(1,128)} %bitcast.10, f32[6,8,1024]{2,1,0:T(8,128)S(1)} %get-tuple-element.31.geo_ref.refs_3_, ...), custom_call_target="tpu_custom_call" | custom-call | tf_op jit(solution)/shard_map/back_edges/pallas_call | solution.py:536
  32.3 5.4 %all-to-all-start = ((f32[4,48,128]{2,1,0:T(8,128)}), f32[4,48,128]{2,1,0:T(8,128)S(1)}, u32[]{:S(2)}, u32[]{:S(2)}) async-start(f32[4,48,128]{2,1,0:T(8,128)} %get-tuple-element.57), calls=%async_computation | async-start | bytes 196608 | tf_op jit(solution)/shard_map/all_to_all | solution.py:788
  37.7 0.1 pad_add_fusion.bead_ref
  37.8 5.8 %all-to-all-done.source_ref = f32[4,48,128]{2,1,0:T(8,128)S(1)} async-done(((f32[4,48,128]{2,1,0:T(8,128)}), f32[4,48,128]{2,1,0:T(8,128)S(1)}, u32[]{:S(2)}, u32[]{:S(2)}) %all-to-all-start) | async-done | bytes 98336 | tf_op jit(solution)/shard_map/all_to_all | solution.py:788
  43.5 0.6 %turn.1 = f32[8,32,128]{2,1,0:T(8,128)S(1)} custom-call(s32[2]{0:T(128)S(1)} %pad_add_fusion.bead_ref, f32[32,128]{1,0:T(8,128)S(1)} %get-tuple-element.56.mass_ref, f32[4,48,128]{2,1,0:T(8,128)S(1)} %all-to-all-done.source_ref), custom_call_target="tpu_custom_call" | custom-call | tf_op jit(solution)/shard_map/turn/pallas_call | solution.py:791
  44.1 8.5 %all_to_all.10.arrived_ref = f32[8,32,128]{2,1,0:T(8,128)S(1)} all-to-all(f32[8,32,128]{2,1,0:T(8,128)S(1)} %turn.1), channel_id=1, replica_groups={{0,1,2,3,4,5,6,7},{8,9,10,11,12,13,14,15},{16,17,18,19,20,21,22,23},{24..., dimensions={0} | all-to-all | bytes 262144 | tf_op jit(solution)/shard_map/all_to_all | solution.py:800
  52.6 0.6 %sum.1 = (f32[3,1,512]{2,1,0:T(1,128)}, f32[3,1,512]{2,1,0:T(1,128)}) custom-call(f32[8,32,128]{2,1,0:T(8,128)S(1)} %all_to_all.10.arrived_ref), custom_call_target="tpu_custom_call" | custom-call | tf_op jit(solution)/shard_map/sum/pallas_call | solution.py:801
Async XLA Ops:
  1.4 4.9 %collective-permute-start = (f32[16,512]{1,0:T(8,128)S(1)}, f32[16,512]{1,0:T(8,128)S(1)}, u32[]{:S(2)}, u32[]{:S(2)}) collective-permute-start(f32[16,512]{1,0:T(8,128)S(1)} %pack.1.refs_0_.block_ref), channel_id=1, source_target_pairs={{0,1},{1,0},{2,3},{3,2},{4,5},{5,4},{6,7},{7,6},{8,9},{9,8},{10,11... | collective-permute-start | bytes 98312 | tf_op jit(solution)/shard_map/ppermute | solution.py:784
  32.3 11.2 %all-to-all-start = ((f32[4,48,128]{2,1,0:T(8,128)}), f32[4,48,128]{2,1,0:T(8,128)S(1)}, u32[]{:S(2)}, u32[]{:S(2)}) async-start(f32[4,48,128]{2,1,0:T(8,128)} %get-tuple-element.57), calls=%async_computation | async-start | bytes 196608 | tf_op jit(solution)/shard_map/all_to_all | solution.py:788

commit v4 on v3

--- a/solution.py
+++ b/solution.py
@@ -40,6 +40,17 @@
 
 def dot_nt(a, b):
     return lax.dot_general(a, b, (((1,), (1,)), ((), ())), preferred_element_type=f32)
+
+
+def in_pairs(start, stop, step):
+    per_turn = 2 if (stop - start) % 2 == 0 else 1
+
+    def turn(i, carry):
+        for j in range(per_turn):
+            step(start + i * per_turn + j)
+        return carry
+
+    lax.fori_loop(0, (stop - start) // per_turn, turn, 0)
 
 
 def row(x, rows=8):
@@ -218,7 +229,7 @@
     chan = m1_ref.shape[1]
     n_near = m1_ref.shape[2]
 
-    def sums(t, carry):
+    def sums(t):
         here = pl.ds(pl.multiple_of(t * LANES, LANES), LANES)
         low = [None] * ORDERS
         for k in range(slots):
@@ -230,16 +241,15 @@
             both = split_rows(low[l]).astype(bf16)
             as_ref[l, 0 : 4 * bases, here] = both
             as_ref[l, 4 * bases : 8 * bases, here] = both
-        return carry
-
-    lax.fori_loop(0, n_near // LANES, sums, 0)
+
+    in_pairs(0, n_near // LANES, sums)
     for q in range(len(near)):
         flag_ref[0:1, q * atoms : (q + 1) * atoms] = blocks[q][3:4, :]
     wide_cols = 2 * LANES
     emb0_col = side_ref[:, 0:1]
     embd_col = side_ref[:, 1:2]
 
-    def first(j, carry):
+    def first(j):
         here = pl.ds(pl.multiple_of(j * wide_cols, wide_cols), wide_cols)
         inv = [None, None, None]
         for l in range(ORDERS):
@@ -254,9 +264,8 @@
         hi, lo = split(hidden)
         hs_ref[0:chan, here] = hi
         hs_ref[chan : 2 * chan, here] = lo
-        return carry
-
-    lax.fori_loop(0, n_near // wide_cols, first, 0)
+
+    in_pairs(0, n_near // wide_cols, first)
 
 
 def gather_kernel(hs_ref, oh_ref, pick_ref, bt_ref, r2c_ref, hj_ref, w_ref, car_ref, ext_ref):
@@ -270,7 +279,7 @@
     ext_ref[:, half : half + atoms] = hs_ref[:, 0:atoms]
     ext_ref[:, half + atoms :] = ghosts[:, half:]
 
-    def gather(k, carry):
+    def gather(k):
         here = pl.ds(pl.multiple_of(k * atoms, LANES), atoms)
         both = dot(ext_ref[...], oh_ref[:, here])
         feat = both[:chan] + both[chan:]
@@ -279,47 +288,45 @@
         hj_ref[:, here] = feat
         w_ref[:, here] = weight
         car_ref[:, here] = feat * weight
-        return carry
-
-    lax.fori_loop(0, slots, gather, 0)
+
+    in_pairs(0, slots, gather)
 
 
 def moment_kernel(car_ref, yb_ref, mixa_ref, mixt_ref, side_ref, m2_ref, dinv_ref, inv_ref):
     slots = yb_ref.shape[1]
     chan, atoms = m2_ref.shape[1:]
     tiles = atoms // LANES
-    pairs = chan // 16
     wide_cols = 2 * LANES
+    rows = 32
+    groups = chan // rows
 
     def moments(step, carry):
-        t = step // pairs
-        c = step % pairs
+        t = step // groups
+        c = step % groups
         cols = pl.ds(pl.multiple_of(t * LANES, LANES), LANES)
-        base = pl.multiple_of(c * 16, 16)
-        acc = [[None] * ORDERS, [None] * ORDERS]
+        base = pl.multiple_of(c * rows, rows)
+        acc = [[None] * ORDERS for _ in range(rows // 8)]
         for k in range(slots):
             at = pl.ds(pl.multiple_of(k * atoms + t * LANES, LANES), LANES)
-            got = car_ref[pl.ds(base, 16), at]
+            got = car_ref[pl.ds(base, rows), at]
             for l in range(ORDERS):
                 yb = yb_ref[l - 1, k, :, cols] if l else None
-                for h in range(2):
+                for h in range(rows // 8):
                     part = got[8 * h : 8 * h + 8]
                     term = part * yb if l else part
                     acc[h][l] = term if acc[h][l] is None else acc[h][l] + term
-        inv = [[None] * 3, [None] * 3]
-        for l in range(ORDERS):
-            m2_ref[l, pl.ds(base, 16), cols] = jnp.concatenate([acc[0][l], acc[1][l]], axis=0)
-            for h in range(2):
+        for h in range(rows // 8):
+            inv = [None] * 3
+            for l in range(ORDERS):
+                m2_ref[l, pl.ds(pl.multiple_of(base + 8 * h, 8), 8), cols] = acc[h][l]
                 sq = acc[h][l] * acc[h][l]
                 g = GROUP[l]
-                inv[h][g] = sq if inv[h][g] is None else inv[h][g] + sq
-        for g in range(3):
-            inv_ref[pl.ds(pl.multiple_of(g * chan + c * 16, 16), 16), cols] = jnp.concatenate(
-                [inv[0][g], inv[1][g]], axis=0
-            )
+                inv[g] = sq if inv[g] is None else inv[g] + sq
+            for g in range(3):
+                inv_ref[pl.ds(pl.multiple_of(g * chan + base + 8 * h, 8), 8), cols] = inv[g]
         return carry
 
-    lax.fori_loop(0, tiles * pairs, moments, 0)
+    lax.fori_loop(0, tiles * groups, moments, 0)
     read2_col = side_ref[:, 3:4]
     for t in range(atoms // wide_cols):
         cols = slice(t * wide_cols, (t + 1) * wide_cols)
@@ -344,8 +351,7 @@
         k0 = (step % 2) * k_step
         cols = pl.ds(pl.multiple_of(t * LANES, LANES), LANES)
 
-        def over(c, acc):
-            acc = list(acc)
+        def one(c, acc):
             base = pl.multiple_of(c * 16, 16)
             dm = []
             scale = [dinv_ref[pl.ds(pl.multiple_of(g * chan + c * 16, 16), 16), cols] for g in range(3)]
@@ -368,10 +374,15 @@
                     hi, lo = split(dcar * other[pl.ds(base, 16), at])
                     ref[pl.ds(base, 16), at] = hi
                     ref[pl.ds(pl.multiple_of(chan + c * 16, 16), 16), at] = lo
+
+        def over(c, acc):
+            acc = list(acc)
+            one(2 * c, acc)
+            one(2 * c + 1, acc)
             return tuple(acc)
 
         start = tuple(jnp.zeros((8, LANES), f32) for _ in range(k_step * (ORDERS - 1)))
-        acc = lax.fori_loop(0, pairs, over, start)
+        acc = lax.fori_loop(0, pairs // 2, over, start)
         for kk in range(k_step):
             for l in range(1, ORDERS):
                 p_ref[l, pl.ds(pl.multiple_of((k0 + kk) * 8, 8), 8), cols] = acc[kk * (ORDERS - 1) + l - 1]
@@ -407,7 +418,7 @@
         dh_ref[:, atoms:] = spread[atoms:].T
     wide_cols = 2 * LANES
 
-    def back_first(j, carry):
+    def back_first(j):
         here = pl.ds(pl.multiple_of(j * wide_cols, wide_cols), wide_cols)
         hi, lo = split(dh_ref[:, here] * sp1_ref[:, here] * 2.0)
         scale = [dot_parts(mixt_ref[0, g], hi, lo) for g in range(3)]
@@ -415,9 +426,8 @@
             hi, lo = split(m1_ref[l, :, here] * scale[GROUP[l]])
             out = dot(rrr_ref[...], jnp.concatenate([hi, lo], axis=0))
             da_ref[l, :, here] = out[:rows] + out[rows:]
-        return carry
-
-    lax.fori_loop(0, n_near // wide_cols, back_first, 0)
+
+    in_pairs(0, n_near // wide_cols, back_first)
 
 
 def back_edge_kernel(plan, *refs):
@@ -460,18 +470,10 @@
         for i, value in enumerate((dux * back + along * ux, duy * back + along * uy, duz * back + along * uz)):
             dr_ref[i, :, here] = value
 
-    def mine_tile(t, carry):
-        back_geometry(t, True)
-        return carry
-
-    def other_tile(t, carry):
-        back_geometry(t, False)
-        return carry
-
-    lax.fori_loop(0, tiles, mine_tile, 0)
-    lax.fori_loop(tiles, n_near // LANES, other_tile, 0)
-
-    def place_tile(t, carry):
+    in_pairs(0, tiles, lambda t: back_geometry(t, True))
+    in_pairs(tiles, n_near // LANES, lambda t: back_geometry(t, False))
+
+    def place_tile(t):
         here = pl.ds(pl.multiple_of(t * LANES, LANES), LANES)
         gidx = gidx_ref[:, here]
         chunk_no = gidx >> 7
@@ -490,13 +492,11 @@
                 both = [jnp.where(hit, row(part[k : k + 1, :], top_rows), 0.0) for part in parts[i]]
                 val_ref[2 * i * top_rows : 2 * (i + 1) * top_rows, at] = jnp.concatenate(both, axis=0).astype(bf16)
             ohlo_ref[:, at] = jnp.where(place_ids == row(place[k : k + 1, :], LANES), 1.0, 0.0).astype(bf16)
-        return carry
-
-    lax.fori_loop(0, n_near // LANES, place_tile, 0)
+
+    in_pairs(0, n_near // LANES, place_tile)
     landed = dot_nt(ohlo_ref[...], val_ref[...]).T
     fetch.wait()
-    lines = push_ref.shape[1] // (n_wide + 1)
-    one = push_ref.at[0]
+    lines = push_ref.shape[0] // (n_wide + 1)
     for i in range(3):
         total = (
             landed[2 * i * top_rows : (2 * i + 1) * top_rows] + landed[(2 * i + 1) * top_rows : (2 * i + 2) * top_rows]
@@ -512,19 +512,16 @@
                 at = i * tiles + t
                 if g == 0:
                     line = line + moment_ref[i, :, cols]
-                    one[at : at + 1, :] = blocks[0][i : i + 1, cols]
-                one[(1 + g) * lines + at : (1 + g) * lines + at + 1, :] = line
+                    push_ref[at : at + 1, :] = blocks[0][i : i + 1, cols]
+                push_ref[(1 + g) * lines + at : (1 + g) * lines + at + 1, :] = line
                 mass = HEAVY - (HEAVY - 1.0) * blocks[g][3:4, cols]
                 mass_ref[g * lines + at : g * lines + at + 1, :] = mass
     if lines > 3 * tiles:
         for g in range(n_wide + 1):
             blank = slice(g * lines + 3 * tiles, (g + 1) * lines)
-            one[blank, :] = jnp.zeros((lines - 3 * tiles, LANES), f32)
+            push_ref[blank, :] = jnp.zeros((lines - 3 * tiles, LANES), f32)
             if g < n_wide:
                 mass_ref[blank, :] = jnp.ones((lines - 3 * tiles, LANES), f32)
-    whole = push_ref[0]
-    for copy in range(1, push_ref.shape[0]):
-        push_ref[copy] = whole
 
 
 def in_hbm(x):
@@ -571,7 +568,7 @@
     )
 
 
-def pushes(plan, outer, blocks, momenta, chosen):
+def pushes(plan, blocks, momenta, chosen):
     atoms, near, wide, _, _ = plan
     oh, rrc, r2c, sides, rrr, r2r, mixa, mixt = chosen
     chan = rrc.shape[0]
@@ -640,7 +637,7 @@
         "back_edges",
         functools.partial(back_edge_kernel, plan),
         (*blocks, momenta, geo, y, bk, gidx, da, q),
-        (((outer, (len(wide) + 1) * lines, LANES), f32), ((len(wide) * lines, LANES), f32)),
+        ((((len(wide) + 1) * lines, LANES), f32), ((len(wide) * lines, LANES), f32)),
         [
             pltpu.VMEM((6 * top_rows, slots * n_near), bf16),
             pltpu.VMEM((LANES, slots * n_near), bf16),
@@ -696,11 +693,11 @@
     block_ref[HEAD:, :] = slot_ref[...].astype(f32)
 
 
-def turn_kernel(shape, bead_ref, mass_ref, source_ref, message_ref):
+def turn_kernel(shape, bead_ref, domain_ref, mass_ref, source_ref, message_ref):
     outer, inner, domains, wide = shape
     turns = mode_turns(outer * inner)
     lines = mass_ref.shape[0] // len(wide)
-    my_domain = bead_ref[1]
+    my_domain = domain_ref[0]
     my_outer = bead_ref[0] // inner
     my_inner = bead_ref[0] - my_outer * inner
     if domains > len(wide):
@@ -783,19 +780,19 @@
     for offset in wide[1:]:
         blocks.append(lax.ppermute(block, "space", [(i, (i - offset) % domains) for i in range(domains)]))
     chosen = choose(block, embedding, radial_one, radial_two, mix_one, mix_two, read_one, read_two)
-    pushed, masses = pushes(plan, outer, blocks, moment_rows, chosen)
+    pushed, masses = pushes(plan, blocks, moment_rows, chosen)
     columns = [[z * inner + i for z in range(outer)] for i in range(inner)]
-    sources = lax.all_to_all(pushed, "bead", 0, 0, axis_index_groups=columns, tiled=True)
-    here = jnp.stack([lax.axis_index("bead"), lax.axis_index("space")]).astype(jnp.int32)
+    sources = lax.all_gather(pushed, "bead", axis=0, axis_index_groups=columns)
+    here = [lax.axis_index(axis).astype(jnp.int32).reshape(1) for axis in ("bead", "space")]
     lines = line_count(atoms)
     messages = pl.pallas_call(
         functools.partial(turn_kernel, (outer, inner, domains, wide)),
         out_shape=jax.ShapeDtypeStruct((inner * domains, 2 * lines, LANES), f32),
-        in_specs=[smem, vmem, vmem],
+        in_specs=[smem, smem, vmem, vmem],
         out_specs=vmem,
         compiler_params=small,
         name="turn",
-    )(here, masses, sources)
+    )(*here, masses, sources)
     rows = [[z * inner * domains + i for i in range(inner * domains)] for z in range(outer)]
     arrived = lax.all_to_all(messages, ("bead", "space"), 0, 0, axis_index_groups=rows, tiled=True)
     new_q, new_p = pl.pallas_call(

time: 53.6 us -> 57.7 us (1.076)
  blocking collectives: 8.49 us -> 21 us
  local copies, waits for them, and re-layouts: 0 us -> 6.6 us
  waiting for transfers between devices: 6.19 us -> 0.01 us
  starting transfers between devices: 8.39 us -> 3.03 us
  Pallas kernels: 29.4 us -> 26 us
    all_gather x0 -> x1, blocking collectives: none -> 13.5 us  [shards(): sources = lax.all_gather(pushed, 'bead', axis=0, axis_index_groups=columns)]
    unnamed x0 -> x8, local copies, waits for them, and re-layouts: none -> 6.6 us
    all_to_all x1 -> x0, waiting for transfers between devices: 5.76 us -> none  [shards(): lax.all_to_all(pushed, 'bead', 0, 0, axis_index_groups=columns, tiled=True)]
    all_to_all x1 -> x0, starting transfers between devices: 5.36 us -> none  [shards(): lax.all_to_all(pushed, 'bead', 0, 0, axis_index_groups=columns, tiled=True)]
    pallas_call x8, Pallas kernels: 27.4 us -> 24.5 us  [run(): pl.pallas_call(body, out_shape=tuple((jax.ShapeDtypeStruct(shape, dtype)...]
    all_to_all x1, blocking collectives: 8.49 us -> 7.48 us  [shards(): lax.all_to_all(messages, ('bead', 'space'), 0, 0, axis_index_groups=rows,...]
  transfers between devices with their start and end apart: 2 -> 1, of which waited for: 2 -> 0; matrix products, arithmetic and copies ran while one was open for 0% -> 0% of each run, Pallas kernels for 3% -> 3%
where the time goes in v4:
time: 57.7 us; the launch traced here: 57.4 us
  Pallas kernels  26 us (45%)
  blocking collectives  21 us (36%)
  local copies, waits for them, and re-layouts  6.6 us (11%)
  starting transfers between devices  3.03 us (5%)
  between operations  0.73 us (1%)
    pallas_call x8, Pallas kernels, run(): pl.pallas_call(body, out_shape=tuple((jax.ShapeDtypeStruct(shape, dtype)...  24.5 us
    all_gather x1, blocking collectives, shards(): sources = lax.all_gather(pushed, 'bead', axis=0, axis_index_groups=columns)  13.5 us
    all_to_all x1, blocking collectives, shards(): lax.all_to_all(messages, ('bead', 'space'), 0, 0, axis_index_groups=rows,...  7.48 us
    unnamed x8, local copies, waits for them, and re-layouts  6.6 us
    ppermute x1, starting transfers between devices, shards(): lax.ppermute(block, 'space', [(i, (i - offset) % domains) for i in range(...  3.03 us
  transfers between devices with their start and end apart: 1, of which 0 were waited for; matrix products, arithmetic and copies ran while one was open for 0% of the time, Pallas kernels for 3%

profile of v4, /device:TPU:0, one launch (start us, length us, event | category | flops | bytes accessed | tf_op | source)
XLA Modules:
  0.0 57.4 jit_solution(7001925655073255281)
XLA Ops:
  0.6 0.8 %pack.1.refs_0_.block_ref = f32[16,512]{1,0:T(8,128)S(1)} custom-call(f32[3,1,512]{2,1,0:T(1,128)} %bitcast.15, s32[1,512]{1,0:T(1,128)} %bitcast.16, s32[1,512]{1,0:T(1,128)} %bitcast.17, s32[8,512]{1,0:T(8,128)} %slot_src.1), custom_call_target="tpu_custom_call" | custom-call | tf_op jit(solution)/shard_map/pack/pallas_call | solution.py:764
  1.4 3.0 %collective-permute-start = (f32[16,512]{1,0:T(8,128)S(1)}, f32[16,512]{1,0:T(8,128)S(1)}, u32[]{:S(2)}, u32[]{:S(2)}) collective-permute-start(f32[16,512]{1,0:T(8,128)S(1)} %pack.1.refs_0_.block_ref), channel_id=1, source_target_pairs={{0,1},{1,0},{2,3},{3,2},{4,5},{5,4},{6,7},{7,6},{8,9},{9,8},{10,11... | collective-permute-start | bytes 98312 | tf_op jit(solution)/shard_map/ppermute | solution.py:781
  4.5 1.5 %choose.1 = (bf16[1024,4096]{1,0:T(8,128)(2,1)S(1)}, bf16[128,64]{1,0:T(8,128)(2,1)S(1)}, bf16[128,32]{1,0:T(8,128)(2,1)S(1)}, f32[128,128]{1,0:T(8,128)S(1)}, b...) custom-call(f32[16,512]{1,0:T(8,128)S(1)} %pack.1.refs_0_.block_ref,, ...), custom_call_target="tpu_custom_call" | custom-call | flops 2000000000 | bytes 2000000 | tf_op jit(solution)/shard_map/choose/pallas_call | solution.py:533
  5.9 0.0 copy-start
  6.0 3.2 %copy-done = bf16[1024,4096]{1,0:T(8,128)(2,1)} copy-done((bf16[1024,4096]{1,0:T(8,128)(2,1)}, bf16[1024,4096]{1,0:T(8,128)(2,1)S(1)}, u32[]{:S(2)}) %copy-start) | copy-done | bytes 8388632
  9.2 0.0 collective-permute-done.refs_1_
  9.2 1.2 %edges.1 = (f32[6,8,1024]{2,1,0:T(8,128)S(1)}, f32[8,8,1024]{2,1,0:T(8,128)S(1)}, f32[8,8,8,512]{3,2,1,0:T(8,128)S(1)}, f32[8,8,1024]{2,1,0:T(8,128)S(1)}, f32[8...) custom-call(f32[16,512]{1,0:T(8,128)S(1)} %pack.1.refs_0_.block_ref, ...), custom_call_target="tpu_custom_call" | custom-call | tf_op jit(solution)/shard_map/edges/pallas_call | solution.py:533
  10.3 2.5 %first.1 = (f32[9,128,1024]{2,1,0:T(8,128)S(1)}, f32[128,1024]{1,0:T(8,128)S(1)}, bf16[256,1024]{1,0:T(8,128)(2,1)S(1)}) custom-call(f32[16,512]{1,0:T(8,128)S(1)} %pack.1.refs_0_.block_ref, f32[16,512]{1,0:T(8,128)S(1)} %collective-permute-done.refs_1_, f32[8,8,1024]{2,1,0:T(8,128)S(1)} %get-tuple-element.32.refs_2_.refs_4_, ...), custom_call_target="tpu_custom_call" | custom-call | tf_op jit(solution)/shard_map/first/pallas_call | solution.py:533
  12.9 0.0 copy-start.1
  12.9 3.4 %copy-done.1 = bf16[1024,4096]{1,0:T(8,128)(2,1)S(1)} copy-done((bf16[1024,4096]{1,0:T(8,128)(2,1)S(1)}, bf16[1024,4096]{1,0:T(8,128)(2,1)}, u32[]{:S(2)}) %copy-start.1) | copy-done | bytes 8388632
  16.3 3.6 %gather.1 = (f32[128,4096]{1,0:T(8,128)S(1)}, f32[128,4096]{1,0:T(8,128)S(1)}, f32[128,4096]{1,0:T(8,128)S(1)}) custom-call(bf16[256,1024]{1,0:T(8,128)(2,1)S(1)} %get-tuple-element.41.hs_ref, bf16[1024,4096]{1,0:T(8,128)(2,1)S(1)} %copy-done.1, bf16[1024,512]{1,0:T(8,128)(2,1)S(1)} %get-tuple-element.36.pick_ref, ...), custom_call_target="tpu_custom_call" | custom-call | tf_op jit(solution)/shard_map/gather/pallas_call | solution.py:533
  19.9 0.0 slice-start
  19.9 2.7 %moments.1 = (f32[9,128,512]{2,1,0:T(8,128)S(1)}, f32[384,512]{1,0:T(8,128)S(1)}) custom-call(f32[128,4096]{1,0:T(8,128)S(1)} %get-tuple-element.43.car_ref, f32[8,8,8,512]{3,2,1,0:T(8,128)S(1)} %get-tuple-element.44.yb_ref, bf16[2,256,384]{2,1,0:T(8,128)(2,1)S(1)} %get-tuple-element.40.refs_6_.mixa_ref, ...), custom_call_target="tpu_custom_call" | custom-call | tf_op jit(solution)/shard_map/moments/pallas_call | solution.py:533
  22.5 0.0 slice-start.1
  22.6 5.2 %back_second.1 = (bf16[256,4096]{1,0:T(8,128)(2,1)S(1)}, f32[72,512]{1,0:T(8,128)S(1)}) custom-call(f32[9,128,512]{2,1,0:T(8,128)S(1)} %get-tuple-element.46.m2_ref, f32[384,512]{1,0:T(8,128)S(1)} %get-tuple-element.47.dinv_ref, f32[128,4096]{1,0:T(8,128)S(1)} %get-tuple-element.43.car_ref, f32[128,4096]{1,0:T(8,128)S(1)} %get-tuple-element.48.hj_ref, ...), custom_call_target="tpu_custom_call" | custom-call | tf_op jit(solution)/shard_map/back_second/pallas_call | solution.py:533
  27.7 0.0 slice-done
  27.7 0.0 slice-done.1
  27.8 5.3 %back_first.1.refs_7_ = f32[9,16,1024]{2,1,0:T(8,128)S(1)} custom-call(bf16[1024,4096]{1,0:T(8,128)(2,1)S(1)} %bitcast.12, bf16[1024,512]{1,0:T(8,128)(2,1)S(1)} %get-tuple-element.36.pick_ref, bf16[256,4096]{1,0:T(8,128)(2,1)S(1)} %get-tuple-element.51.dhe_ref, f32[128,1024]{1,0:T(8,128)S(1)} %get-tuple-element.52.sp1_ref, ...), custom_call_target="tpu_custom_call" | custom-call | tf_op jit(solution)/shard_map/back_first/pallas_call | solution.py:533
  33.1 2.6 %back_edges.1 = (f32[48,128]{1,0:T(8,128)S(1)}, f32[32,128]{1,0:T(8,128)S(1)}) custom-call(f32[16,512]{1,0:T(8,128)S(1)} %pack.1.refs_0_.block_ref, f32[16,512]{1,0:T(8,128)S(1)} %collective-permute-done.refs_1_, f32[3,1,512]{2,1,0:T(1,128)} %bitcast.14, f32[6,8,1024]{2,1,0:T(8,128)S(1)} %get-tuple-element.31.geo_ref.refs_3_, ...), custom_call_target="tpu_custom_call" | custom-call | tf_op jit(solution)/shard_map/back_edges/pallas_call | solution.py:533
  35.7 13.5 %all-gather = f32[192,128]{1,0:T(8,128)S(1)} all-gather(f32[48,128]{1,0:T(8,128)S(1)} %get-tuple-element.57), channel_id=2, replica_groups={{0,8,16,24},{2,10,18,26},{4,12,20,28},{6,14,22,30},{1,9,17,25},{3,11,19..., dimensions={0}, use_global_device_ids=true | all-gather | bytes 122880 | tf_op jit(solution)/shard_map/all_gather | solution.py:785
  49.2 0.1 turn.1
  49.3 7.5 %all_to_all.5.arrived_ref = f32[8,32,128]{2,1,0:T(8,128)S(1)} all-to-all(f32[8,32,128]{2,1,0:T(8,128)S(1)} %turn.1), channel_id=1, replica_groups={{0,1,2,3,4,5,6,7},{8,9,10,11,12,13,14,15},{16,17,18,19,20,21,22,23},{24..., dimensions={0} | all-to-all | bytes 262144 | tf_op jit(solution)/shard_map/all_to_all | solution.py:797
  56.8 0.6 %sum.1 = (f32[3,1,512]{2,1,0:T(1,128)}, f32[3,1,512]{2,1,0:T(1,128)}) custom-call(f32[8,32,128]{2,1,0:T(8,128)S(1)} %all_to_all.5.arrived_ref), custom_call_target="tpu_custom_call" | custom-call | tf_op jit(solution)/shard_map/sum/pallas_call | solution.py:798
  (1 shorter events, 0.0 us)
Async XLA Ops:
  1.4 7.7 %collective-permute-start = (f32[16,512]{1,0:T(8,128)S(1)}, f32[16,512]{1,0:T(8,128)S(1)}, u32[]{:S(2)}, u32[]{:S(2)}) collective-permute-start(f32[16,512]{1,0:T(8,128)S(1)} %pack.1.refs_0_.block_ref), channel_id=1, source_target_pairs={{0,1},{1,0},{2,3},{3,2},{4,5},{5,4},{6,7},{7,6},{8,9},{9,8},{10,11... | collective-permute-start | bytes 98312 | tf_op jit(solution)/shard_map/ppermute | solution.py:781
  5.9 3.2 %copy-start = (bf16[1024,4096]{1,0:T(8,128)(2,1)}, bf16[1024,4096]{1,0:T(8,128)(2,1)S(1)}, u32[]{:S(2)}) copy-start(bf16[1024,4096]{1,0:T(8,128)(2,1)S(1)} %get-tuple-element.35.oh_ref) | copy-start | bytes 25165828
  12.9 3.4 %copy-start.1 = (bf16[1024,4096]{1,0:T(8,128)(2,1)S(1)}, bf16[1024,4096]{1,0:T(8,128)(2,1)}, u32[]{:S(2)}) copy-start(bf16[1024,4096]{1,0:T(8,128)(2,1)} %copy-done) | copy-start | bytes 25165828
  19.9 7.9 %slice-start = ((s8[8388608]{0:T(1024)(128)(4,1)}), s8[4194304]{0:T(1024)(128)(4,1)S(1)}, s32[]{:S(2)}) async-start(s8[8388608]{0:T(1024)(128)(4,1)} %bitcast.11), calls=%async_computation.1 | async-start | bytes 8388608
  22.5 5.2 %slice-start.1 = ((s8[8388608]{0:T(1024)(128)(4,1)}), s8[4194304]{0:T(1024)(128)(4,1)S(1)}, s32[]{:S(2)}) async-start(s8[8388608]{0:T(1024)(128)(4,1)} %bitcast.11), calls=%async_computation.2 | async-start | bytes 8388608

commit v5 on v4

--- a/solution.py
+++ b/solution.py
@@ -42,8 +42,8 @@
     return lax.dot_general(a, b, (((1,), (1,)), ((), ())), preferred_element_type=f32)
 
 
-def in_pairs(start, stop, step):
-    per_turn = 2 if (stop - start) % 2 == 0 else 1
+def in_turns(start, stop, step, most=4):
+    per_turn = next(n for n in range(most, 0, -1) if (stop - start) % n == 0)
 
     def turn(i, carry):
         for j in range(per_turn):
@@ -242,7 +242,7 @@
             as_ref[l, 0 : 4 * bases, here] = both
             as_ref[l, 4 * bases : 8 * bases, here] = both
 
-    in_pairs(0, n_near // LANES, sums)
+    in_turns(0, n_near // LANES, sums)
     for q in range(len(near)):
         flag_ref[0:1, q * atoms : (q + 1) * atoms] = blocks[q][3:4, :]
     wide_cols = 2 * LANES
@@ -265,7 +265,7 @@
         hs_ref[0:chan, here] = hi
         hs_ref[chan : 2 * chan, here] = lo
 
-    in_pairs(0, n_near // wide_cols, first)
+    in_turns(0, n_near // wide_cols, first)
 
 
 def gather_kernel(hs_ref, oh_ref, pick_ref, bt_ref, r2c_ref, hj_ref, w_ref, car_ref, ext_ref):
@@ -289,7 +289,7 @@
         w_ref[:, here] = weight
         car_ref[:, here] = feat * weight
 
-    in_pairs(0, slots, gather)
+    in_turns(0, slots, gather)
 
 
 def moment_kernel(car_ref, yb_ref, mixa_ref, mixt_ref, side_ref, m2_ref, dinv_ref, inv_ref):
@@ -345,6 +345,7 @@
     tiles = atoms // LANES
     pairs = chan // 16
     k_step = slots // 2
+    per_turn = 4 if pairs % 4 == 0 else 1
 
     def back_moments(step, carry):
         t = step // 2
@@ -377,12 +378,12 @@
 
         def over(c, acc):
             acc = list(acc)
-            one(2 * c, acc)
-            one(2 * c + 1, acc)
+            for i in range(per_turn):
+                one(per_turn * c + i, acc)
             return tuple(acc)
 
         start = tuple(jnp.zeros((8, LANES), f32) for _ in range(k_step * (ORDERS - 1)))
-        acc = lax.fori_loop(0, pairs // 2, over, start)
+        acc = lax.fori_loop(0, pairs // per_turn, over, start)
         for kk in range(k_step):
             for l in range(1, ORDERS):
                 p_ref[l, pl.ds(pl.multiple_of((k0 + kk) * 8, 8), 8), cols] = acc[kk * (ORDERS - 1) + l - 1]
@@ -403,11 +404,10 @@
         q_ref[8 * l : 8 * l + 8, :] = dot(adder, split_rows(p_ref[l, :, :]).astype(bf16))
 
 
-def back_first_kernel(oh_ref, pick_ref, dhe_ref, sp1_ref, m1_ref, mixt_ref, rrr_ref, side_ref, da_ref, dh_ref):
-    chan, n_near = sp1_ref.shape
+def scatter_kernel(oh_ref, pick_ref, dhe_ref, side_ref, dh_ref):
+    chan, n_near = dh_ref.shape
     atoms = pick_ref.shape[1]
     half = atoms // 2
-    rows = rrr_ref.shape[0] // 2
     both = dot_nt(oh_ref[...], dhe_ref[...])
     ext = both[:, :chan] + both[:, chan:]
     hi, lo = split(jnp.concatenate([ext[:half], ext[half + atoms :]], axis=0))
@@ -416,6 +416,11 @@
     dh_ref[:, 0:atoms] = (spread[:atoms] + ext[half : half + atoms]).T + side_ref[:, 2:3]
     if n_near > atoms:
         dh_ref[:, atoms:] = spread[atoms:].T
+
+
+def back_first_kernel(dh_ref, sp1_ref, m1_ref, mixt_ref, rrr_ref, da_ref):
+    n_near = sp1_ref.shape[1]
+    rows = rrr_ref.shape[0] // 2
     wide_cols = 2 * LANES
 
     def back_first(j):
@@ -427,7 +432,7 @@
             out = dot(rrr_ref[...], jnp.concatenate([hi, lo], axis=0))
             da_ref[l, :, here] = out[:rows] + out[rows:]
 
-    in_pairs(0, n_near // wide_cols, back_first)
+    in_turns(0, n_near // wide_cols, back_first)
 
 
 def back_edge_kernel(plan, *refs):
@@ -470,8 +475,8 @@
         for i, value in enumerate((dux * back + along * ux, duy * back + along * uy, duz * back + along * uz)):
             dr_ref[i, :, here] = value
 
-    in_pairs(0, tiles, lambda t: back_geometry(t, True))
-    in_pairs(tiles, n_near // LANES, lambda t: back_geometry(t, False))
+    in_turns(0, tiles, lambda t: back_geometry(t, True))
+    in_turns(tiles, n_near // LANES, lambda t: back_geometry(t, False))
 
     def place_tile(t):
         here = pl.ds(pl.multiple_of(t * LANES, LANES), LANES)
@@ -493,7 +498,7 @@
                 val_ref[2 * i * top_rows : 2 * (i + 1) * top_rows, at] = jnp.concatenate(both, axis=0).astype(bf16)
             ohlo_ref[:, at] = jnp.where(place_ids == row(place[k : k + 1, :], LANES), 1.0, 0.0).astype(bf16)
 
-    in_pairs(0, n_near // LANES, place_tile)
+    in_turns(0, n_near // LANES, place_tile)
     landed = dot_nt(ohlo_ref[...], val_ref[...]).T
     fetch.wait()
     lines = push_ref.shape[0] // (n_wide + 1)
@@ -528,7 +533,11 @@
     return pltpu.with_memory_space_constraint(x, pltpu.HBM)
 
 
-def run(name, body, operands, results, scratch=(), far=(), mib=20, cost=None):
+def run(name, body, operands, results, scratch=(), far=(), cost=None):
+    sizes = [math.prod(x.shape) * x.dtype.itemsize for i, x in enumerate(operands) if i not in far]
+    sizes += [math.prod(shape) * jnp.dtype(dtype).itemsize for shape, dtype in results]
+    sizes += [math.prod(x.shape) * x.dtype.itemsize for x in scratch if x.memory_space == pltpu.VMEM]
+    limit = sum(sizes) + 4 * MIB
     specs = [pl.BlockSpec(memory_space=pltpu.HBM if i in far else pltpu.VMEM) for i in range(len(operands))]
     return pl.pallas_call(
         body,
@@ -536,7 +545,7 @@
         in_specs=specs,
         out_specs=tuple(pl.BlockSpec(memory_space=pltpu.VMEM) for _ in results),
         scratch_shapes=list(scratch),
-        compiler_params=pltpu.CompilerParams(vmem_limit_bytes=mib * MIB),
+        compiler_params=pltpu.CompilerParams(vmem_limit_bytes=limit),
         cost_estimate=cost,
         name=name,
     )(*[in_hbm(x) if i in far else x for i, x in enumerate(operands)])
@@ -578,7 +587,6 @@
     edges = slots * atoms
     top_rows = -(-len(wide) * atoms // LANES // 8) * 8
     lines = line_count(atoms)
-    mib = 12 + 6 * len(near)
     geo, y, yb, bk, bt, gidx, pick = run(
         "edges",
         functools.partial(edge_kernel, plan),
@@ -599,7 +607,6 @@
         (*blocks, y, bt, rrc, sides, mixa),
         (((ORDERS, chan, n_near), f32), ((chan, n_near), f32), ((2 * chan, n_near), bf16)),
         [pltpu.VMEM((ORDERS, 8 * bases, n_near), bf16), pltpu.VMEM((8, n_near), f32)],
-        mib=mib,
     )
     hj, w, car = run(
         "gather",
@@ -607,7 +614,6 @@
         (hs, oh, pick, bt, r2c),
         (((chan, edges), f32),) * 3,
         [pltpu.VMEM((2 * chan, 2 * atoms), bf16)],
-        mib=mib,
     )
     m2, dinv = run(
         "moments",
@@ -615,7 +621,6 @@
         (car, yb, mixa, mixt, sides),
         (((ORDERS, chan, atoms), f32), ((3 * chan, atoms), f32)),
         [pltpu.VMEM((3 * chan, atoms), f32)],
-        mib=mib,
     )
     dhe, q = run(
         "back_second",
@@ -623,16 +628,9 @@
         (m2, dinv, car, hj, w, yb, bt, geo, r2r),
         (((2 * chan, edges), bf16), ((8 * ORDERS, atoms), f32)),
         [pltpu.VMEM((2 * chan, edges), bf16), pltpu.VMEM((ORDERS, 8 * slots, atoms), f32)],
-        mib=mib,
     )
-    (da,) = run(
-        "back_first",
-        back_first_kernel,
-        (oh, pick, dhe, sp1, m1, mixt, rrr, sides),
-        (((ORDERS, 2 * bases, n_near), f32),),
-        [pltpu.VMEM((chan, n_near), f32)],
-        mib=mib,
-    )
+    (dh,) = run("scatter", scatter_kernel, (oh, pick, dhe, sides), (((chan, n_near), f32),))
+    (da,) = run("back_first", back_first_kernel, (dh, sp1, m1, mixt, rrr), (((ORDERS, 2 * bases, n_near), f32),))
     return run(
         "back_edges",
         functools.partial(back_edge_kernel, plan),
@@ -646,7 +644,6 @@
             pltpu.SemaphoreType.DMA(()),
         ],
         (len(blocks),),
-        mib=mib,
     )
 
 
@@ -693,20 +690,19 @@
     block_ref[HEAD:, :] = slot_ref[...].astype(f32)
 
 
-def turn_kernel(shape, bead_ref, domain_ref, mass_ref, source_ref, message_ref):
+def turn_kernel(shape, bead_ref, domain_ref, mass_ref, *refs):
     outer, inner, domains, wide = shape
+    message_ref = refs[outer]
     turns = mode_turns(outer * inner)
     lines = mass_ref.shape[0] // len(wide)
     my_domain = domain_ref[0]
-    my_outer = bead_ref[0] // inner
-    my_inner = bead_ref[0] - my_outer * inner
+    my_inner = lax.rem(bead_ref[0], inner)
     if domains > len(wide):
         message_ref[...] = jnp.zeros_like(message_ref)
     masses = [mass_ref[g * lines : (g + 1) * lines, :] for g in range(len(wide))]
     sources = []
     for z in range(outer):
-        at = lax.rem(my_outer + outer - z, outer)
-        sources.append([source_ref[at, pl.ds(g * lines, lines), :] for g in range(len(wide) + 1)])
+        sources.append([refs[z][g * lines : (g + 1) * lines, :] for g in range(len(wide) + 1)])
     for s in range(inner):
         wraps = jnp.full((lines, LANES), my_inner + s) >= inner
         weights = []
@@ -781,18 +777,19 @@
         blocks.append(lax.ppermute(block, "space", [(i, (i - offset) % domains) for i in range(domains)]))
     chosen = choose(block, embedding, radial_one, radial_two, mix_one, mix_two, read_one, read_two)
     pushed, masses = pushes(plan, blocks, moment_rows, chosen)
-    columns = [[z * inner + i for z in range(outer)] for i in range(inner)]
-    sources = lax.all_gather(pushed, "bead", axis=0, axis_index_groups=columns)
+    sources = [pushed]
+    for z in range(1, outer):
+        sources.append(lax.ppermute(pushed, "bead", [(b, (b + z * inner) % beads) for b in range(beads)]))
     here = [lax.axis_index(axis).astype(jnp.int32).reshape(1) for axis in ("bead", "space")]
     lines = line_count(atoms)
     messages = pl.pallas_call(
         functools.partial(turn_kernel, (outer, inner, domains, wide)),
         out_shape=jax.ShapeDtypeStruct((inner * domains, 2 * lines, LANES), f32),
-        in_specs=[smem, smem, vmem, vmem],
+        in_specs=[smem, smem, vmem] + [vmem] * outer,
         out_specs=vmem,
         compiler_params=small,
         name="turn",
-    )(*here, masses, sources)
+    )(*here, masses, *sources)
     rows = [[z * inner * domains + i for i in range(inner * domains)] for z in range(outer)]
     arrived = lax.all_to_all(messages, ("bead", "space"), 0, 0, axis_index_groups=rows, tiled=True)
     new_q, new_p = pl.pallas_call(

time: 57.7 us -> 46.5 us (0.81)
  blocking collectives: 21 us -> 8.48 us
  local copies, waits for them, and re-layouts: 6.6 us -> 0 us
  starting transfers between devices: 3.03 us -> 9.1 us
  waiting for transfers between devices: 0.01 us -> 2.91 us
  Pallas kernels: 26 us -> 25 us
    all_gather x1 -> x0, blocking collectives: 13.5 us -> none  [shards(): sources = lax.all_gather(pushed, 'bead', axis=0, axis_index_groups=columns)]
    unnamed x8 -> x0, local copies, waits for them, and re-layouts: 6.6 us -> none
    ppermute x0 -> x3, starting transfers between devices: none -> 6.07 us  [shards(): lax.ppermute(pushed, 'bead', [(b, (b + z * inner) % beads) for b in range...]
    ppermute x0 -> x3, waiting for transfers between devices: none -> 2.48 us  [shards(): lax.ppermute(pushed, 'bead', [(b, (b + z * inner) % beads) for b in range...]
    pallas_call x8 -> x9, Pallas kernels: 24.5 us -> 23.5 us  [run(): pl.pallas_call(body, out_shape=tuple((jax.ShapeDtypeStruct(shape, dtype)...]
    all_to_all x1, blocking collectives: 7.48 us -> 8.48 us  [shards(): lax.all_to_all(messages, ('bead', 'space'), 0, 0, axis_index_groups=rows,...]
  transfers between devices with their start and end apart: 1 -> 4, of which waited for: 0 -> 3; matrix products, arithmetic and copies ran while one was open for 0% -> 0% of each run, Pallas kernels for 3% -> 3%
where the time goes in v5:
time: 46.5 us; the launch traced here: 46.1 us
  Pallas kernels  25 us (54%)
  starting transfers between devices  9.1 us (20%)
  blocking collectives  8.48 us (18%)
  waiting for transfers between devices  2.91 us (6%)
  between operations  0.69 us (1%)
    pallas_call x9, Pallas kernels, run(): pl.pallas_call(body, out_shape=tuple((jax.ShapeDtypeStruct(shape, dtype)...  23.5 us
    all_to_all x1, blocking collectives, shards(): lax.all_to_all(messages, ('bead', 'space'), 0, 0, axis_index_groups=rows,...  8.48 us
    ppermute x3, starting transfers between devices, shards(): lax.ppermute(pushed, 'bead', [(b, (b + z * inner) % beads) for b in range...  6.07 us
    ppermute x1, starting transfers between devices, shards(): lax.ppermute(block, 'space', [(i, (i - offset) % domains) for i in range(...  3.03 us
    ppermute x3, waiting for transfers between devices, shards(): lax.ppermute(pushed, 'bead', [(b, (b + z * inner) % beads) for b in range...  2.48 us
  transfers between devices with their start and end apart: 4, of which 3 were waited for; matrix products, arithmetic and copies ran while one was open for 0% of the time, Pallas kernels for 3%

profile of v5, /device:TPU:0, one launch (start us, length us, event | category | flops | bytes accessed | tf_op | source)
XLA Modules:
  0.0 46.1 jit_solution(12464421736972532522)
XLA Ops:
  0.6 0.8 %pack.1.refs_0_.block_ref = f32[16,512]{1,0:T(8,128)S(1)} custom-call(f32[3,1,512]{2,1,0:T(1,128)} %bitcast.11, s32[1,512]{1,0:T(1,128)} %bitcast.12, s32[1,512]{1,0:T(1,128)} %bitcast.13, s32[8,512]{1,0:T(8,128)} %slot_src.1), custom_call_target="tpu_custom_call" | custom-call | tf_op jit(solution)/shard_map/pack/pallas_call | solution.py:760
  1.4 3.0 %collective-permute-start = (f32[16,512]{1,0:T(8,128)S(1)}, f32[16,512]{1,0:T(8,128)S(1)}, u32[]{:S(2)}, u32[]{:S(2)}) collective-permute-start(f32[16,512]{1,0:T(8,128)S(1)} %pack.1.refs_0_.block_ref), channel_id=1, source_target_pairs={{0,1},{1,0},{2,3},{3,2},{4,5},{5,4},{6,7},{7,6},{8,9},{9,8},{10,11... | collective-permute-start | bytes 98312 | tf_op jit(solution)/shard_map/ppermute | solution.py:777
  4.5 1.5 %choose.1 = (bf16[1024,4096]{1,0:T(8,128)(2,1)S(1)}, bf16[128,64]{1,0:T(8,128)(2,1)S(1)}, bf16[128,32]{1,0:T(8,128)(2,1)S(1)}, f32[128,128]{1,0:T(8,128)S(1)}, b...) custom-call(f32[16,512]{1,0:T(8,128)S(1)} %pack.1.refs_0_.block_ref,, ...), custom_call_target="tpu_custom_call" | custom-call | flops 2000000000 | bytes 2000000 | tf_op jit(solution)/shard_map/choose/pallas_call | solution.py:542
  5.9 0.4 collective-permute-done.refs_1_
  6.4 1.1 %edges.1 = (f32[6,8,1024]{2,1,0:T(8,128)S(1)}, f32[8,8,1024]{2,1,0:T(8,128)S(1)}, f32[8,8,8,512]{3,2,1,0:T(8,128)S(1)}, f32[8,8,1024]{2,1,0:T(8,128)S(1)}, f32[8...) custom-call(f32[16,512]{1,0:T(8,128)S(1)} %pack.1.refs_0_.block_ref, ...), custom_call_target="tpu_custom_call" | custom-call | tf_op jit(solution)/shard_map/edges/pallas_call | solution.py:542
  7.5 2.3 %first.1 = (f32[9,128,1024]{2,1,0:T(8,128)S(1)}, f32[128,1024]{1,0:T(8,128)S(1)}, bf16[256,1024]{1,0:T(8,128)(2,1)S(1)}) custom-call(f32[16,512]{1,0:T(8,128)S(1)} %pack.1.refs_0_.block_ref, f32[16,512]{1,0:T(8,128)S(1)} %collective-permute-done.refs_1_, f32[8,8,1024]{2,1,0:T(8,128)S(1)} %get-tuple-element.32.refs_2_.refs_4_, ...), custom_call_target="tpu_custom_call" | custom-call | tf_op jit(solution)/shard_map/first/pallas_call | solution.py:542
  9.8 3.2 %gather.1 = (f32[128,4096]{1,0:T(8,128)S(1)}, f32[128,4096]{1,0:T(8,128)S(1)}, f32[128,4096]{1,0:T(8,128)S(1)}) custom-call(bf16[256,1024]{1,0:T(8,128)(2,1)S(1)} %get-tuple-element.41.hs_ref, bf16[1024,4096]{1,0:T(8,128)(2,1)S(1)} %get-tuple-element.35.oh_ref, bf16[1024,512]{1,0:T(8,128)(2,1)S(1)} %get-tuple-element.36.pick_ref, ...), custom_call_target="tpu_custom_call" | custom-call | tf_op jit(solution)/shard_map/gather/pallas_call | solution.py:542
  13.1 2.7 %moments.1 = (f32[9,128,512]{2,1,0:T(8,128)S(1)}, f32[384,512]{1,0:T(8,128)S(1)}) custom-call(f32[128,4096]{1,0:T(8,128)S(1)} %get-tuple-element.43.car_ref, f32[8,8,8,512]{3,2,1,0:T(8,128)S(1)} %get-tuple-element.44.yb_ref, bf16[2,256,384]{2,1,0:T(8,128)(2,1)S(1)} %get-tuple-element.40.refs_6_.mixa_ref, ...), custom_call_target="tpu_custom_call" | custom-call | tf_op jit(solution)/shard_map/moments/pallas_call | solution.py:542
  15.8 4.9 %back_second.1 = (bf16[256,4096]{1,0:T(8,128)(2,1)S(1)}, f32[72,512]{1,0:T(8,128)S(1)}) custom-call(f32[9,128,512]{2,1,0:T(8,128)S(1)} %get-tuple-element.46.m2_ref, f32[384,512]{1,0:T(8,128)S(1)} %get-tuple-element.47.dinv_ref, f32[128,4096]{1,0:T(8,128)S(1)} %get-tuple-element.43.car_ref, f32[128,4096]{1,0:T(8,128)S(1)} %get-tuple-element.48.hj_ref, ...), custom_call_target="tpu_custom_call" | custom-call | tf_op jit(solution)/shard_map/back_second/pallas_call | solution.py:542
  20.7 3.2 %scatter.1.dh_ref = f32[128,1024]{1,0:T(8,128)S(1)} custom-call(bf16[1024,4096]{1,0:T(8,128)(2,1)S(1)} %get-tuple-element.35.oh_ref, bf16[1024,512]{1,0:T(8,128)(2,1)S(1)} %get-tuple-element.36.pick_ref, bf16[256,4096]{1,0:T(8,128)(2,1)S(1)} %get-tuple-element.51.dhe_ref, f32[128,128]{1,0:T(8,128)S(1)} %get-tuple-element.39.refs_5_.side_ref), custom_call_target="tpu_custom_call" | custom-call | tf_op jit(solution)/shard_map/scatter/pallas_call | solution.py:542
  23.9 2.0 %back_first.1.refs_7_ = f32[9,16,1024]{2,1,0:T(8,128)S(1)} custom-call(f32[128,1024]{1,0:T(8,128)S(1)} %scatter.1.dh_ref, f32[128,1024]{1,0:T(8,128)S(1)} %get-tuple-element.52.sp1_ref, f32[9,128,1024]{2,1,0:T(8,128)S(1)} %get-tuple-element.53.m1_ref, bf16[2,3,256,128]{3,2,1,0:T(8,128)(2,1)S(1)} %get-tuple-element.45.mixt_ref, ...), custom_call_target="tpu_custom_call" | custom-call | tf_op jit(solution)/shard_map/back_first/pallas_call | solution.py:542
  25.9 2.5 %back_edges.1 = (f32[48,128]{1,0:T(8,128)S(1)}, f32[32,128]{1,0:T(8,128)S(1)}) custom-call(f32[16,512]{1,0:T(8,128)S(1)} %pack.1.refs_0_.block_ref, f32[16,512]{1,0:T(8,128)S(1)} %collective-permute-done.refs_1_, f32[3,1,512]{2,1,0:T(1,128)} %bitcast.10, f32[6,8,1024]{2,1,0:T(8,128)S(1)} %get-tuple-element.31.geo_ref.refs_3_, ...), custom_call_target="tpu_custom_call" | custom-call | tf_op jit(solution)/shard_map/back_edges/pallas_call | solution.py:542
  28.4 2.1 %collective-permute-start.1 = (f32[48,128]{1,0:T(8,128)S(1)}, f32[48,128]{1,0:T(8,128)S(1)}, u32[]{:S(2)}, u32[]{:S(2)}) collective-permute-start(f32[48,128]{1,0:T(8,128)S(1)} %get-tuple-element.57.refs_0_), channel_id=1, source_target_pairs={{0,8},{2,10},{4,12},{6,14},{8,16},{10,18},{12,20},{14,22},{16,24},... | collective-permute-start | bytes 73736 | tf_op jit(solution)/shard_map/ppermute | solution.py:782
  30.6 2.6 %collective-permute-start.2 = (f32[48,128]{1,0:T(8,128)S(1)}, f32[48,128]{1,0:T(8,128)S(1)}, u32[]{:S(2)}, u32[]{:S(2)}) collective-permute-start(f32[48,128]{1,0:T(8,128)S(1)} %get-tuple-element.57.refs_0_), channel_id=1, source_target_pairs={{0,16},{2,18},{4,20},{6,22},{8,24},{10,26},{12,28},{14,30},{16,0},... | collective-permute-start | bytes 73736 | tf_op jit(solution)/shard_map/ppermute | solution.py:782
  33.1 1.3 %collective-permute-start.3 = (f32[48,128]{1,0:T(8,128)S(1)}, f32[48,128]{1,0:T(8,128)S(1)}, u32[]{:S(2)}, u32[]{:S(2)}) collective-permute-start(f32[48,128]{1,0:T(8,128)S(1)} %get-tuple-element.57.refs_0_), channel_id=1, source_target_pairs={{0,24},{2,26},{4,28},{6,30},{8,0},{10,2},{12,4},{14,6},{16,8},{18,... | collective-permute-start | bytes 73736 | tf_op jit(solution)/shard_map/ppermute | solution.py:782
  34.5 0.0 collective-permute-done.1.refs_1_
  34.5 0.8 %collective-permute-done.2.refs_2_ = f32[48,128]{1,0:T(8,128)S(1)} collective-permute-done((f32[48,128]{1,0:T(8,128)S(1)}, f32[48,128]{1,0:T(8,128)S(1)}, u32[]{:S(2)}, u32[]{:S(2)}) %collective-permute-start.2) | collective-permute-done | bytes 24608 | tf_op jit(solution)/shard_map/ppermute | solution.py:782
  35.3 1.7 %collective-permute-done.3.refs_3_ = f32[48,128]{1,0:T(8,128)S(1)} collective-permute-done((f32[48,128]{1,0:T(8,128)S(1)}, f32[48,128]{1,0:T(8,128)S(1)}, u32[]{:S(2)}, u32[]{:S(2)}) %collective-permute-start.3) | collective-permute-done | bytes 24608 | tf_op jit(solution)/shard_map/ppermute | solution.py:782
  37.0 0.1 turn.1
  37.0 8.5 %all_to_all.5.arrived_ref = f32[8,32,128]{2,1,0:T(8,128)S(1)} all-to-all(f32[8,32,128]{2,1,0:T(8,128)S(1)} %turn.1), channel_id=1, replica_groups={{0,1,2,3,4,5,6,7},{8,9,10,11,12,13,14,15},{16,17,18,19,20,21,22,23},{24..., dimensions={0} | all-to-all | bytes 262144 | tf_op jit(solution)/shard_map/all_to_all | solution.py:794
  45.5 0.6 %sum.1 = (f32[3,1,512]{2,1,0:T(1,128)}, f32[3,1,512]{2,1,0:T(1,128)}) custom-call(f32[8,32,128]{2,1,0:T(8,128)S(1)} %all_to_all.5.arrived_ref), custom_call_target="tpu_custom_call" | custom-call | tf_op jit(solution)/shard_map/sum/pallas_call | solution.py:795
Async XLA Ops:
  1.4 4.9 %collective-permute-start = (f32[16,512]{1,0:T(8,128)S(1)}, f32[16,512]{1,0:T(8,128)S(1)}, u32[]{:S(2)}, u32[]{:S(2)}) collective-permute-start(f32[16,512]{1,0:T(8,128)S(1)} %pack.1.refs_0_.block_ref), channel_id=1, source_target_pairs={{0,1},{1,0},{2,3},{3,2},{4,5},{5,4},{6,7},{7,6},{8,9},{9,8},{10,11... | collective-permute-start | bytes 98312 | tf_op jit(solution)/shard_map/ppermute | solution.py:777
  28.4 6.1 %collective-permute-start.1 = (f32[48,128]{1,0:T(8,128)S(1)}, f32[48,128]{1,0:T(8,128)S(1)}, u32[]{:S(2)}, u32[]{:S(2)}) collective-permute-start(f32[48,128]{1,0:T(8,128)S(1)} %get-tuple-element.57.refs_0_), channel_id=1, source_target_pairs={{0,8},{2,10},{4,12},{6,14},{8,16},{10,18},{12,20},{14,22},{16,24},... | collective-permute-start | bytes 73736 | tf_op jit(solution)/shard_map/ppermute | solution.py:782
  30.6 4.7 %collective-permute-start.2 = (f32[48,128]{1,0:T(8,128)S(1)}, f32[48,128]{1,0:T(8,128)S(1)}, u32[]{:S(2)}, u32[]{:S(2)}) collective-permute-start(f32[48,128]{1,0:T(8,128)S(1)} %get-tuple-element.57.refs_0_), channel_id=1, source_target_pairs={{0,16},{2,18},{4,20},{6,22},{8,24},{10,26},{12,28},{14,30},{16,0},... | collective-permute-start | bytes 73736 | tf_op jit(solution)/shard_map/ppermute | solution.py:782
  33.1 3.8 %collective-permute-start.3 = (f32[48,128]{1,0:T(8,128)S(1)}, f32[48,128]{1,0:T(8,128)S(1)}, u32[]{:S(2)}, u32[]{:S(2)}) collective-permute-start(f32[48,128]{1,0:T(8,128)S(1)} %get-tuple-element.57.refs_0_), channel_id=1, source_target_pairs={{0,24},{2,26},{4,28},{6,30},{8,0},{10,2},{12,4},{14,6},{16,8},{18,... | collective-permute-start | bytes 73736 | tf_op jit(solution)/shard_map/ppermute | solution.py:782

commit v6 on v5

--- a/solution.py
+++ b/solution.py
@@ -223,7 +223,7 @@
     atoms, near, wide, _, _ = plan
     n_wide = len(wide)
     blocks = refs[:n_wide]
-    y_ref, bt_ref, rrc_ref, side_ref, mixa_ref, m1_ref, sp1_ref, hs_ref, as_ref, flag_ref = refs[n_wide:]
+    y_ref, bt_ref, rrc_ref, side_ref, mixa_ref, m1_ref, sp1_ref, hid_ref, as_ref, flag_ref = refs[n_wide:]
     slots = bt_ref.shape[0]
     bases = bt_ref.shape[1] // 2
     chan = m1_ref.shape[1]
@@ -260,36 +260,41 @@
         value = dot_parts(mixa_ref[0], hi, lo)
         act, slope = silu_parts(value)
         sp1_ref[:, here] = slope
-        hidden = act + emb0_col + embd_col * flag_ref[0:1, here]
-        hi, lo = split(hidden)
-        hs_ref[0:chan, here] = hi
-        hs_ref[chan : 2 * chan, here] = lo
+        hid_ref[:, here] = act + emb0_col + embd_col * flag_ref[0:1, here]
 
     in_turns(0, n_near // wide_cols, first)
 
 
-def gather_kernel(hs_ref, oh_ref, pick_ref, bt_ref, r2c_ref, hj_ref, w_ref, car_ref, ext_ref):
+def gather_kernel(hid_ref, gidx_ref, bt_ref, r2c_ref, hj_ref, w_ref, car_ref):
     slots = bt_ref.shape[0]
     bases = bt_ref.shape[1] // 2
-    chan = hj_ref.shape[0]
+    chan, n_near = hid_ref.shape
     atoms = hj_ref.shape[1] // slots
-    half = atoms // 2
-    ghosts = dot(hs_ref[...], pick_ref[...]).astype(bf16)
-    ext_ref[:, 0:half] = ghosts[:, :half]
-    ext_ref[:, half : half + atoms] = hs_ref[:, 0:atoms]
-    ext_ref[:, half + atoms :] = ghosts[:, half:]
-
-    def gather(k):
-        here = pl.ds(pl.multiple_of(k * atoms, LANES), atoms)
-        both = dot(ext_ref[...], oh_ref[:, here])
-        feat = both[:chan] + both[chan:]
+
+    for k in range(slots):
+        here = slice(k * atoms, (k + 1) * atoms)
         basis = split_rows(bt_ref[k, 0:bases, 0:atoms])
-        weight = dot(r2c_ref[...], jnp.concatenate([basis, basis], axis=0).astype(bf16))
-        hj_ref[:, here] = feat
-        w_ref[:, here] = weight
-        car_ref[:, here] = feat * weight
-
-    in_turns(0, slots, gather)
+        w_ref[:, here] = dot(r2c_ref[...], jnp.concatenate([basis, basis], axis=0).astype(bf16))
+
+    def gather(t, carry):
+        gidx = gidx_ref[:, pl.ds(pl.multiple_of(t * LANES, LANES), LANES)]
+        for k in range(slots):
+            at = pl.ds(pl.multiple_of(k * atoms + t * LANES, LANES), LANES)
+            mine = row(gidx[k : k + 1, :])
+            chunk_no = mine >> 7
+            place = mine & 127
+            for c in range(chan // 8):
+                rows = slice(8 * c, 8 * c + 8)
+                feat = None
+                for chunk in range(n_near // LANES):
+                    held = hid_ref[rows, chunk * LANES : (chunk + 1) * LANES]
+                    got = jnp.take_along_axis(held, place, axis=1, mode="promise_in_bounds")
+                    feat = got if feat is None else jnp.where(chunk_no == chunk, got, feat)
+                hj_ref[rows, at] = feat
+                car_ref[rows, at] = feat * w_ref[rows, at]
+        return carry
+
+    lax.fori_loop(0, atoms // LANES, gather, 0)
 
 
 def moment_kernel(car_ref, yb_ref, mixa_ref, mixt_ref, side_ref, m2_ref, dinv_ref, inv_ref):
@@ -408,14 +413,14 @@
     chan, n_near = dh_ref.shape
     atoms = pick_ref.shape[1]
     half = atoms // 2
-    both = dot_nt(oh_ref[...], dhe_ref[...])
-    ext = both[:, :chan] + both[:, chan:]
-    hi, lo = split(jnp.concatenate([ext[:half], ext[half + atoms :]], axis=0))
-    spread = dot(pick_ref[...], jnp.concatenate([hi, lo], axis=1))
-    spread = spread[:, :chan] + spread[:, chan:]
-    dh_ref[:, 0:atoms] = (spread[:atoms] + ext[half : half + atoms]).T + side_ref[:, 2:3]
+    both = dot_nt(dhe_ref[...], oh_ref[...])
+    ext = both[:chan] + both[chan:]
+    hi, lo = split(jnp.concatenate([ext[:, :half], ext[:, half + atoms :]], axis=1))
+    spread = dot_nt(jnp.concatenate([hi, lo], axis=0), pick_ref[...])
+    spread = spread[:chan] + spread[chan:]
+    dh_ref[:, 0:atoms] = spread[:, :atoms] + ext[:, half : half + atoms] + side_ref[:, 2:3]
     if n_near > atoms:
-        dh_ref[:, atoms:] = spread[atoms:].T
+        dh_ref[:, atoms:] = spread[:, atoms:]
 
 
 def back_first_kernel(dh_ref, sp1_ref, m1_ref, mixt_ref, rrr_ref, da_ref):
@@ -601,19 +606,18 @@
             ((n_near, atoms), bf16),
         ),
     )
-    m1, sp1, hs = run(
+    m1, sp1, hid = run(
         "first",
         functools.partial(first_kernel, plan),
         (*blocks, y, bt, rrc, sides, mixa),
-        (((ORDERS, chan, n_near), f32), ((chan, n_near), f32), ((2 * chan, n_near), bf16)),
+        (((ORDERS, chan, n_near), f32), ((chan, n_near), f32), ((chan, n_near), f32)),
         [pltpu.VMEM((ORDERS, 8 * bases, n_near), bf16), pltpu.VMEM((8, n_near), f32)],
     )
     hj, w, car = run(
         "gather",
         gather_kernel,
-        (hs, oh, pick, bt, r2c),
+        (hid, gidx, bt, r2c),
         (((chan, edges), f32),) * 3,
-        [pltpu.VMEM((2 * chan, 2 * atoms), bf16)],
     )
     m2, dinv = run(
         "moments",

time: 46.5 us -> 47.7 us (1.026)
  Pallas kernels: 25 us -> 26.2 us
    pallas_call x9, Pallas kernels: 23.5 us -> 24.7 us  [run(): pl.pallas_call(body, out_shape=tuple((jax.ShapeDtypeStruct(shape, dtype)...]
where the time goes in v6:
time: 47.7 us; the launch traced here: 47.4 us
  Pallas kernels  26.2 us (55%)
  starting transfers between devices  9.11 us (19%)
  blocking collectives  8.47 us (18%)
  waiting for transfers between devices  2.91 us (6%)
  between operations  0.7 us (1%)
    pallas_call x9, Pallas kernels, run(): pl.pallas_call(body, out_shape=tuple((jax.ShapeDtypeStruct(shape, dtype)...  24.7 us
    all_to_all x1, blocking collectives, shards(): lax.all_to_all(messages, ('bead', 'space'), 0, 0, axis_index_groups=rows,...  8.47 us
    ppermute x3, starting transfers between devices, shards(): lax.ppermute(pushed, 'bead', [(b, (b + z * inner) % beads) for b in range...  6.07 us
    ppermute x1, starting transfers between devices, shards(): lax.ppermute(block, 'space', [(i, (i - offset) % domains) for i in range(...  3.03 us
    ppermute x3, waiting for transfers between devices, shards(): lax.ppermute(pushed, 'bead', [(b, (b + z * inner) % beads) for b in range...  2.48 us
  transfers between devices with their start and end apart: 4, of which 3 were waited for; matrix products, arithmetic and copies ran while one was open for 0% of the time, Pallas kernels for 3%

profile of v6, /device:TPU:0, one launch (start us, length us, event | category | flops | bytes accessed | tf_op | source)
XLA Modules:
  0.0 47.4 jit_solution(14191223822557995203)
XLA Ops:
  0.6 0.8 %pack.1.refs_0_.block_ref = f32[16,512]{1,0:T(8,128)S(1)} custom-call(f32[3,1,512]{2,1,0:T(1,128)} %bitcast.11, s32[1,512]{1,0:T(1,128)} %bitcast.12, s32[1,512]{1,0:T(1,128)} %bitcast.13, s32[8,512]{1,0:T(8,128)} %slot_src.1), custom_call_target="tpu_custom_call" | custom-call | tf_op jit(solution)/shard_map/pack/pallas_call | solution.py:764
  1.4 3.0 %collective-permute-start = (f32[16,512]{1,0:T(8,128)S(1)}, f32[16,512]{1,0:T(8,128)S(1)}, u32[]{:S(2)}, u32[]{:S(2)}) collective-permute-start(f32[16,512]{1,0:T(8,128)S(1)} %pack.1.refs_0_.block_ref), channel_id=1, source_target_pairs={{0,1},{1,0},{2,3},{3,2},{4,5},{5,4},{6,7},{7,6},{8,9},{9,8},{10,11... | collective-permute-start | bytes 98312 | tf_op jit(solution)/shard_map/ppermute | solution.py:781
  4.5 1.5 %choose.1 = (bf16[1024,4096]{1,0:T(8,128)(2,1)S(1)}, bf16[128,64]{1,0:T(8,128)(2,1)S(1)}, bf16[128,32]{1,0:T(8,128)(2,1)S(1)}, f32[128,128]{1,0:T(8,128)S(1)}, b...) custom-call(f32[16,512]{1,0:T(8,128)S(1)} %pack.1.refs_0_.block_ref,, ...), custom_call_target="tpu_custom_call" | custom-call | flops 2000000000 | bytes 2000000 | tf_op jit(solution)/shard_map/choose/pallas_call | solution.py:547
  5.9 0.4 collective-permute-done.refs_1_
  6.4 1.1 %edges.1 = (f32[6,8,1024]{2,1,0:T(8,128)S(1)}, f32[8,8,1024]{2,1,0:T(8,128)S(1)}, f32[8,8,8,512]{3,2,1,0:T(8,128)S(1)}, f32[8,8,1024]{2,1,0:T(8,128)S(1)}, f32[8...) custom-call(f32[16,512]{1,0:T(8,128)S(1)} %pack.1.refs_0_.block_ref, ...), custom_call_target="tpu_custom_call" | custom-call | tf_op jit(solution)/shard_map/edges/pallas_call | solution.py:547
  7.5 2.2 %first.1 = (f32[9,128,1024]{2,1,0:T(8,128)S(1)}, f32[128,1024]{1,0:T(8,128)S(1)}, f32[128,1024]{1,0:T(8,128)S(1)}) custom-call(f32[16,512]{1,0:T(8,128)S(1)} %pack.1.refs_0_.block_ref, f32[16,512]{1,0:T(8,128)S(1)} %collective-permute-done.refs_1_, f32[8,8,1024]{2,1,0:T(8,128)S(1)} %get-tuple-element.32.refs_2_.refs_4_, ...), custom_call_target="tpu_custom_call" | custom-call | tf_op jit(solution)/shard_map/first/pallas_call | solution.py:547
  9.7 5.1 %gather.1 = (f32[128,4096]{1,0:T(8,128)S(1)}, f32[128,4096]{1,0:T(8,128)S(1)}, f32[128,4096]{1,0:T(8,128)S(1)}) custom-call(f32[128,1024]{1,0:T(8,128)S(1)} %get-tuple-element.41.hid_ref, s32[8,1024]{1,0:T(8,128)S(1)} %get-tuple-element.34.gidx_ref.refs_6_, f32[8,16,1024]{2,1,0:T(8,128)S(1)} %get-tuple-element.37.refs_3_.bt_ref, ...), custom_call_target="tpu_custom_call" | custom-call | tf_op jit(solution)/shard_map/gather/pallas_call | solution.py:547
  14.9 2.7 %moments.1 = (f32[9,128,512]{2,1,0:T(8,128)S(1)}, f32[384,512]{1,0:T(8,128)S(1)}) custom-call(f32[128,4096]{1,0:T(8,128)S(1)} %get-tuple-element.43.car_ref, f32[8,8,8,512]{3,2,1,0:T(8,128)S(1)} %get-tuple-element.44.yb_ref, bf16[2,256,384]{2,1,0:T(8,128)(2,1)S(1)} %get-tuple-element.40.refs_6_.mixa_ref, ...), custom_call_target="tpu_custom_call" | custom-call | tf_op jit(solution)/shard_map/moments/pallas_call | solution.py:547
  17.5 4.9 %back_second.1 = (bf16[256,4096]{1,0:T(8,128)(2,1)S(1)}, f32[72,512]{1,0:T(8,128)S(1)}) custom-call(f32[9,128,512]{2,1,0:T(8,128)S(1)} %get-tuple-element.46.m2_ref, f32[384,512]{1,0:T(8,128)S(1)} %get-tuple-element.47.dinv_ref, f32[128,4096]{1,0:T(8,128)S(1)} %get-tuple-element.43.car_ref, f32[128,4096]{1,0:T(8,128)S(1)} %get-tuple-element.48.hj_ref, ...), custom_call_target="tpu_custom_call" | custom-call | tf_op jit(solution)/shard_map/back_second/pallas_call | solution.py:547
  22.5 2.7 %scatter.1.dh_ref = f32[128,1024]{1,0:T(8,128)S(1)} custom-call(bf16[1024,4096]{1,0:T(8,128)(2,1)S(1)} %get-tuple-element.35.oh_ref, bf16[1024,512]{1,0:T(8,128)(2,1)S(1)} %get-tuple-element.36.pick_ref, bf16[256,4096]{1,0:T(8,128)(2,1)S(1)} %get-tuple-element.51.dhe_ref, f32[128,128]{1,0:T(8,128)S(1)} %get-tuple-element.39.refs_5_.side_ref), custom_call_target="tpu_custom_call" | custom-call | tf_op jit(solution)/shard_map/scatter/pallas_call | solution.py:547
  25.2 1.9 %back_first.1.refs_7_ = f32[9,16,1024]{2,1,0:T(8,128)S(1)} custom-call(f32[128,1024]{1,0:T(8,128)S(1)} %scatter.1.dh_ref, f32[128,1024]{1,0:T(8,128)S(1)} %get-tuple-element.52.sp1_ref, f32[9,128,1024]{2,1,0:T(8,128)S(1)} %get-tuple-element.53.m1_ref, bf16[2,3,256,128]{3,2,1,0:T(8,128)(2,1)S(1)} %get-tuple-element.45.mixt_ref, ...), custom_call_target="tpu_custom_call" | custom-call | tf_op jit(solution)/shard_map/back_first/pallas_call | solution.py:547
  27.1 2.5 %back_edges.1 = (f32[48,128]{1,0:T(8,128)S(1)}, f32[32,128]{1,0:T(8,128)S(1)}) custom-call(f32[16,512]{1,0:T(8,128)S(1)} %pack.1.refs_0_.block_ref, f32[16,512]{1,0:T(8,128)S(1)} %collective-permute-done.refs_1_, f32[3,1,512]{2,1,0:T(1,128)} %bitcast.10, f32[6,8,1024]{2,1,0:T(8,128)S(1)} %get-tuple-element.31.geo_ref.refs_3_, ...), custom_call_target="tpu_custom_call" | custom-call | tf_op jit(solution)/shard_map/back_edges/pallas_call | solution.py:547
  29.7 2.1 %collective-permute-start.1 = (f32[48,128]{1,0:T(8,128)S(1)}, f32[48,128]{1,0:T(8,128)S(1)}, u32[]{:S(2)}, u32[]{:S(2)}) collective-permute-start(f32[48,128]{1,0:T(8,128)S(1)} %get-tuple-element.57.refs_0_), channel_id=1, source_target_pairs={{0,8},{2,10},{4,12},{6,14},{8,16},{10,18},{12,20},{14,22},{16,24},... | collective-permute-start | bytes 73736 | tf_op jit(solution)/shard_map/ppermute | solution.py:786
  31.8 2.6 %collective-permute-start.2 = (f32[48,128]{1,0:T(8,128)S(1)}, f32[48,128]{1,0:T(8,128)S(1)}, u32[]{:S(2)}, u32[]{:S(2)}) collective-permute-start(f32[48,128]{1,0:T(8,128)S(1)} %get-tuple-element.57.refs_0_), channel_id=1, source_target_pairs={{0,16},{2,18},{4,20},{6,22},{8,24},{10,26},{12,28},{14,30},{16,0},... | collective-permute-start | bytes 73736 | tf_op jit(solution)/shard_map/ppermute | solution.py:786
  34.4 1.3 %collective-permute-start.3 = (f32[48,128]{1,0:T(8,128)S(1)}, f32[48,128]{1,0:T(8,128)S(1)}, u32[]{:S(2)}, u32[]{:S(2)}) collective-permute-start(f32[48,128]{1,0:T(8,128)S(1)} %get-tuple-element.57.refs_0_), channel_id=1, source_target_pairs={{0,24},{2,26},{4,28},{6,30},{8,0},{10,2},{12,4},{14,6},{16,8},{18,... | collective-permute-start | bytes 73736 | tf_op jit(solution)/shard_map/ppermute | solution.py:786
  35.7 0.0 collective-permute-done.1.refs_1_
  35.7 0.8 %collective-permute-done.2.refs_2_ = f32[48,128]{1,0:T(8,128)S(1)} collective-permute-done((f32[48,128]{1,0:T(8,128)S(1)}, f32[48,128]{1,0:T(8,128)S(1)}, u32[]{:S(2)}, u32[]{:S(2)}) %collective-permute-start.2) | collective-permute-done | bytes 24608 | tf_op jit(solution)/shard_map/ppermute | solution.py:786
  36.5 1.7 %collective-permute-done.3.refs_3_ = f32[48,128]{1,0:T(8,128)S(1)} collective-permute-done((f32[48,128]{1,0:T(8,128)S(1)}, f32[48,128]{1,0:T(8,128)S(1)}, u32[]{:S(2)}, u32[]{:S(2)}) %collective-permute-start.3) | collective-permute-done | bytes 24608 | tf_op jit(solution)/shard_map/ppermute | solution.py:786
  38.2 0.1 turn.1
  38.3 8.5 %all_to_all.5.arrived_ref = f32[8,32,128]{2,1,0:T(8,128)S(1)} all-to-all(f32[8,32,128]{2,1,0:T(8,128)S(1)} %turn.1), channel_id=1, replica_groups={{0,1,2,3,4,5,6,7},{8,9,10,11,12,13,14,15},{16,17,18,19,20,21,22,23},{24..., dimensions={0} | all-to-all | bytes 262144 | tf_op jit(solution)/shard_map/all_to_all | solution.py:798
  46.8 0.6 %sum.1 = (f32[3,1,512]{2,1,0:T(1,128)}, f32[3,1,512]{2,1,0:T(1,128)}) custom-call(f32[8,32,128]{2,1,0:T(8,128)S(1)} %all_to_all.5.arrived_ref), custom_call_target="tpu_custom_call" | custom-call | tf_op jit(solution)/shard_map/sum/pallas_call | solution.py:799
Async XLA Ops:
  1.4 4.9 %collective-permute-start = (f32[16,512]{1,0:T(8,128)S(1)}, f32[16,512]{1,0:T(8,128)S(1)}, u32[]{:S(2)}, u32[]{:S(2)}) collective-permute-start(f32[16,512]{1,0:T(8,128)S(1)} %pack.1.refs_0_.block_ref), channel_id=1, source_target_pairs={{0,1},{1,0},{2,3},{3,2},{4,5},{5,4},{6,7},{7,6},{8,9},{9,8},{10,11... | collective-permute-start | bytes 98312 | tf_op jit(solution)/shard_map/ppermute | solution.py:781
  29.7 6.1 %collective-permute-start.1 = (f32[48,128]{1,0:T(8,128)S(1)}, f32[48,128]{1,0:T(8,128)S(1)}, u32[]{:S(2)}, u32[]{:S(2)}) collective-permute-start(f32[48,128]{1,0:T(8,128)S(1)} %get-tuple-element.57.refs_0_), channel_id=1, source_target_pairs={{0,8},{2,10},{4,12},{6,14},{8,16},{10,18},{12,20},{14,22},{16,24},... | collective-permute-start | bytes 73736 | tf_op jit(solution)/shard_map/ppermute | solution.py:786
  31.8 4.7 %collective-permute-start.2 = (f32[48,128]{1,0:T(8,128)S(1)}, f32[48,128]{1,0:T(8,128)S(1)}, u32[]{:S(2)}, u32[]{:S(2)}) collective-permute-start(f32[48,128]{1,0:T(8,128)S(1)} %get-tuple-element.57.refs_0_), channel_id=1, source_target_pairs={{0,16},{2,18},{4,20},{6,22},{8,24},{10,26},{12,28},{14,30},{16,0},... | collective-permute-start | bytes 73736 | tf_op jit(solution)/shard_map/ppermute | solution.py:786
  34.4 3.8 %collective-permute-start.3 = (f32[48,128]{1,0:T(8,128)S(1)}, f32[48,128]{1,0:T(8,128)S(1)}, u32[]{:S(2)}, u32[]{:S(2)}) collective-permute-start(f32[48,128]{1,0:T(8,128)S(1)} %get-tuple-element.57.refs_0_), channel_id=1, source_target_pairs={{0,24},{2,26},{4,28},{6,30},{8,0},{10,2},{12,4},{14,6},{16,8},{18,... | collective-permute-start | bytes 73736 | tf_op jit(solution)/shard_map/ppermute | solution.py:786

commit v7 on v6

--- a/solution.py
+++ b/solution.py
@@ -223,7 +223,7 @@
     atoms, near, wide, _, _ = plan
     n_wide = len(wide)
     blocks = refs[:n_wide]
-    y_ref, bt_ref, rrc_ref, side_ref, mixa_ref, m1_ref, sp1_ref, hid_ref, as_ref, flag_ref = refs[n_wide:]
+    y_ref, bt_ref, rrc_ref, side_ref, mixa_ref, m1_ref, sp1_ref, hid_ref, hs_ref, as_ref, flag_ref = refs[n_wide:]
     slots = bt_ref.shape[0]
     bases = bt_ref.shape[1] // 2
     chan = m1_ref.shape[1]
@@ -260,27 +260,41 @@
         value = dot_parts(mixa_ref[0], hi, lo)
         act, slope = silu_parts(value)
         sp1_ref[:, here] = slope
-        hid_ref[:, here] = act + emb0_col + embd_col * flag_ref[0:1, here]
+        hidden = act + emb0_col + embd_col * flag_ref[0:1, here]
+        hid_ref[:, here] = hidden
+        hi, lo = split(hidden)
+        hs_ref[0:chan, here] = hi
+        hs_ref[chan : 2 * chan, here] = lo
 
     in_turns(0, n_near // wide_cols, first)
 
 
-def gather_kernel(hid_ref, gidx_ref, bt_ref, r2c_ref, hj_ref, w_ref, car_ref):
+def gather_kernel(hid_ref, hs_ref, oh_ref, pick_ref, gidx_ref, bt_ref, r2c_ref, hj_ref, w_ref, car_ref, ext_ref):
     slots = bt_ref.shape[0]
     bases = bt_ref.shape[1] // 2
     chan, n_near = hid_ref.shape
     atoms = hj_ref.shape[1] // slots
-
+    half = atoms // 2
+    by_lane = 2 * LANES if atoms > 2 * LANES else 0
+    by_product = 2 * atoms - by_lane
+    ghosts = dot(hs_ref[...], pick_ref[...]).astype(bf16)
+    ext_ref[:, 0:half] = ghosts[:, :half]
+    ext_ref[:, half : half + atoms] = hs_ref[:, 0:atoms]
+    ext_ref[:, half + atoms :] = ghosts[:, half:]
     for k in range(slots):
         here = slice(k * atoms, (k + 1) * atoms)
         basis = split_rows(bt_ref[k, 0:bases, 0:atoms])
         w_ref[:, here] = dot(r2c_ref[...], jnp.concatenate([basis, basis], axis=0).astype(bf16))
 
-    def gather(t, carry):
-        gidx = gidx_ref[:, pl.ds(pl.multiple_of(t * LANES, LANES), LANES)]
-        for k in range(slots):
-            at = pl.ds(pl.multiple_of(k * atoms + t * LANES, LANES), LANES)
-            mine = row(gidx[k : k + 1, :])
+    def gather(pair, carry):
+        first = pl.multiple_of(pair * 2 * atoms, LANES)
+        here = pl.ds(first, by_product)
+        both = dot(ext_ref[...], oh_ref[:, here])
+        wanted = gidx_ref[pl.ds(2 * pair + 1, 1), 0:atoms]
+        for t in range(by_lane // LANES):
+            at = pl.ds(pl.multiple_of(first + (by_product + t * LANES), LANES), LANES)
+            start = atoms - by_lane + t * LANES
+            mine = row(wanted[:, start : start + LANES])
             chunk_no = mine >> 7
             place = mine & 127
             for c in range(chan // 8):
@@ -292,9 +306,12 @@
                     feat = got if feat is None else jnp.where(chunk_no == chunk, got, feat)
                 hj_ref[rows, at] = feat
                 car_ref[rows, at] = feat * w_ref[rows, at]
+        feat = both[:chan] + both[chan:]
+        hj_ref[:, here] = feat
+        car_ref[:, here] = feat * w_ref[:, here]
         return carry
 
-    lax.fori_loop(0, atoms // LANES, gather, 0)
+    lax.fori_loop(0, slots // 2, gather, 0)
 
 
 def moment_kernel(car_ref, yb_ref, mixa_ref, mixt_ref, side_ref, m2_ref, dinv_ref, inv_ref):
@@ -342,10 +359,8 @@
             dinv_ref[g * chan : (g + 1) * chan, cols] = dot_parts(mixt_ref[1, g], hi, lo)
 
 
-def back_second_kernel(m2_ref, dinv_ref, car_ref, hj_ref, w_ref, yb_ref, bt_ref, geo_ref, r2r_ref,
-                       dhe_ref, q_ref, dw_ref, p_ref):
+def back_second_kernel(m2_ref, dinv_ref, car_ref, hj_ref, w_ref, yb_ref, dhe_ref, dw_ref, p_ref):
     slots = yb_ref.shape[1]
-    bases = bt_ref.shape[1] // 2
     chan, atoms = m2_ref.shape[1:]
     tiles = atoms // LANES
     pairs = chan // 16
@@ -391,29 +406,38 @@
         acc = lax.fori_loop(0, pairs // per_turn, over, start)
         for kk in range(k_step):
             for l in range(1, ORDERS):
-                p_ref[l, pl.ds(pl.multiple_of((k0 + kk) * 8, 8), 8), cols] = acc[kk * (ORDERS - 1) + l - 1]
+                p_ref[l - 1, pl.ds(pl.multiple_of((k0 + kk) * 8, 8), 8), cols] = acc[kk * (ORDERS - 1) + l - 1]
         return carry
 
     lax.fori_loop(0, tiles * 2, back_moments, 0)
+
+
+def scatter_kernel(oh_ref, pick_ref, dhe_ref, side_ref, dw_ref, p_ref, bt_ref, geo_ref, r2r_ref, gidx_ref,
+                   dh_ref, q_ref, ohlo_ref, ds_ref):
+    chan, n_near = dh_ref.shape
+    slots = bt_ref.shape[0]
+    bases = bt_ref.shape[1] // 2
+    atoms = pick_ref.shape[1]
+    half = atoms // 2
+    both = dot_nt(dhe_ref[...], oh_ref[...])
+    ids16 = lax.broadcasted_iota(jnp.int32, (LANES, n_near), 0).astype(jnp.int16)
+    one16 = jnp.ones((LANES, n_near), bf16)
+    zero16 = jnp.zeros((LANES, n_near), bf16)
+    for k in range(slots):
+        place = jnp.broadcast_to(gidx_ref[k : k + 1, :] & 127, (LANES, n_near)).astype(jnp.int16)
+        ohlo_ref[:, k * n_near : (k + 1) * n_near] = jnp.where(place == ids16, one16, zero16)
     for k in range(slots):
         here = slice(k * atoms, (k + 1) * atoms)
-        both = dot(r2r_ref[...], dw_ref[:, here])
-        dbasis = both[:bases] + both[bases:]
+        small = dot(r2r_ref[...], dw_ref[:, here])
+        dbasis = small[:bases] + small[bases:]
         basis = bt_ref[k, 0:bases, 0:atoms]
         reach = 1.0 + lax.broadcasted_iota(jnp.int32, (bases, atoms), 0).astype(f32)
-        p_ref[0, k * 8 : k * 8 + 8, :] = dbasis * basis * (reach - row(geo_ref[4, k : k + 1, 0:atoms], bases))
+        ds_ref[k * 8 : k * 8 + 8, :] = dbasis * basis * (reach - row(geo_ref[4, k : k + 1, 0:atoms], bases))
     lane = lax.broadcasted_iota(jnp.int32, (slots, 16 * slots), 1)
     sub = lax.broadcasted_iota(jnp.int32, (slots, 16 * slots), 0)
     adder = jnp.where(((lane >> 3) & (slots - 1)) == sub, 1.0, 0.0).astype(bf16)
     for l in range(ORDERS):
-        q_ref[8 * l : 8 * l + 8, :] = dot(adder, split_rows(p_ref[l, :, :]).astype(bf16))
-
-
-def scatter_kernel(oh_ref, pick_ref, dhe_ref, side_ref, dh_ref):
-    chan, n_near = dh_ref.shape
-    atoms = pick_ref.shape[1]
-    half = atoms // 2
-    both = dot_nt(dhe_ref[...], oh_ref[...])
+        q_ref[8 * l : 8 * l + 8, :] = dot(adder, split_rows(p_ref[l - 1, :, :] if l else ds_ref[...]).astype(bf16))
     ext = both[:chan] + both[chan:]
     hi, lo = split(jnp.concatenate([ext[:, :half], ext[:, half + atoms :]], axis=1))
     spread = dot_nt(jnp.concatenate([hi, lo], axis=0), pick_ref[...])
@@ -444,8 +468,8 @@
     atoms, near, wide, _, _ = plan
     n_wide = len(wide)
     blocks = refs[:n_wide]
-    moment_src, geo_ref, y_ref, bk_ref, gidx_ref, da_ref, q_ref = refs[n_wide : n_wide + 7]
-    push_ref, mass_ref, val_ref, ohlo_ref, dr_ref, moment_ref, sem = refs[n_wide + 7 :]
+    moment_src, geo_ref, y_ref, bk_ref, gidx_ref, da_ref, q_ref, ohlo_ref = refs[n_wide : n_wide + 8]
+    push_ref, mass_ref, val_ref, dr_ref, moment_ref, sem = refs[n_wide + 8 :]
     fetch = pltpu.make_async_copy(moment_src, moment_ref, sem)
     fetch.start()
     bases, slots, n_near = bk_ref.shape
@@ -487,24 +511,21 @@
         here = pl.ds(pl.multiple_of(t * LANES, LANES), LANES)
         gidx = gidx_ref[:, here]
         chunk_no = gidx >> 7
-        place = gidx & 127
         parts = []
         for i in range(3):
             value = dr_ref[i, :, here]
             hi = value.astype(bf16).astype(f32)
             parts.append((hi, value - hi))
         chunk_ids = lax.broadcasted_iota(jnp.int32, (top_rows, LANES), 0)
-        place_ids = lax.broadcasted_iota(jnp.int32, (LANES, LANES), 0)
         for k in range(slots):
             at = pl.ds(pl.multiple_of(k * n_near + t * LANES, LANES), LANES)
             hit = chunk_ids == row(chunk_no[k : k + 1, :], top_rows)
             for i in range(3):
                 both = [jnp.where(hit, row(part[k : k + 1, :], top_rows), 0.0) for part in parts[i]]
                 val_ref[2 * i * top_rows : 2 * (i + 1) * top_rows, at] = jnp.concatenate(both, axis=0).astype(bf16)
-            ohlo_ref[:, at] = jnp.where(place_ids == row(place[k : k + 1, :], LANES), 1.0, 0.0).astype(bf16)
 
     in_turns(0, n_near // LANES, place_tile)
-    landed = dot_nt(ohlo_ref[...], val_ref[...]).T
+    landed = dot_nt(val_ref[...], ohlo_ref[...])
     fetch.wait()
     lines = push_ref.shape[0] // (n_wide + 1)
     for i in range(3):
@@ -606,18 +627,19 @@
             ((n_near, atoms), bf16),
         ),
     )
-    m1, sp1, hid = run(
+    m1, sp1, hid, hs = run(
         "first",
         functools.partial(first_kernel, plan),
         (*blocks, y, bt, rrc, sides, mixa),
-        (((ORDERS, chan, n_near), f32), ((chan, n_near), f32), ((chan, n_near), f32)),
+        (((ORDERS, chan, n_near), f32), ((chan, n_near), f32), ((chan, n_near), f32), ((2 * chan, n_near), bf16)),
         [pltpu.VMEM((ORDERS, 8 * bases, n_near), bf16), pltpu.VMEM((8, n_near), f32)],
     )
     hj, w, car = run(
         "gather",
         gather_kernel,
-        (hid, gidx, bt, r2c),
+        (hid, hs, oh, pick, gidx, bt, r2c),
         (((chan, edges), f32),) * 3,
+        [pltpu.VMEM((2 * chan, 2 * atoms), bf16)],
     )
     m2, dinv = run(
         "moments",
@@ -626,23 +648,27 @@
         (((ORDERS, chan, atoms), f32), ((3 * chan, atoms), f32)),
         [pltpu.VMEM((3 * chan, atoms), f32)],
     )
-    dhe, q = run(
+    dhe, dw, p = run(
         "back_second",
         back_second_kernel,
-        (m2, dinv, car, hj, w, yb, bt, geo, r2r),
-        (((2 * chan, edges), bf16), ((8 * ORDERS, atoms), f32)),
-        [pltpu.VMEM((2 * chan, edges), bf16), pltpu.VMEM((ORDERS, 8 * slots, atoms), f32)],
-    )
-    (dh,) = run("scatter", scatter_kernel, (oh, pick, dhe, sides), (((chan, n_near), f32),))
+        (m2, dinv, car, hj, w, yb),
+        (((2 * chan, edges), bf16), ((2 * chan, edges), bf16), ((ORDERS - 1, 8 * slots, atoms), f32)),
+    )
+    dh, q, ohlo = run(
+        "scatter",
+        scatter_kernel,
+        (oh, pick, dhe, sides, dw, p, bt, geo, r2r, gidx),
+        (((chan, n_near), f32), ((8 * ORDERS, atoms), f32), ((LANES, slots * n_near), bf16)),
+        [pltpu.VMEM((8 * slots, atoms), f32)],
+    )
     (da,) = run("back_first", back_first_kernel, (dh, sp1, m1, mixt, rrr), (((ORDERS, 2 * bases, n_near), f32),))
     return run(
         "back_edges",
         functools.partial(back_edge_kernel, plan),
-        (*blocks, momenta, geo, y, bk, gidx, da, q),
+        (*blocks, momenta, geo, y, bk, gidx, da, q, ohlo),
         ((((len(wide) + 1) * lines, LANES), f32), ((len(wide) * lines, LANES), f32)),
         [
             pltpu.VMEM((6 * top_rows, slots * n_near), bf16),
-            pltpu.VMEM((LANES, slots * n_near), bf16),
             pltpu.VMEM((3, slots, n_near), f32),
             pltpu.VMEM(momenta.shape, f32),
             pltpu.SemaphoreType.DMA(()),

time: 47.7 us -> 45.2 us (0.948)
  Pallas kernels: 26.2 us -> 23.7 us
    pallas_call x9, Pallas kernels: 24.7 us -> 22.2 us  [run(): pl.pallas_call(body, out_shape=tuple((jax.ShapeDtypeStruct(shape, dtype)...]
where the time goes in v7:
time: 45.2 us; the launch traced here: 44.9 us
  Pallas kernels  23.7 us (52%)
  starting transfers between devices  9.09 us (20%)
  blocking collectives  8.47 us (19%)
  waiting for transfers between devices  2.92 us (6%)
  between operations  0.71 us (2%)
    pallas_call x9, Pallas kernels, run(): pl.pallas_call(body, out_shape=tuple((jax.ShapeDtypeStruct(shape, dtype)...  22.2 us
    all_to_all x1, blocking collectives, shards(): lax.all_to_all(messages, ('bead', 'space'), 0, 0, axis_index_groups=rows,...  8.47 us
    ppermute x3, starting transfers between devices, shards(): lax.ppermute(pushed, 'bead', [(b, (b + z * inner) % beads) for b in range...  6.06 us
    ppermute x1, starting transfers between devices, shards(): lax.ppermute(block, 'space', [(i, (i - offset) % domains) for i in range(...  3.03 us
    ppermute x3, waiting for transfers between devices, shards(): lax.ppermute(pushed, 'bead', [(b, (b + z * inner) % beads) for b in range...  2.49 us
  transfers between devices with their start and end apart: 4, of which 3 were waited for; matrix products, arithmetic and copies ran while one was open for 0% of the time, Pallas kernels for 3%

profile of v7, /device:TPU:0, one launch (start us, length us, event | category | flops | bytes accessed | tf_op | source)
XLA Modules:
  0.0 44.9 jit_solution(13991961024496003765)
XLA Ops:
  0.6 0.8 %pack.1.refs_0_.block_ref = f32[16,512]{1,0:T(8,128)S(1)} custom-call(f32[3,1,512]{2,1,0:T(1,128)} %bitcast.10, s32[1,512]{1,0:T(1,128)} %bitcast.12, s32[1,512]{1,0:T(1,128)} %bitcast.13, s32[8,512]{1,0:T(8,128)} %slot_src.1), custom_call_target="tpu_custom_call" | custom-call | tf_op jit(solution)/shard_map/pack/pallas_call | solution.py:790
  1.4 3.0 %collective-permute-start = (f32[16,512]{1,0:T(8,128)S(1)}, f32[16,512]{1,0:T(8,128)S(1)}, u32[]{:S(2)}, u32[]{:S(2)}) collective-permute-start(f32[16,512]{1,0:T(8,128)S(1)} %pack.1.refs_0_.block_ref), channel_id=1, source_target_pairs={{0,1},{1,0},{2,3},{3,2},{4,5},{5,4},{6,7},{7,6},{8,9},{9,8},{10,11... | collective-permute-start | bytes 98312 | tf_op jit(solution)/shard_map/ppermute | solution.py:807
  4.5 1.5 %choose.1 = (bf16[1024,4096]{1,0:T(8,128)(2,1)S(1)}, bf16[128,64]{1,0:T(8,128)(2,1)S(1)}, bf16[128,32]{1,0:T(8,128)(2,1)S(1)}, f32[128,128]{1,0:T(8,128)S(1)}, b...) custom-call(f32[16,512]{1,0:T(8,128)S(1)} %pack.1.refs_0_.block_ref,, ...), custom_call_target="tpu_custom_call" | custom-call | flops 2000000000 | bytes 2000000 | tf_op jit(solution)/shard_map/choose/pallas_call | solution.py:568
  5.9 0.4 collective-permute-done.refs_1_
  6.4 1.1 %edges.1 = (f32[6,8,1024]{2,1,0:T(8,128)S(1)}, f32[8,8,1024]{2,1,0:T(8,128)S(1)}, f32[8,8,8,512]{3,2,1,0:T(8,128)S(1)}, f32[8,8,1024]{2,1,0:T(8,128)S(1)}, f32[8...) custom-call(f32[16,512]{1,0:T(8,128)S(1)} %pack.1.refs_0_.block_ref, ...), custom_call_target="tpu_custom_call" | custom-call | tf_op jit(solution)/shard_map/edges/pallas_call | solution.py:568
  7.5 2.3 %first.1 = (f32[9,128,1024]{2,1,0:T(8,128)S(1)}, f32[128,1024]{1,0:T(8,128)S(1)}, f32[128,1024]{1,0:T(8,128)S(1)}, bf16[256,1024]{1,0:T(8,128)(2,1)S(1)}) custom-call(f32[16,512]{1,0:T(8,128)S(1)} %pack.1.refs_0_.block_ref, f32[16,512]{1,0:T(8,128)S(1)} %collective-permute-done.refs_1_, f32[8,8,1024]{2,1,0:T(8,128)S(1)} %get-tuple-element.37.refs_2_.refs_4_, ...), custom_call_target="tpu_custom_call" | custom-call | tf_op jit(solution)/shard_map/first/pallas_call | solution.py:568
  9.8 3.2 %gather.1 = (f32[128,4096]{1,0:T(8,128)S(1)}, f32[128,4096]{1,0:T(8,128)S(1)}, f32[128,4096]{1,0:T(8,128)S(1)}) custom-call(f32[128,1024]{1,0:T(8,128)S(1)} %get-tuple-element.46.hid_ref, bf16[256,1024]{1,0:T(8,128)(2,1)S(1)} %get-tuple-element.47.hs_ref, bf16[1024,4096]{1,0:T(8,128)(2,1)S(1)} %get-tuple-element.40.oh_ref, ...), custom_call_target="tpu_custom_call" | custom-call | tf_op jit(solution)/shard_map/gather/pallas_call | solution.py:568
  13.0 2.7 %moments.1 = (f32[9,128,512]{2,1,0:T(8,128)S(1)}, f32[384,512]{1,0:T(8,128)S(1)}) custom-call(f32[128,4096]{1,0:T(8,128)S(1)} %get-tuple-element.49.car_ref, f32[8,8,8,512]{3,2,1,0:T(8,128)S(1)} %get-tuple-element.50.yb_ref, bf16[2,256,384]{2,1,0:T(8,128)(2,1)S(1)} %get-tuple-element.45.refs_6_.mixa_ref, ...), custom_call_target="tpu_custom_call" | custom-call | tf_op jit(solution)/shard_map/moments/pallas_call | solution.py:568
  15.7 4.4 %back_second.1 = (bf16[256,4096]{1,0:T(8,128)(2,1)S(1)}, bf16[256,4096]{1,0:T(8,128)(2,1)S(1)}, f32[8,64,512]{2,1,0:T(8,128)S(1)}) custom-call(f32[9,128,512]{2,1,0:T(8,128)S(1)} %get-tuple-element.52.m2_ref, f32[384,512]{1,0:T(8,128)S(1)} %get-tuple-element.53.dinv_ref, f32[128,4096]{1,0:T(8,128)S(1)} %get-tuple-element.49.car_ref, ...), custom_call_target="tpu_custom_call" | custom-call | tf_op jit(solution)/shard_map/back_second/pallas_call | solution.py:568
  20.1 3.3 %scatter.1 = (f32[128,1024]{1,0:T(8,128)S(1)}, f32[72,512]{1,0:T(8,128)S(1)}, bf16[128,8192]{1,0:T(8,128)(2,1)S(1)}) custom-call(bf16[1024,4096]{1,0:T(8,128)(2,1)S(1)} %get-tuple-element.40.oh_ref, bf16[1024,512]{1,0:T(8,128)(2,1)S(1)} %get-tuple-element.41.pick_ref, bf16[256,4096]{1,0:T(8,128)(2,1)S(1)} %get-tuple-element.56.dhe_ref, ...), custom_call_target="tpu_custom_call" | custom-call | tf_op jit(solution)/shard_map/scatter/pallas_call | solution.py:568
  23.4 2.0 %back_first.1.refs_7_ = f32[9,16,1024]{2,1,0:T(8,128)S(1)} custom-call(f32[128,1024]{1,0:T(8,128)S(1)} %get-tuple-element.60.dh_ref, f32[128,1024]{1,0:T(8,128)S(1)} %get-tuple-element.61.sp1_ref, f32[9,128,1024]{2,1,0:T(8,128)S(1)} %get-tuple-element.62.m1_ref, bf16[2,3,256,128]{3,2,1,0:T(8,128)(2,1)S(1)} %get-tuple-element.51.mixt_ref, ...), custom_call_target="tpu_custom_call" | custom-call | tf_op jit(solution)/shard_map/back_first/pallas_call | solution.py:568
  25.4 1.8 %back_edges.1 = (f32[48,128]{1,0:T(8,128)S(1)}, f32[32,128]{1,0:T(8,128)S(1)}) custom-call(f32[16,512]{1,0:T(8,128)S(1)} %pack.1.refs_0_.block_ref, f32[16,512]{1,0:T(8,128)S(1)} %collective-permute-done.refs_1_, f32[3,1,512]{2,1,0:T(1,128)} %bitcast.11, f32[6,8,1024]{2,1,0:T(8,128)S(1)} %get-tuple-element.36.geo_ref.refs_3_, ...), custom_call_target="tpu_custom_call" | custom-call | tf_op jit(solution)/shard_map/back_edges/pallas_call | solution.py:568
  27.1 2.1 %collective-permute-start.1 = (f32[48,128]{1,0:T(8,128)S(1)}, f32[48,128]{1,0:T(8,128)S(1)}, u32[]{:S(2)}, u32[]{:S(2)}) collective-permute-start(f32[48,128]{1,0:T(8,128)S(1)} %get-tuple-element.67.refs_0_), channel_id=1, source_target_pairs={{0,8},{2,10},{4,12},{6,14},{8,16},{10,18},{12,20},{14,22},{16,24},... | collective-permute-start | bytes 73736 | tf_op jit(solution)/shard_map/ppermute | solution.py:812
  29.3 2.6 %collective-permute-start.2 = (f32[48,128]{1,0:T(8,128)S(1)}, f32[48,128]{1,0:T(8,128)S(1)}, u32[]{:S(2)}, u32[]{:S(2)}) collective-permute-start(f32[48,128]{1,0:T(8,128)S(1)} %get-tuple-element.67.refs_0_), channel_id=1, source_target_pairs={{0,16},{2,18},{4,20},{6,22},{8,24},{10,26},{12,28},{14,30},{16,0},... | collective-permute-start | bytes 73736 | tf_op jit(solution)/shard_map/ppermute | solution.py:812
  31.9 1.3 %collective-permute-start.3 = (f32[48,128]{1,0:T(8,128)S(1)}, f32[48,128]{1,0:T(8,128)S(1)}, u32[]{:S(2)}, u32[]{:S(2)}) collective-permute-start(f32[48,128]{1,0:T(8,128)S(1)} %get-tuple-element.67.refs_0_), channel_id=1, source_target_pairs={{0,24},{2,26},{4,28},{6,30},{8,0},{10,2},{12,4},{14,6},{16,8},{18,... | collective-permute-start | bytes 73736 | tf_op jit(solution)/shard_map/ppermute | solution.py:812
  33.2 0.0 collective-permute-done.1.refs_1_
  33.2 0.8 %collective-permute-done.2.refs_2_ = f32[48,128]{1,0:T(8,128)S(1)} collective-permute-done((f32[48,128]{1,0:T(8,128)S(1)}, f32[48,128]{1,0:T(8,128)S(1)}, u32[]{:S(2)}, u32[]{:S(2)}) %collective-permute-start.2) | collective-permute-done | bytes 24608 | tf_op jit(solution)/shard_map/ppermute | solution.py:812
  34.0 1.7 %collective-permute-done.3.refs_3_ = f32[48,128]{1,0:T(8,128)S(1)} collective-permute-done((f32[48,128]{1,0:T(8,128)S(1)}, f32[48,128]{1,0:T(8,128)S(1)}, u32[]{:S(2)}, u32[]{:S(2)}) %collective-permute-start.3) | collective-permute-done | bytes 24608 | tf_op jit(solution)/shard_map/ppermute | solution.py:812
  35.7 0.1 turn.1
  35.8 8.5 %all_to_all.5.arrived_ref = f32[8,32,128]{2,1,0:T(8,128)S(1)} all-to-all(f32[8,32,128]{2,1,0:T(8,128)S(1)} %turn.1), channel_id=1, replica_groups={{0,1,2,3,4,5,6,7},{8,9,10,11,12,13,14,15},{16,17,18,19,20,21,22,23},{24..., dimensions={0} | all-to-all | bytes 262144 | tf_op jit(solution)/shard_map/all_to_all | solution.py:824
  44.2 0.6 %sum.1 = (f32[3,1,512]{2,1,0:T(1,128)}, f32[3,1,512]{2,1,0:T(1,128)}) custom-call(f32[8,32,128]{2,1,0:T(8,128)S(1)} %all_to_all.5.arrived_ref), custom_call_target="tpu_custom_call" | custom-call | tf_op jit(solution)/shard_map/sum/pallas_call | solution.py:825
Async XLA Ops:
  1.4 4.9 %collective-permute-start = (f32[16,512]{1,0:T(8,128)S(1)}, f32[16,512]{1,0:T(8,128)S(1)}, u32[]{:S(2)}, u32[]{:S(2)}) collective-permute-start(f32[16,512]{1,0:T(8,128)S(1)} %pack.1.refs_0_.block_ref), channel_id=1, source_target_pairs={{0,1},{1,0},{2,3},{3,2},{4,5},{5,4},{6,7},{7,6},{8,9},{9,8},{10,11... | collective-permute-start | bytes 98312 | tf_op jit(solution)/shard_map/ppermute | solution.py:807
  27.1 6.1 %collective-permute-start.1 = (f32[48,128]{1,0:T(8,128)S(1)}, f32[48,128]{1,0:T(8,128)S(1)}, u32[]{:S(2)}, u32[]{:S(2)}) collective-permute-start(f32[48,128]{1,0:T(8,128)S(1)} %get-tuple-element.67.refs_0_), channel_id=1, source_target_pairs={{0,8},{2,10},{4,12},{6,14},{8,16},{10,18},{12,20},{14,22},{16,24},... | collective-permute-start | bytes 73736 | tf_op jit(solution)/shard_map/ppermute | solution.py:812
  29.3 4.7 %collective-permute-start.2 = (f32[48,128]{1,0:T(8,128)S(1)}, f32[48,128]{1,0:T(8,128)S(1)}, u32[]{:S(2)}, u32[]{:S(2)}) collective-permute-start(f32[48,128]{1,0:T(8,128)S(1)} %get-tuple-element.67.refs_0_), channel_id=1, source_target_pairs={{0,16},{2,18},{4,20},{6,22},{8,24},{10,26},{12,28},{14,30},{16,0},... | collective-permute-start | bytes 73736 | tf_op jit(solution)/shard_map/ppermute | solution.py:812
  31.9 3.8 %collective-permute-start.3 = (f32[48,128]{1,0:T(8,128)S(1)}, f32[48,128]{1,0:T(8,128)S(1)}, u32[]{:S(2)}, u32[]{:S(2)}) collective-permute-start(f32[48,128]{1,0:T(8,128)S(1)} %get-tuple-element.67.refs_0_), channel_id=1, source_target_pairs={{0,24},{2,26},{4,28},{6,30},{8,0},{10,2},{12,4},{14,6},{16,8},{18,... | collective-permute-start | bytes 73736 | tf_op jit(solution)/shard_map/ppermute | solution.py:812

commit v8 on v7

--- a/solution.py
+++ b/solution.py
@@ -151,7 +151,7 @@
     atoms, near, wide, before, after = plan
     n_wide = len(wide)
     blocks = refs[:n_wide]
-    geo_ref, y_ref, yb_ref, bk_ref, bt_ref, gidx_ref, pick_ref = refs[n_wide:]
+    geo_ref, y_ref, yb_ref, ub_ref, bk_ref, bt_ref, gidx_ref, pick_ref, as_ref = refs[n_wide:]
     bases = bk_ref.shape[0]
     slots = gidx_ref.shape[0]
     tiles = atoms // LANES
@@ -205,6 +205,10 @@
             ux, uy, uz = rx * back, ry * back, rz * back
             for i, value in enumerate((ux, uy, uz, back, soft, fj)):
                 geo_ref[i, :, here] = value
+            if q == 0:
+                for i, value in enumerate((ux, uy, uz)):
+                    for k in range(slots):
+                        ub_ref[i, k, :, cols] = row(value[k : k + 1, :])
             sphere = harmonics(ux, uy, uz)
             for l in range(1, ORDERS):
                 y_ref[l - 1, :, here] = sphere[l]
@@ -217,32 +221,26 @@
                 basis = jnp.exp(-0.5 * (row(soft[k : k + 1, :], bases) - (1.0 + order_col)) ** 2)
                 bt_ref[k, 0:bases, here] = basis
                 bt_ref[k, bases : 2 * bases, here] = basis * row(fj[k : k + 1, :], bases)
+            low = [None] * ORDERS
+            for k in range(slots):
+                basis = bt_ref[k, :, here]
+                for l in range(ORDERS):
+                    term = basis if l == 0 else basis * row(y_ref[l - 1, k : k + 1, here], 2 * bases)
+                    low[l] = term if low[l] is None else low[l] + term
+            for l in range(ORDERS):
+                both = split_rows(low[l]).astype(bf16)
+                as_ref[l, 0 : 4 * bases, here] = both
+                as_ref[l, 4 * bases : 8 * bases, here] = both
 
 
 def first_kernel(plan, *refs):
     atoms, near, wide, _, _ = plan
     n_wide = len(wide)
     blocks = refs[:n_wide]
-    y_ref, bt_ref, rrc_ref, side_ref, mixa_ref, m1_ref, sp1_ref, hid_ref, hs_ref, as_ref, flag_ref = refs[n_wide:]
-    slots = bt_ref.shape[0]
-    bases = bt_ref.shape[1] // 2
+    as_ref, rrc_ref, side_ref, mixa_ref, m1_ref, sp1_ref, hid_ref, hs_ref, flag_ref = refs[n_wide:]
     chan = m1_ref.shape[1]
     n_near = m1_ref.shape[2]
 
-    def sums(t):
-        here = pl.ds(pl.multiple_of(t * LANES, LANES), LANES)
-        low = [None] * ORDERS
-        for k in range(slots):
-            basis = bt_ref[k, :, here]
-            for l in range(ORDERS):
-                term = basis if l == 0 else basis * row(y_ref[l - 1, k : k + 1, here], 2 * bases)
-                low[l] = term if low[l] is None else low[l] + term
-        for l in range(ORDERS):
-            both = split_rows(low[l]).astype(bf16)
-            as_ref[l, 0 : 4 * bases, here] = both
-            as_ref[l, 4 * bases : 8 * bases, here] = both
-
-    in_turns(0, n_near // LANES, sums)
     for q in range(len(near)):
         flag_ref[0:1, q * atoms : (q + 1) * atoms] = blocks[q][3:4, :]
     wide_cols = 2 * LANES
@@ -322,7 +320,7 @@
     rows = 32
     groups = chan // rows
 
-    def moments(step, carry):
+    def moments(step):
         t = step // groups
         c = step % groups
         cols = pl.ds(pl.multiple_of(t * LANES, LANES), LANES)
@@ -346,50 +344,51 @@
                 inv[g] = sq if inv[g] is None else inv[g] + sq
             for g in range(3):
                 inv_ref[pl.ds(pl.multiple_of(g * chan + base + 8 * h, 8), 8), cols] = inv[g]
-        return carry
-
-    lax.fori_loop(0, tiles * groups, moments, 0)
+
+    in_turns(0, tiles * groups, moments, 2)
     read2_col = side_ref[:, 3:4]
     for t in range(atoms // wide_cols):
         cols = slice(t * wide_cols, (t + 1) * wide_cols)
         hi, lo = split(inv_ref[:, cols])
         _, slope = silu_parts(dot_parts(mixa_ref[1], hi, lo))
         hi, lo = split(slope * (2.0 * read2_col))
-        for g in range(3):
-            dinv_ref[g * chan : (g + 1) * chan, cols] = dot_parts(mixt_ref[1, g], hi, lo)
-
-
-def back_second_kernel(m2_ref, dinv_ref, car_ref, hj_ref, w_ref, yb_ref, dhe_ref, dw_ref, p_ref):
-    slots = yb_ref.shape[1]
+        for g, scale in enumerate((1.0, 0.5 * SQRT3, 0.5 * SQRT15)):
+            dinv_ref[g * chan : (g + 1) * chan, cols] = scale * dot_parts(mixt_ref[1, g], hi, lo)
+
+
+def back_second_kernel(m2_ref, dinv_ref, car_ref, hj_ref, w_ref, ub_ref, dhe_ref, dw_ref, p_ref):
+    slots = ub_ref.shape[1]
     chan, atoms = m2_ref.shape[1:]
     tiles = atoms // LANES
     pairs = chan // 16
-    k_step = slots // 2
-    per_turn = 4 if pairs % 4 == 0 else 1
-
-    def back_moments(step, carry):
-        t = step // 2
-        k0 = (step % 2) * k_step
+    per_turn = 2 if pairs % 2 == 0 else 1
+
+    def back_moments(t, carry):
         cols = pl.ds(pl.multiple_of(t * LANES, LANES), LANES)
 
         def one(c, acc):
+            forms = []
+            for h in range(2):
+                rows = pl.ds(pl.multiple_of(c * 16 + 8 * h, 8), 8)
+                scale = [dinv_ref[pl.ds(pl.multiple_of(g * chan + c * 16 + 8 * h, 8), 8), cols] for g in range(3)]
+                dm = [m2_ref[l, rows, cols] * scale[GROUP[l]] for l in range(ORDERS)]
+                low = dm[6] * (1.0 / SQRT3)
+                forms.append((dm[0], dm[1], dm[2], dm[3], dm[8] - low, -dm[8] - low, low + low, dm[4], dm[5], dm[7]))
             base = pl.multiple_of(c * 16, 16)
-            dm = []
-            scale = [dinv_ref[pl.ds(pl.multiple_of(g * chan + c * 16, 16), 16), cols] for g in range(3)]
-            for l in range(ORDERS):
-                dm.append(m2_ref[l, pl.ds(base, 16), cols] * scale[GROUP[l]])
-            for kk in range(k_step):
-                k = k0 + kk
+            for k in range(slots):
                 at = pl.ds(pl.multiple_of(k * atoms + t * LANES, LANES), LANES)
                 got = car_ref[pl.ds(base, 16), at]
-                out = [dm[0][:8], dm[0][8:]]
-                for l in range(1, ORDERS):
-                    yb = yb_ref[l - 1, k, :, cols]
-                    i = kk * (ORDERS - 1) + l - 1
-                    for h in range(2):
-                        part = dm[l][8 * h : 8 * h + 8]
-                        out[h] = out[h] + part * yb
-                        acc[i] = acc[i] + part * got[8 * h : 8 * h + 8]
+                ux, uy, uz = [ub_ref[i, k, :, cols] for i in range(3)]
+                out = []
+                for h in range(2):
+                    mid, dx, dy, dz, qxx, qyy, qzz, qxy, qyz, qxz = forms[h]
+                    gx = dx + qxx * ux + qxy * uy + qxz * uz
+                    gy = dy + qxy * ux + qyy * uy + qyz * uz
+                    gz = dz + qxz * ux + qyz * uy + qzz * uz
+                    out.append(mid + (gx + dx) * ux + (gy + dy) * uy + (gz + dz) * uz)
+                    part = got[8 * h : 8 * h + 8]
+                    for i, g in enumerate((gx, gy, gz)):
+                        acc[3 * k + i] = acc[3 * k + i] + part * g
                 dcar = jnp.concatenate(out, axis=0)
                 for ref, other in ((dhe_ref, w_ref), (dw_ref, hj_ref)):
                     hi, lo = split(dcar * other[pl.ds(base, 16), at])
@@ -402,14 +401,14 @@
                 one(per_turn * c + i, acc)
             return tuple(acc)
 
-        start = tuple(jnp.zeros((8, LANES), f32) for _ in range(k_step * (ORDERS - 1)))
+        start = tuple(jnp.zeros((8, LANES), f32) for _ in range(3 * slots))
         acc = lax.fori_loop(0, pairs // per_turn, over, start)
-        for kk in range(k_step):
-            for l in range(1, ORDERS):
-                p_ref[l - 1, pl.ds(pl.multiple_of((k0 + kk) * 8, 8), 8), cols] = acc[kk * (ORDERS - 1) + l - 1]
+        for k in range(slots):
+            for i in range(3):
+                p_ref[i, 8 * k : 8 * k + 8, cols] = acc[3 * k + i]
         return carry
 
-    lax.fori_loop(0, tiles * 2, back_moments, 0)
+    lax.fori_loop(0, tiles, back_moments, 0)
 
 
 def scatter_kernel(oh_ref, pick_ref, dhe_ref, side_ref, dw_ref, p_ref, bt_ref, geo_ref, r2r_ref, gidx_ref,
@@ -436,8 +435,9 @@
     lane = lax.broadcasted_iota(jnp.int32, (slots, 16 * slots), 1)
     sub = lax.broadcasted_iota(jnp.int32, (slots, 16 * slots), 0)
     adder = jnp.where(((lane >> 3) & (slots - 1)) == sub, 1.0, 0.0).astype(bf16)
-    for l in range(ORDERS):
-        q_ref[8 * l : 8 * l + 8, :] = dot(adder, split_rows(p_ref[l - 1, :, :] if l else ds_ref[...]).astype(bf16))
+    for i in range(4):
+        total = dot(adder, split_rows(p_ref[i - 1, :, :] if i else ds_ref[...]).astype(bf16))
+        q_ref[8 * i : 8 * i + 8, :] = 2.0 * total if i else total
     ext = both[:chan] + both[chan:]
     hi, lo = split(jnp.concatenate([ext[:, :half], ext[:, half + atoms :]], axis=1))
     spread = dot_nt(jnp.concatenate([hi, lo], axis=0), pick_ref[...])
@@ -495,11 +495,11 @@
             ds = db if ds is None else ds + db
         if mine:
             ds = ds + q_ref[0:8, here]
-            for l in range(1, ORDERS):
-                dy[l] = dy[l] + q_ref[8 * l : 8 * l + 8, here]
         dux = SQRT3 * dy[1] + SQRT15 * (uy * dy[4] + uz * dy[7] + ux * dy[8]) - SQRT5 * ux * dy[6]
         duy = SQRT3 * dy[2] + SQRT15 * (ux * dy[4] + uz * dy[5] - uy * dy[8]) - SQRT5 * uy * dy[6]
         duz = SQRT3 * dy[3] + SQRT15 * (uy * dy[5] + ux * dy[7]) + 2.0 * SQRT5 * uz * dy[6]
+        if mine:
+            dux, duy, duz = [d + q_ref[8 * i : 8 * i + 8, here] for i, d in ((1, dux), (2, duy), (3, duz))]
         along = ds - (ux * dux + uy * duy + uz * duz) * back
         for i, value in enumerate((dux * back + along * ux, duy * back + along * uy, duz * back + along * uz)):
             dr_ref[i, :, here] = value
@@ -613,7 +613,7 @@
     edges = slots * atoms
     top_rows = -(-len(wide) * atoms // LANES // 8) * 8
     lines = line_count(atoms)
-    geo, y, yb, bk, bt, gidx, pick = run(
+    geo, y, yb, ub, bk, bt, gidx, pick, as1 = run(
         "edges",
         functools.partial(edge_kernel, plan),
         blocks,
@@ -621,18 +621,20 @@
             ((6, slots, n_near), f32),
             ((ORDERS - 1, slots, n_near), f32),
             ((ORDERS - 1, slots, 8, atoms), f32),
+            ((3, slots, 8, atoms), f32),
             ((bases, slots, n_near), f32),
             ((slots, 2 * bases, n_near), f32),
             ((slots, n_near), jnp.int32),
             ((n_near, atoms), bf16),
+            ((ORDERS, 8 * bases, n_near), bf16),
         ),
     )
     m1, sp1, hid, hs = run(
         "first",
         functools.partial(first_kernel, plan),
-        (*blocks, y, bt, rrc, sides, mixa),
+        (*blocks, as1, rrc, sides, mixa),
         (((ORDERS, chan, n_near), f32), ((chan, n_near), f32), ((chan, n_near), f32), ((2 * chan, n_near), bf16)),
-        [pltpu.VMEM((ORDERS, 8 * bases, n_near), bf16), pltpu.VMEM((8, n_near), f32)],
+        [pltpu.VMEM((8, n_near), f32)],
     )
     hj, w, car = run(
         "gather",
@@ -651,14 +653,14 @@
     dhe, dw, p = run(
         "back_second",
         back_second_kernel,
-        (m2, dinv, car, hj, w, yb),
-        (((2 * chan, edges), bf16), ((2 * chan, edges), bf16), ((ORDERS - 1, 8 * slots, atoms), f32)),
+        (m2, dinv, car, hj, w, ub),
+        (((2 * chan, edges), bf16), ((2 * chan, edges), bf16), ((3, 8 * slots, atoms), f32)),
     )
     dh, q, ohlo = run(
         "scatter",
         scatter_kernel,
         (oh, pick, dhe, sides, dw, p, bt, geo, r2r, gidx),
-        (((chan, n_near), f32), ((8 * ORDERS, atoms), f32), ((LANES, slots * n_near), bf16)),
+        (((chan, n_near), f32), ((4 * slots, atoms), f32), ((LANES, slots * n_near), bf16)),
         [pltpu.VMEM((8 * slots, atoms), f32)],
     )
     (da,) = run("back_first", back_first_kernel, (dh, sp1, m1, mixt, rrr), (((ORDERS, 2 * bases, n_near), f32),))

time: 45.2 us -> 44.3 us (0.980)
  Pallas kernels: 23.7 us -> 22.8 us
    pallas_call x9, Pallas kernels: 22.2 us -> 21.3 us  [run(): pl.pallas_call(body, out_shape=tuple((jax.ShapeDtypeStruct(shape, dtype)...]
where the time goes in v8:
time: 44.3 us; the launch traced here: 44 us
  Pallas kernels  22.8 us (51%)
  starting transfers between devices  9.1 us (21%)
  blocking collectives  8.47 us (19%)
  waiting for transfers between devices  2.91 us (7%)
  between operations  0.71 us (2%)
    pallas_call x9, Pallas kernels, run(): pl.pallas_call(body, out_shape=tuple((jax.ShapeDtypeStruct(shape, dtype)...  21.3 us
    all_to_all x1, blocking collectives, shards(): lax.all_to_all(messages, ('bead', 'space'), 0, 0, axis_index_groups=rows,...  8.47 us
    ppermute x3, starting transfers between devices, shards(): lax.ppermute(pushed, 'bead', [(b, (b + z * inner) % beads) for b in range...  6.07 us
    ppermute x1, starting transfers between devices, shards(): lax.ppermute(block, 'space', [(i, (i - offset) % domains) for i in range(...  3.03 us
    ppermute x3, waiting for transfers between devices, shards(): lax.ppermute(pushed, 'bead', [(b, (b + z * inner) % beads) for b in range...  2.48 us
  transfers between devices with their start and end apart: 4, of which 3 were waited for; matrix products, arithmetic and copies ran while one was open for 0% of the time, Pallas kernels for 3%

profile of v8, /device:TPU:0, one launch (start us, length us, event | category | flops | bytes accessed | tf_op | source)
XLA Modules:
  0.0 44.0 jit_solution(10604559406435332510)
XLA Ops:
  0.6 0.8 %pack.1.refs_0_.block_ref = f32[16,512]{1,0:T(8,128)S(1)} custom-call(f32[3,1,512]{2,1,0:T(1,128)} %bitcast.10, s32[1,512]{1,0:T(1,128)} %bitcast.12, s32[1,512]{1,0:T(1,128)} %bitcast.13, s32[8,512]{1,0:T(8,128)} %slot_src.1), custom_call_target="tpu_custom_call" | custom-call | tf_op jit(solution)/shard_map/pack/pallas_call | solution.py:792
  1.4 3.0 %collective-permute-start = (f32[16,512]{1,0:T(8,128)S(1)}, f32[16,512]{1,0:T(8,128)S(1)}, u32[]{:S(2)}, u32[]{:S(2)}) collective-permute-start(f32[16,512]{1,0:T(8,128)S(1)} %pack.1.refs_0_.block_ref), channel_id=1, source_target_pairs={{0,1},{1,0},{2,3},{3,2},{4,5},{5,4},{6,7},{7,6},{8,9},{9,8},{10,11... | collective-permute-start | bytes 98312 | tf_op jit(solution)/shard_map/ppermute | solution.py:809
  4.5 1.5 %choose.1 = (bf16[1024,4096]{1,0:T(8,128)(2,1)S(1)}, bf16[128,64]{1,0:T(8,128)(2,1)S(1)}, bf16[128,32]{1,0:T(8,128)(2,1)S(1)}, f32[128,128]{1,0:T(8,128)S(1)}, b...) custom-call(f32[16,512]{1,0:T(8,128)S(1)} %pack.1.refs_0_.block_ref,, ...), custom_call_target="tpu_custom_call" | custom-call | flops 2000000000 | bytes 2000000 | tf_op jit(solution)/shard_map/choose/pallas_call | solution.py:568
  5.9 0.4 collective-permute-done.refs_1_
  6.4 1.7 %edges.1 = (f32[6,8,1024]{2,1,0:T(8,128)S(1)}, f32[8,8,1024]{2,1,0:T(8,128)S(1)}, f32[8,8,8,512]{3,2,1,0:T(8,128)S(1)}, f32[3,8,8,512]{3,2,1,0:T(8,128)S(1)}, f3...) custom-call(f32[16,512]{1,0:T(8,128)S(1)} %pack.1.refs_0_.block_ref,, ...), custom_call_target="tpu_custom_call" | custom-call | tf_op jit(solution)/shard_map/edges/pallas_call | solution.py:568
  8.0 1.7 %first.1 = (f32[9,128,1024]{2,1,0:T(8,128)S(1)}, f32[128,1024]{1,0:T(8,128)S(1)}, f32[128,1024]{1,0:T(8,128)S(1)}, bf16[256,1024]{1,0:T(8,128)(2,1)S(1)}) custom-call(f32[16,512]{1,0:T(8,128)S(1)} %pack.1.refs_0_.block_ref, f32[16,512]{1,0:T(8,128)S(1)} %collective-permute-done.refs_1_, bf16[9,64,1024]{2,1,0:T(8,128)(2,1)S(1)} %get-tuple-element.44.refs_2_, ...), custom_call_target="tpu_custom_call" | custom-call | tf_op jit(solution)/shard_map/first/pallas_call | solution.py:568
  9.8 3.2 %gather.1 = (f32[128,4096]{1,0:T(8,128)S(1)}, f32[128,4096]{1,0:T(8,128)S(1)}, f32[128,4096]{1,0:T(8,128)S(1)}) custom-call(f32[128,1024]{1,0:T(8,128)S(1)} %get-tuple-element.48.hid_ref, bf16[256,1024]{1,0:T(8,128)(2,1)S(1)} %get-tuple-element.49.hs_ref, bf16[1024,4096]{1,0:T(8,128)(2,1)S(1)} %get-tuple-element.42.oh_ref, ...), custom_call_target="tpu_custom_call" | custom-call | tf_op jit(solution)/shard_map/gather/pallas_call | solution.py:568
  12.9 2.5 %moments.1 = (f32[9,128,512]{2,1,0:T(8,128)S(1)}, f32[384,512]{1,0:T(8,128)S(1)}) custom-call(f32[128,4096]{1,0:T(8,128)S(1)} %get-tuple-element.52.car_ref, f32[8,8,8,512]{3,2,1,0:T(8,128)S(1)} %get-tuple-element.53.yb_ref, bf16[2,256,384]{2,1,0:T(8,128)(2,1)S(1)} %get-tuple-element.47.refs_5_.mixa_ref, ...), custom_call_target="tpu_custom_call" | custom-call | tf_op jit(solution)/shard_map/moments/pallas_call | solution.py:568
  15.4 3.8 %back_second.1 = (bf16[256,4096]{1,0:T(8,128)(2,1)S(1)}, bf16[256,4096]{1,0:T(8,128)(2,1)S(1)}, f32[3,64,512]{2,1,0:T(8,128)S(1)}) custom-call(f32[9,128,512]{2,1,0:T(8,128)S(1)} %get-tuple-element.55.m2_ref, f32[384,512]{1,0:T(8,128)S(1)} %get-tuple-element.56.dinv_ref, f32[128,4096]{1,0:T(8,128)S(1)} %get-tuple-element.52.car_ref, ...), custom_call_target="tpu_custom_call" | custom-call | tf_op jit(solution)/shard_map/back_second/pallas_call | solution.py:568
  19.2 3.3 %scatter.1 = (f32[128,1024]{1,0:T(8,128)S(1)}, f32[32,512]{1,0:T(8,128)S(1)}, bf16[128,8192]{1,0:T(8,128)(2,1)S(1)}) custom-call(bf16[1024,4096]{1,0:T(8,128)(2,1)S(1)} %get-tuple-element.42.oh_ref, bf16[1024,512]{1,0:T(8,128)(2,1)S(1)} %get-tuple-element.43.pick_ref, bf16[256,4096]{1,0:T(8,128)(2,1)S(1)} %get-tuple-element.60.dhe_ref, ...), custom_call_target="tpu_custom_call" | custom-call | tf_op jit(solution)/shard_map/scatter/pallas_call | solution.py:568
  22.5 2.0 %back_first.1.refs_7_ = f32[9,16,1024]{2,1,0:T(8,128)S(1)} custom-call(f32[128,1024]{1,0:T(8,128)S(1)} %get-tuple-element.64.dh_ref, f32[128,1024]{1,0:T(8,128)S(1)} %get-tuple-element.65.sp1_ref, f32[9,128,1024]{2,1,0:T(8,128)S(1)} %get-tuple-element.66.m1_ref, bf16[2,3,256,128]{3,2,1,0:T(8,128)(2,1)S(1)} %get-tuple-element.54.mixt_ref, ...), custom_call_target="tpu_custom_call" | custom-call | tf_op jit(solution)/shard_map/back_first/pallas_call | solution.py:568
  24.5 1.8 %back_edges.1 = (f32[48,128]{1,0:T(8,128)S(1)}, f32[32,128]{1,0:T(8,128)S(1)}) custom-call(f32[16,512]{1,0:T(8,128)S(1)} %pack.1.refs_0_.block_ref, f32[16,512]{1,0:T(8,128)S(1)} %collective-permute-done.refs_1_, f32[3,1,512]{2,1,0:T(1,128)} %bitcast.11, f32[6,8,1024]{2,1,0:T(8,128)S(1)} %get-tuple-element.38.geo_ref.refs_3_, ...), custom_call_target="tpu_custom_call" | custom-call | tf_op jit(solution)/shard_map/back_edges/pallas_call | solution.py:568
  26.3 2.1 %collective-permute-start.1 = (f32[48,128]{1,0:T(8,128)S(1)}, f32[48,128]{1,0:T(8,128)S(1)}, u32[]{:S(2)}, u32[]{:S(2)}) collective-permute-start(f32[48,128]{1,0:T(8,128)S(1)} %get-tuple-element.71.refs_0_), channel_id=1, source_target_pairs={{0,8},{2,10},{4,12},{6,14},{8,16},{10,18},{12,20},{14,22},{16,24},... | collective-permute-start | bytes 73736 | tf_op jit(solution)/shard_map/ppermute | solution.py:814
  28.4 2.6 %collective-permute-start.2 = (f32[48,128]{1,0:T(8,128)S(1)}, f32[48,128]{1,0:T(8,128)S(1)}, u32[]{:S(2)}, u32[]{:S(2)}) collective-permute-start(f32[48,128]{1,0:T(8,128)S(1)} %get-tuple-element.71.refs_0_), channel_id=1, source_target_pairs={{0,16},{2,18},{4,20},{6,22},{8,24},{10,26},{12,28},{14,30},{16,0},... | collective-permute-start | bytes 73736 | tf_op jit(solution)/shard_map/ppermute | solution.py:814
  31.0 1.3 %collective-permute-start.3 = (f32[48,128]{1,0:T(8,128)S(1)}, f32[48,128]{1,0:T(8,128)S(1)}, u32[]{:S(2)}, u32[]{:S(2)}) collective-permute-start(f32[48,128]{1,0:T(8,128)S(1)} %get-tuple-element.71.refs_0_), channel_id=1, source_target_pairs={{0,24},{2,26},{4,28},{6,30},{8,0},{10,2},{12,4},{14,6},{16,8},{18,... | collective-permute-start | bytes 73736 | tf_op jit(solution)/shard_map/ppermute | solution.py:814
  32.3 0.0 collective-permute-done.1.refs_1_
  32.3 0.8 %collective-permute-done.2.refs_2_ = f32[48,128]{1,0:T(8,128)S(1)} collective-permute-done((f32[48,128]{1,0:T(8,128)S(1)}, f32[48,128]{1,0:T(8,128)S(1)}, u32[]{:S(2)}, u32[]{:S(2)}) %collective-permute-start.2) | collective-permute-done | bytes 24608 | tf_op jit(solution)/shard_map/ppermute | solution.py:814
  33.1 1.7 %collective-permute-done.3.refs_3_ = f32[48,128]{1,0:T(8,128)S(1)} collective-permute-done((f32[48,128]{1,0:T(8,128)S(1)}, f32[48,128]{1,0:T(8,128)S(1)}, u32[]{:S(2)}, u32[]{:S(2)}) %collective-permute-start.3) | collective-permute-done | bytes 24608 | tf_op jit(solution)/shard_map/ppermute | solution.py:814
  34.8 0.1 turn.1
  34.9 8.5 %all_to_all.5.arrived_ref = f32[8,32,128]{2,1,0:T(8,128)S(1)} all-to-all(f32[8,32,128]{2,1,0:T(8,128)S(1)} %turn.1), channel_id=1, replica_groups={{0,1,2,3,4,5,6,7},{8,9,10,11,12,13,14,15},{16,17,18,19,20,21,22,23},{24..., dimensions={0} | all-to-all | bytes 262144 | tf_op jit(solution)/shard_map/all_to_all | solution.py:826
  43.4 0.6 %sum.1 = (f32[3,1,512]{2,1,0:T(1,128)}, f32[3,1,512]{2,1,0:T(1,128)}) custom-call(f32[8,32,128]{2,1,0:T(8,128)S(1)} %all_to_all.5.arrived_ref), custom_call_target="tpu_custom_call" | custom-call | tf_op jit(solution)/shard_map/sum/pallas_call | solution.py:827
Async XLA Ops:
  1.4 4.9 %collective-permute-start = (f32[16,512]{1,0:T(8,128)S(1)}, f32[16,512]{1,0:T(8,128)S(1)}, u32[]{:S(2)}, u32[]{:S(2)}) collective-permute-start(f32[16,512]{1,0:T(8,128)S(1)} %pack.1.refs_0_.block_ref), channel_id=1, source_target_pairs={{0,1},{1,0},{2,3},{3,2},{4,5},{5,4},{6,7},{7,6},{8,9},{9,8},{10,11... | collective-permute-start | bytes 98312 | tf_op jit(solution)/shard_map/ppermute | solution.py:809
  26.3 6.1 %collective-permute-start.1 = (f32[48,128]{1,0:T(8,128)S(1)}, f32[48,128]{1,0:T(8,128)S(1)}, u32[]{:S(2)}, u32[]{:S(2)}) collective-permute-start(f32[48,128]{1,0:T(8,128)S(1)} %get-tuple-element.71.refs_0_), channel_id=1, source_target_pairs={{0,8},{2,10},{4,12},{6,14},{8,16},{10,18},{12,20},{14,22},{16,24},... | collective-permute-start | bytes 73736 | tf_op jit(solution)/shard_map/ppermute | solution.py:814
  28.4 4.7 %collective-permute-start.2 = (f32[48,128]{1,0:T(8,128)S(1)}, f32[48,128]{1,0:T(8,128)S(1)}, u32[]{:S(2)}, u32[]{:S(2)}) collective-permute-start(f32[48,128]{1,0:T(8,128)S(1)} %get-tuple-element.71.refs_0_), channel_id=1, source_target_pairs={{0,16},{2,18},{4,20},{6,22},{8,24},{10,26},{12,28},{14,30},{16,0},... | collective-permute-start | bytes 73736 | tf_op jit(solution)/shard_map/ppermute | solution.py:814
  31.0 3.8 %collective-permute-start.3 = (f32[48,128]{1,0:T(8,128)S(1)}, f32[48,128]{1,0:T(8,128)S(1)}, u32[]{:S(2)}, u32[]{:S(2)}) collective-permute-start(f32[48,128]{1,0:T(8,128)S(1)} %get-tuple-element.71.refs_0_), channel_id=1, source_target_pairs={{0,24},{2,26},{4,28},{6,30},{8,0},{10,2},{12,4},{14,6},{16,8},{18,... | collective-permute-start | bytes 73736 | tf_op jit(solution)/shard_map/ppermute | solution.py:814

commit v9 on v8

--- a/solution.py
+++ b/solution.py
@@ -724,37 +724,37 @@
 
 def turn_kernel(shape, bead_ref, domain_ref, mass_ref, *refs):
     outer, inner, domains, wide = shape
-    message_ref = refs[outer]
-    turns = mode_turns(outer * inner)
+    sources, message_ref = refs[:inner], refs[inner]
+    beads = outer * inner
+    turns = mode_turns(beads)
     lines = mass_ref.shape[0] // len(wide)
     my_domain = domain_ref[0]
     my_inner = lax.rem(bead_ref[0], inner)
+    my_outer = (bead_ref[0] - my_inner) // inner
     if domains > len(wide):
         message_ref[...] = jnp.zeros_like(message_ref)
     masses = [mass_ref[g * lines : (g + 1) * lines, :] for g in range(len(wide))]
-    sources = []
+    held = [[source[g * lines : (g + 1) * lines, :] for g in range(len(wide) + 1)] for source in sources]
+    wraps = [jnp.full((lines, LANES), my_inner) < s for s in range(inner)]
     for z in range(outer):
-        sources.append([refs[z][g * lines : (g + 1) * lines, :] for g in range(len(wide) + 1)])
-    for s in range(inner):
-        wraps = jnp.full((lines, LANES), my_inner + s) >= inner
         weights = []
         for turn in turns:
             row_of = []
-            for z in range(outer):
-                there = turn[(z * inner + s) % (outer * inner)]
-                round_it = turn[(z * inner + s - inner) % (outer * inner)]
-                row_of.append(jnp.where(wraps, jnp.full((lines, LANES), round_it), jnp.full((lines, LANES), there)))
+            for s in range(inner):
+                there = turn[(z * inner + s) % beads]
+                round_it = turn[(z * inner + s - inner) % beads]
+                row_of.append(jnp.where(wraps[s], jnp.full((lines, LANES), round_it), jnp.full((lines, LANES), there)))
             weights.append(row_of)
-        to_inner = lax.rem(my_inner + s, inner)
+        to_outer = lax.rem(my_outer + z, outer)
         for g in range(len(wide)):
-            turned = sum(weights[0][z] * sources[z][1 + g] for z in range(outer))
-            drift = sum(weights[1][z] * sources[z][1 + g] for z in range(outer))
+            turned = sum(weights[0][s] * held[s][1 + g] for s in range(inner))
+            drift = sum(weights[1][s] * held[s][1 + g] for s in range(inner))
             new_q = drift / masses[g]
             new_p = turned
             if g == 0:
-                new_q = new_q + sum(weights[0][z] * sources[z][0] for z in range(outer))
-                new_p = new_p - masses[g] * sum(weights[2][z] * sources[z][0] for z in range(outer))
-            to = to_inner * domains + lax.rem(my_domain + wide[g], domains)
+                new_q = new_q + sum(weights[0][s] * held[s][0] for s in range(inner))
+                new_p = new_p - masses[g] * sum(weights[2][s] * held[s][0] for s in range(inner))
+            to = to_outer * domains + lax.rem(my_domain + wide[g], domains)
             message_ref[to, 0:lines, :] = new_q
             message_ref[to, lines:, :] = new_p
 
@@ -779,8 +779,8 @@
     slots, atoms = neighbours.shape
     domains = lax.axis_size("space")
     beads = lax.axis_size("bead")
-    inner = next(d for d in range(1, beads + 1) if beads % d == 0 and d * d >= beads)
-    outer = beads // inner
+    outer = next(d for d in range(1, beads + 1) if beads % d == 0 and d * d >= beads)
+    inner = beads // outer
     plan = ring_plan(domains, atoms)
     wide = plan[2]
     vmem = pl.BlockSpec(memory_space=pltpu.VMEM)
@@ -810,19 +810,20 @@
     chosen = choose(block, embedding, radial_one, radial_two, mix_one, mix_two, read_one, read_two)
     pushed, masses = pushes(plan, blocks, moment_rows, chosen)
     sources = [pushed]
-    for z in range(1, outer):
-        sources.append(lax.ppermute(pushed, "bead", [(b, (b + z * inner) % beads) for b in range(beads)]))
+    for shift in range(1, inner):
+        pairs = [(b, b - b % inner + (b + shift) % inner) for b in range(beads)]
+        sources.append(lax.ppermute(pushed, "bead", pairs))
     here = [lax.axis_index(axis).astype(jnp.int32).reshape(1) for axis in ("bead", "space")]
     lines = line_count(atoms)
     messages = pl.pallas_call(
         functools.partial(turn_kernel, (outer, inner, domains, wide)),
-        out_shape=jax.ShapeDtypeStruct((inner * domains, 2 * lines, LANES), f32),
-        in_specs=[smem, smem, vmem] + [vmem] * outer,
+        out_shape=jax.ShapeDtypeStruct((outer * domains, 2 * lines, LANES), f32),
+        in_specs=[smem, smem, vmem] + [vmem] * inner,
         out_specs=vmem,
         compiler_params=small,
         name="turn",
     )(*here, masses, *sources)
-    rows = [[z * inner * domains + i for i in range(inner * domains)] for z in range(outer)]
+    rows = [[(z * inner + i) * domains + d for z in range(outer) for d in range(domains)] for i in range(inner)]
     arrived = lax.all_to_all(messages, ("bead", "space"), 0, 0, axis_index_groups=rows, tiled=True)
     new_q, new_p = pl.pallas_call(
         sum_kernel,

time: 44.3 us -> 45.8 us (1.034)
  blocking collectives: 8.47 us -> 13.4 us
  starting transfers between devices: 9.1 us -> 6.54 us
  waiting for transfers between devices: 2.91 us -> 1.95 us
    all_to_all x1, blocking collectives: 8.47 us -> 13.4 us  [shards(): lax.all_to_all(messages, ('bead', 'space'), 0, 0, axis_index_groups=rows,...]
    ppermute x3, starting transfers between devices: 6.07 us -> 3.5 us  [shards(): sources.append(lax.ppermute(pushed, 'bead', pairs))]
    ppermute x3, waiting for transfers between devices: 2.48 us -> 1.52 us  [shards(): sources.append(lax.ppermute(pushed, 'bead', pairs))]
where the time goes in v9:
time: 45.8 us; the launch traced here: 45.4 us
  Pallas kernels  22.8 us (50%)
  blocking collectives  13.4 us (29%)
  starting transfers between devices  6.54 us (14%)
  waiting for transfers between devices  1.95 us (4%)
  between operations  0.72 us (2%)
    pallas_call x9, Pallas kernels, run(): pl.pallas_call(body, out_shape=tuple((jax.ShapeDtypeStruct(shape, dtype)...  21.3 us
    all_to_all x1, blocking collectives, shards(): lax.all_to_all(messages, ('bead', 'space'), 0, 0, axis_index_groups=rows,...  13.4 us
    ppermute x3, starting transfers between devices, shards(): sources.append(lax.ppermute(pushed, 'bead', pairs))  3.5 us
    ppermute x1, starting transfers between devices, shards(): lax.ppermute(block, 'space', [(i, (i - offset) % domains) for i in range(...  3.03 us
    ppermute x3, waiting for transfers between devices, shards(): sources.append(lax.ppermute(pushed, 'bead', pairs))  1.52 us
  transfers between devices with their start and end apart: 4, of which 3 were waited for; matrix products, arithmetic and copies ran while one was open for 0% of the time, Pallas kernels for 3%

profile of v9, /device:TPU:0, one launch (start us, length us, event | category | flops | bytes accessed | tf_op | source)
XLA Modules:
  0.0 45.4 jit_solution(13087347987393169869)
XLA Ops:
  0.6 0.8 %pack.1.refs_0_.block_ref = f32[16,512]{1,0:T(8,128)S(1)} custom-call(f32[3,1,512]{2,1,0:T(1,128)} %bitcast.10, s32[1,512]{1,0:T(1,128)} %bitcast.12, s32[1,512]{1,0:T(1,128)} %bitcast.13, s32[8,512]{1,0:T(8,128)} %slot_src.1), custom_call_target="tpu_custom_call" | custom-call | tf_op jit(solution)/shard_map/pack/pallas_call | solution.py:792
  1.4 3.0 %collective-permute-start = (f32[16,512]{1,0:T(8,128)S(1)}, f32[16,512]{1,0:T(8,128)S(1)}, u32[]{:S(2)}, u32[]{:S(2)}) collective-permute-start(f32[16,512]{1,0:T(8,128)S(1)} %pack.1.refs_0_.block_ref), channel_id=1, source_target_pairs={{0,1},{1,0},{2,3},{3,2},{4,5},{5,4},{6,7},{7,6},{8,9},{9,8},{10,11... | collective-permute-start | bytes 98312 | tf_op jit(solution)/shard_map/ppermute | solution.py:809
  4.5 1.5 %choose.1 = (bf16[1024,4096]{1,0:T(8,128)(2,1)S(1)}, bf16[128,64]{1,0:T(8,128)(2,1)S(1)}, bf16[128,32]{1,0:T(8,128)(2,1)S(1)}, f32[128,128]{1,0:T(8,128)S(1)}, b...) custom-call(f32[16,512]{1,0:T(8,128)S(1)} %pack.1.refs_0_.block_ref,, ...), custom_call_target="tpu_custom_call" | custom-call | flops 2000000000 | bytes 2000000 | tf_op jit(solution)/shard_map/choose/pallas_call | solution.py:568
  5.9 0.4 collective-permute-done.refs_1_
  6.4 1.7 %edges.1 = (f32[6,8,1024]{2,1,0:T(8,128)S(1)}, f32[8,8,1024]{2,1,0:T(8,128)S(1)}, f32[8,8,8,512]{3,2,1,0:T(8,128)S(1)}, f32[3,8,8,512]{3,2,1,0:T(8,128)S(1)}, f3...) custom-call(f32[16,512]{1,0:T(8,128)S(1)} %pack.1.refs_0_.block_ref,, ...), custom_call_target="tpu_custom_call" | custom-call | tf_op jit(solution)/shard_map/edges/pallas_call | solution.py:568
  8.0 1.7 %first.1 = (f32[9,128,1024]{2,1,0:T(8,128)S(1)}, f32[128,1024]{1,0:T(8,128)S(1)}, f32[128,1024]{1,0:T(8,128)S(1)}, bf16[256,1024]{1,0:T(8,128)(2,1)S(1)}) custom-call(f32[16,512]{1,0:T(8,128)S(1)} %pack.1.refs_0_.block_ref, f32[16,512]{1,0:T(8,128)S(1)} %collective-permute-done.refs_1_, bf16[9,64,1024]{2,1,0:T(8,128)(2,1)S(1)} %get-tuple-element.44.refs_2_, ...), custom_call_target="tpu_custom_call" | custom-call | tf_op jit(solution)/shard_map/first/pallas_call | solution.py:568
  9.8 3.2 %gather.1 = (f32[128,4096]{1,0:T(8,128)S(1)}, f32[128,4096]{1,0:T(8,128)S(1)}, f32[128,4096]{1,0:T(8,128)S(1)}) custom-call(f32[128,1024]{1,0:T(8,128)S(1)} %get-tuple-element.48.hid_ref, bf16[256,1024]{1,0:T(8,128)(2,1)S(1)} %get-tuple-element.49.hs_ref, bf16[1024,4096]{1,0:T(8,128)(2,1)S(1)} %get-tuple-element.42.oh_ref, ...), custom_call_target="tpu_custom_call" | custom-call | tf_op jit(solution)/shard_map/gather/pallas_call | solution.py:568
  12.9 2.5 %moments.1 = (f32[9,128,512]{2,1,0:T(8,128)S(1)}, f32[384,512]{1,0:T(8,128)S(1)}) custom-call(f32[128,4096]{1,0:T(8,128)S(1)} %get-tuple-element.52.car_ref, f32[8,8,8,512]{3,2,1,0:T(8,128)S(1)} %get-tuple-element.53.yb_ref, bf16[2,256,384]{2,1,0:T(8,128)(2,1)S(1)} %get-tuple-element.47.refs_5_.mixa_ref, ...), custom_call_target="tpu_custom_call" | custom-call | tf_op jit(solution)/shard_map/moments/pallas_call | solution.py:568
  15.4 3.8 %back_second.1 = (bf16[256,4096]{1,0:T(8,128)(2,1)S(1)}, bf16[256,4096]{1,0:T(8,128)(2,1)S(1)}, f32[3,64,512]{2,1,0:T(8,128)S(1)}) custom-call(f32[9,128,512]{2,1,0:T(8,128)S(1)} %get-tuple-element.55.m2_ref, f32[384,512]{1,0:T(8,128)S(1)} %get-tuple-element.56.dinv_ref, f32[128,4096]{1,0:T(8,128)S(1)} %get-tuple-element.52.car_ref, ...), custom_call_target="tpu_custom_call" | custom-call | tf_op jit(solution)/shard_map/back_second/pallas_call | solution.py:568
  19.2 3.3 %scatter.1 = (f32[128,1024]{1,0:T(8,128)S(1)}, f32[32,512]{1,0:T(8,128)S(1)}, bf16[128,8192]{1,0:T(8,128)(2,1)S(1)}) custom-call(bf16[1024,4096]{1,0:T(8,128)(2,1)S(1)} %get-tuple-element.42.oh_ref, bf16[1024,512]{1,0:T(8,128)(2,1)S(1)} %get-tuple-element.43.pick_ref, bf16[256,4096]{1,0:T(8,128)(2,1)S(1)} %get-tuple-element.60.dhe_ref, ...), custom_call_target="tpu_custom_call" | custom-call | tf_op jit(solution)/shard_map/scatter/pallas_call | solution.py:568
  22.5 2.0 %back_first.1.refs_7_ = f32[9,16,1024]{2,1,0:T(8,128)S(1)} custom-call(f32[128,1024]{1,0:T(8,128)S(1)} %get-tuple-element.64.dh_ref, f32[128,1024]{1,0:T(8,128)S(1)} %get-tuple-element.65.sp1_ref, f32[9,128,1024]{2,1,0:T(8,128)S(1)} %get-tuple-element.66.m1_ref, bf16[2,3,256,128]{3,2,1,0:T(8,128)(2,1)S(1)} %get-tuple-element.54.mixt_ref, ...), custom_call_target="tpu_custom_call" | custom-call | tf_op jit(solution)/shard_map/back_first/pallas_call | solution.py:568
  24.5 1.8 %back_edges.1 = (f32[48,128]{1,0:T(8,128)S(1)}, f32[32,128]{1,0:T(8,128)S(1)}) custom-call(f32[16,512]{1,0:T(8,128)S(1)} %pack.1.refs_0_.block_ref, f32[16,512]{1,0:T(8,128)S(1)} %collective-permute-done.refs_1_, f32[3,1,512]{2,1,0:T(1,128)} %bitcast.11, f32[6,8,1024]{2,1,0:T(8,128)S(1)} %get-tuple-element.38.geo_ref.refs_3_, ...), custom_call_target="tpu_custom_call" | custom-call | tf_op jit(solution)/shard_map/back_edges/pallas_call | solution.py:568
  26.3 0.1 collective-permute-start.1
  26.3 2.1 %collective-permute-start.2 = (f32[48,128]{1,0:T(8,128)S(1)}, f32[48,128]{1,0:T(8,128)S(1)}, u32[]{:S(2)}, u32[]{:S(2)}) collective-permute-start(f32[48,128]{1,0:T(8,128)S(1)} %get-tuple-element.71.refs_0_), channel_id=1, source_target_pairs={{0,4},{2,6},{4,0},{6,2},{8,12},{10,14},{12,8},{14,10},{16,20},{18,... | collective-permute-start | bytes 73736 | tf_op jit(solution)/shard_map/ppermute | solution.py:815
  28.4 1.4 %collective-permute-start.3 = (f32[48,128]{1,0:T(8,128)S(1)}, f32[48,128]{1,0:T(8,128)S(1)}, u32[]{:S(2)}, u32[]{:S(2)}) collective-permute-start(f32[48,128]{1,0:T(8,128)S(1)} %get-tuple-element.71.refs_0_), channel_id=1, source_target_pairs={{0,6},{2,0},{4,2},{6,4},{8,14},{10,8},{12,10},{14,12},{16,22},{18,... | collective-permute-start | bytes 73736 | tf_op jit(solution)/shard_map/ppermute | solution.py:815
  29.8 0.0 collective-permute-done.1.refs_1_
  29.8 0.4 collective-permute-done.2.refs_2_
  30.2 1.1 %collective-permute-done.3.refs_3_ = f32[48,128]{1,0:T(8,128)S(1)} collective-permute-done((f32[48,128]{1,0:T(8,128)S(1)}, f32[48,128]{1,0:T(8,128)S(1)}, u32[]{:S(2)}, u32[]{:S(2)}) %collective-permute-start.3) | collective-permute-done | bytes 24608 | tf_op jit(solution)/shard_map/ppermute | solution.py:815
  31.3 0.1 turn.1
  31.4 13.4 %all_to_all.5.arrived_ref = f32[8,32,128]{2,1,0:T(8,128)S(1)} all-to-all(f32[8,32,128]{2,1,0:T(8,128)S(1)} %turn.1), channel_id=1, replica_groups={{0,1,8,9,16,17,24,25},{2,3,10,11,18,19,26,27},{4,5,12,13,20,21,28,29},{..., dimensions={0} | all-to-all | bytes 262144 | tf_op jit(solution)/shard_map/all_to_all | solution.py:827
  44.8 0.6 %sum.1 = (f32[3,1,512]{2,1,0:T(1,128)}, f32[3,1,512]{2,1,0:T(1,128)}) custom-call(f32[8,32,128]{2,1,0:T(8,128)S(1)} %all_to_all.5.arrived_ref), custom_call_target="tpu_custom_call" | custom-call | tf_op jit(solution)/shard_map/sum/pallas_call | solution.py:828
Async XLA Ops:
  1.4 4.9 %collective-permute-start = (f32[16,512]{1,0:T(8,128)S(1)}, f32[16,512]{1,0:T(8,128)S(1)}, u32[]{:S(2)}, u32[]{:S(2)}) collective-permute-start(f32[16,512]{1,0:T(8,128)S(1)} %pack.1.refs_0_.block_ref), channel_id=1, source_target_pairs={{0,1},{1,0},{2,3},{3,2},{4,5},{5,4},{6,7},{7,6},{8,9},{9,8},{10,11... | collective-permute-start | bytes 98312 | tf_op jit(solution)/shard_map/ppermute | solution.py:809
  26.3 3.5 %collective-permute-start.1 = (f32[48,128]{1,0:T(8,128)S(1)}, f32[48,128]{1,0:T(8,128)S(1)}, u32[]{:S(2)}, u32[]{:S(2)}) collective-permute-start(f32[48,128]{1,0:T(8,128)S(1)} %get-tuple-element.71.refs_0_), channel_id=1, source_target_pairs={{0,2},{2,4},{4,6},{6,0},{8,10},{10,12},{12,14},{14,8},{16,18},{18,... | collective-permute-start | bytes 73736 | tf_op jit(solution)/shard_map/ppermute | solution.py:815
  26.3 3.9 %collective-permute-start.2 = (f32[48,128]{1,0:T(8,128)S(1)}, f32[48,128]{1,0:T(8,128)S(1)}, u32[]{:S(2)}, u32[]{:S(2)}) collective-permute-start(f32[48,128]{1,0:T(8,128)S(1)} %get-tuple-element.71.refs_0_), channel_id=1, source_target_pairs={{0,4},{2,6},{4,0},{6,2},{8,12},{10,14},{12,8},{14,10},{16,20},{18,... | collective-permute-start | bytes 73736 | tf_op jit(solution)/shard_map/ppermute | solution.py:815
  28.4 2.9 %collective-permute-start.3 = (f32[48,128]{1,0:T(8,128)S(1)}, f32[48,128]{1,0:T(8,128)S(1)}, u32[]{:S(2)}, u32[]{:S(2)}) collective-permute-start(f32[48,128]{1,0:T(8,128)S(1)} %get-tuple-element.71.refs_0_), channel_id=1, source_target_pairs={{0,6},{2,0},{4,2},{6,4},{8,14},{10,8},{12,10},{14,12},{16,22},{18,... | collective-permute-start | bytes 73736 | tf_op jit(solution)/shard_map/ppermute | solution.py:815

commit v10 on v8

--- a/solution.py
+++ b/solution.py
@@ -98,15 +98,17 @@
     atoms = block_ref.shape[1]
     slots = block_ref.shape[0] - HEAD
 
-    ids16 = lax.broadcasted_iota(jnp.int32, (LANES, atoms), 0).astype(jnp.int16)
-    one16 = jnp.ones((LANES, atoms), bf16)
-    zero16 = jnp.zeros((LANES, atoms), bf16)
-    for k in range(slots):
-        slot = block_ref[HEAD + k : HEAD + k + 1, :].astype(jnp.int32)
-        wanted = jnp.broadcast_to(slot, (LANES, atoms)).astype(jnp.int16)
+    tile_edges = slots * LANES
+    ids16 = lax.broadcasted_iota(jnp.int32, (LANES, tile_edges), 0).astype(jnp.int16)
+    one16 = jnp.ones((LANES, tile_edges), bf16)
+    zero16 = jnp.zeros((LANES, tile_edges), bf16)
+    for t in range(atoms // LANES):
+        slot = block_ref[HEAD : HEAD + slots, t * LANES : (t + 1) * LANES].astype(jnp.int32)
+        line = jnp.concatenate([slot[k : k + 1, :] for k in range(slots)], axis=1)
+        wanted = jnp.broadcast_to(line, (LANES, tile_edges)).astype(jnp.int16)
         for r in range(oh_ref.shape[0] // LANES):
             hit = wanted - jnp.int16(r * LANES) == ids16
-            oh_ref[r * LANES : (r + 1) * LANES, k * atoms : (k + 1) * atoms] = jnp.where(hit, one16, zero16)
+            oh_ref[r * LANES : (r + 1) * LANES, t * tile_edges : (t + 1) * tile_edges] = jnp.where(hit, one16, zero16)
 
     for fetch in fetches:
         fetch.wait()
@@ -237,7 +239,7 @@
     atoms, near, wide, _, _ = plan
     n_wide = len(wide)
     blocks = refs[:n_wide]
-    as_ref, rrc_ref, side_ref, mixa_ref, m1_ref, sp1_ref, hid_ref, hs_ref, flag_ref = refs[n_wide:]
+    as_ref, rrc_ref, side_ref, mixa_ref, m1_ref, sp1_ref, hs_ref, flag_ref = refs[n_wide:]
     chan = m1_ref.shape[1]
     n_near = m1_ref.shape[2]
 
@@ -259,7 +261,6 @@
         act, slope = silu_parts(value)
         sp1_ref[:, here] = slope
         hidden = act + emb0_col + embd_col * flag_ref[0:1, here]
-        hid_ref[:, here] = hidden
         hi, lo = split(hidden)
         hs_ref[0:chan, here] = hi
         hs_ref[chan : 2 * chan, here] = lo
@@ -267,68 +268,42 @@
     in_turns(0, n_near // wide_cols, first)
 
 
-def gather_kernel(hid_ref, hs_ref, oh_ref, pick_ref, gidx_ref, bt_ref, r2c_ref, hj_ref, w_ref, car_ref, ext_ref):
-    slots = bt_ref.shape[0]
+def second_kernel(hs_ref, oh_ref, pick_ref, bt_ref, r2c_ref, yb_ref, mixa_ref, mixt_ref, side_ref,
+                  hj_ref, w_ref, car_ref, m2_ref, dinv_ref, ext_ref, inv_ref):
+    slots = yb_ref.shape[1]
     bases = bt_ref.shape[1] // 2
-    chan, n_near = hid_ref.shape
-    atoms = hj_ref.shape[1] // slots
+    chan, atoms = m2_ref.shape[1:]
+    tiles = atoms // LANES
     half = atoms // 2
-    by_lane = 2 * LANES if atoms > 2 * LANES else 0
-    by_product = 2 * atoms - by_lane
+    wide_cols = 2 * LANES
+    tile_edges = slots * LANES
+    turns = tile_edges // wide_cols
+    rows = chan // turns
     ghosts = dot(hs_ref[...], pick_ref[...]).astype(bf16)
     ext_ref[:, 0:half] = ghosts[:, :half]
     ext_ref[:, half : half + atoms] = hs_ref[:, 0:atoms]
     ext_ref[:, half + atoms :] = ghosts[:, half:]
-    for k in range(slots):
-        here = slice(k * atoms, (k + 1) * atoms)
-        basis = split_rows(bt_ref[k, 0:bases, 0:atoms])
-        w_ref[:, here] = dot(r2c_ref[...], jnp.concatenate([basis, basis], axis=0).astype(bf16))
-
-    def gather(pair, carry):
-        first = pl.multiple_of(pair * 2 * atoms, LANES)
-        here = pl.ds(first, by_product)
+    for t in range(tiles):
+        cols = slice(t * LANES, (t + 1) * LANES)
+        basis = jnp.concatenate([split_rows(bt_ref[k, 0:bases, cols]) for k in range(slots)], axis=1)
+        w_ref[:, t * tile_edges : (t + 1) * tile_edges] = dot(
+            r2c_ref[...], jnp.concatenate([basis, basis], axis=0).astype(bf16)
+        )
+
+    def gather(t, turn):
+        here = pl.ds(pl.multiple_of(t * tile_edges + turn * wide_cols, LANES), wide_cols)
         both = dot(ext_ref[...], oh_ref[:, here])
-        wanted = gidx_ref[pl.ds(2 * pair + 1, 1), 0:atoms]
-        for t in range(by_lane // LANES):
-            at = pl.ds(pl.multiple_of(first + (by_product + t * LANES), LANES), LANES)
-            start = atoms - by_lane + t * LANES
-            mine = row(wanted[:, start : start + LANES])
-            chunk_no = mine >> 7
-            place = mine & 127
-            for c in range(chan // 8):
-                rows = slice(8 * c, 8 * c + 8)
-                feat = None
-                for chunk in range(n_near // LANES):
-                    held = hid_ref[rows, chunk * LANES : (chunk + 1) * LANES]
-                    got = jnp.take_along_axis(held, place, axis=1, mode="promise_in_bounds")
-                    feat = got if feat is None else jnp.where(chunk_no == chunk, got, feat)
-                hj_ref[rows, at] = feat
-                car_ref[rows, at] = feat * w_ref[rows, at]
         feat = both[:chan] + both[chan:]
         hj_ref[:, here] = feat
         car_ref[:, here] = feat * w_ref[:, here]
-        return carry
-
-    lax.fori_loop(0, slots // 2, gather, 0)
-
-
-def moment_kernel(car_ref, yb_ref, mixa_ref, mixt_ref, side_ref, m2_ref, dinv_ref, inv_ref):
-    slots = yb_ref.shape[1]
-    chan, atoms = m2_ref.shape[1:]
-    tiles = atoms // LANES
-    wide_cols = 2 * LANES
-    rows = 32
-    groups = chan // rows
-
-    def moments(step):
-        t = step // groups
-        c = step % groups
-        cols = pl.ds(pl.multiple_of(t * LANES, LANES), LANES)
-        base = pl.multiple_of(c * rows, rows)
+
+    def moments(t, turn):
+        cols = slice(t * LANES, (t + 1) * LANES)
+        base = pl.multiple_of(turn * rows, rows)
         acc = [[None] * ORDERS for _ in range(rows // 8)]
         for k in range(slots):
-            at = pl.ds(pl.multiple_of(k * atoms + t * LANES, LANES), LANES)
-            got = car_ref[pl.ds(base, rows), at]
+            at = t * tile_edges + k * LANES
+            got = car_ref[pl.ds(base, rows), at : at + LANES]
             for l in range(ORDERS):
                 yb = yb_ref[l - 1, k, :, cols] if l else None
                 for h in range(rows // 8):
@@ -345,7 +320,17 @@
             for g in range(3):
                 inv_ref[pl.ds(pl.multiple_of(g * chan + base + 8 * h, 8), 8), cols] = inv[g]
 
-    in_turns(0, tiles * groups, moments, 2)
+    for turn in range(turns):
+        gather(0, turn)
+    for t in range(tiles):
+
+        def both_parts(turn, carry, t=t):
+            moments(t, turn)
+            if t + 1 < tiles:
+                gather(t + 1, turn)
+            return carry
+
+        lax.fori_loop(0, turns, both_parts, 0)
     read2_col = side_ref[:, 3:4]
     for t in range(atoms // wide_cols):
         cols = slice(t * wide_cols, (t + 1) * wide_cols)
@@ -356,88 +341,72 @@
             dinv_ref[g * chan : (g + 1) * chan, cols] = scale * dot_parts(mixt_ref[1, g], hi, lo)
 
 
-def back_second_kernel(m2_ref, dinv_ref, car_ref, hj_ref, w_ref, ub_ref, dhe_ref, dw_ref, p_ref):
+def back_second_kernel(m2_ref, dinv_ref, car_ref, hj_ref, w_ref, ub_ref, oh_ref, pick_ref, side_ref, bt_ref, geo_ref,
+                       r2r_ref, gidx_ref, dh_ref, q_ref, ohlo_ref, ds_ref, p_ref, sum_ref, *tile_refs):
     slots = ub_ref.shape[1]
+    bases = bt_ref.shape[1] // 2
     chan, atoms = m2_ref.shape[1:]
+    n_near = dh_ref.shape[1]
     tiles = atoms // LANES
-    pairs = chan // 16
-    per_turn = 2 if pairs % 2 == 0 else 1
-
-    def back_moments(t, carry):
-        cols = pl.ds(pl.multiple_of(t * LANES, LANES), LANES)
-
-        def one(c, acc):
-            forms = []
+    half = atoms // 2
+    tile_edges = slots * LANES
+    dhe_refs, dw_refs = tile_refs[:tiles], tile_refs[tiles:]
+    turns, _, span = sum_ref.shape
+    per_turn = chan // 16 // turns
+
+    def spread_part(t, turn):
+        picked = oh_ref[pl.ds(pl.multiple_of(turn * span, span), span), t * tile_edges : (t + 1) * tile_edges]
+        part = dot_nt(dhe_refs[t][...], picked)
+        return part if t == 0 else sum_ref[turn] + part
+
+    def one(t, c, acc):
+        cols = slice(t * LANES, (t + 1) * LANES)
+        forms = []
+        for h in range(2):
+            rows = pl.ds(pl.multiple_of(c * 16 + 8 * h, 8), 8)
+            scale = [dinv_ref[pl.ds(pl.multiple_of(g * chan + c * 16 + 8 * h, 8), 8), cols] for g in range(3)]
+            dm = [m2_ref[l, rows, cols] * scale[GROUP[l]] for l in range(ORDERS)]
+            low = dm[6] * (1.0 / SQRT3)
+            forms.append((dm[0], dm[1], dm[2], dm[3], dm[8] - low, -dm[8] - low, low + low, dm[4], dm[5], dm[7]))
+        base = pl.multiple_of(c * 16, 16)
+        for k in range(slots):
+            at = slice(t * tile_edges + k * LANES, t * tile_edges + (k + 1) * LANES)
+            in_tile = slice(k * LANES, (k + 1) * LANES)
+            got = car_ref[pl.ds(base, 16), at]
+            ux, uy, uz = [ub_ref[i, k, :, cols] for i in range(3)]
+            out = []
             for h in range(2):
-                rows = pl.ds(pl.multiple_of(c * 16 + 8 * h, 8), 8)
-                scale = [dinv_ref[pl.ds(pl.multiple_of(g * chan + c * 16 + 8 * h, 8), 8), cols] for g in range(3)]
-                dm = [m2_ref[l, rows, cols] * scale[GROUP[l]] for l in range(ORDERS)]
-                low = dm[6] * (1.0 / SQRT3)
-                forms.append((dm[0], dm[1], dm[2], dm[3], dm[8] - low, -dm[8] - low, low + low, dm[4], dm[5], dm[7]))
-            base = pl.multiple_of(c * 16, 16)
-            for k in range(slots):
-                at = pl.ds(pl.multiple_of(k * atoms + t * LANES, LANES), LANES)
-                got = car_ref[pl.ds(base, 16), at]
-                ux, uy, uz = [ub_ref[i, k, :, cols] for i in range(3)]
-                out = []
-                for h in range(2):
-                    mid, dx, dy, dz, qxx, qyy, qzz, qxy, qyz, qxz = forms[h]
-                    gx = dx + qxx * ux + qxy * uy + qxz * uz
-                    gy = dy + qxy * ux + qyy * uy + qyz * uz
-                    gz = dz + qxz * ux + qyz * uy + qzz * uz
-                    out.append(mid + (gx + dx) * ux + (gy + dy) * uy + (gz + dz) * uz)
-                    part = got[8 * h : 8 * h + 8]
-                    for i, g in enumerate((gx, gy, gz)):
-                        acc[3 * k + i] = acc[3 * k + i] + part * g
-                dcar = jnp.concatenate(out, axis=0)
-                for ref, other in ((dhe_ref, w_ref), (dw_ref, hj_ref)):
-                    hi, lo = split(dcar * other[pl.ds(base, 16), at])
-                    ref[pl.ds(base, 16), at] = hi
-                    ref[pl.ds(pl.multiple_of(chan + c * 16, 16), 16), at] = lo
-
-        def over(c, acc):
+                mid, dx, dy, dz, qxx, qyy, qzz, qxy, qyz, qxz = forms[h]
+                gx = dx + qxx * ux + qxy * uy + qxz * uz
+                gy = dy + qxy * ux + qyy * uy + qyz * uz
+                gz = dz + qxz * ux + qyz * uy + qzz * uz
+                out.append(mid + (gx + dx) * ux + (gy + dy) * uy + (gz + dz) * uz)
+                part = got[8 * h : 8 * h + 8]
+                for i, g in enumerate((gx, gy, gz)):
+                    acc[3 * k + i] = acc[3 * k + i] + part * g
+            dcar = jnp.concatenate(out, axis=0)
+            for ref, other in ((dhe_refs[t], w_ref), (dw_refs[t], hj_ref)):
+                hi, lo = split(dcar * other[pl.ds(base, 16), at])
+                ref[pl.ds(base, 16), in_tile] = hi
+                ref[pl.ds(pl.multiple_of(chan + c * 16, 16), 16), in_tile] = lo
+
+    for t in range(tiles):
+        cols = slice(t * LANES, (t + 1) * LANES)
+
+        def both_parts(turn, acc, t=t):
             acc = list(acc)
             for i in range(per_turn):
-                one(per_turn * c + i, acc)
+                one(t, per_turn * turn + i, acc)
+            if t:
+                sum_ref[turn] = spread_part(t - 1, turn)
             return tuple(acc)
 
         start = tuple(jnp.zeros((8, LANES), f32) for _ in range(3 * slots))
-        acc = lax.fori_loop(0, pairs // per_turn, over, start)
+        acc = lax.fori_loop(0, turns, both_parts, start)
         for k in range(slots):
             for i in range(3):
                 p_ref[i, 8 * k : 8 * k + 8, cols] = acc[3 * k + i]
-        return carry
-
-    lax.fori_loop(0, tiles, back_moments, 0)
-
-
-def scatter_kernel(oh_ref, pick_ref, dhe_ref, side_ref, dw_ref, p_ref, bt_ref, geo_ref, r2r_ref, gidx_ref,
-                   dh_ref, q_ref, ohlo_ref, ds_ref):
-    chan, n_near = dh_ref.shape
-    slots = bt_ref.shape[0]
-    bases = bt_ref.shape[1] // 2
-    atoms = pick_ref.shape[1]
-    half = atoms // 2
-    both = dot_nt(dhe_ref[...], oh_ref[...])
-    ids16 = lax.broadcasted_iota(jnp.int32, (LANES, n_near), 0).astype(jnp.int16)
-    one16 = jnp.ones((LANES, n_near), bf16)
-    zero16 = jnp.zeros((LANES, n_near), bf16)
-    for k in range(slots):
-        place = jnp.broadcast_to(gidx_ref[k : k + 1, :] & 127, (LANES, n_near)).astype(jnp.int16)
-        ohlo_ref[:, k * n_near : (k + 1) * n_near] = jnp.where(place == ids16, one16, zero16)
-    for k in range(slots):
-        here = slice(k * atoms, (k + 1) * atoms)
-        small = dot(r2r_ref[...], dw_ref[:, here])
-        dbasis = small[:bases] + small[bases:]
-        basis = bt_ref[k, 0:bases, 0:atoms]
-        reach = 1.0 + lax.broadcasted_iota(jnp.int32, (bases, atoms), 0).astype(f32)
-        ds_ref[k * 8 : k * 8 + 8, :] = dbasis * basis * (reach - row(geo_ref[4, k : k + 1, 0:atoms], bases))
-    lane = lax.broadcasted_iota(jnp.int32, (slots, 16 * slots), 1)
-    sub = lax.broadcasted_iota(jnp.int32, (slots, 16 * slots), 0)
-    adder = jnp.where(((lane >> 3) & (slots - 1)) == sub, 1.0, 0.0).astype(bf16)
-    for i in range(4):
-        total = dot(adder, split_rows(p_ref[i - 1, :, :] if i else ds_ref[...]).astype(bf16))
-        q_ref[8 * i : 8 * i + 8, :] = 2.0 * total if i else total
+    both = jnp.concatenate([spread_part(tiles - 1, turn) for turn in range(turns)], axis=1)
     ext = both[:chan] + both[chan:]
     hi, lo = split(jnp.concatenate([ext[:, :half], ext[:, half + atoms :]], axis=1))
     spread = dot_nt(jnp.concatenate([hi, lo], axis=0), pick_ref[...])
@@ -445,6 +414,27 @@
     dh_ref[:, 0:atoms] = spread[:, :atoms] + ext[:, half : half + atoms] + side_ref[:, 2:3]
     if n_near > atoms:
         dh_ref[:, atoms:] = spread[:, atoms:]
+
+    ids16 = lax.broadcasted_iota(jnp.int32, (LANES, n_near), 0).astype(jnp.int16)
+    one16 = jnp.ones((LANES, n_near), bf16)
+    zero16 = jnp.zeros((LANES, n_near), bf16)
+    for k in range(slots):
+        place = jnp.broadcast_to(gidx_ref[k : k + 1, :] & 127, (LANES, n_near)).astype(jnp.int16)
+        ohlo_ref[:, k * n_near : (k + 1) * n_near] = jnp.where(place == ids16, one16, zero16)
+    reach = 1.0 + lax.broadcasted_iota(jnp.int32, (bases, LANES), 0).astype(f32)
+    for t in range(tiles):
+        cols = slice(t * LANES, (t + 1) * LANES)
+        small = dot(r2r_ref[...], dw_refs[t][...])
+        dbasis = small[:bases] + small[bases:]
+        for k in range(slots):
+            far = reach - row(geo_ref[4, k : k + 1, cols], bases)
+            ds_ref[k * 8 : k * 8 + 8, cols] = dbasis[:, k * LANES : (k + 1) * LANES] * bt_ref[k, 0:bases, cols] * far
+    lane = lax.broadcasted_iota(jnp.int32, (slots, 16 * slots), 1)
+    sub = lax.broadcasted_iota(jnp.int32, (slots, 16 * slots), 0)
+    adder = jnp.where(((lane >> 3) & (slots - 1)) == sub, 1.0, 0.0).astype(bf16)
+    for i in range(4):
+        total = dot(adder, split_rows(p_ref[i - 1, :, :] if i else ds_ref[...]).astype(bf16))
+        q_ref[8 * i : 8 * i + 8, :] = 2.0 * total if i else total
 
 
 def back_first_kernel(dh_ref, sp1_ref, m1_ref, mixt_ref, rrr_ref, da_ref):
@@ -560,7 +550,7 @@
 
 
 def run(name, body, operands, results, scratch=(), far=(), cost=None):
-    sizes = [math.prod(x.shape) * x.dtype.itemsize for i, x in enumerate(operands) if i not in far]
+    sizes = [math.prod(x.shape) * x.dtype.itemsize // 3 for i, x in enumerate(operands) if i not in far]
     sizes += [math.prod(shape) * jnp.dtype(dtype).itemsize for shape, dtype in results]
     sizes += [math.prod(x.shape) * x.dtype.itemsize for x in scratch if x.memory_space == pltpu.VMEM]
     limit = sum(sizes) + 4 * MIB
@@ -629,39 +619,33 @@
             ((ORDERS, 8 * bases, n_near), bf16),
         ),
     )
-    m1, sp1, hid, hs = run(
+    m1, sp1, hs = run(
         "first",
         functools.partial(first_kernel, plan),
         (*blocks, as1, rrc, sides, mixa),
-        (((ORDERS, chan, n_near), f32), ((chan, n_near), f32), ((chan, n_near), f32), ((2 * chan, n_near), bf16)),
+        (((ORDERS, chan, n_near), f32), ((chan, n_near), f32), ((2 * chan, n_near), bf16)),
         [pltpu.VMEM((8, n_near), f32)],
     )
-    hj, w, car = run(
-        "gather",
-        gather_kernel,
-        (hid, hs, oh, pick, gidx, bt, r2c),
-        (((chan, edges), f32),) * 3,
-        [pltpu.VMEM((2 * chan, 2 * atoms), bf16)],
+    tiles = atoms // LANES
+    turns = slots // 2
+    hj, w, car, m2, dinv = run(
+        "second",
+        second_kernel,
+        (hs, oh, pick, bt, r2c, yb, mixa, mixt, sides),
+        (((chan, edges), f32),) * 3 + (((ORDERS, chan, atoms), f32), ((3 * chan, atoms), f32)),
+        [pltpu.VMEM((2 * chan, 2 * atoms), bf16), pltpu.VMEM((3 * chan, atoms), f32)],
     )
-    m2, dinv = run(
-        "moments",
-        moment_kernel,
-        (car, yb, mixa, mixt, sides),
-        (((ORDERS, chan, atoms), f32), ((3 * chan, atoms), f32)),
-        [pltpu.VMEM((3 * chan, atoms), f32)],
-    )
-    dhe, dw, p = run(
+    dh, q, ohlo = run(
         "back_second",
         back_second_kernel,
-        (m2, dinv, car, hj, w, ub),
-        (((2 * chan, edges), bf16), ((2 * chan, edges), bf16), ((3, 8 * slots, atoms), f32)),
-    )
-    dh, q, ohlo = run(
-        "scatter",
-        scatter_kernel,
-        (oh, pick, dhe, sides, dw, p, bt, geo, r2r, gidx),
+        (m2, dinv, car, hj, w, ub, oh, pick, sides, bt, geo, r2r, gidx),
         (((chan, n_near), f32), ((4 * slots, atoms), f32), ((LANES, slots * n_near), bf16)),
-        [pltpu.VMEM((8 * slots, atoms), f32)],
+        [
+            pltpu.VMEM((8 * slots, atoms), f32),
+            pltpu.VMEM((3, 8 * slots, atoms), f32),
+            pltpu.VMEM((turns, 2 * chan, 2 * atoms // turns), f32),
+        ]
+        + [pltpu.VMEM((2 * chan, slots * LANES), bf16)] * (2 * tiles),
     )
     (da,) = run("back_first", back_first_kernel, (dh, sp1, m1, mixt, rrr), (((ORDERS, 2 * bases, n_near), f32),))
     return run(

time: 44.3 us -> 47.4 us (1.070)
  Pallas kernels: 22.8 us -> 25.9 us
    pallas_call x9 -> x7, Pallas kernels: 21.3 us -> 24.4 us  [run(): pl.pallas_call(body, out_shape=tuple((jax.ShapeDtypeStruct(shape, dtype)...]
where the time goes in v10:
time: 47.4 us; the launch traced here: 47.1 us
  Pallas kernels  25.9 us (55%)
  starting transfers between devices  9.11 us (19%)
  blocking collectives  8.47 us (18%)
  waiting for transfers between devices  2.9 us (6%)
  between operations  0.69 us (1%)
    pallas_call x7, Pallas kernels, run(): pl.pallas_call(body, out_shape=tuple((jax.ShapeDtypeStruct(shape, dtype)...  24.4 us
    all_to_all x1, blocking collectives, shards(): lax.all_to_all(messages, ('bead', 'space'), 0, 0, axis_index_groups=rows,...  8.47 us
    ppermute x3, starting transfers between devices, shards(): lax.ppermute(pushed, 'bead', [(b, (b + z * inner) % beads) for b in range...  6.07 us
    ppermute x1, starting transfers between devices, shards(): lax.ppermute(block, 'space', [(i, (i - offset) % domains) for i in range(...  3.03 us
    ppermute x3, waiting for transfers between devices, shards(): lax.ppermute(pushed, 'bead', [(b, (b + z * inner) % beads) for b in range...  2.47 us
  transfers between devices with their start and end apart: 4, of which 3 were waited for; matrix products, arithmetic and copies ran while one was open for 0% of the time, Pallas kernels for 3%

profile of v10, /device:TPU:0, one launch (start us, length us, event | category | flops | bytes accessed | tf_op | source)
XLA Modules:
  0.0 47.1 jit_solution(11136371650749379519)
XLA Ops:
  0.6 0.8 %pack.1.refs_0_.block_ref = f32[16,512]{1,0:T(8,128)S(1)} custom-call(f32[3,1,512]{2,1,0:T(1,128)} %bitcast.10, s32[1,512]{1,0:T(1,128)} %bitcast.12, s32[1,512]{1,0:T(1,128)} %bitcast.13, s32[8,512]{1,0:T(8,128)} %slot_src.1), custom_call_target="tpu_custom_call" | custom-call | tf_op jit(solution)/shard_map/pack/pallas_call | solution.py:776
  1.4 3.0 %collective-permute-start = (f32[16,512]{1,0:T(8,128)S(1)}, f32[16,512]{1,0:T(8,128)S(1)}, u32[]{:S(2)}, u32[]{:S(2)}) collective-permute-start(f32[16,512]{1,0:T(8,128)S(1)} %pack.1.refs_0_.block_ref), channel_id=1, source_target_pairs={{0,1},{1,0},{2,3},{3,2},{4,5},{5,4},{6,7},{7,6},{8,9},{9,8},{10,11... | collective-permute-start | bytes 98312 | tf_op jit(solution)/shard_map/ppermute | solution.py:793
  4.5 1.5 %choose.1 = (bf16[1024,4096]{1,0:T(8,128)(2,1)S(1)}, bf16[128,64]{1,0:T(8,128)(2,1)S(1)}, bf16[128,32]{1,0:T(8,128)(2,1)S(1)}, f32[128,128]{1,0:T(8,128)S(1)}, b...) custom-call(f32[16,512]{1,0:T(8,128)S(1)} %pack.1.refs_0_.block_ref,, ...), custom_call_target="tpu_custom_call" | custom-call | flops 2000000000 | bytes 2000000 | tf_op jit(solution)/shard_map/choose/pallas_call | solution.py:558
  5.9 0.4 collective-permute-done.refs_1_
  6.4 1.7 %edges.1 = (f32[6,8,1024]{2,1,0:T(8,128)S(1)}, f32[8,8,1024]{2,1,0:T(8,128)S(1)}, f32[8,8,8,512]{3,2,1,0:T(8,128)S(1)}, f32[3,8,8,512]{3,2,1,0:T(8,128)S(1)}, f3...) custom-call(f32[16,512]{1,0:T(8,128)S(1)} %pack.1.refs_0_.block_ref,, ...), custom_call_target="tpu_custom_call" | custom-call | tf_op jit(solution)/shard_map/edges/pallas_call | solution.py:558
  8.1 1.7 %first.1 = (f32[9,128,1024]{2,1,0:T(8,128)S(1)}, f32[128,1024]{1,0:T(8,128)S(1)}, bf16[256,1024]{1,0:T(8,128)(2,1)S(1)}) custom-call(f32[16,512]{1,0:T(8,128)S(1)} %pack.1.refs_0_.block_ref, f32[16,512]{1,0:T(8,128)S(1)} %collective-permute-done.refs_1_, bf16[9,64,1024]{2,1,0:T(8,128)(2,1)S(1)} %get-tuple-element.38.refs_2_, ...), custom_call_target="tpu_custom_call" | custom-call | tf_op jit(solution)/shard_map/first/pallas_call | solution.py:558
  9.8 6.7 %second.1 = (f32[128,4096]{1,0:T(8,128)S(1)}, f32[128,4096]{1,0:T(8,128)S(1)}, f32[128,4096]{1,0:T(8,128)S(1)}, f32[9,128,512]{2,1,0:T(8,128)S(1)}, f32[384,512]{1,0:T(8,128)S(1)}) custom-call(bf16[256,1024]{1,0:T(8,128)(2,1)S(1)} %get-tuple-element.42.hs_ref, bf16[1024,4096]{1,0:T(8,128)(2,1)S(1)} %get-tuple-element.43.oh_ref, ...), custom_call_target="tpu_custom_call" | custom-call | tf_op jit(solution)/shard_map/second/pallas_call | solution.py:558
  16.4 9.1 %back_second.1 = (f32[128,1024]{1,0:T(8,128)S(1)}, f32[32,512]{1,0:T(8,128)S(1)}, bf16[128,8192]{1,0:T(8,128)(2,1)S(1)}) custom-call(f32[9,128,512]{2,1,0:T(8,128)S(1)} %get-tuple-element.49.m2_ref, f32[384,512]{1,0:T(8,128)S(1)} %get-tuple-element.50.dinv_ref, f32[128,4096]{1,0:T(8,128)S(1)} %get-tuple-element.51.car_ref, ...), custom_call_target="tpu_custom_call" | custom-call | tf_op jit(solution)/shard_map/back_second/pallas_call | solution.py:558
  25.5 2.0 %back_first.1.refs_7_ = f32[9,16,1024]{2,1,0:T(8,128)S(1)} custom-call(f32[128,1024]{1,0:T(8,128)S(1)} %get-tuple-element.56.dh_ref, f32[128,1024]{1,0:T(8,128)S(1)} %get-tuple-element.57.sp1_ref, f32[9,128,1024]{2,1,0:T(8,128)S(1)} %get-tuple-element.58.m1_ref, bf16[2,3,256,128]{3,2,1,0:T(8,128)(2,1)S(1)} %get-tuple-element.48.mixt_ref, ...), custom_call_target="tpu_custom_call" | custom-call | tf_op jit(solution)/shard_map/back_first/pallas_call | solution.py:558
  27.6 1.8 %back_edges.1 = (f32[48,128]{1,0:T(8,128)S(1)}, f32[32,128]{1,0:T(8,128)S(1)}) custom-call(f32[16,512]{1,0:T(8,128)S(1)} %pack.1.refs_0_.block_ref, f32[16,512]{1,0:T(8,128)S(1)} %collective-permute-done.refs_1_, f32[3,1,512]{2,1,0:T(1,128)} %bitcast.11, f32[6,8,1024]{2,1,0:T(8,128)S(1)} %get-tuple-element.34.geo_ref.refs_3_, ...), custom_call_target="tpu_custom_call" | custom-call | tf_op jit(solution)/shard_map/back_edges/pallas_call | solution.py:558
  29.4 2.1 %collective-permute-start.1 = (f32[48,128]{1,0:T(8,128)S(1)}, f32[48,128]{1,0:T(8,128)S(1)}, u32[]{:S(2)}, u32[]{:S(2)}) collective-permute-start(f32[48,128]{1,0:T(8,128)S(1)} %get-tuple-element.63.refs_0_), channel_id=1, source_target_pairs={{0,8},{2,10},{4,12},{6,14},{8,16},{10,18},{12,20},{14,22},{16,24},... | collective-permute-start | bytes 73736 | tf_op jit(solution)/shard_map/ppermute | solution.py:798
  31.5 2.6 %collective-permute-start.2 = (f32[48,128]{1,0:T(8,128)S(1)}, f32[48,128]{1,0:T(8,128)S(1)}, u32[]{:S(2)}, u32[]{:S(2)}) collective-permute-start(f32[48,128]{1,0:T(8,128)S(1)} %get-tuple-element.63.refs_0_), channel_id=1, source_target_pairs={{0,16},{2,18},{4,20},{6,22},{8,24},{10,26},{12,28},{14,30},{16,0},... | collective-permute-start | bytes 73736 | tf_op jit(solution)/shard_map/ppermute | solution.py:798
  34.1 1.4 %collective-permute-start.3 = (f32[48,128]{1,0:T(8,128)S(1)}, f32[48,128]{1,0:T(8,128)S(1)}, u32[]{:S(2)}, u32[]{:S(2)}) collective-permute-start(f32[48,128]{1,0:T(8,128)S(1)} %get-tuple-element.63.refs_0_), channel_id=1, source_target_pairs={{0,24},{2,26},{4,28},{6,30},{8,0},{10,2},{12,4},{14,6},{16,8},{18,... | collective-permute-start | bytes 73736 | tf_op jit(solution)/shard_map/ppermute | solution.py:798
  35.4 0.0 collective-permute-done.1.refs_1_
  35.4 0.8 %collective-permute-done.2.refs_2_ = f32[48,128]{1,0:T(8,128)S(1)} collective-permute-done((f32[48,128]{1,0:T(8,128)S(1)}, f32[48,128]{1,0:T(8,128)S(1)}, u32[]{:S(2)}, u32[]{:S(2)}) %collective-permute-start.2) | collective-permute-done | bytes 24608 | tf_op jit(solution)/shard_map/ppermute | solution.py:798
  36.2 1.7 %collective-permute-done.3.refs_3_ = f32[48,128]{1,0:T(8,128)S(1)} collective-permute-done((f32[48,128]{1,0:T(8,128)S(1)}, f32[48,128]{1,0:T(8,128)S(1)}, u32[]{:S(2)}, u32[]{:S(2)}) %collective-permute-start.3) | collective-permute-done | bytes 24608 | tf_op jit(solution)/shard_map/ppermute | solution.py:798
  37.9 0.1 turn.1
  38.0 8.5 %all_to_all.5.arrived_ref = f32[8,32,128]{2,1,0:T(8,128)S(1)} all-to-all(f32[8,32,128]{2,1,0:T(8,128)S(1)} %turn.1), channel_id=1, replica_groups={{0,1,2,3,4,5,6,7},{8,9,10,11,12,13,14,15},{16,17,18,19,20,21,22,23},{24..., dimensions={0} | all-to-all | bytes 262144 | tf_op jit(solution)/shard_map/all_to_all | solution.py:810
  46.5 0.6 %sum.1 = (f32[3,1,512]{2,1,0:T(1,128)}, f32[3,1,512]{2,1,0:T(1,128)}) custom-call(f32[8,32,128]{2,1,0:T(8,128)S(1)} %all_to_all.5.arrived_ref), custom_call_target="tpu_custom_call" | custom-call | tf_op jit(solution)/shard_map/sum/pallas_call | solution.py:811
Async XLA Ops:
  1.4 4.9 %collective-permute-start = (f32[16,512]{1,0:T(8,128)S(1)}, f32[16,512]{1,0:T(8,128)S(1)}, u32[]{:S(2)}, u32[]{:S(2)}) collective-permute-start(f32[16,512]{1,0:T(8,128)S(1)} %pack.1.refs_0_.block_ref), channel_id=1, source_target_pairs={{0,1},{1,0},{2,3},{3,2},{4,5},{5,4},{6,7},{7,6},{8,9},{9,8},{10,11... | collective-permute-start | bytes 98312 | tf_op jit(solution)/shard_map/ppermute | solution.py:793
  29.4 6.1 %collective-permute-start.1 = (f32[48,128]{1,0:T(8,128)S(1)}, f32[48,128]{1,0:T(8,128)S(1)}, u32[]{:S(2)}, u32[]{:S(2)}) collective-permute-start(f32[48,128]{1,0:T(8,128)S(1)} %get-tuple-element.63.refs_0_), channel_id=1, source_target_pairs={{0,8},{2,10},{4,12},{6,14},{8,16},{10,18},{12,20},{14,22},{16,24},... | collective-permute-start | bytes 73736 | tf_op jit(solution)/shard_map/ppermute | solution.py:798
  31.5 4.7 %collective-permute-start.2 = (f32[48,128]{1,0:T(8,128)S(1)}, f32[48,128]{1,0:T(8,128)S(1)}, u32[]{:S(2)}, u32[]{:S(2)}) collective-permute-start(f32[48,128]{1,0:T(8,128)S(1)} %get-tuple-element.63.refs_0_), channel_id=1, source_target_pairs={{0,16},{2,18},{4,20},{6,22},{8,24},{10,26},{12,28},{14,30},{16,0},... | collective-permute-start | bytes 73736 | tf_op jit(solution)/shard_map/ppermute | solution.py:798
  34.1 3.8 %collective-permute-start.3 = (f32[48,128]{1,0:T(8,128)S(1)}, f32[48,128]{1,0:T(8,128)S(1)}, u32[]{:S(2)}, u32[]{:S(2)}) collective-permute-start(f32[48,128]{1,0:T(8,128)S(1)} %get-tuple-element.63.refs_0_), channel_id=1, source_target_pairs={{0,24},{2,26},{4,28},{6,30},{8,0},{10,2},{12,4},{14,6},{16,8},{18,... | collective-permute-start | bytes 73736 | tf_op jit(solution)/shard_map/ppermute | solution.py:798

commit v11 on v8

--- a/solution.py
+++ b/solution.py
@@ -284,13 +284,13 @@
         basis = split_rows(bt_ref[k, 0:bases, 0:atoms])
         w_ref[:, here] = dot(r2c_ref[...], jnp.concatenate([basis, basis], axis=0).astype(bf16))
 
-    def gather(pair, carry):
-        first = pl.multiple_of(pair * 2 * atoms, LANES)
-        here = pl.ds(first, by_product)
+    for pair in range(slots // 2):
+        first = pair * 2 * atoms
+        here = slice(first, first + by_product)
         both = dot(ext_ref[...], oh_ref[:, here])
-        wanted = gidx_ref[pl.ds(2 * pair + 1, 1), 0:atoms]
+        wanted = gidx_ref[2 * pair + 1 : 2 * pair + 2, 0:atoms]
         for t in range(by_lane // LANES):
-            at = pl.ds(pl.multiple_of(first + (by_product + t * LANES), LANES), LANES)
+            at = slice(first + by_product + t * LANES, first + by_product + (t + 1) * LANES)
             start = atoms - by_lane + t * LANES
             mine = row(wanted[:, start : start + LANES])
             chunk_no = mine >> 7
@@ -307,9 +307,6 @@
         feat = both[:chan] + both[chan:]
         hj_ref[:, here] = feat
         car_ref[:, here] = feat * w_ref[:, here]
-        return carry
-
-    lax.fori_loop(0, slots // 2, gather, 0)
 
 
 def moment_kernel(car_ref, yb_ref, mixa_ref, mixt_ref, side_ref, m2_ref, dinv_ref, inv_ref):
@@ -345,7 +342,7 @@
             for g in range(3):
                 inv_ref[pl.ds(pl.multiple_of(g * chan + base + 8 * h, 8), 8), cols] = inv[g]
 
-    in_turns(0, tiles * groups, moments, 2)
+    in_turns(0, tiles * groups, moments, 4)
     read2_col = side_ref[:, 3:4]
     for t in range(atoms // wide_cols):
         cols = slice(t * wide_cols, (t + 1) * wide_cols)
@@ -361,7 +358,7 @@
     chan, atoms = m2_ref.shape[1:]
     tiles = atoms // LANES
     pairs = chan // 16
-    per_turn = 2 if pairs % 2 == 0 else 1
+    per_turn = 4 if pairs % 4 == 0 else 1
 
     def back_moments(t, carry):
         cols = pl.ds(pl.multiple_of(t * LANES, LANES), LANES)
@@ -418,7 +415,14 @@
     bases = bt_ref.shape[1] // 2
     atoms = pick_ref.shape[1]
     half = atoms // 2
-    both = dot_nt(dhe_ref[...], oh_ref[...])
+    both = dot_nt(dhe_ref[...], jnp.concatenate([oh_ref[:half], oh_ref[half + atoms :]], axis=0))
+    hi, lo = split(both[:chan] + both[chan:])
+    spread = dot_nt(jnp.concatenate([hi, lo], axis=0), pick_ref[...])
+    spread = spread[:chan] + spread[chan:]
+    both = dot_nt(dhe_ref[...], oh_ref[half : half + atoms])
+    dh_ref[:, 0:atoms] = spread[:, :atoms] + both[:chan] + both[chan:] + side_ref[:, 2:3]
+    if n_near > atoms:
+        dh_ref[:, atoms:] = spread[:, atoms:]
     ids16 = lax.broadcasted_iota(jnp.int32, (LANES, n_near), 0).astype(jnp.int16)
     one16 = jnp.ones((LANES, n_near), bf16)
     zero16 = jnp.zeros((LANES, n_near), bf16)
@@ -438,13 +442,6 @@
     for i in range(4):
         total = dot(adder, split_rows(p_ref[i - 1, :, :] if i else ds_ref[...]).astype(bf16))
         q_ref[8 * i : 8 * i + 8, :] = 2.0 * total if i else total
-    ext = both[:chan] + both[chan:]
-    hi, lo = split(jnp.concatenate([ext[:, :half], ext[:, half + atoms :]], axis=1))
-    spread = dot_nt(jnp.concatenate([hi, lo], axis=0), pick_ref[...])
-    spread = spread[:chan] + spread[chan:]
-    dh_ref[:, 0:atoms] = spread[:, :atoms] + ext[:, half : half + atoms] + side_ref[:, 2:3]
-    if n_near > atoms:
-        dh_ref[:, atoms:] = spread[:, atoms:]
 
 
 def back_first_kernel(dh_ref, sp1_ref, m1_ref, mixt_ref, rrr_ref, da_ref):
@@ -560,7 +557,7 @@
 
 
 def run(name, body, operands, results, scratch=(), far=(), cost=None):
-    sizes = [math.prod(x.shape) * x.dtype.itemsize for i, x in enumerate(operands) if i not in far]
+    sizes = [math.prod(x.shape) * x.dtype.itemsize // 2 for i, x in enumerate(operands) if i not in far]
     sizes += [math.prod(shape) * jnp.dtype(dtype).itemsize for shape, dtype in results]
     sizes += [math.prod(x.shape) * x.dtype.itemsize for x in scratch if x.memory_space == pltpu.VMEM]
     limit = sum(sizes) + 4 * MIB

time: 44.3 us -> 44 us (level)
  no operation moved by 1% of the time
where the time goes in v11:
time: 44 us; the launch traced here: 43.7 us
  Pallas kernels  22.5 us (51%)
  starting transfers between devices  9.1 us (21%)
  blocking collectives  8.47 us (19%)
  waiting for transfers between devices  2.91 us (7%)
  between operations  0.7 us (2%)
    pallas_call x9, Pallas kernels, run(): pl.pallas_call(body, out_shape=tuple((jax.ShapeDtypeStruct(shape, dtype)...  21 us
    all_to_all x1, blocking collectives, shards(): lax.all_to_all(messages, ('bead', 'space'), 0, 0, axis_index_groups=rows,...  8.47 us
    ppermute x3, starting transfers between devices, shards(): lax.ppermute(pushed, 'bead', [(b, (b + z * inner) % beads) for b in range...  6.07 us
    ppermute x1, starting transfers between devices, shards(): lax.ppermute(block, 'space', [(i, (i - offset) % domains) for i in range(...  3.03 us
    ppermute x3, waiting for transfers between devices, shards(): lax.ppermute(pushed, 'bead', [(b, (b + z * inner) % beads) for b in range...  2.48 us
  transfers between devices with their start and end apart: 4, of which 3 were waited for; matrix products, arithmetic and copies ran while one was open for 0% of the time, Pallas kernels for 3%

profile of v11, /device:TPU:0, one launch (start us, length us, event | category | flops | bytes accessed | tf_op | source)
XLA Modules:
  0.0 43.7 jit_solution(17721597422529046440)
XLA Ops:
  0.6 0.8 %pack.1.refs_0_.block_ref = f32[16,512]{1,0:T(8,128)S(1)} custom-call(f32[3,1,512]{2,1,0:T(1,128)} %bitcast.10, s32[1,512]{1,0:T(1,128)} %bitcast.12, s32[1,512]{1,0:T(1,128)} %bitcast.13, s32[8,512]{1,0:T(8,128)} %slot_src.1), custom_call_target="tpu_custom_call" | custom-call | tf_op jit(solution)/shard_map/pack/pallas_call | solution.py:789
  1.4 3.0 %collective-permute-start = (f32[16,512]{1,0:T(8,128)S(1)}, f32[16,512]{1,0:T(8,128)S(1)}, u32[]{:S(2)}, u32[]{:S(2)}) collective-permute-start(f32[16,512]{1,0:T(8,128)S(1)} %pack.1.refs_0_.block_ref), channel_id=1, source_target_pairs={{0,1},{1,0},{2,3},{3,2},{4,5},{5,4},{6,7},{7,6},{8,9},{9,8},{10,11... | collective-permute-start | bytes 98312 | tf_op jit(solution)/shard_map/ppermute | solution.py:806
  4.5 1.5 %choose.1 = (bf16[1024,4096]{1,0:T(8,128)(2,1)S(1)}, bf16[128,64]{1,0:T(8,128)(2,1)S(1)}, bf16[128,32]{1,0:T(8,128)(2,1)S(1)}, f32[128,128]{1,0:T(8,128)S(1)}, b...) custom-call(f32[16,512]{1,0:T(8,128)S(1)} %pack.1.refs_0_.block_ref,, ...), custom_call_target="tpu_custom_call" | custom-call | flops 2000000000 | bytes 2000000 | tf_op jit(solution)/shard_map/choose/pallas_call | solution.py:565
  5.9 0.4 collective-permute-done.refs_1_
  6.4 1.7 %edges.1 = (f32[6,8,1024]{2,1,0:T(8,128)S(1)}, f32[8,8,1024]{2,1,0:T(8,128)S(1)}, f32[8,8,8,512]{3,2,1,0:T(8,128)S(1)}, f32[3,8,8,512]{3,2,1,0:T(8,128)S(1)}, f3...) custom-call(f32[16,512]{1,0:T(8,128)S(1)} %pack.1.refs_0_.block_ref,, ...), custom_call_target="tpu_custom_call" | custom-call | tf_op jit(solution)/shard_map/edges/pallas_call | solution.py:565
  8.1 1.7 %first.1 = (f32[9,128,1024]{2,1,0:T(8,128)S(1)}, f32[128,1024]{1,0:T(8,128)S(1)}, f32[128,1024]{1,0:T(8,128)S(1)}, bf16[256,1024]{1,0:T(8,128)(2,1)S(1)}) custom-call(f32[16,512]{1,0:T(8,128)S(1)} %pack.1.refs_0_.block_ref, f32[16,512]{1,0:T(8,128)S(1)} %collective-permute-done.refs_1_, bf16[9,64,1024]{2,1,0:T(8,128)(2,1)S(1)} %get-tuple-element.44.refs_2_, ...), custom_call_target="tpu_custom_call" | custom-call | tf_op jit(solution)/shard_map/first/pallas_call | solution.py:565
  9.8 2.5 %gather.1 = (f32[128,4096]{1,0:T(8,128)S(1)}, f32[128,4096]{1,0:T(8,128)S(1)}, f32[128,4096]{1,0:T(8,128)S(1)}) custom-call(f32[128,1024]{1,0:T(8,128)S(1)} %get-tuple-element.48.hid_ref, bf16[256,1024]{1,0:T(8,128)(2,1)S(1)} %get-tuple-element.49.hs_ref, bf16[1024,4096]{1,0:T(8,128)(2,1)S(1)} %get-tuple-element.42.oh_ref, ...), custom_call_target="tpu_custom_call" | custom-call | tf_op jit(solution)/shard_map/gather/pallas_call | solution.py:565
  12.3 2.9 %moments.1 = (f32[9,128,512]{2,1,0:T(8,128)S(1)}, f32[384,512]{1,0:T(8,128)S(1)}) custom-call(f32[128,4096]{1,0:T(8,128)S(1)} %get-tuple-element.52.car_ref, f32[8,8,8,512]{3,2,1,0:T(8,128)S(1)} %get-tuple-element.53.yb_ref, bf16[2,256,384]{2,1,0:T(8,128)(2,1)S(1)} %get-tuple-element.47.refs_5_.mixa_ref, ...), custom_call_target="tpu_custom_call" | custom-call | tf_op jit(solution)/shard_map/moments/pallas_call | solution.py:565
  15.1 3.8 %back_second.1 = (bf16[256,4096]{1,0:T(8,128)(2,1)S(1)}, bf16[256,4096]{1,0:T(8,128)(2,1)S(1)}, f32[3,64,512]{2,1,0:T(8,128)S(1)}) custom-call(f32[9,128,512]{2,1,0:T(8,128)S(1)} %get-tuple-element.55.m2_ref, f32[384,512]{1,0:T(8,128)S(1)} %get-tuple-element.56.dinv_ref, f32[128,4096]{1,0:T(8,128)S(1)} %get-tuple-element.52.car_ref, ...), custom_call_target="tpu_custom_call" | custom-call | tf_op jit(solution)/shard_map/back_second/pallas_call | solution.py:565
  18.9 3.3 %scatter.1 = (f32[128,1024]{1,0:T(8,128)S(1)}, f32[32,512]{1,0:T(8,128)S(1)}, bf16[128,8192]{1,0:T(8,128)(2,1)S(1)}) custom-call(bf16[1024,4096]{1,0:T(8,128)(2,1)S(1)} %get-tuple-element.42.oh_ref, bf16[1024,512]{1,0:T(8,128)(2,1)S(1)} %get-tuple-element.43.pick_ref, bf16[256,4096]{1,0:T(8,128)(2,1)S(1)} %get-tuple-element.60.dhe_ref, ...), custom_call_target="tpu_custom_call" | custom-call | tf_op jit(solution)/shard_map/scatter/pallas_call | solution.py:565
  22.2 2.0 %back_first.1.refs_7_ = f32[9,16,1024]{2,1,0:T(8,128)S(1)} custom-call(f32[128,1024]{1,0:T(8,128)S(1)} %get-tuple-element.64.dh_ref, f32[128,1024]{1,0:T(8,128)S(1)} %get-tuple-element.65.sp1_ref, f32[9,128,1024]{2,1,0:T(8,128)S(1)} %get-tuple-element.66.m1_ref, bf16[2,3,256,128]{3,2,1,0:T(8,128)(2,1)S(1)} %get-tuple-element.54.mixt_ref, ...), custom_call_target="tpu_custom_call" | custom-call | tf_op jit(solution)/shard_map/back_first/pallas_call | solution.py:565
  24.2 1.8 %back_edges.1 = (f32[48,128]{1,0:T(8,128)S(1)}, f32[32,128]{1,0:T(8,128)S(1)}) custom-call(f32[16,512]{1,0:T(8,128)S(1)} %pack.1.refs_0_.block_ref, f32[16,512]{1,0:T(8,128)S(1)} %collective-permute-done.refs_1_, f32[3,1,512]{2,1,0:T(1,128)} %bitcast.11, f32[6,8,1024]{2,1,0:T(8,128)S(1)} %get-tuple-element.38.geo_ref.refs_3_, ...), custom_call_target="tpu_custom_call" | custom-call | tf_op jit(solution)/shard_map/back_edges/pallas_call | solution.py:565
  26.0 2.1 %collective-permute-start.1 = (f32[48,128]{1,0:T(8,128)S(1)}, f32[48,128]{1,0:T(8,128)S(1)}, u32[]{:S(2)}, u32[]{:S(2)}) collective-permute-start(f32[48,128]{1,0:T(8,128)S(1)} %get-tuple-element.71.refs_0_), channel_id=1, source_target_pairs={{0,8},{2,10},{4,12},{6,14},{8,16},{10,18},{12,20},{14,22},{16,24},... | collective-permute-start | bytes 73736 | tf_op jit(solution)/shard_map/ppermute | solution.py:811
  28.1 2.6 %collective-permute-start.2 = (f32[48,128]{1,0:T(8,128)S(1)}, f32[48,128]{1,0:T(8,128)S(1)}, u32[]{:S(2)}, u32[]{:S(2)}) collective-permute-start(f32[48,128]{1,0:T(8,128)S(1)} %get-tuple-element.71.refs_0_), channel_id=1, source_target_pairs={{0,16},{2,18},{4,20},{6,22},{8,24},{10,26},{12,28},{14,30},{16,0},... | collective-permute-start | bytes 73736 | tf_op jit(solution)/shard_map/ppermute | solution.py:811
  30.7 1.3 %collective-permute-start.3 = (f32[48,128]{1,0:T(8,128)S(1)}, f32[48,128]{1,0:T(8,128)S(1)}, u32[]{:S(2)}, u32[]{:S(2)}) collective-permute-start(f32[48,128]{1,0:T(8,128)S(1)} %get-tuple-element.71.refs_0_), channel_id=1, source_target_pairs={{0,24},{2,26},{4,28},{6,30},{8,0},{10,2},{12,4},{14,6},{16,8},{18,... | collective-permute-start | bytes 73736 | tf_op jit(solution)/shard_map/ppermute | solution.py:811
  32.0 0.0 collective-permute-done.1.refs_1_
  32.0 0.8 %collective-permute-done.2.refs_2_ = f32[48,128]{1,0:T(8,128)S(1)} collective-permute-done((f32[48,128]{1,0:T(8,128)S(1)}, f32[48,128]{1,0:T(8,128)S(1)}, u32[]{:S(2)}, u32[]{:S(2)}) %collective-permute-start.2) | collective-permute-done | bytes 24608 | tf_op jit(solution)/shard_map/ppermute | solution.py:811
  32.8 1.7 %collective-permute-done.3.refs_3_ = f32[48,128]{1,0:T(8,128)S(1)} collective-permute-done((f32[48,128]{1,0:T(8,128)S(1)}, f32[48,128]{1,0:T(8,128)S(1)}, u32[]{:S(2)}, u32[]{:S(2)}) %collective-permute-start.3) | collective-permute-done | bytes 24608 | tf_op jit(solution)/shard_map/ppermute | solution.py:811
  34.5 0.1 turn.1
  34.6 8.5 %all_to_all.5.arrived_ref = f32[8,32,128]{2,1,0:T(8,128)S(1)} all-to-all(f32[8,32,128]{2,1,0:T(8,128)S(1)} %turn.1), channel_id=1, replica_groups={{0,1,2,3,4,5,6,7},{8,9,10,11,12,13,14,15},{16,17,18,19,20,21,22,23},{24..., dimensions={0} | all-to-all | bytes 262144 | tf_op jit(solution)/shard_map/all_to_all | solution.py:823
  43.1 0.6 %sum.1 = (f32[3,1,512]{2,1,0:T(1,128)}, f32[3,1,512]{2,1,0:T(1,128)}) custom-call(f32[8,32,128]{2,1,0:T(8,128)S(1)} %all_to_all.5.arrived_ref), custom_call_target="tpu_custom_call" | custom-call | tf_op jit(solution)/shard_map/sum/pallas_call | solution.py:824
Async XLA Ops:
  1.4 4.9 %collective-permute-start = (f32[16,512]{1,0:T(8,128)S(1)}, f32[16,512]{1,0:T(8,128)S(1)}, u32[]{:S(2)}, u32[]{:S(2)}) collective-permute-start(f32[16,512]{1,0:T(8,128)S(1)} %pack.1.refs_0_.block_ref), channel_id=1, source_target_pairs={{0,1},{1,0},{2,3},{3,2},{4,5},{5,4},{6,7},{7,6},{8,9},{9,8},{10,11... | collective-permute-start | bytes 98312 | tf_op jit(solution)/shard_map/ppermute | solution.py:806
  26.0 6.1 %collective-permute-start.1 = (f32[48,128]{1,0:T(8,128)S(1)}, f32[48,128]{1,0:T(8,128)S(1)}, u32[]{:S(2)}, u32[]{:S(2)}) collective-permute-start(f32[48,128]{1,0:T(8,128)S(1)} %get-tuple-element.71.refs_0_), channel_id=1, source_target_pairs={{0,8},{2,10},{4,12},{6,14},{8,16},{10,18},{12,20},{14,22},{16,24},... | collective-permute-start | bytes 73736 | tf_op jit(solution)/shard_map/ppermute | solution.py:811
  28.1 4.7 %collective-permute-start.2 = (f32[48,128]{1,0:T(8,128)S(1)}, f32[48,128]{1,0:T(8,128)S(1)}, u32[]{:S(2)}, u32[]{:S(2)}) collective-permute-start(f32[48,128]{1,0:T(8,128)S(1)} %get-tuple-element.71.refs_0_), channel_id=1, source_target_pairs={{0,16},{2,18},{4,20},{6,22},{8,24},{10,26},{12,28},{14,30},{16,0},... | collective-permute-start | bytes 73736 | tf_op jit(solution)/shard_map/ppermute | solution.py:811
  30.7 3.8 %collective-permute-start.3 = (f32[48,128]{1,0:T(8,128)S(1)}, f32[48,128]{1,0:T(8,128)S(1)}, u32[]{:S(2)}, u32[]{:S(2)}) collective-permute-start(f32[48,128]{1,0:T(8,128)S(1)} %get-tuple-element.71.refs_0_), channel_id=1, source_target_pairs={{0,24},{2,26},{4,28},{6,30},{8,0},{10,2},{12,4},{14,6},{16,8},{18,... | collective-permute-start | bytes 73736 | tf_op jit(solution)/shard_map/ppermute | solution.py:811

commit v12 on v11

--- a/solution.py
+++ b/solution.py
@@ -86,9 +86,9 @@
 
 def choose_kernel(block_ref, *refs):
     sources = refs[:7]
-    oh_ref, rrc_ref, r2c_ref, side_ref, rrr_ref, r2r_ref, mixa_ref, mixt_ref = refs[7:15]
-    held = refs[15:22]
-    sems = refs[22]
+    oh_ref, rrc_ref, r2c_ref, side_ref, rrr_ref, mixa_ref, mixt_ref = refs[7:14]
+    held = refs[14:21]
+    sems = refs[21]
     emb_ref, rad1_ref, rad2_ref, mix1_ref, mix2_ref, read1_ref, read2_ref = held
     fetches = [pltpu.make_async_copy(src, dst, sems.at[i]) for i, (src, dst) in enumerate(zip(sources, held))]
     for fetch in fetches:
@@ -127,9 +127,6 @@
     side_ref[...] = jnp.concatenate([sides] + [zeros] * 15, axis=0).T
     rrr_ref[...] = jnp.concatenate(
         [jnp.concatenate([rr_hi, rr_hi], axis=1), jnp.concatenate([rr_lo, jnp.zeros_like(rr_lo)], axis=1)], axis=0
-    ).astype(bf16)
-    r2r_ref[...] = jnp.concatenate(
-        [jnp.concatenate([r2_hi, r2_hi], axis=1), jnp.concatenate([r2_lo, jnp.zeros_like(r2_lo)], axis=1)], axis=0
     ).astype(bf16)
     for i, ref in enumerate((mix1_ref, mix2_ref)):
         hi, lo = split(ref[...])
@@ -267,24 +264,28 @@
     in_turns(0, n_near // wide_cols, first)
 
 
-def gather_kernel(hid_ref, hs_ref, oh_ref, pick_ref, gidx_ref, bt_ref, r2c_ref, hj_ref, w_ref, car_ref, ext_ref):
+def gather_kernel(hid_ref, hs_ref, oh_ref, pick_ref, gidx_ref, bt_ref, geo_ref, r2c_ref,
+                  hj_ref, w_ref, slope_ref, car_ref, ext_ref):
     slots = bt_ref.shape[0]
     bases = bt_ref.shape[1] // 2
     chan, n_near = hid_ref.shape
     atoms = hj_ref.shape[1] // slots
     half = atoms // 2
-    by_lane = 2 * LANES if atoms > 2 * LANES else 0
-    by_product = 2 * atoms - by_lane
     ghosts = dot(hs_ref[...], pick_ref[...]).astype(bf16)
     ext_ref[:, 0:half] = ghosts[:, :half]
     ext_ref[:, half : half + atoms] = hs_ref[:, 0:atoms]
     ext_ref[:, half + atoms :] = ghosts[:, half:]
+    reach = 1.0 + lax.broadcasted_iota(jnp.int32, (bases, atoms), 0).astype(f32)
     for k in range(slots):
         here = slice(k * atoms, (k + 1) * atoms)
-        basis = split_rows(bt_ref[k, 0:bases, 0:atoms])
-        w_ref[:, here] = dot(r2c_ref[...], jnp.concatenate([basis, basis], axis=0).astype(bf16))
+        basis = bt_ref[k, 0:bases, 0:atoms]
+        for ref, value in ((w_ref, basis), (slope_ref, basis * (reach - row(geo_ref[4, k : k + 1, 0:atoms], bases)))):
+            both = split_rows(value)
+            ref[:, here] = dot(r2c_ref[...], jnp.concatenate([both, both], axis=0).astype(bf16))
 
     for pair in range(slots // 2):
+        by_lane = (2 + 2 * (pair % 2)) * LANES if atoms >= 4 * LANES else 0
+        by_product = 2 * atoms - by_lane
         first = pair * 2 * atoms
         here = slice(first, first + by_product)
         both = dot(ext_ref[...], oh_ref[:, here])
@@ -342,7 +343,7 @@
             for g in range(3):
                 inv_ref[pl.ds(pl.multiple_of(g * chan + base + 8 * h, 8), 8), cols] = inv[g]
 
-    in_turns(0, tiles * groups, moments, 4)
+    in_turns(0, tiles * groups, moments, 2)
     read2_col = side_ref[:, 3:4]
     for t in range(atoms // wide_cols):
         cols = slice(t * wide_cols, (t + 1) * wide_cols)
@@ -353,17 +354,18 @@
             dinv_ref[g * chan : (g + 1) * chan, cols] = scale * dot_parts(mixt_ref[1, g], hi, lo)
 
 
-def back_second_kernel(m2_ref, dinv_ref, car_ref, hj_ref, w_ref, ub_ref, dhe_ref, dw_ref, p_ref):
+def back_second_kernel(m2_ref, dinv_ref, car_ref, hj_ref, w_ref, slope_ref, ub_ref, dhe_ref, p_ref):
     slots = ub_ref.shape[1]
     chan, atoms = m2_ref.shape[1:]
     tiles = atoms // LANES
     pairs = chan // 16
     per_turn = 4 if pairs % 4 == 0 else 1
+    k_step = slots // 2
 
     def back_moments(t, carry):
         cols = pl.ds(pl.multiple_of(t * LANES, LANES), LANES)
 
-        def one(c, acc):
+        def one(c, acc, k0):
             forms = []
             for h in range(2):
                 rows = pl.ds(pl.multiple_of(c * 16 + 8 * h, 8), 8)
@@ -372,9 +374,10 @@
                 low = dm[6] * (1.0 / SQRT3)
                 forms.append((dm[0], dm[1], dm[2], dm[3], dm[8] - low, -dm[8] - low, low + low, dm[4], dm[5], dm[7]))
             base = pl.multiple_of(c * 16, 16)
-            for k in range(slots):
+            for k in range(k0, k0 + k_step):
                 at = pl.ds(pl.multiple_of(k * atoms + t * LANES, LANES), LANES)
                 got = car_ref[pl.ds(base, 16), at]
+                stretch = hj_ref[pl.ds(base, 16), at] * slope_ref[pl.ds(base, 16), at]
                 ux, uy, uz = [ub_ref[i, k, :, cols] for i in range(3)]
                 out = []
                 for h in range(2):
@@ -384,35 +387,35 @@
                     gz = dz + qxz * ux + qyz * uy + qzz * uz
                     out.append(mid + (gx + dx) * ux + (gy + dy) * uy + (gz + dz) * uz)
                     part = got[8 * h : 8 * h + 8]
+                    at_acc = 4 * (k - k0)
                     for i, g in enumerate((gx, gy, gz)):
-                        acc[3 * k + i] = acc[3 * k + i] + part * g
-                dcar = jnp.concatenate(out, axis=0)
-                for ref, other in ((dhe_ref, w_ref), (dw_ref, hj_ref)):
-                    hi, lo = split(dcar * other[pl.ds(base, 16), at])
-                    ref[pl.ds(base, 16), at] = hi
-                    ref[pl.ds(pl.multiple_of(chan + c * 16, 16), 16), at] = lo
-
-        def over(c, acc):
-            acc = list(acc)
-            for i in range(per_turn):
-                one(per_turn * c + i, acc)
-            return tuple(acc)
-
-        start = tuple(jnp.zeros((8, LANES), f32) for _ in range(3 * slots))
-        acc = lax.fori_loop(0, pairs // per_turn, over, start)
-        for k in range(slots):
-            for i in range(3):
-                p_ref[i, 8 * k : 8 * k + 8, cols] = acc[3 * k + i]
+                        acc[at_acc + i] = acc[at_acc + i] + part * g
+                    acc[at_acc + 3] = acc[at_acc + 3] + out[h] * stretch[8 * h : 8 * h + 8]
+                hi, lo = split(jnp.concatenate(out, axis=0) * w_ref[pl.ds(base, 16), at])
+                dhe_ref[pl.ds(base, 16), at] = hi
+                dhe_ref[pl.ds(pl.multiple_of(chan + c * 16, 16), 16), at] = lo
+
+        for k0 in range(0, slots, k_step):
+
+            def over(c, acc, k0=k0):
+                acc = list(acc)
+                for i in range(per_turn):
+                    one(per_turn * c + i, acc, k0)
+                return tuple(acc)
+
+            start = tuple(jnp.zeros((8, LANES), f32) for _ in range(4 * k_step))
+            acc = lax.fori_loop(0, pairs // per_turn, over, start)
+            for k in range(k_step):
+                for i in range(4):
+                    p_ref[i, 8 * (k0 + k) : 8 * (k0 + k) + 8, cols] = acc[4 * k + i]
         return carry
 
     lax.fori_loop(0, tiles, back_moments, 0)
 
 
-def scatter_kernel(oh_ref, pick_ref, dhe_ref, side_ref, dw_ref, p_ref, bt_ref, geo_ref, r2r_ref, gidx_ref,
-                   dh_ref, q_ref, ohlo_ref, ds_ref):
+def scatter_kernel(oh_ref, pick_ref, dhe_ref, side_ref, p_ref, gidx_ref, dh_ref, q_ref, ohlo_ref):
     chan, n_near = dh_ref.shape
-    slots = bt_ref.shape[0]
-    bases = bt_ref.shape[1] // 2
+    slots = gidx_ref.shape[0]
     atoms = pick_ref.shape[1]
     half = atoms // 2
     both = dot_nt(dhe_ref[...], jnp.concatenate([oh_ref[:half], oh_ref[half + atoms :]], axis=0))
@@ -429,19 +432,12 @@
     for k in range(slots):
         place = jnp.broadcast_to(gidx_ref[k : k + 1, :] & 127, (LANES, n_near)).astype(jnp.int16)
         ohlo_ref[:, k * n_near : (k + 1) * n_near] = jnp.where(place == ids16, one16, zero16)
-    for k in range(slots):
-        here = slice(k * atoms, (k + 1) * atoms)
-        small = dot(r2r_ref[...], dw_ref[:, here])
-        dbasis = small[:bases] + small[bases:]
-        basis = bt_ref[k, 0:bases, 0:atoms]
-        reach = 1.0 + lax.broadcasted_iota(jnp.int32, (bases, atoms), 0).astype(f32)
-        ds_ref[k * 8 : k * 8 + 8, :] = dbasis * basis * (reach - row(geo_ref[4, k : k + 1, 0:atoms], bases))
     lane = lax.broadcasted_iota(jnp.int32, (slots, 16 * slots), 1)
     sub = lax.broadcasted_iota(jnp.int32, (slots, 16 * slots), 0)
     adder = jnp.where(((lane >> 3) & (slots - 1)) == sub, 1.0, 0.0).astype(bf16)
     for i in range(4):
-        total = dot(adder, split_rows(p_ref[i - 1, :, :] if i else ds_ref[...]).astype(bf16))
-        q_ref[8 * i : 8 * i + 8, :] = 2.0 * total if i else total
+        total = dot(adder, split_rows(p_ref[i]).astype(bf16))
+        q_ref[8 * i : 8 * i + 8, :] = 2.0 * total if i < 3 else total
 
 
 def back_first_kernel(dh_ref, sp1_ref, m1_ref, mixt_ref, rrr_ref, da_ref):
@@ -491,12 +487,12 @@
             db = db * basis * ((1.0 + n) - soft)
             ds = db if ds is None else ds + db
         if mine:
-            ds = ds + q_ref[0:8, here]
+            ds = ds + q_ref[24:32, here]
         dux = SQRT3 * dy[1] + SQRT15 * (uy * dy[4] + uz * dy[7] + ux * dy[8]) - SQRT5 * ux * dy[6]
         duy = SQRT3 * dy[2] + SQRT15 * (ux * dy[4] + uz * dy[5] - uy * dy[8]) - SQRT5 * uy * dy[6]
         duz = SQRT3 * dy[3] + SQRT15 * (uy * dy[5] + ux * dy[7]) + 2.0 * SQRT5 * uz * dy[6]
         if mine:
-            dux, duy, duz = [d + q_ref[8 * i : 8 * i + 8, here] for i, d in ((1, dux), (2, duy), (3, duz))]
+            dux, duy, duz = [d + q_ref[8 * i : 8 * i + 8, here] for i, d in enumerate((dux, duy, duz))]
         along = ds - (ux * dux + uy * duy + uz * duz) * back
         for i, value in enumerate((dux * back + along * ux, duy * back + along * uy, duz * back + along * uz)):
             dr_ref[i, :, here] = value
@@ -590,7 +586,6 @@
             ((chan, 4 * bases), bf16),
             ((chan, LANES), f32),
             ((4 * bases, 2 * chan), bf16),
-            ((2 * bases, 2 * chan), bf16),
             ((2, 2 * chan, 3 * chan), bf16),
             ((2, 3, 2 * chan, chan), bf16),
         ),
@@ -602,9 +597,9 @@
 
 def pushes(plan, blocks, momenta, chosen):
     atoms, near, wide, _, _ = plan
-    oh, rrc, r2c, sides, rrr, r2r, mixa, mixt = chosen
+    oh, rrc, r2c, sides, rrr, mixa, mixt = chosen
     chan = rrc.shape[0]
-    bases = r2r.shape[0] // 2
+    bases = rrr.shape[0] // 4
     slots = blocks[0].shape[0] - HEAD
     n_near = len(near) * atoms
     edges = slots * atoms
@@ -633,11 +628,11 @@
         (((ORDERS, chan, n_near), f32), ((chan, n_near), f32), ((chan, n_near), f32), ((2 * chan, n_near), bf16)),
         [pltpu.VMEM((8, n_near), f32)],
     )
-    hj, w, car = run(
+    hj, w, slope, car = run(
         "gather",
         gather_kernel,
-        (hid, hs, oh, pick, gidx, bt, r2c),
-        (((chan, edges), f32),) * 3,
+        (hid, hs, oh, pick, gidx, bt, geo, r2c),
+        (((chan, edges), f32),) * 4,
         [pltpu.VMEM((2 * chan, 2 * atoms), bf16)],
     )
     m2, dinv = run(
@@ -647,18 +642,17 @@
         (((ORDERS, chan, atoms), f32), ((3 * chan, atoms), f32)),
         [pltpu.VMEM((3 * chan, atoms), f32)],
     )
-    dhe, dw, p = run(
+    dhe, p = run(
         "back_second",
         back_second_kernel,
-        (m2, dinv, car, hj, w, ub),
-        (((2 * chan, edges), bf16), ((2 * chan, edges), bf16), ((3, 8 * slots, atoms), f32)),
+        (m2, dinv, car, hj, w, slope, ub),
+        (((2 * chan, edges), bf16), ((4, 8 * slots, atoms), f32)),
     )
     dh, q, ohlo = run(
         "scatter",
         scatter_kernel,
-        (oh, pick, dhe, sides, dw, p, bt, geo, r2r, gidx),
+        (oh, pick, dhe, sides, p, gidx),
         (((chan, n_near), f32), ((4 * slots, atoms), f32), ((LANES, slots * n_near), bf16)),
-        [pltpu.VMEM((8 * slots, atoms), f32)],
     )
     (da,) = run("back_first", back_first_kernel, (dh, sp1, m1, mixt, rrr), (((ORDERS, 2 * bases, n_near), f32),))
     return run(

time: 44 us -> 43.6 us (level)
  no operation moved by 1% of the time
where the time goes in v12:
time: 43.6 us; the launch traced here: 43.3 us
  Pallas kernels  22.1 us (51%)
  starting transfers between devices  9.11 us (21%)
  blocking collectives  8.47 us (19%)
  waiting for transfers between devices  2.9 us (7%)
  between operations  0.7 us (2%)
    pallas_call x9, Pallas kernels, run(): pl.pallas_call(body, out_shape=tuple((jax.ShapeDtypeStruct(shape, dtype)...  20.6 us
    all_to_all x1, blocking collectives, shards(): lax.all_to_all(messages, ('bead', 'space'), 0, 0, axis_index_groups=rows,...  8.47 us
    ppermute x3, starting transfers between devices, shards(): lax.ppermute(pushed, 'bead', [(b, (b + z * inner) % beads) for b in range...  6.07 us
    ppermute x1, starting transfers between devices, shards(): lax.ppermute(block, 'space', [(i, (i - offset) % domains) for i in range(...  3.03 us
    ppermute x3, waiting for transfers between devices, shards(): lax.ppermute(pushed, 'bead', [(b, (b + z * inner) % beads) for b in range...  2.47 us
  transfers between devices with their start and end apart: 4, of which 3 were waited for; matrix products, arithmetic and copies ran while one was open for 0% of the time, Pallas kernels for 3%

profile of v12, /device:TPU:0, one launch (start us, length us, event | category | flops | bytes accessed | tf_op | source)
XLA Modules:
  0.0 43.3 jit_solution(13702846966470304755)
XLA Ops:
  0.6 0.8 %pack.1.refs_0_.block_ref = f32[16,512]{1,0:T(8,128)S(1)} custom-call(f32[3,1,512]{2,1,0:T(1,128)} %bitcast.10, s32[1,512]{1,0:T(1,128)} %bitcast.12, s32[1,512]{1,0:T(1,128)} %bitcast.13, s32[8,512]{1,0:T(8,128)} %slot_src.1), custom_call_target="tpu_custom_call" | custom-call | tf_op jit(solution)/shard_map/pack/pallas_call | solution.py:783
  1.4 3.0 %collective-permute-start = (f32[16,512]{1,0:T(8,128)S(1)}, f32[16,512]{1,0:T(8,128)S(1)}, u32[]{:S(2)}, u32[]{:S(2)}) collective-permute-start(f32[16,512]{1,0:T(8,128)S(1)} %pack.1.refs_0_.block_ref), channel_id=1, source_target_pairs={{0,1},{1,0},{2,3},{3,2},{4,5},{5,4},{6,7},{7,6},{8,9},{9,8},{10,11... | collective-permute-start | bytes 98312 | tf_op jit(solution)/shard_map/ppermute | solution.py:800
  4.5 1.5 %choose.1 = (bf16[1024,4096]{1,0:T(8,128)(2,1)S(1)}, bf16[128,64]{1,0:T(8,128)(2,1)S(1)}, bf16[128,32]{1,0:T(8,128)(2,1)S(1)}, f32[128,128]{1,0:T(8,128)S(1)}, b...) custom-call(f32[16,512]{1,0:T(8,128)S(1)} %pack.1.refs_0_.block_ref, ...), custom_call_target="tpu_custom_call" | custom-call | flops 2000000000 | bytes 2000000 | tf_op jit(solution)/shard_map/choose/pallas_call | solution.py:561
  5.9 0.4 collective-permute-done.refs_1_
  6.4 1.7 %edges.1 = (f32[6,8,1024]{2,1,0:T(8,128)S(1)}, f32[8,8,1024]{2,1,0:T(8,128)S(1)}, f32[8,8,8,512]{3,2,1,0:T(8,128)S(1)}, f32[3,8,8,512]{3,2,1,0:T(8,128)S(1)}, f3...) custom-call(f32[16,512]{1,0:T(8,128)S(1)} %pack.1.refs_0_.block_ref,, ...), custom_call_target="tpu_custom_call" | custom-call | tf_op jit(solution)/shard_map/edges/pallas_call | solution.py:561
  8.1 1.7 %first.1 = (f32[9,128,1024]{2,1,0:T(8,128)S(1)}, f32[128,1024]{1,0:T(8,128)S(1)}, f32[128,1024]{1,0:T(8,128)S(1)}, bf16[256,1024]{1,0:T(8,128)(2,1)S(1)}) custom-call(f32[16,512]{1,0:T(8,128)S(1)} %pack.1.refs_0_.block_ref, f32[16,512]{1,0:T(8,128)S(1)} %collective-permute-done.refs_1_, bf16[9,64,1024]{2,1,0:T(8,128)(2,1)S(1)} %get-tuple-element.43.refs_2_, ...), custom_call_target="tpu_custom_call" | custom-call | tf_op jit(solution)/shard_map/first/pallas_call | solution.py:561
  9.8 2.4 %gather.1 = (f32[128,4096]{1,0:T(8,128)S(1)}, f32[128,4096]{1,0:T(8,128)S(1)}, f32[128,4096]{1,0:T(8,128)S(1)}, f32[128,4096]{1,0:T(8,128)S(1)}) custom-call(f32[128,1024]{1,0:T(8,128)S(1)} %get-tuple-element.47.hid_ref, bf16[256,1024]{1,0:T(8,128)(2,1)S(1)} %get-tuple-element.48.hs_ref, bf16[1024,4096]{1,0:T(8,128)(2,1)S(1)} %get-tuple-element.41.oh_ref, ...), custom_call_target="tpu_custom_call" | custom-call | tf_op jit(solution)/shard_map/gather/pallas_call | solution.py:561
  12.2 2.7 %moments.1 = (f32[9,128,512]{2,1,0:T(8,128)S(1)}, f32[384,512]{1,0:T(8,128)S(1)}) custom-call(f32[128,4096]{1,0:T(8,128)S(1)} %get-tuple-element.51.car_ref, f32[8,8,8,512]{3,2,1,0:T(8,128)S(1)} %get-tuple-element.52.yb_ref, bf16[2,256,384]{2,1,0:T(8,128)(2,1)S(1)} %get-tuple-element.46.refs_5_.mixa_ref, ...), custom_call_target="tpu_custom_call" | custom-call | tf_op jit(solution)/shard_map/moments/pallas_call | solution.py:561
  14.9 3.9 %back_second.1 = (bf16[256,4096]{1,0:T(8,128)(2,1)S(1)}, f32[4,64,512]{2,1,0:T(8,128)S(1)}) custom-call(f32[9,128,512]{2,1,0:T(8,128)S(1)} %get-tuple-element.54.m2_ref, f32[384,512]{1,0:T(8,128)S(1)} %get-tuple-element.55.dinv_ref, f32[128,4096]{1,0:T(8,128)S(1)} %get-tuple-element.51.car_ref, f32[128,4096]{1,0:T(8,128)S(1)} %get-tuple-element.56.hj_ref, ...), custom_call_target="tpu_custom_call" | custom-call | tf_op jit(solution)/shard_map/back_second/pallas_call | solution.py:561
  18.8 3.0 %scatter.1 = (f32[128,1024]{1,0:T(8,128)S(1)}, f32[32,512]{1,0:T(8,128)S(1)}, bf16[128,8192]{1,0:T(8,128)(2,1)S(1)}) custom-call(bf16[1024,4096]{1,0:T(8,128)(2,1)S(1)} %get-tuple-element.41.oh_ref, bf16[1024,512]{1,0:T(8,128)(2,1)S(1)} %get-tuple-element.42.pick_ref, bf16[256,4096]{1,0:T(8,128)(2,1)S(1)} %get-tuple-element.60.dhe_ref, ...), custom_call_target="tpu_custom_call" | custom-call | tf_op jit(solution)/shard_map/scatter/pallas_call | solution.py:561
  21.8 2.0 %back_first.1.refs_7_ = f32[9,16,1024]{2,1,0:T(8,128)S(1)} custom-call(f32[128,1024]{1,0:T(8,128)S(1)} %get-tuple-element.62.dh_ref, f32[128,1024]{1,0:T(8,128)S(1)} %get-tuple-element.63.sp1_ref, f32[9,128,1024]{2,1,0:T(8,128)S(1)} %get-tuple-element.64.m1_ref, bf16[2,3,256,128]{3,2,1,0:T(8,128)(2,1)S(1)} %get-tuple-element.53.mixt_ref, ...), custom_call_target="tpu_custom_call" | custom-call | tf_op jit(solution)/shard_map/back_first/pallas_call | solution.py:561
  23.8 1.8 %back_edges.1 = (f32[48,128]{1,0:T(8,128)S(1)}, f32[32,128]{1,0:T(8,128)S(1)}) custom-call(f32[16,512]{1,0:T(8,128)S(1)} %pack.1.refs_0_.block_ref, f32[16,512]{1,0:T(8,128)S(1)} %collective-permute-done.refs_1_, f32[3,1,512]{2,1,0:T(1,128)} %bitcast.11, f32[6,8,1024]{2,1,0:T(8,128)S(1)} %get-tuple-element.37.geo_ref.refs_3_, ...), custom_call_target="tpu_custom_call" | custom-call | tf_op jit(solution)/shard_map/back_edges/pallas_call | solution.py:561
  25.6 2.1 %collective-permute-start.1 = (f32[48,128]{1,0:T(8,128)S(1)}, f32[48,128]{1,0:T(8,128)S(1)}, u32[]{:S(2)}, u32[]{:S(2)}) collective-permute-start(f32[48,128]{1,0:T(8,128)S(1)} %get-tuple-element.69.refs_0_), channel_id=1, source_target_pairs={{0,8},{2,10},{4,12},{6,14},{8,16},{10,18},{12,20},{14,22},{16,24},... | collective-permute-start | bytes 73736 | tf_op jit(solution)/shard_map/ppermute | solution.py:805
  27.7 2.6 %collective-permute-start.2 = (f32[48,128]{1,0:T(8,128)S(1)}, f32[48,128]{1,0:T(8,128)S(1)}, u32[]{:S(2)}, u32[]{:S(2)}) collective-permute-start(f32[48,128]{1,0:T(8,128)S(1)} %get-tuple-element.69.refs_0_), channel_id=1, source_target_pairs={{0,16},{2,18},{4,20},{6,22},{8,24},{10,26},{12,28},{14,30},{16,0},... | collective-permute-start | bytes 73736 | tf_op jit(solution)/shard_map/ppermute | solution.py:805
  30.3 1.4 %collective-permute-start.3 = (f32[48,128]{1,0:T(8,128)S(1)}, f32[48,128]{1,0:T(8,128)S(1)}, u32[]{:S(2)}, u32[]{:S(2)}) collective-permute-start(f32[48,128]{1,0:T(8,128)S(1)} %get-tuple-element.69.refs_0_), channel_id=1, source_target_pairs={{0,24},{2,26},{4,28},{6,30},{8,0},{10,2},{12,4},{14,6},{16,8},{18,... | collective-permute-start | bytes 73736 | tf_op jit(solution)/shard_map/ppermute | solution.py:805
  31.6 0.0 collective-permute-done.1.refs_1_
  31.6 0.8 %collective-permute-done.2.refs_2_ = f32[48,128]{1,0:T(8,128)S(1)} collective-permute-done((f32[48,128]{1,0:T(8,128)S(1)}, f32[48,128]{1,0:T(8,128)S(1)}, u32[]{:S(2)}, u32[]{:S(2)}) %collective-permute-start.2) | collective-permute-done | bytes 24608 | tf_op jit(solution)/shard_map/ppermute | solution.py:805
  32.4 1.7 %collective-permute-done.3.refs_3_ = f32[48,128]{1,0:T(8,128)S(1)} collective-permute-done((f32[48,128]{1,0:T(8,128)S(1)}, f32[48,128]{1,0:T(8,128)S(1)}, u32[]{:S(2)}, u32[]{:S(2)}) %collective-permute-start.3) | collective-permute-done | bytes 24608 | tf_op jit(solution)/shard_map/ppermute | solution.py:805
  34.1 0.1 turn.1
  34.2 8.5 %all_to_all.5.arrived_ref = f32[8,32,128]{2,1,0:T(8,128)S(1)} all-to-all(f32[8,32,128]{2,1,0:T(8,128)S(1)} %turn.1), channel_id=1, replica_groups={{0,1,2,3,4,5,6,7},{8,9,10,11,12,13,14,15},{16,17,18,19,20,21,22,23},{24..., dimensions={0} | all-to-all | bytes 262144 | tf_op jit(solution)/shard_map/all_to_all | solution.py:817
  42.7 0.6 %sum.1 = (f32[3,1,512]{2,1,0:T(1,128)}, f32[3,1,512]{2,1,0:T(1,128)}) custom-call(f32[8,32,128]{2,1,0:T(8,128)S(1)} %all_to_all.5.arrived_ref), custom_call_target="tpu_custom_call" | custom-call | tf_op jit(solution)/shard_map/sum/pallas_call | solution.py:818
Async XLA Ops:
  1.4 4.9 %collective-permute-start = (f32[16,512]{1,0:T(8,128)S(1)}, f32[16,512]{1,0:T(8,128)S(1)}, u32[]{:S(2)}, u32[]{:S(2)}) collective-permute-start(f32[16,512]{1,0:T(8,128)S(1)} %pack.1.refs_0_.block_ref), channel_id=1, source_target_pairs={{0,1},{1,0},{2,3},{3,2},{4,5},{5,4},{6,7},{7,6},{8,9},{9,8},{10,11... | collective-permute-start | bytes 98312 | tf_op jit(solution)/shard_map/ppermute | solution.py:800
  25.6 6.1 %collective-permute-start.1 = (f32[48,128]{1,0:T(8,128)S(1)}, f32[48,128]{1,0:T(8,128)S(1)}, u32[]{:S(2)}, u32[]{:S(2)}) collective-permute-start(f32[48,128]{1,0:T(8,128)S(1)} %get-tuple-element.69.refs_0_), channel_id=1, source_target_pairs={{0,8},{2,10},{4,12},{6,14},{8,16},{10,18},{12,20},{14,22},{16,24},... | collective-permute-start | bytes 73736 | tf_op jit(solution)/shard_map/ppermute | solution.py:805
  27.7 4.7 %collective-permute-start.2 = (f32[48,128]{1,0:T(8,128)S(1)}, f32[48,128]{1,0:T(8,128)S(1)}, u32[]{:S(2)}, u32[]{:S(2)}) collective-permute-start(f32[48,128]{1,0:T(8,128)S(1)} %get-tuple-element.69.refs_0_), channel_id=1, source_target_pairs={{0,16},{2,18},{4,20},{6,22},{8,24},{10,26},{12,28},{14,30},{16,0},... | collective-permute-start | bytes 73736 | tf_op jit(solution)/shard_map/ppermute | solution.py:805
  30.3 3.8 %collective-permute-start.3 = (f32[48,128]{1,0:T(8,128)S(1)}, f32[48,128]{1,0:T(8,128)S(1)}, u32[]{:S(2)}, u32[]{:S(2)}) collective-permute-start(f32[48,128]{1,0:T(8,128)S(1)} %get-tuple-element.69.refs_0_), channel_id=1, source_target_pairs={{0,24},{2,26},{4,28},{6,30},{8,0},{10,2},{12,4},{14,6},{16,8},{18,... | collective-permute-start | bytes 73736 | tf_op jit(solution)/shard_map/ppermute | solution.py:805

commit v13 on v12

--- a/solution.py
+++ b/solution.py
@@ -98,15 +98,17 @@
     atoms = block_ref.shape[1]
     slots = block_ref.shape[0] - HEAD
 
-    ids16 = lax.broadcasted_iota(jnp.int32, (LANES, atoms), 0).astype(jnp.int16)
-    one16 = jnp.ones((LANES, atoms), bf16)
-    zero16 = jnp.zeros((LANES, atoms), bf16)
-    for k in range(slots):
-        slot = block_ref[HEAD + k : HEAD + k + 1, :].astype(jnp.int32)
-        wanted = jnp.broadcast_to(slot, (LANES, atoms)).astype(jnp.int16)
+    tile_edges = slots * LANES
+    ids16 = lax.broadcasted_iota(jnp.int32, (LANES, tile_edges), 0).astype(jnp.int16)
+    one16 = jnp.ones((LANES, tile_edges), bf16)
+    zero16 = jnp.zeros((LANES, tile_edges), bf16)
+    for t in range(atoms // LANES):
+        slot = block_ref[HEAD : HEAD + slots, t * LANES : (t + 1) * LANES].astype(jnp.int32)
+        line = jnp.concatenate([slot[k : k + 1, :] for k in range(slots)], axis=1)
+        wanted = jnp.broadcast_to(line, (LANES, tile_edges)).astype(jnp.int16)
         for r in range(oh_ref.shape[0] // LANES):
             hit = wanted - jnp.int16(r * LANES) == ids16
-            oh_ref[r * LANES : (r + 1) * LANES, k * atoms : (k + 1) * atoms] = jnp.where(hit, one16, zero16)
+            oh_ref[r * LANES : (r + 1) * LANES, t * tile_edges : (t + 1) * tile_edges] = jnp.where(hit, one16, zero16)
 
     for fetch in fetches:
         fetch.wait()
@@ -264,69 +266,59 @@
     in_turns(0, n_near // wide_cols, first)
 
 
-def gather_kernel(hid_ref, hs_ref, oh_ref, pick_ref, gidx_ref, bt_ref, geo_ref, r2c_ref,
-                  hj_ref, w_ref, slope_ref, car_ref, ext_ref):
+def second_kernel(hid_ref, hs_ref, oh_ref, pick_ref, gidx_ref, bt_ref, geo_ref, r2c_ref, yb_ref, mixa_ref, mixt_ref,
+                  side_ref, hj_ref, w_ref, slope_ref, car_ref, m2_ref, dinv_ref, ext_ref, inv_ref):
     slots = bt_ref.shape[0]
     bases = bt_ref.shape[1] // 2
     chan, n_near = hid_ref.shape
     atoms = hj_ref.shape[1] // slots
     half = atoms // 2
+    tile_edges = slots * LANES
+    wide_cols = 2 * LANES
+    rows = 32
+    reach = 1.0 + lax.broadcasted_iota(jnp.int32, (bases, LANES), 0).astype(f32)
     ghosts = dot(hs_ref[...], pick_ref[...]).astype(bf16)
     ext_ref[:, 0:half] = ghosts[:, :half]
     ext_ref[:, half : half + atoms] = hs_ref[:, 0:atoms]
     ext_ref[:, half + atoms :] = ghosts[:, half:]
-    reach = 1.0 + lax.broadcasted_iota(jnp.int32, (bases, atoms), 0).astype(f32)
-    for k in range(slots):
-        here = slice(k * atoms, (k + 1) * atoms)
-        basis = bt_ref[k, 0:bases, 0:atoms]
-        for ref, value in ((w_ref, basis), (slope_ref, basis * (reach - row(geo_ref[4, k : k + 1, 0:atoms], bases)))):
-            both = split_rows(value)
+
+    def weights(t):
+        cols = slice(t * LANES, (t + 1) * LANES)
+        here = slice(t * tile_edges, (t + 1) * tile_edges)
+        basis = [bt_ref[k, 0:bases, cols] for k in range(slots)]
+        slopes = [basis[k] * (reach - row(geo_ref[4, k : k + 1, cols], bases)) for k in range(slots)]
+        for ref, values in ((w_ref, basis), (slope_ref, slopes)):
+            both = split_rows(jnp.concatenate(values, axis=1))
             ref[:, here] = dot(r2c_ref[...], jnp.concatenate([both, both], axis=0).astype(bf16))
 
-    for pair in range(slots // 2):
-        by_lane = (2 + 2 * (pair % 2)) * LANES if atoms >= 4 * LANES else 0
-        by_product = 2 * atoms - by_lane
-        first = pair * 2 * atoms
-        here = slice(first, first + by_product)
+    def gather(t):
+        by_lane = 2 + 2 * (t % 2)
+        here = slice(t * tile_edges, t * tile_edges + (slots - by_lane) * LANES)
         both = dot(ext_ref[...], oh_ref[:, here])
-        wanted = gidx_ref[2 * pair + 1 : 2 * pair + 2, 0:atoms]
-        for t in range(by_lane // LANES):
-            at = slice(first + by_product + t * LANES, first + by_product + (t + 1) * LANES)
-            start = atoms - by_lane + t * LANES
-            mine = row(wanted[:, start : start + LANES])
+        for k in range(slots - by_lane, slots):
+            at = slice(t * tile_edges + k * LANES, t * tile_edges + (k + 1) * LANES)
+            mine = row(gidx_ref[k : k + 1, t * LANES : (t + 1) * LANES])
             chunk_no = mine >> 7
             place = mine & 127
             for c in range(chan // 8):
-                rows = slice(8 * c, 8 * c + 8)
+                lines = slice(8 * c, 8 * c + 8)
                 feat = None
                 for chunk in range(n_near // LANES):
-                    held = hid_ref[rows, chunk * LANES : (chunk + 1) * LANES]
+                    held = hid_ref[lines, chunk * LANES : (chunk + 1) * LANES]
                     got = jnp.take_along_axis(held, place, axis=1, mode="promise_in_bounds")
                     feat = got if feat is None else jnp.where(chunk_no == chunk, got, feat)
-                hj_ref[rows, at] = feat
-                car_ref[rows, at] = feat * w_ref[rows, at]
+                hj_ref[lines, at] = feat
+                car_ref[lines, at] = feat * w_ref[lines, at]
         feat = both[:chan] + both[chan:]
         hj_ref[:, here] = feat
         car_ref[:, here] = feat * w_ref[:, here]
 
-
-def moment_kernel(car_ref, yb_ref, mixa_ref, mixt_ref, side_ref, m2_ref, dinv_ref, inv_ref):
-    slots = yb_ref.shape[1]
-    chan, atoms = m2_ref.shape[1:]
-    tiles = atoms // LANES
-    wide_cols = 2 * LANES
-    rows = 32
-    groups = chan // rows
-
-    def moments(step):
-        t = step // groups
-        c = step % groups
-        cols = pl.ds(pl.multiple_of(t * LANES, LANES), LANES)
-        base = pl.multiple_of(c * rows, rows)
+    def moments(t, base):
+        cols = slice(t * LANES, (t + 1) * LANES)
         acc = [[None] * ORDERS for _ in range(rows // 8)]
         for k in range(slots):
-            at = pl.ds(pl.multiple_of(k * atoms + t * LANES, LANES), LANES)
-            got = car_ref[pl.ds(base, rows), at]
+            at = slice(t * tile_edges + k * LANES, t * tile_edges + (k + 1) * LANES)
+            got = car_ref[base : base + rows, at]
             for l in range(ORDERS):
                 yb = yb_ref[l - 1, k, :, cols] if l else None
                 for h in range(rows // 8):
@@ -336,22 +328,26 @@
         for h in range(rows // 8):
             inv = [None] * 3
             for l in range(ORDERS):
-                m2_ref[l, pl.ds(pl.multiple_of(base + 8 * h, 8), 8), cols] = acc[h][l]
+                m2_ref[l, base + 8 * h : base + 8 * h + 8, cols] = acc[h][l]
                 sq = acc[h][l] * acc[h][l]
                 g = GROUP[l]
                 inv[g] = sq if inv[g] is None else inv[g] + sq
             for g in range(3):
-                inv_ref[pl.ds(pl.multiple_of(g * chan + base + 8 * h, 8), 8), cols] = inv[g]
-
-    in_turns(0, tiles * groups, moments, 2)
+                inv_ref[g * chan + base + 8 * h : g * chan + base + 8 * h + 8, cols] = inv[g]
+
     read2_col = side_ref[:, 3:4]
-    for t in range(atoms // wide_cols):
-        cols = slice(t * wide_cols, (t + 1) * wide_cols)
-        hi, lo = split(inv_ref[:, cols])
-        _, slope = silu_parts(dot_parts(mixa_ref[1], hi, lo))
-        hi, lo = split(slope * (2.0 * read2_col))
-        for g, scale in enumerate((1.0, 0.5 * SQRT3, 0.5 * SQRT15)):
-            dinv_ref[g * chan : (g + 1) * chan, cols] = scale * dot_parts(mixt_ref[1, g], hi, lo)
+    for t in range(atoms // LANES):
+        weights(t)
+        gather(t)
+        for base in range(0, chan, rows):
+            moments(t, base)
+        if t % 2:
+            cols = slice((t - 1) * LANES, (t + 1) * LANES)
+            hi, lo = split(inv_ref[:, cols])
+            _, slope = silu_parts(dot_parts(mixa_ref[1], hi, lo))
+            hi, lo = split(slope * (2.0 * read2_col))
+            for g, scale in enumerate((1.0, 0.5 * SQRT3, 0.5 * SQRT15)):
+                dinv_ref[g * chan : (g + 1) * chan, cols] = scale * dot_parts(mixt_ref[1, g], hi, lo)
 
 
 def back_second_kernel(m2_ref, dinv_ref, car_ref, hj_ref, w_ref, slope_ref, ub_ref, dhe_ref, p_ref):
@@ -375,7 +371,7 @@
                 forms.append((dm[0], dm[1], dm[2], dm[3], dm[8] - low, -dm[8] - low, low + low, dm[4], dm[5], dm[7]))
             base = pl.multiple_of(c * 16, 16)
             for k in range(k0, k0 + k_step):
-                at = pl.ds(pl.multiple_of(k * atoms + t * LANES, LANES), LANES)
+                at = pl.ds(pl.multiple_of((t * slots + k) * LANES, LANES), LANES)
                 got = car_ref[pl.ds(base, 16), at]
                 stretch = hj_ref[pl.ds(base, 16), at] * slope_ref[pl.ds(base, 16), at]
                 ux, uy, uz = [ub_ref[i, k, :, cols] for i in range(3)]
@@ -628,19 +624,12 @@
         (((ORDERS, chan, n_near), f32), ((chan, n_near), f32), ((chan, n_near), f32), ((2 * chan, n_near), bf16)),
         [pltpu.VMEM((8, n_near), f32)],
     )
-    hj, w, slope, car = run(
-        "gather",
-        gather_kernel,
-        (hid, hs, oh, pick, gidx, bt, geo, r2c),
-        (((chan, edges), f32),) * 4,
-        [pltpu.VMEM((2 * chan, 2 * atoms), bf16)],
-    )
-    m2, dinv = run(
-        "moments",
-        moment_kernel,
-        (car, yb, mixa, mixt, sides),
-        (((ORDERS, chan, atoms), f32), ((3 * chan, atoms), f32)),
-        [pltpu.VMEM((3 * chan, atoms), f32)],
+    hj, w, slope, car, m2, dinv = run(
+        "second",
+        second_kernel,
+        (hid, hs, oh, pick, gidx, bt, geo, r2c, yb, mixa, mixt, sides),
+        (((chan, edges), f32),) * 4 + (((ORDERS, chan, atoms), f32), ((3 * chan, atoms), f32)),
+        [pltpu.VMEM((2 * chan, 2 * atoms), bf16), pltpu.VMEM((3 * chan, atoms), f32)],
     )
     dhe, p = run(
         "back_second",

time: 43.6 us -> 43.6 us (level)
    pallas_call x9 -> x8, Pallas kernels: 20.6 us -> 20.6 us  [run(): pl.pallas_call(body, out_shape=tuple((jax.ShapeDtypeStruct(shape, dtype)...]
where the time goes in v13:
time: 43.6 us; the launch traced here: 43.3 us
  Pallas kernels  22.1 us (51%)
  starting transfers between devices  9.1 us (21%)
  blocking collectives  8.46 us (19%)
  waiting for transfers between devices  2.91 us (7%)
  between operations  0.69 us (2%)
    pallas_call x8, Pallas kernels, run(): pl.pallas_call(body, out_shape=tuple((jax.ShapeDtypeStruct(shape, dtype)...  20.6 us
    all_to_all x1, blocking collectives, shards(): lax.all_to_all(messages, ('bead', 'space'), 0, 0, axis_index_groups=rows,...  8.46 us
    ppermute x3, starting transfers between devices, shards(): lax.ppermute(pushed, 'bead', [(b, (b + z * inner) % beads) for b in range...  6.07 us
    ppermute x1, starting transfers between devices, shards(): lax.ppermute(block, 'space', [(i, (i - offset) % domains) for i in range(...  3.03 us
    ppermute x3, waiting for transfers between devices, shards(): lax.ppermute(pushed, 'bead', [(b, (b + z * inner) % beads) for b in range...  2.48 us
  transfers between devices with their start and end apart: 4, of which 3 were waited for; matrix products, arithmetic and copies ran while one was open for 0% of the time, Pallas kernels for 3%

profile of v13, /device:TPU:0, one launch (start us, length us, event | category | flops | bytes accessed | tf_op | source)
XLA Modules:
  0.0 43.3 jit_solution(15407055437828506517)
XLA Ops:
  0.6 0.8 %pack.1.refs_0_.block_ref = f32[16,512]{1,0:T(8,128)S(1)} custom-call(f32[3,1,512]{2,1,0:T(1,128)} %bitcast.10, s32[1,512]{1,0:T(1,128)} %bitcast.12, s32[1,512]{1,0:T(1,128)} %bitcast.13, s32[8,512]{1,0:T(8,128)} %slot_src.1), custom_call_target="tpu_custom_call" | custom-call | tf_op jit(solution)/shard_map/pack/pallas_call | solution.py:772
  1.4 3.0 %collective-permute-start = (f32[16,512]{1,0:T(8,128)S(1)}, f32[16,512]{1,0:T(8,128)S(1)}, u32[]{:S(2)}, u32[]{:S(2)}) collective-permute-start(f32[16,512]{1,0:T(8,128)S(1)} %pack.1.refs_0_.block_ref), channel_id=1, source_target_pairs={{0,1},{1,0},{2,3},{3,2},{4,5},{5,4},{6,7},{7,6},{8,9},{9,8},{10,11... | collective-permute-start | bytes 98312 | tf_op jit(solution)/shard_map/ppermute | solution.py:789
  4.5 1.5 %choose.1 = (bf16[1024,4096]{1,0:T(8,128)(2,1)S(1)}, bf16[128,64]{1,0:T(8,128)(2,1)S(1)}, bf16[128,32]{1,0:T(8,128)(2,1)S(1)}, f32[128,128]{1,0:T(8,128)S(1)}, b...) custom-call(f32[16,512]{1,0:T(8,128)S(1)} %pack.1.refs_0_.block_ref, ...), custom_call_target="tpu_custom_call" | custom-call | flops 2000000000 | bytes 2000000 | tf_op jit(solution)/shard_map/choose/pallas_call | solution.py:557
  5.9 0.4 collective-permute-done.refs_1_
  6.4 1.7 %edges.1 = (f32[6,8,1024]{2,1,0:T(8,128)S(1)}, f32[8,8,1024]{2,1,0:T(8,128)S(1)}, f32[8,8,8,512]{3,2,1,0:T(8,128)S(1)}, f32[3,8,8,512]{3,2,1,0:T(8,128)S(1)}, f3...) custom-call(f32[16,512]{1,0:T(8,128)S(1)} %pack.1.refs_0_.block_ref,, ...), custom_call_target="tpu_custom_call" | custom-call | tf_op jit(solution)/shard_map/edges/pallas_call | solution.py:557
  8.1 1.7 %first.1 = (f32[9,128,1024]{2,1,0:T(8,128)S(1)}, f32[128,1024]{1,0:T(8,128)S(1)}, f32[128,1024]{1,0:T(8,128)S(1)}, bf16[256,1024]{1,0:T(8,128)(2,1)S(1)}) custom-call(f32[16,512]{1,0:T(8,128)S(1)} %pack.1.refs_0_.block_ref, f32[16,512]{1,0:T(8,128)S(1)} %collective-permute-done.refs_1_, bf16[9,64,1024]{2,1,0:T(8,128)(2,1)S(1)} %get-tuple-element.43.refs_2_, ...), custom_call_target="tpu_custom_call" | custom-call | tf_op jit(solution)/shard_map/first/pallas_call | solution.py:557
  9.8 5.0 %second.1 = (f32[128,4096]{1,0:T(8,128)S(1)}, f32[128,4096]{1,0:T(8,128)S(1)}, f32[128,4096]{1,0:T(8,128)S(1)}, f32[128,4096]{1,0:T(8,128)S(1)}, f32[9,128,512]{2,1,0:T(8,128)S(1)}, /*index=5*/f32[384,512]{1,0:T(8,128)S(1)}) custom-call(f32[128,1024]{1,0:T(8,128)S(1)} %get-tuple-element.47.hid_ref, bf16[256,1024]{1,0:T(8,128)(2,1)S(1)} %get-tuple-element.48.hs_ref, ...), custom_call_target="tpu_custom_call" | custom-call | tf_op jit(solution)/shard_map/second/pallas_call | solution.py:557
  14.8 4.0 %back_second.1 = (bf16[256,4096]{1,0:T(8,128)(2,1)S(1)}, f32[4,64,512]{2,1,0:T(8,128)S(1)}) custom-call(f32[9,128,512]{2,1,0:T(8,128)S(1)} %get-tuple-element.53.m2_ref, f32[384,512]{1,0:T(8,128)S(1)} %get-tuple-element.54.dinv_ref, f32[128,4096]{1,0:T(8,128)S(1)} %get-tuple-element.55.car_ref, f32[128,4096]{1,0:T(8,128)S(1)} %get-tuple-element.56.hj_ref, ...), custom_call_target="tpu_custom_call" | custom-call | tf_op jit(solution)/shard_map/back_second/pallas_call | solution.py:557
  18.8 3.0 %scatter.1 = (f32[128,1024]{1,0:T(8,128)S(1)}, f32[32,512]{1,0:T(8,128)S(1)}, bf16[128,8192]{1,0:T(8,128)(2,1)S(1)}) custom-call(bf16[1024,4096]{1,0:T(8,128)(2,1)S(1)} %get-tuple-element.41.oh_ref, bf16[1024,512]{1,0:T(8,128)(2,1)S(1)} %get-tuple-element.42.pick_ref, bf16[256,4096]{1,0:T(8,128)(2,1)S(1)} %get-tuple-element.60.dhe_ref, ...), custom_call_target="tpu_custom_call" | custom-call | tf_op jit(solution)/shard_map/scatter/pallas_call | solution.py:557
  21.8 2.0 %back_first.1.refs_7_ = f32[9,16,1024]{2,1,0:T(8,128)S(1)} custom-call(f32[128,1024]{1,0:T(8,128)S(1)} %get-tuple-element.62.dh_ref, f32[128,1024]{1,0:T(8,128)S(1)} %get-tuple-element.63.sp1_ref, f32[9,128,1024]{2,1,0:T(8,128)S(1)} %get-tuple-element.64.m1_ref, bf16[2,3,256,128]{3,2,1,0:T(8,128)(2,1)S(1)} %get-tuple-element.52.mixt_ref, ...), custom_call_target="tpu_custom_call" | custom-call | tf_op jit(solution)/shard_map/back_first/pallas_call | solution.py:557
  23.8 1.8 %back_edges.1 = (f32[48,128]{1,0:T(8,128)S(1)}, f32[32,128]{1,0:T(8,128)S(1)}) custom-call(f32[16,512]{1,0:T(8,128)S(1)} %pack.1.refs_0_.block_ref, f32[16,512]{1,0:T(8,128)S(1)} %collective-permute-done.refs_1_, f32[3,1,512]{2,1,0:T(1,128)} %bitcast.11, f32[6,8,1024]{2,1,0:T(8,128)S(1)} %get-tuple-element.37.geo_ref.refs_3_, ...), custom_call_target="tpu_custom_call" | custom-call | tf_op jit(solution)/shard_map/back_edges/pallas_call | solution.py:557
  25.6 2.1 %collective-permute-start.1 = (f32[48,128]{1,0:T(8,128)S(1)}, f32[48,128]{1,0:T(8,128)S(1)}, u32[]{:S(2)}, u32[]{:S(2)}) collective-permute-start(f32[48,128]{1,0:T(8,128)S(1)} %get-tuple-element.69.refs_0_), channel_id=1, source_target_pairs={{0,8},{2,10},{4,12},{6,14},{8,16},{10,18},{12,20},{14,22},{16,24},... | collective-permute-start | bytes 73736 | tf_op jit(solution)/shard_map/ppermute | solution.py:794
  27.7 2.6 %collective-permute-start.2 = (f32[48,128]{1,0:T(8,128)S(1)}, f32[48,128]{1,0:T(8,128)S(1)}, u32[]{:S(2)}, u32[]{:S(2)}) collective-permute-start(f32[48,128]{1,0:T(8,128)S(1)} %get-tuple-element.69.refs_0_), channel_id=1, source_target_pairs={{0,16},{2,18},{4,20},{6,22},{8,24},{10,26},{12,28},{14,30},{16,0},... | collective-permute-start | bytes 73736 | tf_op jit(solution)/shard_map/ppermute | solution.py:794
  30.3 1.3 %collective-permute-start.3 = (f32[48,128]{1,0:T(8,128)S(1)}, f32[48,128]{1,0:T(8,128)S(1)}, u32[]{:S(2)}, u32[]{:S(2)}) collective-permute-start(f32[48,128]{1,0:T(8,128)S(1)} %get-tuple-element.69.refs_0_), channel_id=1, source_target_pairs={{0,24},{2,26},{4,28},{6,30},{8,0},{10,2},{12,4},{14,6},{16,8},{18,... | collective-permute-start | bytes 73736 | tf_op jit(solution)/shard_map/ppermute | solution.py:794
  31.6 0.0 collective-permute-done.1.refs_1_
  31.6 0.8 %collective-permute-done.2.refs_2_ = f32[48,128]{1,0:T(8,128)S(1)} collective-permute-done((f32[48,128]{1,0:T(8,128)S(1)}, f32[48,128]{1,0:T(8,128)S(1)}, u32[]{:S(2)}, u32[]{:S(2)}) %collective-permute-start.2) | collective-permute-done | bytes 24608 | tf_op jit(solution)/shard_map/ppermute | solution.py:794
  32.4 1.7 %collective-permute-done.3.refs_3_ = f32[48,128]{1,0:T(8,128)S(1)} collective-permute-done((f32[48,128]{1,0:T(8,128)S(1)}, f32[48,128]{1,0:T(8,128)S(1)}, u32[]{:S(2)}, u32[]{:S(2)}) %collective-permute-start.3) | collective-permute-done | bytes 24608 | tf_op jit(solution)/shard_map/ppermute | solution.py:794
  34.1 0.1 turn.1
  34.2 8.5 %all_to_all.5.arrived_ref = f32[8,32,128]{2,1,0:T(8,128)S(1)} all-to-all(f32[8,32,128]{2,1,0:T(8,128)S(1)} %turn.1), channel_id=1, replica_groups={{0,1,2,3,4,5,6,7},{8,9,10,11,12,13,14,15},{16,17,18,19,20,21,22,23},{24..., dimensions={0} | all-to-all | bytes 262144 | tf_op jit(solution)/shard_map/all_to_all | solution.py:806
  42.7 0.6 %sum.1 = (f32[3,1,512]{2,1,0:T(1,128)}, f32[3,1,512]{2,1,0:T(1,128)}) custom-call(f32[8,32,128]{2,1,0:T(8,128)S(1)} %all_to_all.5.arrived_ref), custom_call_target="tpu_custom_call" | custom-call | tf_op jit(solution)/shard_map/sum/pallas_call | solution.py:807
Async XLA Ops:
  1.4 4.9 %collective-permute-start = (f32[16,512]{1,0:T(8,128)S(1)}, f32[16,512]{1,0:T(8,128)S(1)}, u32[]{:S(2)}, u32[]{:S(2)}) collective-permute-start(f32[16,512]{1,0:T(8,128)S(1)} %pack.1.refs_0_.block_ref), channel_id=1, source_target_pairs={{0,1},{1,0},{2,3},{3,2},{4,5},{5,4},{6,7},{7,6},{8,9},{9,8},{10,11... | collective-permute-start | bytes 98312 | tf_op jit(solution)/shard_map/ppermute | solution.py:789
  25.6 6.1 %collective-permute-start.1 = (f32[48,128]{1,0:T(8,128)S(1)}, f32[48,128]{1,0:T(8,128)S(1)}, u32[]{:S(2)}, u32[]{:S(2)}) collective-permute-start(f32[48,128]{1,0:T(8,128)S(1)} %get-tuple-element.69.refs_0_), channel_id=1, source_target_pairs={{0,8},{2,10},{4,12},{6,14},{8,16},{10,18},{12,20},{14,22},{16,24},... | collective-permute-start | bytes 73736 | tf_op jit(solution)/shard_map/ppermute | solution.py:794
  27.7 4.7 %collective-permute-start.2 = (f32[48,128]{1,0:T(8,128)S(1)}, f32[48,128]{1,0:T(8,128)S(1)}, u32[]{:S(2)}, u32[]{:S(2)}) collective-permute-start(f32[48,128]{1,0:T(8,128)S(1)} %get-tuple-element.69.refs_0_), channel_id=1, source_target_pairs={{0,16},{2,18},{4,20},{6,22},{8,24},{10,26},{12,28},{14,30},{16,0},... | collective-permute-start | bytes 73736 | tf_op jit(solution)/shard_map/ppermute | solution.py:794
  30.3 3.8 %collective-permute-start.3 = (f32[48,128]{1,0:T(8,128)S(1)}, f32[48,128]{1,0:T(8,128)S(1)}, u32[]{:S(2)}, u32[]{:S(2)}) collective-permute-start(f32[48,128]{1,0:T(8,128)S(1)} %get-tuple-element.69.refs_0_), channel_id=1, source_target_pairs={{0,24},{2,26},{4,28},{6,30},{8,0},{10,2},{12,4},{14,6},{16,8},{18,... | collective-permute-start | bytes 73736 | tf_op jit(solution)/shard_map/ppermute | solution.py:794

commit v14 on v12

--- a/solution.py
+++ b/solution.py
@@ -34,6 +34,24 @@
     return jnp.concatenate([hi, x - hi], axis=0)
 
 
+def split3(x):
+    hi = x.astype(bf16)
+    rest = x - hi.astype(f32)
+    mid = rest.astype(bf16)
+    return hi, mid, (rest - mid.astype(f32)).astype(bf16)
+
+
+def six_rows(x, order):
+    hi = x.astype(bf16).astype(f32)
+    mid = (x - hi).astype(bf16).astype(f32)
+    parts = (hi, mid, x - hi - mid)
+    return jnp.concatenate([parts[i] for i in order], axis=0)
+
+
+VALUE_ORDER = (0, 1, 0, 1, 2, 0)
+WEIGHT_ORDER = (0, 0, 1, 1, 0, 2)
+
+
 def dot(a, b):
     return jnp.dot(a, b, preferred_element_type=f32)
 
@@ -116,22 +134,19 @@
     rr_hi = rr.astype(bf16).astype(f32)
     rr_lo = rr - rr_hi
     r2 = rad2_ref[...] * (1.0 / slots)
-    r2_hi = r2.astype(bf16).astype(f32)
-    r2_lo = r2 - r2_hi
     zeros = jnp.zeros((8, chan), f32)
-    turned1 = jnp.concatenate([rr_hi, rr_hi, rr_lo, rr_lo] + [zeros] * 8, axis=0).T
+    turned1 = jnp.concatenate([six_rows(rr, WEIGHT_ORDER)] + [zeros] * (16 - 12 * bases // 8), axis=0).T
     sides = jnp.concatenate([emb0, emb_d, read1_ref[...], read2_ref[...], zeros[:4]], axis=0)
-    turned2 = jnp.concatenate([r2_hi, r2_hi, r2_lo, r2_lo] + [zeros] * 12, axis=0).T
-    rrc_ref[...] = turned1[:, : 8 * bases].astype(bf16)
-    r2c_ref[...] = turned2[:, : 4 * bases].astype(bf16)
+    turned2 = jnp.concatenate([six_rows(r2, WEIGHT_ORDER)] + [zeros] * (16 - 6 * bases // 8), axis=0).T
+    rrc_ref[...] = turned1[:, : 12 * bases].astype(bf16)
+    r2c_ref[...] = turned2[:, : 6 * bases].astype(bf16)
     side_ref[...] = jnp.concatenate([sides] + [zeros] * 15, axis=0).T
     rrr_ref[...] = jnp.concatenate(
         [jnp.concatenate([rr_hi, rr_hi], axis=1), jnp.concatenate([rr_lo, jnp.zeros_like(rr_lo)], axis=1)], axis=0
     ).astype(bf16)
     for i, ref in enumerate((mix1_ref, mix2_ref)):
-        hi, lo = split(ref[...])
-        mixa_ref[i, 0:chan, :] = hi
-        mixa_ref[i, chan:, :] = lo
+        for part, value in enumerate(split3(ref[...])):
+            mixa_ref[i, part * chan : (part + 1) * chan, :] = value
         for g in range(3):
             hi, lo = split(ref[:, g * chan : (g + 1) * chan].T)
             mixt_ref[i, g, 0:chan, :] = hi
@@ -142,6 +157,14 @@
     rows = both.shape[0] // 2
     first = dot(both, hi)
     return first[:rows] + first[rows:] + dot(both[:rows], lo)
+
+
+def dot_three(parts, hi, mid, lo):
+    rows = parts.shape[0] // 3
+    first = dot(parts, hi)
+    second = dot(parts[: 2 * rows], mid)
+    third = dot(parts[:rows], lo)
+    return first[:rows] + (first[rows : 2 * rows] + second[:rows]) + (first[2 * rows :] + second[rows:] + third)
 
 
 def edge_kernel(plan, *refs):
@@ -225,9 +248,7 @@
                     term = basis if l == 0 else basis * row(y_ref[l - 1, k : k + 1, here], 2 * bases)
                     low[l] = term if low[l] is None else low[l] + term
             for l in range(ORDERS):
-                both = split_rows(low[l]).astype(bf16)
-                as_ref[l, 0 : 4 * bases, here] = both
-                as_ref[l, 4 * bases : 8 * bases, here] = both
+                as_ref[l, :, here] = six_rows(low[l], VALUE_ORDER).astype(bf16)
 
 
 def first_kernel(plan, *refs):
@@ -251,15 +272,13 @@
             m = dot(rrc_ref[...], as_ref[l, :, here])
             m1_ref[l, :, here] = m
             inv[GROUP[l]] = m * m if inv[GROUP[l]] is None else inv[GROUP[l]] + m * m
-        hi, lo = split(jnp.concatenate(inv, axis=0))
-        value = dot_parts(mixa_ref[0], hi, lo)
+        value = dot_three(mixa_ref[0], *split3(jnp.concatenate(inv, axis=0)))
         act, slope = silu_parts(value)
         sp1_ref[:, here] = slope
         hidden = act + emb0_col + embd_col * flag_ref[0:1, here]
         hid_ref[:, here] = hidden
-        hi, lo = split(hidden)
-        hs_ref[0:chan, here] = hi
-        hs_ref[chan : 2 * chan, here] = lo
+        for part, piece in enumerate(split3(hidden)):
+            hs_ref[part * chan : (part + 1) * chan, here] = piece
 
     in_turns(0, n_near // wide_cols, first)
 
@@ -280,8 +299,7 @@
         here = slice(k * atoms, (k + 1) * atoms)
         basis = bt_ref[k, 0:bases, 0:atoms]
         for ref, value in ((w_ref, basis), (slope_ref, basis * (reach - row(geo_ref[4, k : k + 1, 0:atoms], bases)))):
-            both = split_rows(value)
-            ref[:, here] = dot(r2c_ref[...], jnp.concatenate([both, both], axis=0).astype(bf16))
+            ref[:, here] = dot(r2c_ref[...], six_rows(value, VALUE_ORDER).astype(bf16))
 
     for pair in range(slots // 2):
         by_lane = (2 + 2 * (pair % 2)) * LANES if atoms >= 4 * LANES else 0
@@ -305,7 +323,7 @@
                     feat = got if feat is None else jnp.where(chunk_no == chunk, got, feat)
                 hj_ref[rows, at] = feat
                 car_ref[rows, at] = feat * w_ref[rows, at]
-        feat = both[:chan] + both[chan:]
+        feat = both[:chan] + (both[chan : 2 * chan] + both[2 * chan :])
         hj_ref[:, here] = feat
         car_ref[:, here] = feat * w_ref[:, here]
 
@@ -347,8 +365,7 @@
     read2_col = side_ref[:, 3:4]
     for t in range(atoms // wide_cols):
         cols = slice(t * wide_cols, (t + 1) * wide_cols)
-        hi, lo = split(inv_ref[:, cols])
-        _, slope = silu_parts(dot_parts(mixa_ref[1], hi, lo))
+        _, slope = silu_parts(dot_three(mixa_ref[1], *split3(inv_ref[:, cols])))
         hi, lo = split(slope * (2.0 * read2_col))
         for g, scale in enumerate((1.0, 0.5 * SQRT3, 0.5 * SQRT15)):
             dinv_ref[g * chan : (g + 1) * chan, cols] = scale * dot_parts(mixt_ref[1, g], hi, lo)
@@ -582,11 +599,11 @@
         (block, *weights),
         (
             ((2 * atoms, slots * atoms), bf16),
-            ((chan, 8 * bases), bf16),
-            ((chan, 4 * bases), bf16),
+            ((chan, 12 * bases), bf16),
+            ((chan, 6 * bases), bf16),
             ((chan, LANES), f32),
             ((4 * bases, 2 * chan), bf16),
-            ((2, 2 * chan, 3 * chan), bf16),
+            ((2, 3 * chan, 3 * chan), bf16),
             ((2, 3, 2 * chan, chan), bf16),
         ),
         [pltpu.VMEM(w.shape, f32) for w in weights] + [pltpu.SemaphoreType.DMA((len(weights),))],
@@ -618,14 +635,14 @@
             ((slots, 2 * bases, n_near), f32),
             ((slots, n_near), jnp.int32),
             ((n_near, atoms), bf16),
-            ((ORDERS, 8 * bases, n_near), bf16),
+            ((ORDERS, 12 * bases, n_near), bf16),
         ),
     )
     m1, sp1, hid, hs = run(
         "first",
         functools.partial(first_kernel, plan),
         (*blocks, as1, rrc, sides, mixa),
-        (((ORDERS, chan, n_near), f32), ((chan, n_near), f32), ((chan, n_near), f32), ((2 * chan, n_near), bf16)),
+        (((ORDERS, chan, n_near), f32), ((chan, n_near), f32), ((chan, n_near), f32), ((3 * chan, n_near), bf16)),
         [pltpu.VMEM((8, n_near), f32)],
     )
     hj, w, slope, car = run(
@@ -633,7 +650,7 @@
         gather_kernel,
         (hid, hs, oh, pick, gidx, bt, geo, r2c),
         (((chan, edges), f32),) * 4,
-        [pltpu.VMEM((2 * chan, 2 * atoms), bf16)],
+        [pltpu.VMEM((3 * chan, 2 * atoms), bf16)],
     )
     m2, dinv = run(
         "moments",

time: 43.6 us -> 45.6 us (1.046)
  Pallas kernels: 22.1 us -> 24.1 us
    pallas_call x9, Pallas kernels: 20.6 us -> 22.6 us  [run(): pl.pallas_call(body, out_shape=tuple((jax.ShapeDtypeStruct(shape, dtype)...]
where the time goes in v14:
time: 45.6 us; the launch traced here: 45.2 us
  Pallas kernels  24.1 us (53%)
  starting transfers between devices  9.1 us (20%)
  blocking collectives  8.47 us (19%)
  waiting for transfers between devices  2.85 us (6%)
  between operations  0.7 us (2%)
    pallas_call x9, Pallas kernels, run(): pl.pallas_call(body, out_shape=tuple((jax.ShapeDtypeStruct(shape, dtype)...  22.6 us
    all_to_all x1, blocking collectives, shards(): lax.all_to_all(messages, ('bead', 'space'), 0, 0, axis_index_groups=rows,...  8.47 us
    ppermute x3, starting transfers between devices, shards(): lax.ppermute(pushed, 'bead', [(b, (b + z * inner) % beads) for b in range...  6.07 us
    ppermute x1, starting transfers between devices, shards(): lax.ppermute(block, 'space', [(i, (i - offset) % domains) for i in range(...  3.03 us
    ppermute x3, waiting for transfers between devices, shards(): lax.ppermute(pushed, 'bead', [(b, (b + z * inner) % beads) for b in range...  2.48 us
  transfers between devices with their start and end apart: 4, of which 3 were waited for; matrix products, arithmetic and copies ran while one was open for 0% of the time, Pallas kernels for 3%

profile of v14, /device:TPU:0, one launch (start us, length us, event | category | flops | bytes accessed | tf_op | source)
XLA Modules:
  0.0 45.2 jit_solution(1065314685034461146)
XLA Ops:
  0.6 0.8 %pack.1.refs_0_.block_ref = f32[16,512]{1,0:T(8,128)S(1)} custom-call(f32[3,1,512]{2,1,0:T(1,128)} %bitcast.10, s32[1,512]{1,0:T(1,128)} %bitcast.12, s32[1,512]{1,0:T(1,128)} %bitcast.13, s32[8,512]{1,0:T(8,128)} %slot_src.1), custom_call_target="tpu_custom_call" | custom-call | tf_op jit(solution)/shard_map/pack/pallas_call | solution.py:800
  1.4 3.0 %collective-permute-start = (f32[16,512]{1,0:T(8,128)S(1)}, f32[16,512]{1,0:T(8,128)S(1)}, u32[]{:S(2)}, u32[]{:S(2)}) collective-permute-start(f32[16,512]{1,0:T(8,128)S(1)} %pack.1.refs_0_.block_ref), channel_id=1, source_target_pairs={{0,1},{1,0},{2,3},{3,2},{4,5},{5,4},{6,7},{7,6},{8,9},{9,8},{10,11... | collective-permute-start | bytes 98312 | tf_op jit(solution)/shard_map/ppermute | solution.py:817
  4.5 1.5 %choose.1 = (bf16[1024,4096]{1,0:T(8,128)(2,1)S(1)}, bf16[128,96]{1,0:T(8,128)(2,1)S(1)}, bf16[128,48]{1,0:T(8,128)(2,1)S(1)}, f32[128,128]{1,0:T(8,128)S(1)}, b...) custom-call(f32[16,512]{1,0:T(8,128)S(1)} %pack.1.refs_0_.block_ref, ...), custom_call_target="tpu_custom_call" | custom-call | flops 2000000000 | bytes 2000000 | tf_op jit(solution)/shard_map/choose/pallas_call | solution.py:578
  6.0 0.4 collective-permute-done.refs_1_
  6.4 1.8 %edges.1 = (f32[6,8,1024]{2,1,0:T(8,128)S(1)}, f32[8,8,1024]{2,1,0:T(8,128)S(1)}, f32[8,8,8,512]{3,2,1,0:T(8,128)S(1)}, f32[3,8,8,512]{3,2,1,0:T(8,128)S(1)}, f3...) custom-call(f32[16,512]{1,0:T(8,128)S(1)} %pack.1.refs_0_.block_ref,, ...), custom_call_target="tpu_custom_call" | custom-call | tf_op jit(solution)/shard_map/edges/pallas_call | solution.py:578
  8.2 1.9 %first.1 = (f32[9,128,1024]{2,1,0:T(8,128)S(1)}, f32[128,1024]{1,0:T(8,128)S(1)}, f32[128,1024]{1,0:T(8,128)S(1)}, bf16[384,1024]{1,0:T(8,128)(2,1)S(1)}) custom-call(f32[16,512]{1,0:T(8,128)S(1)} %pack.1.refs_0_.block_ref, f32[16,512]{1,0:T(8,128)S(1)} %collective-permute-done.refs_1_, bf16[9,96,1024]{2,1,0:T(8,128)(2,1)S(1)} %get-tuple-element.43.refs_2_, ...), custom_call_target="tpu_custom_call" | custom-call | tf_op jit(solution)/shard_map/first/pallas_call | solution.py:578
  10.1 3.2 %gather.1 = (f32[128,4096]{1,0:T(8,128)S(1)}, f32[128,4096]{1,0:T(8,128)S(1)}, f32[128,4096]{1,0:T(8,128)S(1)}, f32[128,4096]{1,0:T(8,128)S(1)}) custom-call(f32[128,1024]{1,0:T(8,128)S(1)} %get-tuple-element.47.hid_ref, bf16[384,1024]{1,0:T(8,128)(2,1)S(1)} %get-tuple-element.48.hs_ref, bf16[1024,4096]{1,0:T(8,128)(2,1)S(1)} %get-tuple-element.41.oh_ref, ...), custom_call_target="tpu_custom_call" | custom-call | tf_op jit(solution)/shard_map/gather/pallas_call | solution.py:578
  13.4 3.5 %moments.1 = (f32[9,128,512]{2,1,0:T(8,128)S(1)}, f32[384,512]{1,0:T(8,128)S(1)}) custom-call(f32[128,4096]{1,0:T(8,128)S(1)} %get-tuple-element.51.car_ref, f32[8,8,8,512]{3,2,1,0:T(8,128)S(1)} %get-tuple-element.52.yb_ref, bf16[2,384,384]{2,1,0:T(8,128)(2,1)S(1)} %get-tuple-element.46.refs_5_.mixa_ref, ...), custom_call_target="tpu_custom_call" | custom-call | tf_op jit(solution)/shard_map/moments/pallas_call | solution.py:578
  16.9 3.9 %back_second.1 = (bf16[256,4096]{1,0:T(8,128)(2,1)S(1)}, f32[4,64,512]{2,1,0:T(8,128)S(1)}) custom-call(f32[9,128,512]{2,1,0:T(8,128)S(1)} %get-tuple-element.54.m2_ref, f32[384,512]{1,0:T(8,128)S(1)} %get-tuple-element.55.dinv_ref, f32[128,4096]{1,0:T(8,128)S(1)} %get-tuple-element.51.car_ref, f32[128,4096]{1,0:T(8,128)S(1)} %get-tuple-element.56.hj_ref, ...), custom_call_target="tpu_custom_call" | custom-call | tf_op jit(solution)/shard_map/back_second/pallas_call | solution.py:578
  20.8 3.0 %scatter.1 = (f32[128,1024]{1,0:T(8,128)S(1)}, f32[32,512]{1,0:T(8,128)S(1)}, bf16[128,8192]{1,0:T(8,128)(2,1)S(1)}) custom-call(bf16[1024,4096]{1,0:T(8,128)(2,1)S(1)} %get-tuple-element.41.oh_ref, bf16[1024,512]{1,0:T(8,128)(2,1)S(1)} %get-tuple-element.42.pick_ref, bf16[256,4096]{1,0:T(8,128)(2,1)S(1)} %get-tuple-element.60.dhe_ref, ...), custom_call_target="tpu_custom_call" | custom-call | tf_op jit(solution)/shard_map/scatter/pallas_call | solution.py:578
  23.8 2.0 %back_first.1.refs_7_ = f32[9,16,1024]{2,1,0:T(8,128)S(1)} custom-call(f32[128,1024]{1,0:T(8,128)S(1)} %get-tuple-element.62.dh_ref, f32[128,1024]{1,0:T(8,128)S(1)} %get-tuple-element.63.sp1_ref, f32[9,128,1024]{2,1,0:T(8,128)S(1)} %get-tuple-element.64.m1_ref, bf16[2,3,256,128]{3,2,1,0:T(8,128)(2,1)S(1)} %get-tuple-element.53.mixt_ref, ...), custom_call_target="tpu_custom_call" | custom-call | tf_op jit(solution)/shard_map/back_first/pallas_call | solution.py:578
  25.8 1.8 %back_edges.1 = (f32[48,128]{1,0:T(8,128)S(1)}, f32[32,128]{1,0:T(8,128)S(1)}) custom-call(f32[16,512]{1,0:T(8,128)S(1)} %pack.1.refs_0_.block_ref, f32[16,512]{1,0:T(8,128)S(1)} %collective-permute-done.refs_1_, f32[3,1,512]{2,1,0:T(1,128)} %bitcast.11, f32[6,8,1024]{2,1,0:T(8,128)S(1)} %get-tuple-element.37.geo_ref.refs_3_, ...), custom_call_target="tpu_custom_call" | custom-call | tf_op jit(solution)/shard_map/back_edges/pallas_call | solution.py:578
  27.5 2.1 %collective-permute-start.1 = (f32[48,128]{1,0:T(8,128)S(1)}, f32[48,128]{1,0:T(8,128)S(1)}, u32[]{:S(2)}, u32[]{:S(2)}) collective-permute-start(f32[48,128]{1,0:T(8,128)S(1)} %get-tuple-element.69.refs_0_), channel_id=1, source_target_pairs={{0,8},{2,10},{4,12},{6,14},{8,16},{10,18},{12,20},{14,22},{16,24},... | collective-permute-start | bytes 73736 | tf_op jit(solution)/shard_map/ppermute | solution.py:822
  29.6 2.6 %collective-permute-start.2 = (f32[48,128]{1,0:T(8,128)S(1)}, f32[48,128]{1,0:T(8,128)S(1)}, u32[]{:S(2)}, u32[]{:S(2)}) collective-permute-start(f32[48,128]{1,0:T(8,128)S(1)} %get-tuple-element.69.refs_0_), channel_id=1, source_target_pairs={{0,16},{2,18},{4,20},{6,22},{8,24},{10,26},{12,28},{14,30},{16,0},... | collective-permute-start | bytes 73736 | tf_op jit(solution)/shard_map/ppermute | solution.py:822
  32.2 1.3 %collective-permute-start.3 = (f32[48,128]{1,0:T(8,128)S(1)}, f32[48,128]{1,0:T(8,128)S(1)}, u32[]{:S(2)}, u32[]{:S(2)}) collective-permute-start(f32[48,128]{1,0:T(8,128)S(1)} %get-tuple-element.69.refs_0_), channel_id=1, source_target_pairs={{0,24},{2,26},{4,28},{6,30},{8,0},{10,2},{12,4},{14,6},{16,8},{18,... | collective-permute-start | bytes 73736 | tf_op jit(solution)/shard_map/ppermute | solution.py:822
  33.6 0.0 collective-permute-done.1.refs_1_
  33.6 0.8 %collective-permute-done.2.refs_2_ = f32[48,128]{1,0:T(8,128)S(1)} collective-permute-done((f32[48,128]{1,0:T(8,128)S(1)}, f32[48,128]{1,0:T(8,128)S(1)}, u32[]{:S(2)}, u32[]{:S(2)}) %collective-permute-start.2) | collective-permute-done | bytes 24608 | tf_op jit(solution)/shard_map/ppermute | solution.py:822
  34.4 1.7 %collective-permute-done.3.refs_3_ = f32[48,128]{1,0:T(8,128)S(1)} collective-permute-done((f32[48,128]{1,0:T(8,128)S(1)}, f32[48,128]{1,0:T(8,128)S(1)}, u32[]{:S(2)}, u32[]{:S(2)}) %collective-permute-start.3) | collective-permute-done | bytes 24608 | tf_op jit(solution)/shard_map/ppermute | solution.py:822
  36.1 0.1 turn.1
  36.1 8.5 %all_to_all.5.arrived_ref = f32[8,32,128]{2,1,0:T(8,128)S(1)} all-to-all(f32[8,32,128]{2,1,0:T(8,128)S(1)} %turn.1), channel_id=1, replica_groups={{0,1,2,3,4,5,6,7},{8,9,10,11,12,13,14,15},{16,17,18,19,20,21,22,23},{24..., dimensions={0} | all-to-all | bytes 262144 | tf_op jit(solution)/shard_map/all_to_all | solution.py:834
  44.6 0.6 %sum.1 = (f32[3,1,512]{2,1,0:T(1,128)}, f32[3,1,512]{2,1,0:T(1,128)}) custom-call(f32[8,32,128]{2,1,0:T(8,128)S(1)} %all_to_all.5.arrived_ref), custom_call_target="tpu_custom_call" | custom-call | tf_op jit(solution)/shard_map/sum/pallas_call | solution.py:835
Async XLA Ops:
  1.4 4.9 %collective-permute-start = (f32[16,512]{1,0:T(8,128)S(1)}, f32[16,512]{1,0:T(8,128)S(1)}, u32[]{:S(2)}, u32[]{:S(2)}) collective-permute-start(f32[16,512]{1,0:T(8,128)S(1)} %pack.1.refs_0_.block_ref), channel_id=1, source_target_pairs={{0,1},{1,0},{2,3},{3,2},{4,5},{5,4},{6,7},{7,6},{8,9},{9,8},{10,11... | collective-permute-start | bytes 98312 | tf_op jit(solution)/shard_map/ppermute | solution.py:817
  27.5 6.1 %collective-permute-start.1 = (f32[48,128]{1,0:T(8,128)S(1)}, f32[48,128]{1,0:T(8,128)S(1)}, u32[]{:S(2)}, u32[]{:S(2)}) collective-permute-start(f32[48,128]{1,0:T(8,128)S(1)} %get-tuple-element.69.refs_0_), channel_id=1, source_target_pairs={{0,8},{2,10},{4,12},{6,14},{8,16},{10,18},{12,20},{14,22},{16,24},... | collective-permute-start | bytes 73736 | tf_op jit(solution)/shard_map/ppermute | solution.py:822
  29.6 4.7 %collective-permute-start.2 = (f32[48,128]{1,0:T(8,128)S(1)}, f32[48,128]{1,0:T(8,128)S(1)}, u32[]{:S(2)}, u32[]{:S(2)}) collective-permute-start(f32[48,128]{1,0:T(8,128)S(1)} %get-tuple-element.69.refs_0_), channel_id=1, source_target_pairs={{0,16},{2,18},{4,20},{6,22},{8,24},{10,26},{12,28},{14,30},{16,0},... | collective-permute-start | bytes 73736 | tf_op jit(solution)/shard_map/ppermute | solution.py:822
  32.2 3.8 %collective-permute-start.3 = (f32[48,128]{1,0:T(8,128)S(1)}, f32[48,128]{1,0:T(8,128)S(1)}, u32[]{:S(2)}, u32[]{:S(2)}) collective-permute-start(f32[48,128]{1,0:T(8,128)S(1)} %get-tuple-element.69.refs_0_), channel_id=1, source_target_pairs={{0,24},{2,26},{4,28},{6,30},{8,0},{10,2},{12,4},{14,6},{16,8},{18,... | collective-permute-start | bytes 73736 | tf_op jit(solution)/shard_map/ppermute | solution.py:822

commit v15 on v14

--- a/solution.py
+++ b/solution.py
@@ -145,26 +145,22 @@
         [jnp.concatenate([rr_hi, rr_hi], axis=1), jnp.concatenate([rr_lo, jnp.zeros_like(rr_lo)], axis=1)], axis=0
     ).astype(bf16)
     for i, ref in enumerate((mix1_ref, mix2_ref)):
-        for part, value in enumerate(split3(ref[...])):
-            mixa_ref[i, part * chan : (part + 1) * chan, :] = value
+        parts = split3(ref[...])
+        for at, part in enumerate(WEIGHT_ORDER):
+            mixa_ref[i, :, at * 3 * chan : (at + 1) * 3 * chan] = parts[part]
         for g in range(3):
             hi, lo = split(ref[:, g * chan : (g + 1) * chan].T)
-            mixt_ref[i, g, 0:chan, :] = hi
-            mixt_ref[i, g, chan:, :] = lo
-
-
-def dot_parts(both, hi, lo):
-    rows = both.shape[0] // 2
-    first = dot(both, hi)
-    return first[:rows] + first[rows:] + dot(both[:rows], lo)
-
-
-def dot_three(parts, hi, mid, lo):
-    rows = parts.shape[0] // 3
-    first = dot(parts, hi)
-    second = dot(parts[: 2 * rows], mid)
-    third = dot(parts[:rows], lo)
-    return first[:rows] + (first[rows : 2 * rows] + second[:rows]) + (first[2 * rows :] + second[rows:] + third)
+            mixt_ref[i, g] = jnp.concatenate([hi, hi, lo], axis=1)
+
+
+def six_deep(x):
+    parts = split3(x)
+    return jnp.concatenate([parts[i] for i in VALUE_ORDER], axis=0)
+
+
+def three_deep(x):
+    hi, lo = split(x)
+    return jnp.concatenate([hi, lo, hi], axis=0)
 
 
 def edge_kernel(plan, *refs):
@@ -272,7 +268,7 @@
             m = dot(rrc_ref[...], as_ref[l, :, here])
             m1_ref[l, :, here] = m
             inv[GROUP[l]] = m * m if inv[GROUP[l]] is None else inv[GROUP[l]] + m * m
-        value = dot_three(mixa_ref[0], *split3(jnp.concatenate(inv, axis=0)))
+        value = dot(mixa_ref[0], six_deep(jnp.concatenate(inv, axis=0)))
         act, slope = silu_parts(value)
         sp1_ref[:, here] = slope
         hidden = act + emb0_col + embd_col * flag_ref[0:1, here]
@@ -302,7 +298,7 @@
             ref[:, here] = dot(r2c_ref[...], six_rows(value, VALUE_ORDER).astype(bf16))
 
     for pair in range(slots // 2):
-        by_lane = (2 + 2 * (pair % 2)) * LANES if atoms >= 4 * LANES else 0
+        by_lane = 4 * LANES if atoms >= 4 * LANES else 0
         by_product = 2 * atoms - by_lane
         first = pair * 2 * atoms
         here = slice(first, first + by_product)
@@ -365,10 +361,10 @@
     read2_col = side_ref[:, 3:4]
     for t in range(atoms // wide_cols):
         cols = slice(t * wide_cols, (t + 1) * wide_cols)
-        _, slope = silu_parts(dot_three(mixa_ref[1], *split3(inv_ref[:, cols])))
-        hi, lo = split(slope * (2.0 * read2_col))
+        _, slope = silu_parts(dot(mixa_ref[1], six_deep(inv_ref[:, cols])))
+        slope = three_deep(slope * (2.0 * read2_col))
         for g, scale in enumerate((1.0, 0.5 * SQRT3, 0.5 * SQRT15)):
-            dinv_ref[g * chan : (g + 1) * chan, cols] = scale * dot_parts(mixt_ref[1, g], hi, lo)
+            dinv_ref[g * chan : (g + 1) * chan, cols] = scale * dot(mixt_ref[1, g], slope)
 
 
 def back_second_kernel(m2_ref, dinv_ref, car_ref, hj_ref, w_ref, slope_ref, ub_ref, dhe_ref, p_ref):
@@ -464,8 +460,8 @@
 
     def back_first(j):
         here = pl.ds(pl.multiple_of(j * wide_cols, wide_cols), wide_cols)
-        hi, lo = split(dh_ref[:, here] * sp1_ref[:, here] * 2.0)
-        scale = [dot_parts(mixt_ref[0, g], hi, lo) for g in range(3)]
+        slope = three_deep(dh_ref[:, here] * sp1_ref[:, here] * 2.0)
+        scale = [dot(mixt_ref[0, g], slope) for g in range(3)]
         for l in range(ORDERS):
             hi, lo = split(m1_ref[l, :, here] * scale[GROUP[l]])
             out = dot(rrr_ref[...], jnp.concatenate([hi, lo], axis=0))
@@ -603,8 +599,8 @@
             ((chan, 6 * bases), bf16),
             ((chan, LANES), f32),
             ((4 * bases, 2 * chan), bf16),
-            ((2, 3 * chan, 3 * chan), bf16),
-            ((2, 3, 2 * chan, chan), bf16),
+            ((2, chan, 18 * chan), bf16),
+            ((2, 3, chan, 3 * chan), bf16),
         ),
         [pltpu.VMEM(w.shape, f32) for w in weights] + [pltpu.SemaphoreType.DMA((len(weights),))],
         range(1, 1 + len(weights)),

time: 45.6 us -> 44.8 us (0.982)
  Pallas kernels: 24.1 us -> 23.4 us
    pallas_call x9, Pallas kernels: 22.6 us -> 21.9 us  [run(): pl.pallas_call(body, out_shape=tuple((jax.ShapeDtypeStruct(shape, dtype)...]
  transfers between devices with their start and end apart: 4 -> 4, of which waited for: 3 -> 3; matrix products, arithmetic and copies ran while one was open for 0% -> 0% of each run, Pallas kernels for 3% -> 4%
where the time goes in v15:
time: 44.8 us; the launch traced here: 44.5 us
  Pallas kernels  23.4 us (52%)
  starting transfers between devices  9.1 us (20%)
  blocking collectives  8.47 us (19%)
  waiting for transfers between devices  2.79 us (6%)
  between operations  0.7 us (2%)
    pallas_call x9, Pallas kernels, run(): pl.pallas_call(body, out_shape=tuple((jax.ShapeDtypeStruct(shape, dtype)...  21.9 us
    all_to_all x1, blocking collectives, shards(): lax.all_to_all(messages, ('bead', 'space'), 0, 0, axis_index_groups=rows,...  8.47 us
    ppermute x3, starting transfers between devices, shards(): lax.ppermute(pushed, 'bead', [(b, (b + z * inner) % beads) for b in range...  6.07 us
    ppermute x1, starting transfers between devices, shards(): lax.ppermute(block, 'space', [(i, (i - offset) % domains) for i in range(...  3.03 us
    ppermute x3, waiting for transfers between devices, shards(): lax.ppermute(pushed, 'bead', [(b, (b + z * inner) % beads) for b in range...  2.47 us
  transfers between devices with their start and end apart: 4, of which 3 were waited for; matrix products, arithmetic and copies ran while one was open for 0% of the time, Pallas kernels for 4%

profile of v15, /device:TPU:0, one launch (start us, length us, event | category | flops | bytes accessed | tf_op | source)
XLA Modules:
  0.0 44.5 jit_solution(16514661720784363347)
XLA Ops:
  0.6 0.8 %pack.1.refs_0_.block_ref = f32[16,512]{1,0:T(8,128)S(1)} custom-call(f32[3,1,512]{2,1,0:T(1,128)} %bitcast.10, s32[1,512]{1,0:T(1,128)} %bitcast.12, s32[1,512]{1,0:T(1,128)} %bitcast.13, s32[8,512]{1,0:T(8,128)} %slot_src.1), custom_call_target="tpu_custom_call" | custom-call | tf_op jit(solution)/shard_map/pack/pallas_call | solution.py:796
  1.4 3.0 %collective-permute-start = (f32[16,512]{1,0:T(8,128)S(1)}, f32[16,512]{1,0:T(8,128)S(1)}, u32[]{:S(2)}, u32[]{:S(2)}) collective-permute-start(f32[16,512]{1,0:T(8,128)S(1)} %pack.1.refs_0_.block_ref), channel_id=1, source_target_pairs={{0,1},{1,0},{2,3},{3,2},{4,5},{5,4},{6,7},{7,6},{8,9},{9,8},{10,11... | collective-permute-start | bytes 98312 | tf_op jit(solution)/shard_map/ppermute | solution.py:813
  4.5 1.6 %choose.1 = (bf16[1024,4096]{1,0:T(8,128)(2,1)S(1)}, bf16[128,96]{1,0:T(8,128)(2,1)S(1)}, bf16[128,48]{1,0:T(8,128)(2,1)S(1)}, f32[128,128]{1,0:T(8,128)S(1)}, b...) custom-call(f32[16,512]{1,0:T(8,128)S(1)} %pack.1.refs_0_.block_ref, ...), custom_call_target="tpu_custom_call" | custom-call | flops 2000000000 | bytes 2000000 | tf_op jit(solution)/shard_map/choose/pallas_call | solution.py:574
  6.1 0.3 collective-permute-done.refs_1_
  6.4 1.8 %edges.1 = (f32[6,8,1024]{2,1,0:T(8,128)S(1)}, f32[8,8,1024]{2,1,0:T(8,128)S(1)}, f32[8,8,8,512]{3,2,1,0:T(8,128)S(1)}, f32[3,8,8,512]{3,2,1,0:T(8,128)S(1)}, f3...) custom-call(f32[16,512]{1,0:T(8,128)S(1)} %pack.1.refs_0_.block_ref,, ...), custom_call_target="tpu_custom_call" | custom-call | tf_op jit(solution)/shard_map/edges/pallas_call | solution.py:574
  8.2 1.9 %first.1 = (f32[9,128,1024]{2,1,0:T(8,128)S(1)}, f32[128,1024]{1,0:T(8,128)S(1)}, f32[128,1024]{1,0:T(8,128)S(1)}, bf16[384,1024]{1,0:T(8,128)(2,1)S(1)}) custom-call(f32[16,512]{1,0:T(8,128)S(1)} %pack.1.refs_0_.block_ref, f32[16,512]{1,0:T(8,128)S(1)} %collective-permute-done.refs_1_, bf16[9,96,1024]{2,1,0:T(8,128)(2,1)S(1)} %get-tuple-element.43.refs_2_, ...), custom_call_target="tpu_custom_call" | custom-call | tf_op jit(solution)/shard_map/first/pallas_call | solution.py:574
  10.2 2.8 %gather.1 = (f32[128,4096]{1,0:T(8,128)S(1)}, f32[128,4096]{1,0:T(8,128)S(1)}, f32[128,4096]{1,0:T(8,128)S(1)}, f32[128,4096]{1,0:T(8,128)S(1)}) custom-call(f32[128,1024]{1,0:T(8,128)S(1)} %get-tuple-element.47.hid_ref, bf16[384,1024]{1,0:T(8,128)(2,1)S(1)} %get-tuple-element.48.hs_ref, bf16[1024,4096]{1,0:T(8,128)(2,1)S(1)} %get-tuple-element.41.oh_ref, ...), custom_call_target="tpu_custom_call" | custom-call | tf_op jit(solution)/shard_map/gather/pallas_call | solution.py:574
  13.0 3.2 %moments.1 = (f32[9,128,512]{2,1,0:T(8,128)S(1)}, f32[384,512]{1,0:T(8,128)S(1)}) custom-call(f32[128,4096]{1,0:T(8,128)S(1)} %get-tuple-element.51.car_ref, f32[8,8,8,512]{3,2,1,0:T(8,128)S(1)} %get-tuple-element.52.yb_ref, bf16[2,128,2304]{2,1,0:T(8,128)(2,1)S(1)} %get-tuple-element.46.refs_5_.mixa_ref, ...), custom_call_target="tpu_custom_call" | custom-call | tf_op jit(solution)/shard_map/moments/pallas_call | solution.py:574
  16.2 3.9 %back_second.1 = (bf16[256,4096]{1,0:T(8,128)(2,1)S(1)}, f32[4,64,512]{2,1,0:T(8,128)S(1)}) custom-call(f32[9,128,512]{2,1,0:T(8,128)S(1)} %get-tuple-element.54.m2_ref, f32[384,512]{1,0:T(8,128)S(1)} %get-tuple-element.55.dinv_ref, f32[128,4096]{1,0:T(8,128)S(1)} %get-tuple-element.51.car_ref, f32[128,4096]{1,0:T(8,128)S(1)} %get-tuple-element.56.hj_ref, ...), custom_call_target="tpu_custom_call" | custom-call | tf_op jit(solution)/shard_map/back_second/pallas_call | solution.py:574
  20.0 3.0 %scatter.1 = (f32[128,1024]{1,0:T(8,128)S(1)}, f32[32,512]{1,0:T(8,128)S(1)}, bf16[128,8192]{1,0:T(8,128)(2,1)S(1)}) custom-call(bf16[1024,4096]{1,0:T(8,128)(2,1)S(1)} %get-tuple-element.41.oh_ref, bf16[1024,512]{1,0:T(8,128)(2,1)S(1)} %get-tuple-element.42.pick_ref, bf16[256,4096]{1,0:T(8,128)(2,1)S(1)} %get-tuple-element.60.dhe_ref, ...), custom_call_target="tpu_custom_call" | custom-call | tf_op jit(solution)/shard_map/scatter/pallas_call | solution.py:574
  23.0 2.0 %back_first.1.refs_7_ = f32[9,16,1024]{2,1,0:T(8,128)S(1)} custom-call(f32[128,1024]{1,0:T(8,128)S(1)} %get-tuple-element.62.dh_ref, f32[128,1024]{1,0:T(8,128)S(1)} %get-tuple-element.63.sp1_ref, f32[9,128,1024]{2,1,0:T(8,128)S(1)} %get-tuple-element.64.m1_ref, bf16[2,3,128,384]{3,2,1,0:T(8,128)(2,1)S(1)} %get-tuple-element.53.mixt_ref, ...), custom_call_target="tpu_custom_call" | custom-call | tf_op jit(solution)/shard_map/back_first/pallas_call | solution.py:574
  25.0 1.7 %back_edges.1 = (f32[48,128]{1,0:T(8,128)S(1)}, f32[32,128]{1,0:T(8,128)S(1)}) custom-call(f32[16,512]{1,0:T(8,128)S(1)} %pack.1.refs_0_.block_ref, f32[16,512]{1,0:T(8,128)S(1)} %collective-permute-done.refs_1_, f32[3,1,512]{2,1,0:T(1,128)} %bitcast.11, f32[6,8,1024]{2,1,0:T(8,128)S(1)} %get-tuple-element.37.geo_ref.refs_3_, ...), custom_call_target="tpu_custom_call" | custom-call | tf_op jit(solution)/shard_map/back_edges/pallas_call | solution.py:574
  26.7 2.1 %collective-permute-start.1 = (f32[48,128]{1,0:T(8,128)S(1)}, f32[48,128]{1,0:T(8,128)S(1)}, u32[]{:S(2)}, u32[]{:S(2)}) collective-permute-start(f32[48,128]{1,0:T(8,128)S(1)} %get-tuple-element.69.refs_0_), channel_id=1, source_target_pairs={{0,8},{2,10},{4,12},{6,14},{8,16},{10,18},{12,20},{14,22},{16,24},... | collective-permute-start | bytes 73736 | tf_op jit(solution)/shard_map/ppermute | solution.py:818
  28.9 2.6 %collective-permute-start.2 = (f32[48,128]{1,0:T(8,128)S(1)}, f32[48,128]{1,0:T(8,128)S(1)}, u32[]{:S(2)}, u32[]{:S(2)}) collective-permute-start(f32[48,128]{1,0:T(8,128)S(1)} %get-tuple-element.69.refs_0_), channel_id=1, source_target_pairs={{0,16},{2,18},{4,20},{6,22},{8,24},{10,26},{12,28},{14,30},{16,0},... | collective-permute-start | bytes 73736 | tf_op jit(solution)/shard_map/ppermute | solution.py:818
  31.5 1.4 %collective-permute-start.3 = (f32[48,128]{1,0:T(8,128)S(1)}, f32[48,128]{1,0:T(8,128)S(1)}, u32[]{:S(2)}, u32[]{:S(2)}) collective-permute-start(f32[48,128]{1,0:T(8,128)S(1)} %get-tuple-element.69.refs_0_), channel_id=1, source_target_pairs={{0,24},{2,26},{4,28},{6,30},{8,0},{10,2},{12,4},{14,6},{16,8},{18,... | collective-permute-start | bytes 73736 | tf_op jit(solution)/shard_map/ppermute | solution.py:818
  32.8 0.0 collective-permute-done.1.refs_1_
  32.8 0.8 %collective-permute-done.2.refs_2_ = f32[48,128]{1,0:T(8,128)S(1)} collective-permute-done((f32[48,128]{1,0:T(8,128)S(1)}, f32[48,128]{1,0:T(8,128)S(1)}, u32[]{:S(2)}, u32[]{:S(2)}) %collective-permute-start.2) | collective-permute-done | bytes 24608 | tf_op jit(solution)/shard_map/ppermute | solution.py:818
  33.6 1.7 %collective-permute-done.3.refs_3_ = f32[48,128]{1,0:T(8,128)S(1)} collective-permute-done((f32[48,128]{1,0:T(8,128)S(1)}, f32[48,128]{1,0:T(8,128)S(1)}, u32[]{:S(2)}, u32[]{:S(2)}) %collective-permute-start.3) | collective-permute-done | bytes 24608 | tf_op jit(solution)/shard_map/ppermute | solution.py:818
  35.3 0.1 turn.1
  35.4 8.5 %all_to_all.5.arrived_ref = f32[8,32,128]{2,1,0:T(8,128)S(1)} all-to-all(f32[8,32,128]{2,1,0:T(8,128)S(1)} %turn.1), channel_id=1, replica_groups={{0,1,2,3,4,5,6,7},{8,9,10,11,12,13,14,15},{16,17,18,19,20,21,22,23},{24..., dimensions={0} | all-to-all | bytes 262144 | tf_op jit(solution)/shard_map/all_to_all | solution.py:830
  43.8 0.6 %sum.1 = (f32[3,1,512]{2,1,0:T(1,128)}, f32[3,1,512]{2,1,0:T(1,128)}) custom-call(f32[8,32,128]{2,1,0:T(8,128)S(1)} %all_to_all.5.arrived_ref), custom_call_target="tpu_custom_call" | custom-call | tf_op jit(solution)/shard_map/sum/pallas_call | solution.py:831
Async XLA Ops:
  1.4 4.9 %collective-permute-start = (f32[16,512]{1,0:T(8,128)S(1)}, f32[16,512]{1,0:T(8,128)S(1)}, u32[]{:S(2)}, u32[]{:S(2)}) collective-permute-start(f32[16,512]{1,0:T(8,128)S(1)} %pack.1.refs_0_.block_ref), channel_id=1, source_target_pairs={{0,1},{1,0},{2,3},{3,2},{4,5},{5,4},{6,7},{7,6},{8,9},{9,8},{10,11... | collective-permute-start | bytes 98312 | tf_op jit(solution)/shard_map/ppermute | solution.py:813
  26.7 6.1 %collective-permute-start.1 = (f32[48,128]{1,0:T(8,128)S(1)}, f32[48,128]{1,0:T(8,128)S(1)}, u32[]{:S(2)}, u32[]{:S(2)}) collective-permute-start(f32[48,128]{1,0:T(8,128)S(1)} %get-tuple-element.69.refs_0_), channel_id=1, source_target_pairs={{0,8},{2,10},{4,12},{6,14},{8,16},{10,18},{12,20},{14,22},{16,24},... | collective-permute-start | bytes 73736 | tf_op jit(solution)/shard_map/ppermute | solution.py:818
  28.9 4.7 %collective-permute-start.2 = (f32[48,128]{1,0:T(8,128)S(1)}, f32[48,128]{1,0:T(8,128)S(1)}, u32[]{:S(2)}, u32[]{:S(2)}) collective-permute-start(f32[48,128]{1,0:T(8,128)S(1)} %get-tuple-element.69.refs_0_), channel_id=1, source_target_pairs={{0,16},{2,18},{4,20},{6,22},{8,24},{10,26},{12,28},{14,30},{16,0},... | collective-permute-start | bytes 73736 | tf_op jit(solution)/shard_map/ppermute | solution.py:818
  31.5 3.8 %collective-permute-start.3 = (f32[48,128]{1,0:T(8,128)S(1)}, f32[48,128]{1,0:T(8,128)S(1)}, u32[]{:S(2)}, u32[]{:S(2)}) collective-permute-start(f32[48,128]{1,0:T(8,128)S(1)} %get-tuple-element.69.refs_0_), channel_id=1, source_target_pairs={{0,24},{2,26},{4,28},{6,30},{8,0},{10,2},{12,4},{14,6},{16,8},{18,... | collective-permute-start | bytes 73736 | tf_op jit(solution)/shard_map/ppermute | solution.py:818

commit v16 on v15

--- a/solution.py
+++ b/solution.py
@@ -553,12 +553,6 @@
                 push_ref[(1 + g) * lines + at : (1 + g) * lines + at + 1, :] = line
                 mass = HEAVY - (HEAVY - 1.0) * blocks[g][3:4, cols]
                 mass_ref[g * lines + at : g * lines + at + 1, :] = mass
-    if lines > 3 * tiles:
-        for g in range(n_wide + 1):
-            blank = slice(g * lines + 3 * tiles, (g + 1) * lines)
-            push_ref[blank, :] = jnp.zeros((lines - 3 * tiles, LANES), f32)
-            if g < n_wide:
-                mass_ref[blank, :] = jnp.ones((lines - 3 * tiles, LANES), f32)
 
 
 def in_hbm(x):
@@ -684,7 +678,7 @@
 
 
 def line_count(atoms):
-    return -(-3 * (atoms // LANES) // 8) * 8
+    return 3 * (atoms // LANES)
 
 
 def ring_plan(domains, atoms):

time: 44.8 us -> 44.6 us (level)
  no operation moved by 1% of the time
where the time goes in v16:
time: 44.6 us; the launch traced here: 44.3 us
  Pallas kernels  23.4 us (52%)
  starting transfers between devices  9.1 us (20%)
  blocking collectives  8.33 us (19%)
  waiting for transfers between devices  2.75 us (6%)
  between operations  0.7 us (2%)
    pallas_call x9, Pallas kernels, run(): pl.pallas_call(body, out_shape=tuple((jax.ShapeDtypeStruct(shape, dtype)...  21.9 us
    all_to_all x1, blocking collectives, shards(): lax.all_to_all(messages, ('bead', 'space'), 0, 0, axis_index_groups=rows,...  8.33 us
    ppermute x3, starting transfers between devices, shards(): lax.ppermute(pushed, 'bead', [(b, (b + z * inner) % beads) for b in range...  6.07 us
    ppermute x1, starting transfers between devices, shards(): lax.ppermute(block, 'space', [(i, (i - offset) % domains) for i in range(...  3.03 us
    ppermute x3, waiting for transfers between devices, shards(): lax.ppermute(pushed, 'bead', [(b, (b + z * inner) % beads) for b in range...  2.43 us
  transfers between devices with their start and end apart: 4, of which 3 were waited for; matrix products, arithmetic and copies ran while one was open for 0% of the time, Pallas kernels for 4%

profile of v16, /device:TPU:0, one launch (start us, length us, event | category | flops | bytes accessed | tf_op | source)
XLA Modules:
  0.0 44.3 jit_solution(15693284537280723316)
XLA Ops:
  0.6 0.8 %pack.1.refs_0_.block_ref = f32[16,512]{1,0:T(8,128)S(1)} custom-call(f32[3,1,512]{2,1,0:T(1,128)} %bitcast.10, s32[1,512]{1,0:T(1,128)} %bitcast.12, s32[1,512]{1,0:T(1,128)} %bitcast.13, s32[8,512]{1,0:T(8,128)} %slot_src.1), custom_call_target="tpu_custom_call" | custom-call | tf_op jit(solution)/shard_map/pack/pallas_call | solution.py:790
  1.4 3.0 %collective-permute-start = (f32[16,512]{1,0:T(8,128)S(1)}, f32[16,512]{1,0:T(8,128)S(1)}, u32[]{:S(2)}, u32[]{:S(2)}) collective-permute-start(f32[16,512]{1,0:T(8,128)S(1)} %pack.1.refs_0_.block_ref), channel_id=1, source_target_pairs={{0,1},{1,0},{2,3},{3,2},{4,5},{5,4},{6,7},{7,6},{8,9},{9,8},{10,11... | collective-permute-start | bytes 98312 | tf_op jit(solution)/shard_map/ppermute | solution.py:807
  4.5 1.6 %choose.1 = (bf16[1024,4096]{1,0:T(8,128)(2,1)S(1)}, bf16[128,96]{1,0:T(8,128)(2,1)S(1)}, bf16[128,48]{1,0:T(8,128)(2,1)S(1)}, f32[128,128]{1,0:T(8,128)S(1)}, b...) custom-call(f32[16,512]{1,0:T(8,128)S(1)} %pack.1.refs_0_.block_ref, ...), custom_call_target="tpu_custom_call" | custom-call | flops 2000000000 | bytes 2000000 | tf_op jit(solution)/shard_map/choose/pallas_call | solution.py:568
  6.1 0.3 collective-permute-done.refs_1_
  6.4 1.8 %edges.1 = (f32[6,8,1024]{2,1,0:T(8,128)S(1)}, f32[8,8,1024]{2,1,0:T(8,128)S(1)}, f32[8,8,8,512]{3,2,1,0:T(8,128)S(1)}, f32[3,8,8,512]{3,2,1,0:T(8,128)S(1)}, f3...) custom-call(f32[16,512]{1,0:T(8,128)S(1)} %pack.1.refs_0_.block_ref,, ...), custom_call_target="tpu_custom_call" | custom-call | tf_op jit(solution)/shard_map/edges/pallas_call | solution.py:568
  8.2 1.9 %first.1 = (f32[9,128,1024]{2,1,0:T(8,128)S(1)}, f32[128,1024]{1,0:T(8,128)S(1)}, f32[128,1024]{1,0:T(8,128)S(1)}, bf16[384,1024]{1,0:T(8,128)(2,1)S(1)}) custom-call(f32[16,512]{1,0:T(8,128)S(1)} %pack.1.refs_0_.block_ref, f32[16,512]{1,0:T(8,128)S(1)} %collective-permute-done.refs_1_, bf16[9,96,1024]{2,1,0:T(8,128)(2,1)S(1)} %get-tuple-element.43.refs_2_, ...), custom_call_target="tpu_custom_call" | custom-call | tf_op jit(solution)/shard_map/first/pallas_call | solution.py:568
  10.2 2.8 %gather.1 = (f32[128,4096]{1,0:T(8,128)S(1)}, f32[128,4096]{1,0:T(8,128)S(1)}, f32[128,4096]{1,0:T(8,128)S(1)}, f32[128,4096]{1,0:T(8,128)S(1)}) custom-call(f32[128,1024]{1,0:T(8,128)S(1)} %get-tuple-element.47.hid_ref, bf16[384,1024]{1,0:T(8,128)(2,1)S(1)} %get-tuple-element.48.hs_ref, bf16[1024,4096]{1,0:T(8,128)(2,1)S(1)} %get-tuple-element.41.oh_ref, ...), custom_call_target="tpu_custom_call" | custom-call | tf_op jit(solution)/shard_map/gather/pallas_call | solution.py:568
  13.0 3.2 %moments.1 = (f32[9,128,512]{2,1,0:T(8,128)S(1)}, f32[384,512]{1,0:T(8,128)S(1)}) custom-call(f32[128,4096]{1,0:T(8,128)S(1)} %get-tuple-element.51.car_ref, f32[8,8,8,512]{3,2,1,0:T(8,128)S(1)} %get-tuple-element.52.yb_ref, bf16[2,128,2304]{2,1,0:T(8,128)(2,1)S(1)} %get-tuple-element.46.refs_5_.mixa_ref, ...), custom_call_target="tpu_custom_call" | custom-call | tf_op jit(solution)/shard_map/moments/pallas_call | solution.py:568
  16.2 3.9 %back_second.1 = (bf16[256,4096]{1,0:T(8,128)(2,1)S(1)}, f32[4,64,512]{2,1,0:T(8,128)S(1)}) custom-call(f32[9,128,512]{2,1,0:T(8,128)S(1)} %get-tuple-element.54.m2_ref, f32[384,512]{1,0:T(8,128)S(1)} %get-tuple-element.55.dinv_ref, f32[128,4096]{1,0:T(8,128)S(1)} %get-tuple-element.51.car_ref, f32[128,4096]{1,0:T(8,128)S(1)} %get-tuple-element.56.hj_ref, ...), custom_call_target="tpu_custom_call" | custom-call | tf_op jit(solution)/shard_map/back_second/pallas_call | solution.py:568
  20.0 3.0 %scatter.1 = (f32[128,1024]{1,0:T(8,128)S(1)}, f32[32,512]{1,0:T(8,128)S(1)}, bf16[128,8192]{1,0:T(8,128)(2,1)S(1)}) custom-call(bf16[1024,4096]{1,0:T(8,128)(2,1)S(1)} %get-tuple-element.41.oh_ref, bf16[1024,512]{1,0:T(8,128)(2,1)S(1)} %get-tuple-element.42.pick_ref, bf16[256,4096]{1,0:T(8,128)(2,1)S(1)} %get-tuple-element.60.dhe_ref, ...), custom_call_target="tpu_custom_call" | custom-call | tf_op jit(solution)/shard_map/scatter/pallas_call | solution.py:568
  23.0 2.0 %back_first.1.refs_7_ = f32[9,16,1024]{2,1,0:T(8,128)S(1)} custom-call(f32[128,1024]{1,0:T(8,128)S(1)} %get-tuple-element.62.dh_ref, f32[128,1024]{1,0:T(8,128)S(1)} %get-tuple-element.63.sp1_ref, f32[9,128,1024]{2,1,0:T(8,128)S(1)} %get-tuple-element.64.m1_ref, bf16[2,3,128,384]{3,2,1,0:T(8,128)(2,1)S(1)} %get-tuple-element.53.mixt_ref, ...), custom_call_target="tpu_custom_call" | custom-call | tf_op jit(solution)/shard_map/back_first/pallas_call | solution.py:568
  25.0 1.8 %back_edges.1 = (f32[36,128]{1,0:T(8,128)S(1)}, f32[24,128]{1,0:T(8,128)S(1)}) custom-call(f32[16,512]{1,0:T(8,128)S(1)} %pack.1.refs_0_.block_ref, f32[16,512]{1,0:T(8,128)S(1)} %collective-permute-done.refs_1_, f32[3,1,512]{2,1,0:T(1,128)} %bitcast.11, f32[6,8,1024]{2,1,0:T(8,128)S(1)} %get-tuple-element.37.geo_ref.refs_3_, ...), custom_call_target="tpu_custom_call" | custom-call | tf_op jit(solution)/shard_map/back_edges/pallas_call | solution.py:568
  26.8 2.1 %collective-permute-start.1 = (f32[36,128]{1,0:T(8,128)S(1)}, f32[36,128]{1,0:T(8,128)S(1)}, u32[]{:S(2)}, u32[]{:S(2)}) collective-permute-start(f32[36,128]{1,0:T(8,128)S(1)} %get-tuple-element.69.refs_0_), channel_id=1, source_target_pairs={{0,8},{2,10},{4,12},{6,14},{8,16},{10,18},{12,20},{14,22},{16,24},... | collective-permute-start | bytes 55304 | tf_op jit(solution)/shard_map/ppermute | solution.py:812
  28.9 2.6 %collective-permute-start.2 = (f32[36,128]{1,0:T(8,128)S(1)}, f32[36,128]{1,0:T(8,128)S(1)}, u32[]{:S(2)}, u32[]{:S(2)}) collective-permute-start(f32[36,128]{1,0:T(8,128)S(1)} %get-tuple-element.69.refs_0_), channel_id=1, source_target_pairs={{0,16},{2,18},{4,20},{6,22},{8,24},{10,26},{12,28},{14,30},{16,0},... | collective-permute-start | bytes 55304 | tf_op jit(solution)/shard_map/ppermute | solution.py:812
  31.5 1.4 %collective-permute-start.3 = (f32[36,128]{1,0:T(8,128)S(1)}, f32[36,128]{1,0:T(8,128)S(1)}, u32[]{:S(2)}, u32[]{:S(2)}) collective-permute-start(f32[36,128]{1,0:T(8,128)S(1)} %get-tuple-element.69.refs_0_), channel_id=1, source_target_pairs={{0,24},{2,26},{4,28},{6,30},{8,0},{10,2},{12,4},{14,6},{16,8},{18,... | collective-permute-start | bytes 55304 | tf_op jit(solution)/shard_map/ppermute | solution.py:812
  32.8 0.0 collective-permute-done.1.refs_1_
  32.8 0.7 %collective-permute-done.2.refs_2_ = f32[36,128]{1,0:T(8,128)S(1)} collective-permute-done((f32[36,128]{1,0:T(8,128)S(1)}, f32[36,128]{1,0:T(8,128)S(1)}, u32[]{:S(2)}, u32[]{:S(2)}) %collective-permute-start.2) | collective-permute-done | bytes 18464 | tf_op jit(solution)/shard_map/ppermute | solution.py:812
  33.6 1.7 %collective-permute-done.3.refs_3_ = f32[36,128]{1,0:T(8,128)S(1)} collective-permute-done((f32[36,128]{1,0:T(8,128)S(1)}, f32[36,128]{1,0:T(8,128)S(1)}, u32[]{:S(2)}, u32[]{:S(2)}) %collective-permute-start.3) | collective-permute-done | bytes 18464 | tf_op jit(solution)/shard_map/ppermute | solution.py:812
  35.3 0.1 turn.1
  35.3 8.3 %all_to_all.5.arrived_ref = f32[8,24,128]{2,1,0:T(8,128)S(1)} all-to-all(f32[8,24,128]{2,1,0:T(8,128)S(1)} %turn.1), channel_id=1, replica_groups={{0,1,2,3,4,5,6,7},{8,9,10,11,12,13,14,15},{16,17,18,19,20,21,22,23},{24..., dimensions={0} | all-to-all | bytes 196608 | tf_op jit(solution)/shard_map/all_to_all | solution.py:824
  43.7 0.6 %sum.1 = (f32[3,1,512]{2,1,0:T(1,128)}, f32[3,1,512]{2,1,0:T(1,128)}) custom-call(f32[8,24,128]{2,1,0:T(8,128)S(1)} %all_to_all.5.arrived_ref), custom_call_target="tpu_custom_call" | custom-call | tf_op jit(solution)/shard_map/sum/pallas_call | solution.py:825
Async XLA Ops:
  1.4 4.9 %collective-permute-start = (f32[16,512]{1,0:T(8,128)S(1)}, f32[16,512]{1,0:T(8,128)S(1)}, u32[]{:S(2)}, u32[]{:S(2)}) collective-permute-start(f32[16,512]{1,0:T(8,128)S(1)} %pack.1.refs_0_.block_ref), channel_id=1, source_target_pairs={{0,1},{1,0},{2,3},{3,2},{4,5},{5,4},{6,7},{7,6},{8,9},{9,8},{10,11... | collective-permute-start | bytes 98312 | tf_op jit(solution)/shard_map/ppermute | solution.py:807
  26.8 6.1 %collective-permute-start.1 = (f32[36,128]{1,0:T(8,128)S(1)}, f32[36,128]{1,0:T(8,128)S(1)}, u32[]{:S(2)}, u32[]{:S(2)}) collective-permute-start(f32[36,128]{1,0:T(8,128)S(1)} %get-tuple-element.69.refs_0_), channel_id=1, source_target_pairs={{0,8},{2,10},{4,12},{6,14},{8,16},{10,18},{12,20},{14,22},{16,24},... | collective-permute-start | bytes 55304 | tf_op jit(solution)/shard_map/ppermute | solution.py:812
  28.9 4.7 %collective-permute-start.2 = (f32[36,128]{1,0:T(8,128)S(1)}, f32[36,128]{1,0:T(8,128)S(1)}, u32[]{:S(2)}, u32[]{:S(2)}) collective-permute-start(f32[36,128]{1,0:T(8,128)S(1)} %get-tuple-element.69.refs_0_), channel_id=1, source_target_pairs={{0,16},{2,18},{4,20},{6,22},{8,24},{10,26},{12,28},{14,30},{16,0},... | collective-permute-start | bytes 55304 | tf_op jit(solution)/shard_map/ppermute | solution.py:812
  31.5 3.8 %collective-permute-start.3 = (f32[36,128]{1,0:T(8,128)S(1)}, f32[36,128]{1,0:T(8,128)S(1)}, u32[]{:S(2)}, u32[]{:S(2)}) collective-permute-start(f32[36,128]{1,0:T(8,128)S(1)} %get-tuple-element.69.refs_0_), channel_id=1, source_target_pairs={{0,24},{2,26},{4,28},{6,30},{8,0},{10,2},{12,4},{14,6},{16,8},{18,... | collective-permute-start | bytes 55304 | tf_op jit(solution)/shard_map/ppermute | solution.py:812

commit v17 on v16

--- a/solution.py
+++ b/solution.py
@@ -145,17 +145,20 @@
         [jnp.concatenate([rr_hi, rr_hi], axis=1), jnp.concatenate([rr_lo, jnp.zeros_like(rr_lo)], axis=1)], axis=0
     ).astype(bf16)
     for i, ref in enumerate((mix1_ref, mix2_ref)):
-        parts = split3(ref[...])
-        for at, part in enumerate(WEIGHT_ORDER):
-            mixa_ref[i, :, at * 3 * chan : (at + 1) * 3 * chan] = parts[part]
+        hi, mid, lo = split3(ref[...])
+        for at, pair in enumerate(((hi, hi), (mid, mid), (hi, lo))):
+            mixa_ref[i, at * chan : (at + 1) * chan, :] = jnp.concatenate(pair, axis=1)
         for g in range(3):
             hi, lo = split(ref[:, g * chan : (g + 1) * chan].T)
-            mixt_ref[i, g] = jnp.concatenate([hi, hi, lo], axis=1)
-
-
-def six_deep(x):
-    parts = split3(x)
-    return jnp.concatenate([parts[i] for i in VALUE_ORDER], axis=0)
+            mixt_ref[i, g * chan : (g + 1) * chan, :] = jnp.concatenate([hi, hi, lo], axis=1)
+
+
+def mixed(weights, x):
+    hi, mid, lo = split3(x)
+    rows = weights.shape[0] // 3
+    large = dot(weights[: 2 * rows], jnp.concatenate([hi, mid], axis=0))
+    small = dot(weights[2 * rows :], jnp.concatenate([lo, hi], axis=0))
+    return large[:rows] + (large[rows:] + small)
 
 
 def three_deep(x):
@@ -268,7 +271,7 @@
             m = dot(rrc_ref[...], as_ref[l, :, here])
             m1_ref[l, :, here] = m
             inv[GROUP[l]] = m * m if inv[GROUP[l]] is None else inv[GROUP[l]] + m * m
-        value = dot(mixa_ref[0], six_deep(jnp.concatenate(inv, axis=0)))
+        value = mixed(mixa_ref[0], jnp.concatenate(inv, axis=0))
         act, slope = silu_parts(value)
         sp1_ref[:, here] = slope
         hidden = act + emb0_col + embd_col * flag_ref[0:1, here]
@@ -361,10 +364,10 @@
     read2_col = side_ref[:, 3:4]
     for t in range(atoms // wide_cols):
         cols = slice(t * wide_cols, (t + 1) * wide_cols)
-        _, slope = silu_parts(dot(mixa_ref[1], six_deep(inv_ref[:, cols])))
-        slope = three_deep(slope * (2.0 * read2_col))
+        _, slope = silu_parts(mixed(mixa_ref[1], inv_ref[:, cols]))
+        groups_slope = dot(mixt_ref[1], three_deep(slope * (2.0 * read2_col)))
         for g, scale in enumerate((1.0, 0.5 * SQRT3, 0.5 * SQRT15)):
-            dinv_ref[g * chan : (g + 1) * chan, cols] = scale * dot(mixt_ref[1, g], slope)
+            dinv_ref[g * chan : (g + 1) * chan, cols] = scale * groups_slope[g * chan : (g + 1) * chan]
 
 
 def back_second_kernel(m2_ref, dinv_ref, car_ref, hj_ref, w_ref, slope_ref, ub_ref, dhe_ref, p_ref):
@@ -461,7 +464,9 @@
     def back_first(j):
         here = pl.ds(pl.multiple_of(j * wide_cols, wide_cols), wide_cols)
         slope = three_deep(dh_ref[:, here] * sp1_ref[:, here] * 2.0)
-        scale = [dot(mixt_ref[0, g], slope) for g in range(3)]
+        groups_slope = dot(mixt_ref[0], slope)
+        chan = sp1_ref.shape[0]
+        scale = [groups_slope[g * chan : (g + 1) * chan] for g in range(3)]
         for l in range(ORDERS):
             hi, lo = split(m1_ref[l, :, here] * scale[GROUP[l]])
             out = dot(rrr_ref[...], jnp.concatenate([hi, lo], axis=0))
@@ -593,8 +598,8 @@
             ((chan, 6 * bases), bf16),
             ((chan, LANES), f32),
             ((4 * bases, 2 * chan), bf16),
-            ((2, chan, 18 * chan), bf16),
-            ((2, 3, chan, 3 * chan), bf16),
+            ((2, 3 * chan, 6 * chan), bf16),
+            ((2, 3 * chan, 3 * chan), bf16),
         ),
         [pltpu.VMEM(w.shape, f32) for w in weights] + [pltpu.SemaphoreType.DMA((len(weights),))],
         range(1, 1 + len(weights)),

time: 44.6 us -> 45.2 us (1.013)
  Pallas kernels: 23.4 us -> 23.9 us
    pallas_call x9, Pallas kernels: 21.9 us -> 22.4 us  [run(): pl.pallas_call(body, out_shape=tuple((jax.ShapeDtypeStruct(shape, dtype)...]
  transfers between devices with their start and end apart: 4 -> 4, of which waited for: 3 -> 3; matrix products, arithmetic and copies ran while one was open for 0% -> 0% of each run, Pallas kernels for 4% -> 3%
where the time goes in v17:
time: 45.2 us; the launch traced here: 44.8 us
  Pallas kernels  23.9 us (53%)
  starting transfers between devices  9.09 us (20%)
  blocking collectives  8.32 us (18%)
  waiting for transfers between devices  2.78 us (6%)
  between operations  0.7 us (2%)
    pallas_call x9, Pallas kernels, run(): pl.pallas_call(body, out_shape=tuple((jax.ShapeDtypeStruct(shape, dtype)...  22.4 us
    all_to_all x1, blocking collectives, shards(): lax.all_to_all(messages, ('bead', 'space'), 0, 0, axis_index_groups=rows,...  8.32 us
    ppermute x3, starting transfers between devices, shards(): lax.ppermute(pushed, 'bead', [(b, (b + z * inner) % beads) for b in range...  6.06 us
    ppermute x1, starting transfers between devices, shards(): lax.ppermute(block, 'space', [(i, (i - offset) % domains) for i in range(...  3.03 us
    ppermute x3, waiting for transfers between devices, shards(): lax.ppermute(pushed, 'bead', [(b, (b + z * inner) % beads) for b in range...  2.44 us
  transfers between devices with their start and end apart: 4, of which 3 were waited for; matrix products, arithmetic and copies ran while one was open for 0% of the time, Pallas kernels for 3%

profile of v17, /device:TPU:0, one launch (start us, length us, event | category | flops | bytes accessed | tf_op | source)
XLA Modules:
  0.0 44.8 jit_solution(13009403249502868636)
XLA Ops:
  0.6 0.8 %pack.1.refs_0_.block_ref = f32[16,512]{1,0:T(8,128)S(1)} custom-call(f32[3,1,512]{2,1,0:T(1,128)} %bitcast.10, s32[1,512]{1,0:T(1,128)} %bitcast.12, s32[1,512]{1,0:T(1,128)} %bitcast.13, s32[8,512]{1,0:T(8,128)} %slot_src.1), custom_call_target="tpu_custom_call" | custom-call | tf_op jit(solution)/shard_map/pack/pallas_call | solution.py:795
  1.4 3.0 %collective-permute-start = (f32[16,512]{1,0:T(8,128)S(1)}, f32[16,512]{1,0:T(8,128)S(1)}, u32[]{:S(2)}, u32[]{:S(2)}) collective-permute-start(f32[16,512]{1,0:T(8,128)S(1)} %pack.1.refs_0_.block_ref), channel_id=1, source_target_pairs={{0,1},{1,0},{2,3},{3,2},{4,5},{5,4},{6,7},{7,6},{8,9},{9,8},{10,11... | collective-permute-start | bytes 98312 | tf_op jit(solution)/shard_map/ppermute | solution.py:812
  4.5 1.5 %choose.1 = (bf16[1024,4096]{1,0:T(8,128)(2,1)S(1)}, bf16[128,96]{1,0:T(8,128)(2,1)S(1)}, bf16[128,48]{1,0:T(8,128)(2,1)S(1)}, f32[128,128]{1,0:T(8,128)S(1)}, b...) custom-call(f32[16,512]{1,0:T(8,128)S(1)} %pack.1.refs_0_.block_ref, ...), custom_call_target="tpu_custom_call" | custom-call | flops 2000000000 | bytes 2000000 | tf_op jit(solution)/shard_map/choose/pallas_call | solution.py:573
  6.0 0.3 collective-permute-done.refs_1_
  6.4 1.8 %edges.1 = (f32[6,8,1024]{2,1,0:T(8,128)S(1)}, f32[8,8,1024]{2,1,0:T(8,128)S(1)}, f32[8,8,8,512]{3,2,1,0:T(8,128)S(1)}, f32[3,8,8,512]{3,2,1,0:T(8,128)S(1)}, f3...) custom-call(f32[16,512]{1,0:T(8,128)S(1)} %pack.1.refs_0_.block_ref,, ...), custom_call_target="tpu_custom_call" | custom-call | tf_op jit(solution)/shard_map/edges/pallas_call | solution.py:573
  8.2 2.0 %first.1 = (f32[9,128,1024]{2,1,0:T(8,128)S(1)}, f32[128,1024]{1,0:T(8,128)S(1)}, f32[128,1024]{1,0:T(8,128)S(1)}, bf16[384,1024]{1,0:T(8,128)(2,1)S(1)}) custom-call(f32[16,512]{1,0:T(8,128)S(1)} %pack.1.refs_0_.block_ref, f32[16,512]{1,0:T(8,128)S(1)} %collective-permute-done.refs_1_, bf16[9,96,1024]{2,1,0:T(8,128)(2,1)S(1)} %get-tuple-element.43.refs_2_, ...), custom_call_target="tpu_custom_call" | custom-call | tf_op jit(solution)/shard_map/first/pallas_call | solution.py:573
  10.3 2.8 %gather.1 = (f32[128,4096]{1,0:T(8,128)S(1)}, f32[128,4096]{1,0:T(8,128)S(1)}, f32[128,4096]{1,0:T(8,128)S(1)}, f32[128,4096]{1,0:T(8,128)S(1)}) custom-call(f32[128,1024]{1,0:T(8,128)S(1)} %get-tuple-element.47.hid_ref, bf16[384,1024]{1,0:T(8,128)(2,1)S(1)} %get-tuple-element.48.hs_ref, bf16[1024,4096]{1,0:T(8,128)(2,1)S(1)} %get-tuple-element.41.oh_ref, ...), custom_call_target="tpu_custom_call" | custom-call | tf_op jit(solution)/shard_map/gather/pallas_call | solution.py:573
  13.1 3.2 %moments.1 = (f32[9,128,512]{2,1,0:T(8,128)S(1)}, f32[384,512]{1,0:T(8,128)S(1)}) custom-call(f32[128,4096]{1,0:T(8,128)S(1)} %get-tuple-element.51.car_ref, f32[8,8,8,512]{3,2,1,0:T(8,128)S(1)} %get-tuple-element.52.yb_ref, bf16[2,384,768]{2,1,0:T(8,128)(2,1)S(1)} %get-tuple-element.46.refs_5_.mixa_ref, ...), custom_call_target="tpu_custom_call" | custom-call | tf_op jit(solution)/shard_map/moments/pallas_call | solution.py:573
  16.3 3.9 %back_second.1 = (bf16[256,4096]{1,0:T(8,128)(2,1)S(1)}, f32[4,64,512]{2,1,0:T(8,128)S(1)}) custom-call(f32[9,128,512]{2,1,0:T(8,128)S(1)} %get-tuple-element.54.m2_ref, f32[384,512]{1,0:T(8,128)S(1)} %get-tuple-element.55.dinv_ref, f32[128,4096]{1,0:T(8,128)S(1)} %get-tuple-element.51.car_ref, f32[128,4096]{1,0:T(8,128)S(1)} %get-tuple-element.56.hj_ref, ...), custom_call_target="tpu_custom_call" | custom-call | tf_op jit(solution)/shard_map/back_second/pallas_call | solution.py:573
  20.1 3.0 %scatter.1 = (f32[128,1024]{1,0:T(8,128)S(1)}, f32[32,512]{1,0:T(8,128)S(1)}, bf16[128,8192]{1,0:T(8,128)(2,1)S(1)}) custom-call(bf16[1024,4096]{1,0:T(8,128)(2,1)S(1)} %get-tuple-element.41.oh_ref, bf16[1024,512]{1,0:T(8,128)(2,1)S(1)} %get-tuple-element.42.pick_ref, bf16[256,4096]{1,0:T(8,128)(2,1)S(1)} %get-tuple-element.60.dhe_ref, ...), custom_call_target="tpu_custom_call" | custom-call | tf_op jit(solution)/shard_map/scatter/pallas_call | solution.py:573
  23.1 2.4 %back_first.1.refs_7_ = f32[9,16,1024]{2,1,0:T(8,128)S(1)} custom-call(f32[128,1024]{1,0:T(8,128)S(1)} %get-tuple-element.62.dh_ref, f32[128,1024]{1,0:T(8,128)S(1)} %get-tuple-element.63.sp1_ref, f32[9,128,1024]{2,1,0:T(8,128)S(1)} %get-tuple-element.64.m1_ref, bf16[2,384,384]{2,1,0:T(8,128)(2,1)S(1)} %get-tuple-element.53.mixt_ref, ...), custom_call_target="tpu_custom_call" | custom-call | tf_op jit(solution)/shard_map/back_first/pallas_call | solution.py:573
  25.5 1.8 %back_edges.1 = (f32[36,128]{1,0:T(8,128)S(1)}, f32[24,128]{1,0:T(8,128)S(1)}) custom-call(f32[16,512]{1,0:T(8,128)S(1)} %pack.1.refs_0_.block_ref, f32[16,512]{1,0:T(8,128)S(1)} %collective-permute-done.refs_1_, f32[3,1,512]{2,1,0:T(1,128)} %bitcast.11, f32[6,8,1024]{2,1,0:T(8,128)S(1)} %get-tuple-element.37.geo_ref.refs_3_, ...), custom_call_target="tpu_custom_call" | custom-call | tf_op jit(solution)/shard_map/back_edges/pallas_call | solution.py:573
  27.3 2.1 %collective-permute-start.1 = (f32[36,128]{1,0:T(8,128)S(1)}, f32[36,128]{1,0:T(8,128)S(1)}, u32[]{:S(2)}, u32[]{:S(2)}) collective-permute-start(f32[36,128]{1,0:T(8,128)S(1)} %get-tuple-element.69.refs_0_), channel_id=1, source_target_pairs={{0,8},{2,10},{4,12},{6,14},{8,16},{10,18},{12,20},{14,22},{16,24},... | collective-permute-start | bytes 55304 | tf_op jit(solution)/shard_map/ppermute | solution.py:817
  29.4 2.6 %collective-permute-start.2 = (f32[36,128]{1,0:T(8,128)S(1)}, f32[36,128]{1,0:T(8,128)S(1)}, u32[]{:S(2)}, u32[]{:S(2)}) collective-permute-start(f32[36,128]{1,0:T(8,128)S(1)} %get-tuple-element.69.refs_0_), channel_id=1, source_target_pairs={{0,16},{2,18},{4,20},{6,22},{8,24},{10,26},{12,28},{14,30},{16,0},... | collective-permute-start | bytes 55304 | tf_op jit(solution)/shard_map/ppermute | solution.py:817
  32.0 1.3 %collective-permute-start.3 = (f32[36,128]{1,0:T(8,128)S(1)}, f32[36,128]{1,0:T(8,128)S(1)}, u32[]{:S(2)}, u32[]{:S(2)}) collective-permute-start(f32[36,128]{1,0:T(8,128)S(1)} %get-tuple-element.69.refs_0_), channel_id=1, source_target_pairs={{0,24},{2,26},{4,28},{6,30},{8,0},{10,2},{12,4},{14,6},{16,8},{18,... | collective-permute-start | bytes 55304 | tf_op jit(solution)/shard_map/ppermute | solution.py:817
  33.4 0.0 collective-permute-done.1.refs_1_
  33.4 0.7 %collective-permute-done.2.refs_2_ = f32[36,128]{1,0:T(8,128)S(1)} collective-permute-done((f32[36,128]{1,0:T(8,128)S(1)}, f32[36,128]{1,0:T(8,128)S(1)}, u32[]{:S(2)}, u32[]{:S(2)}) %collective-permute-start.2) | collective-permute-done | bytes 18464 | tf_op jit(solution)/shard_map/ppermute | solution.py:817
  34.1 1.7 %collective-permute-done.3.refs_3_ = f32[36,128]{1,0:T(8,128)S(1)} collective-permute-done((f32[36,128]{1,0:T(8,128)S(1)}, f32[36,128]{1,0:T(8,128)S(1)}, u32[]{:S(2)}, u32[]{:S(2)}) %collective-permute-start.3) | collective-permute-done | bytes 18464 | tf_op jit(solution)/shard_map/ppermute | solution.py:817
  35.8 0.1 turn.1
  35.9 8.3 %all_to_all.5.arrived_ref = f32[8,24,128]{2,1,0:T(8,128)S(1)} all-to-all(f32[8,24,128]{2,1,0:T(8,128)S(1)} %turn.1), channel_id=1, replica_groups={{0,1,2,3,4,5,6,7},{8,9,10,11,12,13,14,15},{16,17,18,19,20,21,22,23},{24..., dimensions={0} | all-to-all | bytes 196608 | tf_op jit(solution)/shard_map/all_to_all | solution.py:829
  44.2 0.6 %sum.1 = (f32[3,1,512]{2,1,0:T(1,128)}, f32[3,1,512]{2,1,0:T(1,128)}) custom-call(f32[8,24,128]{2,1,0:T(8,128)S(1)} %all_to_all.5.arrived_ref), custom_call_target="tpu_custom_call" | custom-call | tf_op jit(solution)/shard_map/sum/pallas_call | solution.py:830
Async XLA Ops:
  1.4 4.9 %collective-permute-start = (f32[16,512]{1,0:T(8,128)S(1)}, f32[16,512]{1,0:T(8,128)S(1)}, u32[]{:S(2)}, u32[]{:S(2)}) collective-permute-start(f32[16,512]{1,0:T(8,128)S(1)} %pack.1.refs_0_.block_ref), channel_id=1, source_target_pairs={{0,1},{1,0},{2,3},{3,2},{4,5},{5,4},{6,7},{7,6},{8,9},{9,8},{10,11... | collective-permute-start | bytes 98312 | tf_op jit(solution)/shard_map/ppermute | solution.py:812
  27.3 6.1 %collective-permute-start.1 = (f32[36,128]{1,0:T(8,128)S(1)}, f32[36,128]{1,0:T(8,128)S(1)}, u32[]{:S(2)}, u32[]{:S(2)}) collective-permute-start(f32[36,128]{1,0:T(8,128)S(1)} %get-tuple-element.69.refs_0_), channel_id=1, source_target_pairs={{0,8},{2,10},{4,12},{6,14},{8,16},{10,18},{12,20},{14,22},{16,24},... | collective-permute-start | bytes 55304 | tf_op jit(solution)/shard_map/ppermute | solution.py:817
  29.4 4.7 %collective-permute-start.2 = (f32[36,128]{1,0:T(8,128)S(1)}, f32[36,128]{1,0:T(8,128)S(1)}, u32[]{:S(2)}, u32[]{:S(2)}) collective-permute-start(f32[36,128]{1,0:T(8,128)S(1)} %get-tuple-element.69.refs_0_), channel_id=1, source_target_pairs={{0,16},{2,18},{4,20},{6,22},{8,24},{10,26},{12,28},{14,30},{16,0},... | collective-permute-start | bytes 55304 | tf_op jit(solution)/shard_map/ppermute | solution.py:817
  32.0 3.8 %collective-permute-start.3 = (f32[36,128]{1,0:T(8,128)S(1)}, f32[36,128]{1,0:T(8,128)S(1)}, u32[]{:S(2)}, u32[]{:S(2)}) collective-permute-start(f32[36,128]{1,0:T(8,128)S(1)} %get-tuple-element.69.refs_0_), channel_id=1, source_target_pairs={{0,24},{2,26},{4,28},{6,30},{8,0},{10,2},{12,4},{14,6},{16,8},{18,... | collective-permute-start | bytes 55304 | tf_op jit(solution)/shard_map/ppermute | solution.py:817

commit v18 on v16

--- a/solution.py
+++ b/solution.py
@@ -807,9 +807,9 @@
         blocks.append(lax.ppermute(block, "space", [(i, (i - offset) % domains) for i in range(domains)]))
     chosen = choose(block, embedding, radial_one, radial_two, mix_one, mix_two, read_one, read_two)
     pushed, masses = pushes(plan, blocks, moment_rows, chosen)
-    sources = [pushed]
-    for z in range(1, outer):
-        sources.append(lax.ppermute(pushed, "bead", [(b, (b + z * inner) % beads) for b in range(beads)]))
+    sources = [pushed] * outer
+    for z in sorted(range(1, outer), key=lambda z: -min(z, outer - z)):
+        sources[z] = lax.ppermute(pushed, "bead", [(b, (b + z * inner) % beads) for b in range(beads)])
     here = [lax.axis_index(axis).astype(jnp.int32).reshape(1) for axis in ("bead", "space")]
     lines = line_count(atoms)
     messages = pl.pallas_call(

time: 44.6 us -> 44.6 us (level)
  no operation moved by 1% of the time
where the time goes in v18:
time: 44.6 us; the launch traced here: 44.3 us
  Pallas kernels  23.4 us (52%)
  starting transfers between devices  9.1 us (20%)
  blocking collectives  8.33 us (19%)
  waiting for transfers between devices  2.75 us (6%)
  between operations  0.7 us (2%)
    pallas_call x9, Pallas kernels, run(): pl.pallas_call(body, out_shape=tuple((jax.ShapeDtypeStruct(shape, dtype)...  21.9 us
    all_to_all x1, blocking collectives, shards(): lax.all_to_all(messages, ('bead', 'space'), 0, 0, axis_index_groups=rows,...  8.33 us
    ppermute x3, starting transfers between devices, shards(): lax.ppermute(pushed, 'bead', [(b, (b + z * inner) % beads) for b in range...  6.07 us
    ppermute x1, starting transfers between devices, shards(): lax.ppermute(block, 'space', [(i, (i - offset) % domains) for i in range(...  3.03 us
    ppermute x3, waiting for transfers between devices, shards(): lax.ppermute(pushed, 'bead', [(b, (b + z * inner) % beads) for b in range...  2.43 us
  transfers between devices with their start and end apart: 4, of which 3 were waited for; matrix products, arithmetic and copies ran while one was open for 0% of the time, Pallas kernels for 4%

profile of v18, /device:TPU:0, one launch (start us, length us, event | category | flops | bytes accessed | tf_op | source)
XLA Modules:
  0.0 44.3 jit_solution(15693284537280723316)
XLA Ops:
  0.6 0.8 %pack.1.refs_0_.block_ref = f32[16,512]{1,0:T(8,128)S(1)} custom-call(f32[3,1,512]{2,1,0:T(1,128)} %bitcast.10, s32[1,512]{1,0:T(1,128)} %bitcast.12, s32[1,512]{1,0:T(1,128)} %bitcast.13, s32[8,512]{1,0:T(8,128)} %slot_src.1), custom_call_target="tpu_custom_call" | custom-call | tf_op jit(solution)/shard_map/pack/pallas_call | solution.py:790
  1.4 3.0 %collective-permute-start = (f32[16,512]{1,0:T(8,128)S(1)}, f32[16,512]{1,0:T(8,128)S(1)}, u32[]{:S(2)}, u32[]{:S(2)}) collective-permute-start(f32[16,512]{1,0:T(8,128)S(1)} %pack.1.refs_0_.block_ref), channel_id=1, source_target_pairs={{0,1},{1,0},{2,3},{3,2},{4,5},{5,4},{6,7},{7,6},{8,9},{9,8},{10,11... | collective-permute-start | bytes 98312 | tf_op jit(solution)/shard_map/ppermute | solution.py:807
  4.5 1.6 %choose.1 = (bf16[1024,4096]{1,0:T(8,128)(2,1)S(1)}, bf16[128,96]{1,0:T(8,128)(2,1)S(1)}, bf16[128,48]{1,0:T(8,128)(2,1)S(1)}, f32[128,128]{1,0:T(8,128)S(1)}, b...) custom-call(f32[16,512]{1,0:T(8,128)S(1)} %pack.1.refs_0_.block_ref, ...), custom_call_target="tpu_custom_call" | custom-call | flops 2000000000 | bytes 2000000 | tf_op jit(solution)/shard_map/choose/pallas_call | solution.py:568
  6.1 0.3 collective-permute-done.refs_1_
  6.4 1.8 %edges.1 = (f32[6,8,1024]{2,1,0:T(8,128)S(1)}, f32[8,8,1024]{2,1,0:T(8,128)S(1)}, f32[8,8,8,512]{3,2,1,0:T(8,128)S(1)}, f32[3,8,8,512]{3,2,1,0:T(8,128)S(1)}, f3...) custom-call(f32[16,512]{1,0:T(8,128)S(1)} %pack.1.refs_0_.block_ref,, ...), custom_call_target="tpu_custom_call" | custom-call | tf_op jit(solution)/shard_map/edges/pallas_call | solution.py:568
  8.2 1.9 %first.1 = (f32[9,128,1024]{2,1,0:T(8,128)S(1)}, f32[128,1024]{1,0:T(8,128)S(1)}, f32[128,1024]{1,0:T(8,128)S(1)}, bf16[384,1024]{1,0:T(8,128)(2,1)S(1)}) custom-call(f32[16,512]{1,0:T(8,128)S(1)} %pack.1.refs_0_.block_ref, f32[16,512]{1,0:T(8,128)S(1)} %collective-permute-done.refs_1_, bf16[9,96,1024]{2,1,0:T(8,128)(2,1)S(1)} %get-tuple-element.43.refs_2_, ...), custom_call_target="tpu_custom_call" | custom-call | tf_op jit(solution)/shard_map/first/pallas_call | solution.py:568
  10.2 2.8 %gather.1 = (f32[128,4096]{1,0:T(8,128)S(1)}, f32[128,4096]{1,0:T(8,128)S(1)}, f32[128,4096]{1,0:T(8,128)S(1)}, f32[128,4096]{1,0:T(8,128)S(1)}) custom-call(f32[128,1024]{1,0:T(8,128)S(1)} %get-tuple-element.47.hid_ref, bf16[384,1024]{1,0:T(8,128)(2,1)S(1)} %get-tuple-element.48.hs_ref, bf16[1024,4096]{1,0:T(8,128)(2,1)S(1)} %get-tuple-element.41.oh_ref, ...), custom_call_target="tpu_custom_call" | custom-call | tf_op jit(solution)/shard_map/gather/pallas_call | solution.py:568
  13.0 3.2 %moments.1 = (f32[9,128,512]{2,1,0:T(8,128)S(1)}, f32[384,512]{1,0:T(8,128)S(1)}) custom-call(f32[128,4096]{1,0:T(8,128)S(1)} %get-tuple-element.51.car_ref, f32[8,8,8,512]{3,2,1,0:T(8,128)S(1)} %get-tuple-element.52.yb_ref, bf16[2,128,2304]{2,1,0:T(8,128)(2,1)S(1)} %get-tuple-element.46.refs_5_.mixa_ref, ...), custom_call_target="tpu_custom_call" | custom-call | tf_op jit(solution)/shard_map/moments/pallas_call | solution.py:568
  16.2 3.9 %back_second.1 = (bf16[256,4096]{1,0:T(8,128)(2,1)S(1)}, f32[4,64,512]{2,1,0:T(8,128)S(1)}) custom-call(f32[9,128,512]{2,1,0:T(8,128)S(1)} %get-tuple-element.54.m2_ref, f32[384,512]{1,0:T(8,128)S(1)} %get-tuple-element.55.dinv_ref, f32[128,4096]{1,0:T(8,128)S(1)} %get-tuple-element.51.car_ref, f32[128,4096]{1,0:T(8,128)S(1)} %get-tuple-element.56.hj_ref, ...), custom_call_target="tpu_custom_call" | custom-call | tf_op jit(solution)/shard_map/back_second/pallas_call | solution.py:568
  20.0 3.0 %scatter.1 = (f32[128,1024]{1,0:T(8,128)S(1)}, f32[32,512]{1,0:T(8,128)S(1)}, bf16[128,8192]{1,0:T(8,128)(2,1)S(1)}) custom-call(bf16[1024,4096]{1,0:T(8,128)(2,1)S(1)} %get-tuple-element.41.oh_ref, bf16[1024,512]{1,0:T(8,128)(2,1)S(1)} %get-tuple-element.42.pick_ref, bf16[256,4096]{1,0:T(8,128)(2,1)S(1)} %get-tuple-element.60.dhe_ref, ...), custom_call_target="tpu_custom_call" | custom-call | tf_op jit(solution)/shard_map/scatter/pallas_call | solution.py:568
  23.0 2.0 %back_first.1.refs_7_ = f32[9,16,1024]{2,1,0:T(8,128)S(1)} custom-call(f32[128,1024]{1,0:T(8,128)S(1)} %get-tuple-element.62.dh_ref, f32[128,1024]{1,0:T(8,128)S(1)} %get-tuple-element.63.sp1_ref, f32[9,128,1024]{2,1,0:T(8,128)S(1)} %get-tuple-element.64.m1_ref, bf16[2,3,128,384]{3,2,1,0:T(8,128)(2,1)S(1)} %get-tuple-element.53.mixt_ref, ...), custom_call_target="tpu_custom_call" | custom-call | tf_op jit(solution)/shard_map/back_first/pallas_call | solution.py:568
  25.0 1.8 %back_edges.1 = (f32[36,128]{1,0:T(8,128)S(1)}, f32[24,128]{1,0:T(8,128)S(1)}) custom-call(f32[16,512]{1,0:T(8,128)S(1)} %pack.1.refs_0_.block_ref, f32[16,512]{1,0:T(8,128)S(1)} %collective-permute-done.refs_1_, f32[3,1,512]{2,1,0:T(1,128)} %bitcast.11, f32[6,8,1024]{2,1,0:T(8,128)S(1)} %get-tuple-element.37.geo_ref.refs_3_, ...), custom_call_target="tpu_custom_call" | custom-call | tf_op jit(solution)/shard_map/back_edges/pallas_call | solution.py:568
  26.8 2.1 %collective-permute-start.1 = (f32[36,128]{1,0:T(8,128)S(1)}, f32[36,128]{1,0:T(8,128)S(1)}, u32[]{:S(2)}, u32[]{:S(2)}) collective-permute-start(f32[36,128]{1,0:T(8,128)S(1)} %get-tuple-element.69.refs_0_), channel_id=1, source_target_pairs={{0,8},{2,10},{4,12},{6,14},{8,16},{10,18},{12,20},{14,22},{16,24},... | collective-permute-start | bytes 55304 | tf_op jit(solution)/shard_map/ppermute | solution.py:812
  28.9 2.6 %collective-permute-start.2 = (f32[36,128]{1,0:T(8,128)S(1)}, f32[36,128]{1,0:T(8,128)S(1)}, u32[]{:S(2)}, u32[]{:S(2)}) collective-permute-start(f32[36,128]{1,0:T(8,128)S(1)} %get-tuple-element.69.refs_0_), channel_id=1, source_target_pairs={{0,16},{2,18},{4,20},{6,22},{8,24},{10,26},{12,28},{14,30},{16,0},... | collective-permute-start | bytes 55304 | tf_op jit(solution)/shard_map/ppermute | solution.py:812
  31.5 1.4 %collective-permute-start.3 = (f32[36,128]{1,0:T(8,128)S(1)}, f32[36,128]{1,0:T(8,128)S(1)}, u32[]{:S(2)}, u32[]{:S(2)}) collective-permute-start(f32[36,128]{1,0:T(8,128)S(1)} %get-tuple-element.69.refs_0_), channel_id=1, source_target_pairs={{0,24},{2,26},{4,28},{6,30},{8,0},{10,2},{12,4},{14,6},{16,8},{18,... | collective-permute-start | bytes 55304 | tf_op jit(solution)/shard_map/ppermute | solution.py:812
  32.8 0.0 collective-permute-done.1.refs_1_
  32.8 0.7 %collective-permute-done.2.refs_2_ = f32[36,128]{1,0:T(8,128)S(1)} collective-permute-done((f32[36,128]{1,0:T(8,128)S(1)}, f32[36,128]{1,0:T(8,128)S(1)}, u32[]{:S(2)}, u32[]{:S(2)}) %collective-permute-start.2) | collective-permute-done | bytes 18464 | tf_op jit(solution)/shard_map/ppermute | solution.py:812
  33.6 1.7 %collective-permute-done.3.refs_3_ = f32[36,128]{1,0:T(8,128)S(1)} collective-permute-done((f32[36,128]{1,0:T(8,128)S(1)}, f32[36,128]{1,0:T(8,128)S(1)}, u32[]{:S(2)}, u32[]{:S(2)}) %collective-permute-start.3) | collective-permute-done | bytes 18464 | tf_op jit(solution)/shard_map/ppermute | solution.py:812
  35.3 0.1 turn.1
  35.3 8.3 %all_to_all.5.arrived_ref = f32[8,24,128]{2,1,0:T(8,128)S(1)} all-to-all(f32[8,24,128]{2,1,0:T(8,128)S(1)} %turn.1), channel_id=1, replica_groups={{0,1,2,3,4,5,6,7},{8,9,10,11,12,13,14,15},{16,17,18,19,20,21,22,23},{24..., dimensions={0} | all-to-all | bytes 196608 | tf_op jit(solution)/shard_map/all_to_all | solution.py:824
  43.7 0.6 %sum.1 = (f32[3,1,512]{2,1,0:T(1,128)}, f32[3,1,512]{2,1,0:T(1,128)}) custom-call(f32[8,24,128]{2,1,0:T(8,128)S(1)} %all_to_all.5.arrived_ref), custom_call_target="tpu_custom_call" | custom-call | tf_op jit(solution)/shard_map/sum/pallas_call | solution.py:825
Async XLA Ops:
  1.4 4.9 %collective-permute-start = (f32[16,512]{1,0:T(8,128)S(1)}, f32[16,512]{1,0:T(8,128)S(1)}, u32[]{:S(2)}, u32[]{:S(2)}) collective-permute-start(f32[16,512]{1,0:T(8,128)S(1)} %pack.1.refs_0_.block_ref), channel_id=1, source_target_pairs={{0,1},{1,0},{2,3},{3,2},{4,5},{5,4},{6,7},{7,6},{8,9},{9,8},{10,11... | collective-permute-start | bytes 98312 | tf_op jit(solution)/shard_map/ppermute | solution.py:807
  26.8 6.1 %collective-permute-start.1 = (f32[36,128]{1,0:T(8,128)S(1)}, f32[36,128]{1,0:T(8,128)S(1)}, u32[]{:S(2)}, u32[]{:S(2)}) collective-permute-start(f32[36,128]{1,0:T(8,128)S(1)} %get-tuple-element.69.refs_0_), channel_id=1, source_target_pairs={{0,8},{2,10},{4,12},{6,14},{8,16},{10,18},{12,20},{14,22},{16,24},... | collective-permute-start | bytes 55304 | tf_op jit(solution)/shard_map/ppermute | solution.py:812
  28.9 4.7 %collective-permute-start.2 = (f32[36,128]{1,0:T(8,128)S(1)}, f32[36,128]{1,0:T(8,128)S(1)}, u32[]{:S(2)}, u32[]{:S(2)}) collective-permute-start(f32[36,128]{1,0:T(8,128)S(1)} %get-tuple-element.69.refs_0_), channel_id=1, source_target_pairs={{0,16},{2,18},{4,20},{6,22},{8,24},{10,26},{12,28},{14,30},{16,0},... | collective-permute-start | bytes 55304 | tf_op jit(solution)/shard_map/ppermute | solution.py:812
  31.5 3.8 %collective-permute-start.3 = (f32[36,128]{1,0:T(8,128)S(1)}, f32[36,128]{1,0:T(8,128)S(1)}, u32[]{:S(2)}, u32[]{:S(2)}) collective-permute-start(f32[36,128]{1,0:T(8,128)S(1)} %get-tuple-element.69.refs_0_), channel_id=1, source_target_pairs={{0,24},{2,26},{4,28},{6,30},{8,0},{10,2},{12,4},{14,6},{16,8},{18,... | collective-permute-start | bytes 55304 | tf_op jit(solution)/shard_map/ppermute | solution.py:812

commit v19 on v18

--- a/solution.py
+++ b/solution.py
@@ -372,7 +372,7 @@
     chan, atoms = m2_ref.shape[1:]
     tiles = atoms // LANES
     pairs = chan // 16
-    per_turn = 4 if pairs % 4 == 0 else 1
+    per_turn = 8 if pairs % 8 == 0 else 1
     k_step = slots // 2
 
     def back_moments(t, carry):

time: 44.6 us -> 44.7 us (level)
  no operation moved by 1% of the time
where the time goes in v19:
time: 44.7 us; the launch traced here: 44.4 us
  Pallas kernels  23.5 us (53%)
  starting transfers between devices  9.1 us (20%)
  blocking collectives  8.33 us (19%)
  waiting for transfers between devices  2.75 us (6%)
  between operations  0.7 us (2%)
    pallas_call x9, Pallas kernels, run(): pl.pallas_call(body, out_shape=tuple((jax.ShapeDtypeStruct(shape, dtype)...  22 us
    all_to_all x1, blocking collectives, shards(): lax.all_to_all(messages, ('bead', 'space'), 0, 0, axis_index_groups=rows,...  8.33 us
    ppermute x3, starting transfers between devices, shards(): lax.ppermute(pushed, 'bead', [(b, (b + z * inner) % beads) for b in range...  6.07 us
    ppermute x1, starting transfers between devices, shards(): lax.ppermute(block, 'space', [(i, (i - offset) % domains) for i in range(...  3.03 us
    ppermute x3, waiting for transfers between devices, shards(): lax.ppermute(pushed, 'bead', [(b, (b + z * inner) % beads) for b in range...  2.43 us
  transfers between devices with their start and end apart: 4, of which 3 were waited for; matrix products, arithmetic and copies ran while one was open for 0% of the time, Pallas kernels for 4%

profile of v19, /device:TPU:0, one launch (start us, length us, event | category | flops | bytes accessed | tf_op | source)
XLA Modules:
  0.0 44.4 jit_solution(5149266047338540046)
XLA Ops:
  0.6 0.8 %pack.1.refs_0_.block_ref = f32[16,512]{1,0:T(8,128)S(1)} custom-call(f32[3,1,512]{2,1,0:T(1,128)} %bitcast.10, s32[1,512]{1,0:T(1,128)} %bitcast.12, s32[1,512]{1,0:T(1,128)} %bitcast.13, s32[8,512]{1,0:T(8,128)} %slot_src.1), custom_call_target="tpu_custom_call" | custom-call | tf_op jit(solution)/shard_map/pack/pallas_call | solution.py:790
  1.4 3.0 %collective-permute-start = (f32[16,512]{1,0:T(8,128)S(1)}, f32[16,512]{1,0:T(8,128)S(1)}, u32[]{:S(2)}, u32[]{:S(2)}) collective-permute-start(f32[16,512]{1,0:T(8,128)S(1)} %pack.1.refs_0_.block_ref), channel_id=1, source_target_pairs={{0,1},{1,0},{2,3},{3,2},{4,5},{5,4},{6,7},{7,6},{8,9},{9,8},{10,11... | collective-permute-start | bytes 98312 | tf_op jit(solution)/shard_map/ppermute | solution.py:807
  4.5 1.6 %choose.1 = (bf16[1024,4096]{1,0:T(8,128)(2,1)S(1)}, bf16[128,96]{1,0:T(8,128)(2,1)S(1)}, bf16[128,48]{1,0:T(8,128)(2,1)S(1)}, f32[128,128]{1,0:T(8,128)S(1)}, b...) custom-call(f32[16,512]{1,0:T(8,128)S(1)} %pack.1.refs_0_.block_ref, ...), custom_call_target="tpu_custom_call" | custom-call | flops 2000000000 | bytes 2000000 | tf_op jit(solution)/shard_map/choose/pallas_call | solution.py:568
  6.1 0.3 collective-permute-done.refs_1_
  6.4 1.8 %edges.1 = (f32[6,8,1024]{2,1,0:T(8,128)S(1)}, f32[8,8,1024]{2,1,0:T(8,128)S(1)}, f32[8,8,8,512]{3,2,1,0:T(8,128)S(1)}, f32[3,8,8,512]{3,2,1,0:T(8,128)S(1)}, f3...) custom-call(f32[16,512]{1,0:T(8,128)S(1)} %pack.1.refs_0_.block_ref,, ...), custom_call_target="tpu_custom_call" | custom-call | tf_op jit(solution)/shard_map/edges/pallas_call | solution.py:568
  8.2 1.9 %first.1 = (f32[9,128,1024]{2,1,0:T(8,128)S(1)}, f32[128,1024]{1,0:T(8,128)S(1)}, f32[128,1024]{1,0:T(8,128)S(1)}, bf16[384,1024]{1,0:T(8,128)(2,1)S(1)}) custom-call(f32[16,512]{1,0:T(8,128)S(1)} %pack.1.refs_0_.block_ref, f32[16,512]{1,0:T(8,128)S(1)} %collective-permute-done.refs_1_, bf16[9,96,1024]{2,1,0:T(8,128)(2,1)S(1)} %get-tuple-element.43.refs_2_, ...), custom_call_target="tpu_custom_call" | custom-call | tf_op jit(solution)/shard_map/first/pallas_call | solution.py:568
  10.2 2.8 %gather.1 = (f32[128,4096]{1,0:T(8,128)S(1)}, f32[128,4096]{1,0:T(8,128)S(1)}, f32[128,4096]{1,0:T(8,128)S(1)}, f32[128,4096]{1,0:T(8,128)S(1)}) custom-call(f32[128,1024]{1,0:T(8,128)S(1)} %get-tuple-element.47.hid_ref, bf16[384,1024]{1,0:T(8,128)(2,1)S(1)} %get-tuple-element.48.hs_ref, bf16[1024,4096]{1,0:T(8,128)(2,1)S(1)} %get-tuple-element.41.oh_ref, ...), custom_call_target="tpu_custom_call" | custom-call | tf_op jit(solution)/shard_map/gather/pallas_call | solution.py:568
  13.0 3.2 %moments.1 = (f32[9,128,512]{2,1,0:T(8,128)S(1)}, f32[384,512]{1,0:T(8,128)S(1)}) custom-call(f32[128,4096]{1,0:T(8,128)S(1)} %get-tuple-element.51.car_ref, f32[8,8,8,512]{3,2,1,0:T(8,128)S(1)} %get-tuple-element.52.yb_ref, bf16[2,128,2304]{2,1,0:T(8,128)(2,1)S(1)} %get-tuple-element.46.refs_5_.mixa_ref, ...), custom_call_target="tpu_custom_call" | custom-call | tf_op jit(solution)/shard_map/moments/pallas_call | solution.py:568
  16.2 3.9 %back_second.1 = (bf16[256,4096]{1,0:T(8,128)(2,1)S(1)}, f32[4,64,512]{2,1,0:T(8,128)S(1)}) custom-call(f32[9,128,512]{2,1,0:T(8,128)S(1)} %get-tuple-element.54.m2_ref, f32[384,512]{1,0:T(8,128)S(1)} %get-tuple-element.55.dinv_ref, f32[128,4096]{1,0:T(8,128)S(1)} %get-tuple-element.51.car_ref, f32[128,4096]{1,0:T(8,128)S(1)} %get-tuple-element.56.hj_ref, ...), custom_call_target="tpu_custom_call" | custom-call | tf_op jit(solution)/shard_map/back_second/pallas_call | solution.py:568
  20.1 3.0 %scatter.1 = (f32[128,1024]{1,0:T(8,128)S(1)}, f32[32,512]{1,0:T(8,128)S(1)}, bf16[128,8192]{1,0:T(8,128)(2,1)S(1)}) custom-call(bf16[1024,4096]{1,0:T(8,128)(2,1)S(1)} %get-tuple-element.41.oh_ref, bf16[1024,512]{1,0:T(8,128)(2,1)S(1)} %get-tuple-element.42.pick_ref, bf16[256,4096]{1,0:T(8,128)(2,1)S(1)} %get-tuple-element.60.dhe_ref, ...), custom_call_target="tpu_custom_call" | custom-call | tf_op jit(solution)/shard_map/scatter/pallas_call | solution.py:568
  23.1 2.0 %back_first.1.refs_7_ = f32[9,16,1024]{2,1,0:T(8,128)S(1)} custom-call(f32[128,1024]{1,0:T(8,128)S(1)} %get-tuple-element.62.dh_ref, f32[128,1024]{1,0:T(8,128)S(1)} %get-tuple-element.63.sp1_ref, f32[9,128,1024]{2,1,0:T(8,128)S(1)} %get-tuple-element.64.m1_ref, bf16[2,3,128,384]{3,2,1,0:T(8,128)(2,1)S(1)} %get-tuple-element.53.mixt_ref, ...), custom_call_target="tpu_custom_call" | custom-call | tf_op jit(solution)/shard_map/back_first/pallas_call | solution.py:568
  25.1 1.8 %back_edges.1 = (f32[36,128]{1,0:T(8,128)S(1)}, f32[24,128]{1,0:T(8,128)S(1)}) custom-call(f32[16,512]{1,0:T(8,128)S(1)} %pack.1.refs_0_.block_ref, f32[16,512]{1,0:T(8,128)S(1)} %collective-permute-done.refs_1_, f32[3,1,512]{2,1,0:T(1,128)} %bitcast.11, f32[6,8,1024]{2,1,0:T(8,128)S(1)} %get-tuple-element.37.geo_ref.refs_3_, ...), custom_call_target="tpu_custom_call" | custom-call | tf_op jit(solution)/shard_map/back_edges/pallas_call | solution.py:568
  26.8 2.1 %collective-permute-start.1 = (f32[36,128]{1,0:T(8,128)S(1)}, f32[36,128]{1,0:T(8,128)S(1)}, u32[]{:S(2)}, u32[]{:S(2)}) collective-permute-start(f32[36,128]{1,0:T(8,128)S(1)} %get-tuple-element.69.refs_0_), channel_id=1, source_target_pairs={{0,8},{2,10},{4,12},{6,14},{8,16},{10,18},{12,20},{14,22},{16,24},... | collective-permute-start | bytes 55304 | tf_op jit(solution)/shard_map/ppermute | solution.py:812
  29.0 2.6 %collective-permute-start.2 = (f32[36,128]{1,0:T(8,128)S(1)}, f32[36,128]{1,0:T(8,128)S(1)}, u32[]{:S(2)}, u32[]{:S(2)}) collective-permute-start(f32[36,128]{1,0:T(8,128)S(1)} %get-tuple-element.69.refs_0_), channel_id=1, source_target_pairs={{0,16},{2,18},{4,20},{6,22},{8,24},{10,26},{12,28},{14,30},{16,0},... | collective-permute-start | bytes 55304 | tf_op jit(solution)/shard_map/ppermute | solution.py:812
  31.6 1.4 %collective-permute-start.3 = (f32[36,128]{1,0:T(8,128)S(1)}, f32[36,128]{1,0:T(8,128)S(1)}, u32[]{:S(2)}, u32[]{:S(2)}) collective-permute-start(f32[36,128]{1,0:T(8,128)S(1)} %get-tuple-element.69.refs_0_), channel_id=1, source_target_pairs={{0,24},{2,26},{4,28},{6,30},{8,0},{10,2},{12,4},{14,6},{16,8},{18,... | collective-permute-start | bytes 55304 | tf_op jit(solution)/shard_map/ppermute | solution.py:812
  32.9 0.0 collective-permute-done.1.refs_1_
  32.9 0.7 %collective-permute-done.2.refs_2_ = f32[36,128]{1,0:T(8,128)S(1)} collective-permute-done((f32[36,128]{1,0:T(8,128)S(1)}, f32[36,128]{1,0:T(8,128)S(1)}, u32[]{:S(2)}, u32[]{:S(2)}) %collective-permute-start.2) | collective-permute-done | bytes 18464 | tf_op jit(solution)/shard_map/ppermute | solution.py:812
  33.7 1.7 %collective-permute-done.3.refs_3_ = f32[36,128]{1,0:T(8,128)S(1)} collective-permute-done((f32[36,128]{1,0:T(8,128)S(1)}, f32[36,128]{1,0:T(8,128)S(1)}, u32[]{:S(2)}, u32[]{:S(2)}) %collective-permute-start.3) | collective-permute-done | bytes 18464 | tf_op jit(solution)/shard_map/ppermute | solution.py:812
  35.3 0.1 turn.1
  35.4 8.3 %all_to_all.5.arrived_ref = f32[8,24,128]{2,1,0:T(8,128)S(1)} all-to-all(f32[8,24,128]{2,1,0:T(8,128)S(1)} %turn.1), channel_id=1, replica_groups={{0,1,2,3,4,5,6,7},{8,9,10,11,12,13,14,15},{16,17,18,19,20,21,22,23},{24..., dimensions={0} | all-to-all | bytes 196608 | tf_op jit(solution)/shard_map/all_to_all | solution.py:824
  43.7 0.6 %sum.1 = (f32[3,1,512]{2,1,0:T(1,128)}, f32[3,1,512]{2,1,0:T(1,128)}) custom-call(f32[8,24,128]{2,1,0:T(8,128)S(1)} %all_to_all.5.arrived_ref), custom_call_target="tpu_custom_call" | custom-call | tf_op jit(solution)/shard_map/sum/pallas_call | solution.py:825
Async XLA Ops:
  1.4 4.9 %collective-permute-start = (f32[16,512]{1,0:T(8,128)S(1)}, f32[16,512]{1,0:T(8,128)S(1)}, u32[]{:S(2)}, u32[]{:S(2)}) collective-permute-start(f32[16,512]{1,0:T(8,128)S(1)} %pack.1.refs_0_.block_ref), channel_id=1, source_target_pairs={{0,1},{1,0},{2,3},{3,2},{4,5},{5,4},{6,7},{7,6},{8,9},{9,8},{10,11... | collective-permute-start | bytes 98312 | tf_op jit(solution)/shard_map/ppermute | solution.py:807
  26.8 6.1 %collective-permute-start.1 = (f32[36,128]{1,0:T(8,128)S(1)}, f32[36,128]{1,0:T(8,128)S(1)}, u32[]{:S(2)}, u32[]{:S(2)}) collective-permute-start(f32[36,128]{1,0:T(8,128)S(1)} %get-tuple-element.69.refs_0_), channel_id=1, source_target_pairs={{0,8},{2,10},{4,12},{6,14},{8,16},{10,18},{12,20},{14,22},{16,24},... | collective-permute-start | bytes 55304 | tf_op jit(solution)/shard_map/ppermute | solution.py:812
  29.0 4.7 %collective-permute-start.2 = (f32[36,128]{1,0:T(8,128)S(1)}, f32[36,128]{1,0:T(8,128)S(1)}, u32[]{:S(2)}, u32[]{:S(2)}) collective-permute-start(f32[36,128]{1,0:T(8,128)S(1)} %get-tuple-element.69.refs_0_), channel_id=1, source_target_pairs={{0,16},{2,18},{4,20},{6,22},{8,24},{10,26},{12,28},{14,30},{16,0},... | collective-permute-start | bytes 55304 | tf_op jit(solution)/shard_map/ppermute | solution.py:812
  31.6 3.8 %collective-permute-start.3 = (f32[36,128]{1,0:T(8,128)S(1)}, f32[36,128]{1,0:T(8,128)S(1)}, u32[]{:S(2)}, u32[]{:S(2)}) collective-permute-start(f32[36,128]{1,0:T(8,128)S(1)} %get-tuple-element.69.refs_0_), channel_id=1, source_target_pairs={{0,24},{2,26},{4,28},{6,30},{8,0},{10,2},{12,4},{14,6},{16,8},{18,... | collective-permute-start | bytes 55304 | tf_op jit(solution)/shard_map/ppermute | solution.py:812
